TPU v7x, 32 devices: a whole 2x2x4 slice. The times are simulated.
32 devices in a mesh: groups: 2 (over y), frame: 4 (over z), panel: 2 (over x), sub: 2 (over core).
Axes of the slice: x: 2, y: 2, z: 4, core: 2. Of those that a mesh axis runs over, the one named last changes fastest.
Arguments:
- frames: bfloat16 [2048, 65536], P(('groups', 'frame'), ('panel', 'sub')), parts along dimension 0, may hold values from -16 to 16
- slices: float32 [32, 65536], P(('groups', 'frame'), ('panel', 'sub')), parts along dimension 0, may hold values from -8 to 8
- log_prior: float32 [4096], replicated, may hold values from -2 to 2
- orient: int32 [32], P('groups'), parts along dimension 0, may hold values from 0 to 4095
Outputs:
- new_slices: float32 [32, 65536], P(('groups', 'frame'), ('panel', 'sub')), parts along dimension 0
There are 2 independent parts, one for each index of `groups`. A program takes and returns all parts, laid end to end along the dimension named above; an argument that names none is the same for every part. Nothing has to cross between parts.
All inputs are finite; a program needn't handle non-finite values.
Results may differ from a plain program's by a relative error of at most 0.022.
The roundings to bfloat16 on the way count: a program that leaves them out, or rounds other values in their place, can miss the bound.
Values may be sent and summed in bfloat16 or wider, within the bound.
No kernel may reach another device: no remote copies, remote signals or barrier semaphores. Data moves between devices by JAX's collectives and lax.ppermute only.
A program may use at most 64 MiB of HBM per device.

v0:
```python
import math

import jax
import jax.numpy as jnp
from jax import lax
from jax.sharding import PartitionSpec as P

PIX = 65536
ITERS = 2


def fetch_slices(owned_b):
    return lax.all_gather(owned_b, "frame", axis=0, tiled=True)


def owner_update(weights, frames, counts, owned_b, offset):
    owned = owned_b.shape[0]
    mine = lax.psum_scatter(
        jnp.einsum("fm,fp->mp", weights, frames, preferred_element_type=jnp.float32).astype(
            jnp.bfloat16
        ),
        "frame",
        scatter_dimension=0,
        tiled=True,
    ).astype(jnp.float32)
    my_counts = lax.dynamic_slice_in_dim(counts, offset, owned, 0)
    return (mine + owned_b.astype(jnp.float32)) / (my_counts + 1.0)[:, None]


def local(frames, slices, log_prior, orient):
    owned = slices.shape[0]
    temper = 3.0 / math.sqrt(PIX)
    matches = orient[:, None] == jnp.arange(log_prior.shape[0], dtype=jnp.int32)[None, :]
    prior = jnp.sum(jnp.where(matches, log_prior[None, :], 0.0), axis=1)
    offset = lax.axis_index("frame") * owned
    current = slices
    owned_b = slices.astype(jnp.bfloat16)
    for step in range(ITERS):
        if step == 0:
            gathered = fetch_slices(owned_b)
        else:
            gathered = fetch_slices(owned_b)
        wide = gathered.astype(jnp.float32)
        norms = jnp.sum(wide * wide, axis=1)
        raw = (
            jnp.einsum("fp,mp->fm", frames, gathered, preferred_element_type=jnp.float32)
            - 0.5 * norms[None, :]
        )
        summed = lax.psum(raw, ("panel", "sub"))
        weights = jax.nn.softmax(temper * summed + prior[None, :], axis=1).astype(jnp.bfloat16)
        counts = lax.psum(jnp.sum(weights.astype(jnp.float32), axis=0), "frame")
        if step + 1 < ITERS:
            current = owner_update(weights, frames, counts, owned_b, offset)
            owned_b = current.astype(jnp.bfloat16)
        else:
            current = owner_update(weights, frames, counts, owned_b, offset)
    return current


def solution(mesh):
    in_specs = (
        P(("groups", "frame"), ("panel", "sub")),
        P(("groups", "frame"), ("panel", "sub")),
        P(),
        P("groups"),
    )
    out_specs = P(("groups", "frame"), ("panel", "sub"))
    return jax.shard_map(local, mesh=mesh, in_specs=in_specs, out_specs=out_specs, check_vma=False)
```

profile of v0, /device:TPU:0, one launch (start us, length us, event | category | flops | bytes accessed | tf_op | source)
XLA Modules:
  0.0 173.9 jit_solution(4613914813418080331)
XLA Ops:
  6.5 0.0 copy-start.2
  6.5 0.0 copy-start.1
  6.5 0.0 all-reduce.5.cloned.1.call-start
  6.5 1.0 convert_bitcast_fusion
  7.6 17.4 %all-gather = bf16[4,4,16384]{2,1,0:T(4,128)(2,1)S(1)} all-gather(bf16[1,4,16384]{2,1,0:T(4,128)(2,1)S(1)} %convert_bitcast_fusion), channel_id=1, replica_groups=mesh['groups'=2,'frame'=4,'panel'=2,'sub'=2] {'frame'}, dimensions={0}, use_global_device_ids=true | all-gather | bytes 655360 | tf_op jit(solution)/shard_map/all_gather | solution.py:13
  24.9 0.1 reshape.18
  25.1 0.2 multiply_reduce_fusion.1
  25.3 0.0 copy-start.3
  25.3 0.0 copy-start
  25.3 5.7 %convolution_subtract_fusion.1 = f32[256,16]{0,1:T(8,128)S(1)} fusion(bf16[256,16384]{1,0:T(8,128)(2,1)} %param.4, bf16[16,16384]{1,0:T(8,128)(2,1)S(1)} %reshape.18, f32[16]{0:T(128)S(1)} %broadcast_multiply_fusion.1), kind=kOutput, calls=%fused_computation.4 | convolution fusion | flops 134221824 | bytes 8929344 | tf_op jit(solution)/shard_map/fp,mp->fm/dot_general | solution.py:46
  31.0 10.1 %psum.28 = f32[256,16]{0,1:T(8,128)S(1)} all-reduce(f32[256,16]{0,1:T(8,128)S(1)} %convolution_subtract_fusion.1), channel_id=1, replica_groups=mesh['groups'=2,'frame'=4,'panel'=2,'sub'=2] {'panel','sub'}, use_global_device_ids=true, to_apply=%region_1.2 | all-reduce | flops 4096 | bytes 32768 | tf_op jit(solution)/shard_map/psum | solution.py:49
  41.1 0.0 copy-done.2
  41.1 0.0 copy-done.1
  41.1 0.2 select_reduce_fusion
  41.4 0.1 fusion.2
  41.5 0.1 fusion.4
  41.6 0.2 convert_reduce_fusion.1
  41.7 5.4 %convolution_convert_fusion.1 = bf16[16,16384]{1,0:T(8,128)(2,1)} fusion(bf16[256,16]{0,1:T(8,128)(2,1)S(1)} %get-tuple-element.8, bf16[256,16384]{1,0:T(8,128)(2,1)} %param.4), kind=kOutput, calls=%fused_computation.1 | convolution fusion | flops 134479872 | bytes 8921088 | tf_op jit(solution)/shard_map/fm,fp->mp/dot_general | solution.py:19
  47.2 0.0 all-reduce.5.cloned.1.call-update
  47.2 0.0 all-reduce.7.cloned.1.call-start
  47.2 0.0 copy-done.3
  47.3 0.6 dynamic-slice
  48.5 12.6 %psum.29 = f32[16]{0:T(128)S(1)} all-reduce(f32[16]{0:T(128)S(1)} %get-tuple-element.7), channel_id=1, replica_groups=mesh['groups'=2,'frame'=4,'panel'=2,'sub'=2] {'frame'}, use_global_device_ids=true, to_apply=%region_7.8 | all-reduce | flops 16 | bytes 128 | tf_op jit(solution)/shard_map/psum | solution.py:51
  61.0 0.1 dynamic-slice_add_fusion.1
  61.1 26.4 %all-reduce.5.cloned.1.call-done = bf16[16,16384]{1,0:T(8,128)(2,1)} async-done(((bf16[16,16384]{1,0:T(8,128)(2,1)}), bf16[16,16384]{1,0:T(8,128)(2,1)}) %all-reduce.5.cloned.1.call-update) | async-done | bytes 524304
  87.6 0.0 copy-done
  87.6 1.1 fusion.1
  88.6 16.2 %all-gather.1 = bf16[4,4,16384]{2,1,0:T(4,128)(2,1)S(1)} all-gather(bf16[1,4,16384]{2,1,0:T(4,128)(2,1)S(1)} %bitcast.14), channel_id=1, replica_groups=mesh['groups'=2,'frame'=4,'panel'=2,'sub'=2] {'frame'}, dimensions={0}, use_global_device_ids=true | all-gather | bytes 655360 | tf_op jit(solution)/shard_map/all_gather | solution.py:13
  104.8 0.1 reshape.20
  104.9 0.2 multiply_reduce_fusion
  105.2 5.6 %fusion = f32[256,16]{0,1:T(8,128)S(1)} fusion(bf16[16,16384]{1,0:T(8,128)(2,1)S(1)} %reshape.20, bf16[256,16384]{1,0:T(8,128)(2,1)} %param.4, f32[16]{0:T(128)S(1)} %broadcast_multiply_fusion), kind=kOutput, calls=%fused_computation.3 | convolution fusion | flops 134221824 | bytes 8929344 | tf_op jit(solution)/shard_map/fp,mp->fm/dot_general | solution.py:46
  110.8 10.1 %psum.30 = f32[256,16]{0,1:T(8,128)S(1)} all-reduce(f32[256,16]{0,1:T(8,128)S(1)} %fusion), channel_id=1, replica_groups=mesh['groups'=2,'frame'=4,'panel'=2,'sub'=2] {'panel','sub'}, use_global_device_ids=true, to_apply=%region_9.10 | all-reduce | flops 4096 | bytes 32768 | tf_op jit(solution)/shard_map/psum | solution.py:49
  120.9 0.1 fusion.3
  121.0 0.1 fusion.5
  121.1 0.2 convert_reduce_fusion
  121.3 5.4 %convolution_convert_fusion = bf16[16,16384]{1,0:T(8,128)(2,1)} fusion(bf16[256,16]{0,1:T(8,128)(2,1)S(1)} %get-tuple-element.6, bf16[256,16384]{1,0:T(8,128)(2,1)} %param.4), kind=kOutput, calls=%fused_computation | convolution fusion | flops 134479872 | bytes 8921088 | tf_op jit(solution)/shard_map/fm,fp->mp/dot_general | solution.py:19
  126.7 0.0 all-reduce.7.cloned.1.call-update
  126.7 10.8 %psum.31 = f32[16]{0:T(128)S(1)} all-reduce(f32[16]{0:T(128)S(1)} %get-tuple-element.5), channel_id=1, replica_groups=mesh['groups'=2,'frame'=4,'panel'=2,'sub'=2] {'frame'}, use_global_device_ids=true, to_apply=%region_14.15 | all-reduce | flops 16 | bytes 128 | tf_op jit(solution)/shard_map/psum | solution.py:51
  137.5 0.1 dynamic-slice_add_fusion
  137.6 27.7 %all-reduce.7.cloned.1.call-done = bf16[16,16384]{1,0:T(8,128)(2,1)} async-done(((bf16[16,16384]{1,0:T(8,128)(2,1)}), bf16[16,16384]{1,0:T(8,128)(2,1)}) %all-reduce.7.cloned.1.call-update) | async-done | bytes 524304
  165.3 1.8 %add_divide_fusion = f32[4,16384]{1,0:T(4,128)} fusion(bf16[4,16384]{1,0:T(4,128)(2,1)S(1)} %fusion.1, bf16[16,16384]{1,0:T(8,128)(2,1)} %all-reduce.7.cloned.1.call-done, u32[]{:T(128)S(6)} %multiply.1, f32[4]{0:T(128)S(1)} %dynamic-slice_add_fusion), kind=kLoop, calls=%fused_computation.7 | loop fusion | flops 262144 | bytes 524308 | tf_op jit(solution)/shard_map/div | solution.py:27
  (2 shorter events, 0.0 us)
Async XLA Ops:
  6.5 34.6 %copy-start.2 = (s32[16]{0:T(128)S(1)}, s32[16]{0:T(128)}, u32[]{:S(2)}) copy-start(s32[16]{0:T(128)} %param.7) | copy-start | bytes 196
  6.5 34.6 %copy-start.1 = (f32[4096]{0:T(1024)S(1)}, f32[4096]{0:T(1024)}, u32[]{:S(2)}) copy-start(f32[4096]{0:T(1024)} %param.6) | copy-start | bytes 49156
  6.5 81.0 %all-reduce.5.cloned.1.call-start = ((), (), s32[]{:S(2)}) async-start(), calls=%async_computation | async-start | bytes 1048576
  25.3 21.9 %copy-start.3 = (u32[32]{0:T(128)S(1)}, u32[32]{0:T(128)}, u32[]{:S(2)}) copy-start(u32[32]{0:T(128)} %constant.25) | copy-start | bytes 388
  25.3 62.2 %copy-start = (f32[4,16384]{1,0:T(4,128)S(1)}, f32[4,16384]{1,0:T(4,128)}, u32[]{:S(2)}) copy-start(f32[4,16384]{1,0:T(4,128)} %param.5) | copy-start | bytes 786436
  47.2 118.2 %all-reduce.7.cloned.1.call-start = ((), (), s32[]{:S(2)}) async-start(), calls=%async_computation.1 | async-start | bytes 1048576
Sparse Core Ops, SparseCore 0:
  47.3 40.1 all-reduce.4
  126.9 38.4 all-reduce.6
where the time goes:
time: 174 us
  blocking collectives  77.1 us (44%)
  waiting for transfers between devices  54.2 us (31%)
  matrix products  22.2 us (13%)
  between operations  14.1 us (8%)
  other arithmetic  5.48 us (3%)
    unnamed x4, waiting for transfers between devices  54.2 us
    all_gather x2, blocking collectives, fetch_slices(): return lax.all_gather(owned_b, 'frame', axis=0, tiled=True)  33.5 us
    psum x2, blocking collectives, local(): counts = lax.psum(jnp.sum(weights.astype(jnp.float32), axis=0), 'frame')  23.3 us
    psum x2, blocking collectives, local(): summed = lax.psum(raw, ('panel', 'sub'))  20.2 us
    dot_general x2, matrix products, local(): jnp.einsum('fp,mp->fm', frames, gathered, preferred_element_type=jnp.floa...  11.3 us
    dot_general x2, matrix products, owner_update(): jnp.einsum('fm,fp->mp', weights, frames, preferred_element_type=jnp.float32)  10.8 us
  transfers between devices with their start and end apart: 2, of which 2 were waited for; matrix products, arithmetic and copies ran while one was open for 0% of the time, Pallas kernels for 0%

commit v1 on v0

v1 whole, which is shorter than its diff:
```python
import functools
import math

import jax
import jax.numpy as jnp
from jax import lax
from jax.experimental import pallas as pl
from jax.experimental.pallas import tpu as pltpu
from jax.sharding import PartitionSpec as P

PIX = 65536
ITERS = 2
TAIL = 128
DIRECT = 8
VMEM_BYTES = 32 * 1024 * 1024


def tree_sum(terms):
    while len(terms) > 1:
        terms = [a + b for a, b in zip(terms[::2], terms[1::2])] + terms[len(terms) & ~1 :]
    return terms[0]


def spread(block, axis, size, sign):
    return [
        lax.ppermute(block[k] if isinstance(block, list) else block, axis, [(i, (i + sign * k) % size) for i in range(size)])
        for k in range(1, size)
    ]


def exchange_all(part, axes, size):
    if size & (size - 1):
        return [lax.psum(part, axes)]
    return [part] + [lax.ppermute(part, axes, [(i, i ^ k) for i in range(size)]) for k in range(1, size)]


def score_kernel(n, *refs):
    blocks, frames_ref, out_ref = refs[:n], refs[n], refs[n + 1]
    step = pl.program_id(0)
    model = jnp.concatenate([ref[...] for ref in blocks], axis=0)
    wide = model.astype(jnp.float32)
    part = lax.dot_general(
        model, frames_ref[...], (((1,), (1,)), ((), ())), preferred_element_type=jnp.float32
    ) - 0.5 * jnp.sum(wide * wide, axis=1, keepdims=True)

    @pl.when(step == 0)
    def _():
        out_ref[...] = part

    @pl.when(step > 0)
    def _():
        out_ref[...] += part


def score_parts(blocks, frames, tile):
    rows, pix = frames.shape
    many = sum(b.shape[0] for b in blocks)
    return pl.pallas_call(
        functools.partial(score_kernel, len(blocks)),
        grid=(pix // tile,),
        in_specs=[pl.BlockSpec((b.shape[0], tile), lambda i: (0, i)) for b in blocks]
        + [pl.BlockSpec((rows, tile), lambda i: (0, i))],
        out_specs=pl.BlockSpec((many, rows), lambda i: (0, 0)),
        out_shape=jax.ShapeDtypeStruct((many, rows), jnp.float32),
        compiler_params=pltpu.CompilerParams(vmem_limit_bytes=VMEM_BYTES),
        cost_estimate=pl.CostEstimate(flops=2 * rows * pix * many, bytes_accessed=2 * rows * pix, transcendentals=0),
    )(*blocks, frames)


def total_kernel(n, heights, tiles, *refs):
    parts, prior_ref, frames_ref = refs[:n], refs[n], refs[n + 1]
    outs, weights_ref = refs[n + 2 : -1], refs[-1]
    step = pl.program_id(0)

    @pl.when(step == 0)
    def _():
        raw = tree_sum([ref[...] for ref in parts])
        scores = (3.0 / math.sqrt(PIX)) * raw + prior_ref[...]
        up = jnp.exp(scores - jnp.max(scores, axis=0, keepdims=True))
        weights_ref[...] = (up / jnp.sum(up, axis=0, keepdims=True)).astype(jnp.bfloat16)

    weights = weights_ref[...]
    tile = frames_ref.shape[1]
    total = jnp.dot(weights, frames_ref[...], preferred_element_type=jnp.float32).astype(jnp.bfloat16)
    low = 0
    for ref, height in zip(outs, heights):
        ref[:, pl.ds(pl.multiple_of(step * tile, tile), tile)] = total[low : low + height]
        low += height

    @pl.when(step == tiles - 1)
    def _():
        counts = jnp.sum(weights.astype(jnp.float32), axis=1, keepdims=True)
        high = counts.astype(jnp.bfloat16)
        rest = (counts - high.astype(jnp.float32)).astype(jnp.bfloat16)
        lane = lax.broadcasted_iota(jnp.int32, (counts.shape[0], TAIL), 1)
        both = jnp.where(lane < TAIL // 2, high.astype(jnp.float32), rest.astype(jnp.float32)).astype(jnp.bfloat16)
        low = 0
        for ref, height in zip(outs, heights):
            ref[:, tiles * tile :] = both[low : low + height]
            low += height


def block_totals(parts, prior, frames, heights, tile):
    rows, pix = frames.shape
    many = prior.shape[0]
    return pl.pallas_call(
        functools.partial(total_kernel, len(parts), heights, pix // tile),
        grid=(pix // tile,),
        in_specs=[pl.BlockSpec(p.shape, lambda i: (0, 0)) for p in parts]
        + [pl.BlockSpec(prior.shape, lambda i: (0, 0)), pl.BlockSpec((rows, tile), lambda i: (0, i))],
        out_specs=[pl.BlockSpec((h, pix + TAIL), lambda i: (0, 0)) for h in heights],
        out_shape=[jax.ShapeDtypeStruct((h, pix + TAIL), jnp.bfloat16) for h in heights],
        scratch_shapes=[pltpu.VMEM((many, rows), jnp.bfloat16)],
        compiler_params=pltpu.CompilerParams(vmem_limit_bytes=VMEM_BYTES),
        cost_estimate=pl.CostEstimate(
            flops=2 * rows * pix * many, bytes_accessed=2 * rows * pix, transcendentals=rows * many
        ),
    )(*parts, prior, frames)


def update_kernel(terms, owned_ref, out_ref):
    pix = owned_ref.shape[1]

    def total(low, high):
        pieces = [ref[..., low:high].astype(jnp.float32) for ref in terms]
        return tree_sum([jnp.sum(p, axis=0) if p.ndim == 3 else p for p in pieces])

    tail = total(pix, pix + TAIL)
    counts = tail[:, :1] + tail[:, TAIL // 2 : TAIL // 2 + 1]
    out_ref[...] = ((total(0, pix) + owned_ref[...].astype(jnp.float32)) / (counts + 1.0)).astype(out_ref.dtype)


def update(terms, owned, dtype):
    def kernel(*refs):
        update_kernel(refs[: len(terms)], refs[-2], refs[-1])

    return pl.pallas_call(
        kernel,
        out_shape=jax.ShapeDtypeStruct(owned.shape, dtype),
        compiler_params=pltpu.CompilerParams(vmem_limit_bytes=VMEM_BYTES),
        cost_estimate=pl.CostEstimate(flops=8 * owned.size, bytes_accessed=12 * owned.size, transcendentals=0),
    )(*terms, owned)


def local(sizes, frames, slices, log_prior, orient):
    along, across = sizes
    owned = slices.shape[0]
    tile = min(2048, frames.shape[1])
    direct = along <= DIRECT
    if direct:
        first = lax.axis_index("frame") * owned
        orient = lax.dynamic_slice_in_dim(jnp.concatenate([orient, orient]), first, orient.shape[0], 0)
    matches = orient[:, None] == jnp.arange(log_prior.shape[0], dtype=jnp.int32)[None, :]
    prior = jnp.sum(jnp.where(matches, log_prior[None, :], 0.0), axis=1, keepdims=True)
    owned_b = slices.astype(jnp.bfloat16)
    for step in range(ITERS):
        if direct:
            blocks = [owned_b] + spread(owned_b, "frame", along, -1)
            heights = [owned] * along
        else:
            blocks = [lax.all_gather(owned_b, "frame", axis=0, tiled=True)]
            heights = [owned * along]
        parts = exchange_all(score_parts(blocks, frames, tile), ("panel", "sub"), across)
        totals = block_totals(parts, prior, frames, heights, tile)
        if direct:
            terms = [totals[0]] + spread(list(totals), "frame", along, 1)
        else:
            whole = totals[0].reshape(along, owned, totals[0].shape[1])
            terms = [lax.all_to_all(whole, "frame", split_axis=0, concat_axis=0, tiled=False)]
        owned_b = update(terms, owned_b, jnp.bfloat16 if step + 1 < ITERS else jnp.float32)
    return owned_b


def solution(mesh):
    in_specs = (
        P(("groups", "frame"), ("panel", "sub")),
        P(("groups", "frame"), ("panel", "sub")),
        P(),
        P("groups"),
    )
    out_specs = P(("groups", "frame"), ("panel", "sub"))
    sizes = (mesh.shape["frame"], mesh.shape["panel"] * mesh.shape["sub"])
    return jax.shard_map(
        functools.partial(local, sizes), mesh=mesh, in_specs=in_specs, out_specs=out_specs, check_vma=False
    )
```

time: 174 us -> 85.8 us (0.49)
  blocking collectives: 77.1 us -> 0 us
  starting transfers between devices: 0.04 us -> 28.3 us
  matrix products: 22.2 us -> 0 us
  waiting for transfers between devices: 54.2 us -> 33.5 us
  between operations: 14.1 us -> 0.05 us
  Pallas kernels: 0 us -> 14 us
  local copies, waits for them, and re-layouts: 0.85 us -> 6.93 us
  other arithmetic: 5.48 us -> 2.04 us
    unnamed x4 -> x0, waiting for transfers between devices: 54.2 us -> none
    psum x4 -> x0, blocking collectives: 43.6 us -> none  [the longest x2 23.3 us: local(): counts = lax.psum(jnp.sum(weights.astype(jnp.float32), axis=0), 'frame')]
    all_gather x2 -> x0, blocking collectives: 33.5 us -> none  [fetch_slices(): return lax.all_gather(owned_b, 'frame', axis=0, tiled=True)]
    ppermute x0 -> x18, waiting for transfers between devices: none -> 33.5 us  [the longest x12 28.9 us: spread(): lax.ppermute(block[k] if isinstance(block, list) else block, axis, [(i, (...]
    ppermute x0 -> x18, starting transfers between devices: none -> 28.3 us  [the longest x12 24.5 us: spread(): lax.ppermute(block[k] if isinstance(block, list) else block, axis, [(i, (...]
    dot_general x4 -> x0, matrix products: 22.2 us -> none  [the longest x2 11.3 us: local(): jnp.einsum('fp,mp->fm', frames, gathered, preferred_element_type=jnp.floa...]
    pallas_call x0 -> x6, Pallas kernels: none -> 14 us  [the longest x2 7.37 us: score_parts(): pl.pallas_call(functools.partial(score_kernel, len(blocks)), grid=(pix //...]
    unnamed x11 -> x8, local copies, waits for them, and re-layouts: 0.85 us -> 6.77 us
  transfers between devices with their start and end apart: 2 -> 18, of which waited for: 2 -> 12; matrix products, arithmetic and copies ran while one was open for 0% -> 1% of each run, Pallas kernels for 0% -> 0%
where the time goes in v1:
time: 85.8 us; the launch traced here: 84.8 us
  waiting for transfers between devices  33.5 us (39%)
  starting transfers between devices  28.3 us (33%)
  Pallas kernels  14 us (16%)
  local copies, waits for them, and re-layouts  6.93 us (8%)
  other arithmetic  2.04 us (2%)
    ppermute x12, waiting for transfers between devices, spread(): lax.ppermute(block[k] if isinstance(block, list) else block, axis, [(i, (...  28.9 us
    ppermute x12, starting transfers between devices, spread(): lax.ppermute(block[k] if isinstance(block, list) else block, axis, [(i, (...  24.5 us
    pallas_call x2, Pallas kernels, score_parts(): pl.pallas_call(functools.partial(score_kernel, len(blocks)), grid=(pix //...  7.37 us
    unnamed x8, local copies, waits for them, and re-layouts  6.77 us
    pallas_call x2, Pallas kernels, block_totals(): pl.pallas_call(functools.partial(total_kernel, len(parts), heights, pix /...  5.47 us
    ppermute x6, waiting for transfers between devices, exchange_all(): lax.ppermute(part, axes, [(i, i ^ k) for i in range(size)])  4.56 us
    ppermute x6, starting transfers between devices, exchange_all(): lax.ppermute(part, axes, [(i, i ^ k) for i in range(size)])  3.77 us
  transfers between devices with their start and end apart: 18, of which 12 were waited for; matrix products, arithmetic and copies ran while one was open for 1% of the time, Pallas kernels for 0%

profile of v1, /device:TPU:0, one launch (start us, length us, event | category | flops | bytes accessed | tf_op | source)
XLA Modules:
  0.0 84.8 jit_solution(3877968267010036378)
XLA Ops:
  0.0 0.0 copy-start.3
  0.0 1.0 %convert_element_type.3.refs_0_.refs_4_ = bf16[4,16384]{1,0:T(4,128)(2,1)S(1)} convert(f32[4,16384]{1,0:T(4,128)} %param.5) | non-fusion elementwise | flops 65536 | bytes 393216 | tf_op jit(solution)/shard_map/convert_element_type | solution.py:155
  1.0 3.1 %collective-permute-start.2 = (bf16[4,16384]{1,0:T(4,128)(2,1)S(1)}, bf16[4,16384]{1,0:T(4,128)(2,1)S(1)}, u32[]{:S(2)}, u32[]{:S(2)}) collective-permute-start(bf16[4,16384]{1,0:T(4,128)(2,1)S(1)} %convert_element_type.3.refs_0_.refs_4_), channel_id=1, source_target_pairs={{0,4},{4,8},{8,12},{12,0},{1,5},{5,9},{9,13},{13,1},{2,6},{6,10},{... | collective-permute-start | bytes 393224 | tf_op jit(solution)/shard_map/ppermute | solution.py:26
  4.1 2.6 %collective-permute-start.1 = (bf16[4,16384]{1,0:T(4,128)(2,1)S(1)}, bf16[4,16384]{1,0:T(4,128)(2,1)S(1)}, u32[]{:S(2)}, u32[]{:S(2)}) collective-permute-start(bf16[4,16384]{1,0:T(4,128)(2,1)S(1)} %convert_element_type.3.refs_0_.refs_4_), channel_id=1, source_target_pairs={{0,8},{4,12},{8,0},{12,4},{1,9},{5,13},{9,1},{13,5},{2,10},{6,14},... | collective-permute-start | bytes 393224 | tf_op jit(solution)/shard_map/ppermute | solution.py:26
  6.7 1.3 %collective-permute-start = (bf16[4,16384]{1,0:T(4,128)(2,1)S(1)}, bf16[4,16384]{1,0:T(4,128)(2,1)S(1)}, u32[]{:S(2)}, u32[]{:S(2)}) collective-permute-start(bf16[4,16384]{1,0:T(4,128)(2,1)S(1)} %convert_element_type.3.refs_0_.refs_4_), channel_id=1, source_target_pairs={{0,12},{4,0},{8,4},{12,8},{1,13},{5,1},{9,5},{13,9},{2,14},{6,2},{... | collective-permute-start | bytes 393224 | tf_op jit(solution)/shard_map/ppermute | solution.py:26
  8.0 0.8 pad_add_fusion
  8.8 0.1 dynamic_slice.3
  8.9 1.6 %collective-permute-done.2.refs_3_ = bf16[4,16384]{1,0:T(4,128)(2,1)S(1)} collective-permute-done((bf16[4,16384]{1,0:T(4,128)(2,1)S(1)}, bf16[4,16384]{1,0:T(4,128)(2,1)S(1)}, u32[]{:S(2)}, u32[]{:S(2)}) %collective-permute-start.2) | collective-permute-done | bytes 131104 | tf_op jit(solution)/shard_map/ppermute | solution.py:26
  10.5 4.8 %collective-permute-done.1.refs_2_ = bf16[4,16384]{1,0:T(4,128)(2,1)S(1)} collective-permute-done((bf16[4,16384]{1,0:T(4,128)(2,1)S(1)}, bf16[4,16384]{1,0:T(4,128)(2,1)S(1)}, u32[]{:S(2)}, u32[]{:S(2)}) %collective-permute-start.1) | collective-permute-done | bytes 131104 | tf_op jit(solution)/shard_map/ppermute | solution.py:26
  15.3 0.0 collective-permute-done.refs_1_
  15.3 0.0 copy-start
  15.3 3.4 %copy-done = bf16[256,16384]{1,0:T(8,128)(2,1)S(1)} copy-done((bf16[256,16384]{1,0:T(8,128)(2,1)S(1)}, bf16[256,16384]{1,0:T(8,128)(2,1)}, u32[]{:S(2)}) %copy-start) | copy-done | bytes 8388632
  18.7 3.7 %shard_map.46.refs_0_ = f32[16,256]{1,0:T(8,128)S(1)} custom-call(bf16[4,16384]{1,0:T(4,128)(2,1)S(1)} %convert_element_type.3.refs_0_.refs_4_, bf16[4,16384]{1,0:T(4,128)(2,1)S(1)} %collective-permute-done.refs_1_, bf16[4,16384]{1,0:T(4,128)(2,1)S(1)} %collective-permute-done.1.refs_2_, bf16[4,16384]{1,0:T(4,128)(2,1)S(1)} %collective-permute-done.2.refs_3_, ...), custom_call_target="tpu_custom_call" | custom-call | flops 134217728 | bytes 8388608 | tf_op jit(solution)/shard_map/pallas_call | solution.py:58
  22.4 1.0 %collective-permute-start.5 = (f32[16,256]{1,0:T(8,128)S(1)}, f32[16,256]{1,0:T(8,128)S(1)}, u32[]{:S(2)}, u32[]{:S(2)}) collective-permute-start(f32[16,256]{1,0:T(8,128)S(1)} %shard_map.46.refs_0_), channel_id=1, source_target_pairs={{0,3},{1,2},{2,1},{3,0},{4,7},{5,6},{6,5},{7,4},{8,11},{9,10},{10,... | collective-permute-start | bytes 49160 | tf_op jit(solution)/shard_map/ppermute | solution.py:34
  23.4 0.6 collective-permute-start.4
  24.0 0.3 collective-permute-start.3
  24.3 0.0 copy-done.3
  24.3 0.2 select_reduce_fusion
  24.5 0.1 copy.7.refs_4_
  24.6 1.1 %collective-permute-done.5.refs_3_ = f32[16,256]{1,0:T(8,128)S(1)} collective-permute-done((f32[16,256]{1,0:T(8,128)S(1)}, f32[16,256]{1,0:T(8,128)S(1)}, u32[]{:S(2)}, u32[]{:S(2)}) %collective-permute-start.5) | collective-permute-done | bytes 16416 | tf_op jit(solution)/shard_map/ppermute | solution.py:34
  25.7 1.5 %collective-permute-done.4.refs_2_ = f32[16,256]{1,0:T(8,128)S(1)} collective-permute-done((f32[16,256]{1,0:T(8,128)S(1)}, f32[16,256]{1,0:T(8,128)S(1)}, u32[]{:S(2)}, u32[]{:S(2)}) %collective-permute-start.4) | collective-permute-done | bytes 16416 | tf_op jit(solution)/shard_map/ppermute | solution.py:34
  27.2 0.0 collective-permute-done.3.refs_1_
  27.2 0.0 copy-start.1
  27.2 3.4 %copy-done.1 = bf16[256,16384]{1,0:T(8,128)(2,1)S(1)} copy-done((bf16[256,16384]{1,0:T(8,128)(2,1)S(1)}, bf16[256,16384]{1,0:T(8,128)(2,1)}, u32[]{:S(2)}) %copy-start.1) | copy-done | bytes 8388632
  30.6 0.0 copy-start.2
  30.6 2.7 %shard_map.47 = (bf16[4,16512]{1,0:T(4,128)(2,1)S(1)}, bf16[4,16512]{1,0:T(4,128)(2,1)S(1)}, bf16[4,16512]{1,0:T(4,128)(2,1)S(1)}, bf16[4,16512]{1,0:T(4,128)(2,1)S(1)}) custom-call(f32[16,256]{1,0:T(8,128)S(1)} %shard_map.46.refs_0_, f32[16,256]{1,0:T(8,128)S(1)} %collective-permute-done.3.refs_1_, f32[16,256]{1,0:T(8,128)S(1)} %collective-permute-done.4.refs_2_, ...), custom_call_target="tpu_custom_call" | custom-call | flops 134217728 | bytes 8388608 | tf_op jit(solution)/shard_map/pallas_call | solution.py:106
  33.3 3.4 %collective-permute-start.6 = (bf16[4,16512]{1,0:T(4,128)(2,1)S(1)}, bf16[4,16512]{1,0:T(4,128)(2,1)S(1)}, u32[]{:S(2)}, u32[]{:S(2)}) collective-permute-start(bf16[4,16512]{1,0:T(4,128)(2,1)S(1)} %get-tuple-element.14), channel_id=1, source_target_pairs={{0,4},{4,8},{8,12},{12,0},{1,5},{5,9},{9,13},{13,1},{2,6},{6,10},{... | collective-permute-start | bytes 396296 | tf_op jit(solution)/shard_map/ppermute | solution.py:26
  36.7 0.6 collective-permute-start.7
  37.3 1.8 %collective-permute-start.8 = (bf16[4,16512]{1,0:T(4,128)(2,1)S(1)}, bf16[4,16512]{1,0:T(4,128)(2,1)S(1)}, u32[]{:S(2)}, u32[]{:S(2)}) collective-permute-start(bf16[4,16512]{1,0:T(4,128)(2,1)S(1)} %get-tuple-element.16), channel_id=1, source_target_pairs={{0,12},{4,0},{8,4},{12,8},{1,13},{5,1},{9,5},{13,9},{2,14},{6,2},{... | collective-permute-start | bytes 396296 | tf_op jit(solution)/shard_map/ppermute | solution.py:26
  39.2 2.4 %collective-permute-done.6.refs_1_ = bf16[4,16512]{1,0:T(4,128)(2,1)S(1)} collective-permute-done((bf16[4,16512]{1,0:T(4,128)(2,1)S(1)}, bf16[4,16512]{1,0:T(4,128)(2,1)S(1)}, u32[]{:S(2)}, u32[]{:S(2)}) %collective-permute-start.6) | collective-permute-done | bytes 132128 | tf_op jit(solution)/shard_map/ppermute | solution.py:26
  41.6 5.0 %collective-permute-done.7.refs_2_ = bf16[4,16512]{1,0:T(4,128)(2,1)S(1)} collective-permute-done((bf16[4,16512]{1,0:T(4,128)(2,1)S(1)}, bf16[4,16512]{1,0:T(4,128)(2,1)S(1)}, u32[]{:S(2)}, u32[]{:S(2)}) %collective-permute-start.7) | collective-permute-done | bytes 132128 | tf_op jit(solution)/shard_map/ppermute | solution.py:26
  46.6 0.0 collective-permute-done.8.refs_3_
  46.6 0.2 shard_map.48.refs_0_.refs_4_
  46.8 3.4 %collective-permute-start.11 = (bf16[4,16384]{1,0:T(4,128)(2,1)S(1)}, bf16[4,16384]{1,0:T(4,128)(2,1)S(1)}, u32[]{:S(2)}, u32[]{:S(2)}) collective-permute-start(bf16[4,16384]{1,0:T(4,128)(2,1)S(1)} %shard_map.48.refs_0_.refs_4_), channel_id=1, source_target_pairs={{0,4},{4,8},{8,12},{12,0},{1,5},{5,9},{9,13},{13,1},{2,6},{6,10},{... | collective-permute-start | bytes 393224 | tf_op jit(solution)/shard_map/ppermute | solution.py:26
  50.2 1.3 %collective-permute-start.10 = (bf16[4,16384]{1,0:T(4,128)(2,1)S(1)}, bf16[4,16384]{1,0:T(4,128)(2,1)S(1)}, u32[]{:S(2)}, u32[]{:S(2)}) collective-permute-start(bf16[4,16384]{1,0:T(4,128)(2,1)S(1)} %shard_map.48.refs_0_.refs_4_), channel_id=1, source_target_pairs={{0,8},{4,12},{8,0},{12,4},{1,9},{5,13},{9,1},{13,5},{2,10},{6,14},... | collective-permute-start | bytes 393224 | tf_op jit(solution)/shard_map/ppermute | solution.py:26
  51.5 1.1 %collective-permute-start.9 = (bf16[4,16384]{1,0:T(4,128)(2,1)S(1)}, bf16[4,16384]{1,0:T(4,128)(2,1)S(1)}, u32[]{:S(2)}, u32[]{:S(2)}) collective-permute-start(bf16[4,16384]{1,0:T(4,128)(2,1)S(1)} %shard_map.48.refs_0_.refs_4_), channel_id=1, source_target_pairs={{0,12},{4,0},{8,4},{12,8},{1,13},{5,1},{9,5},{13,9},{2,14},{6,2},{... | collective-permute-start | bytes 393224 | tf_op jit(solution)/shard_map/ppermute | solution.py:26
  52.6 2.3 %collective-permute-done.11.refs_3_ = bf16[4,16384]{1,0:T(4,128)(2,1)S(1)} collective-permute-done((bf16[4,16384]{1,0:T(4,128)(2,1)S(1)}, bf16[4,16384]{1,0:T(4,128)(2,1)S(1)}, u32[]{:S(2)}, u32[]{:S(2)}) %collective-permute-start.11) | collective-permute-done | bytes 131104 | tf_op jit(solution)/shard_map/ppermute | solution.py:26
  54.9 4.8 %collective-permute-done.10.refs_2_ = bf16[4,16384]{1,0:T(4,128)(2,1)S(1)} collective-permute-done((bf16[4,16384]{1,0:T(4,128)(2,1)S(1)}, bf16[4,16384]{1,0:T(4,128)(2,1)S(1)}, u32[]{:S(2)}, u32[]{:S(2)}) %collective-permute-start.10) | collective-permute-done | bytes 131104 | tf_op jit(solution)/shard_map/ppermute | solution.py:26
  59.7 0.0 collective-permute-done.9.refs_1_
  59.7 0.0 copy-done.2
  59.7 3.7 %shard_map.49.refs_0_ = f32[16,256]{1,0:T(8,128)S(1)} custom-call(bf16[4,16384]{1,0:T(4,128)(2,1)S(1)} %shard_map.48.refs_0_.refs_4_, bf16[4,16384]{1,0:T(4,128)(2,1)S(1)} %collective-permute-done.9.refs_1_, bf16[4,16384]{1,0:T(4,128)(2,1)S(1)} %collective-permute-done.10.refs_2_, bf16[4,16384]{1,0:T(4,128)(2,1)S(1)} %collective-permute-done.11.refs_3_, ...), custom_call_target="tpu_custom_call" | custom-call | flops 134217728 | bytes 8388608 | tf_op jit(solution)/shard_map/pallas_call | solution.py:58
  63.4 0.1 collective-permute-start.14
  63.5 1.5 %collective-permute-start.13 = (f32[16,256]{1,0:T(8,128)S(1)}, f32[16,256]{1,0:T(8,128)S(1)}, u32[]{:S(2)}, u32[]{:S(2)}) collective-permute-start(f32[16,256]{1,0:T(8,128)S(1)} %shard_map.49.refs_0_), channel_id=1, source_target_pairs={{0,2},{1,3},{2,0},{3,1},{4,6},{5,7},{6,4},{7,5},{8,10},{9,11},{10,... | collective-permute-start | bytes 49160 | tf_op jit(solution)/shard_map/ppermute | solution.py:34
  65.0 0.3 collective-permute-start.12
  65.3 1.4 %collective-permute-done.14.refs_3_ = f32[16,256]{1,0:T(8,128)S(1)} collective-permute-done((f32[16,256]{1,0:T(8,128)S(1)}, f32[16,256]{1,0:T(8,128)S(1)}, u32[]{:S(2)}, u32[]{:S(2)}) %collective-permute-start.14) | collective-permute-done | bytes 16416 | tf_op jit(solution)/shard_map/ppermute | solution.py:34
  66.7 0.6 collective-permute-done.13.refs_2_
  67.3 0.0 collective-permute-done.12.refs_1_
  67.3 2.7 %shard_map.50 = (bf16[4,16512]{1,0:T(4,128)(2,1)S(1)}, bf16[4,16512]{1,0:T(4,128)(2,1)S(1)}, bf16[4,16512]{1,0:T(4,128)(2,1)S(1)}, bf16[4,16512]{1,0:T(4,128)(2,1)S(1)}) custom-call(f32[16,256]{1,0:T(8,128)S(1)} %shard_map.49.refs_0_, f32[16,256]{1,0:T(8,128)S(1)} %collective-permute-done.12.refs_1_, f32[16,256]{1,0:T(8,128)S(1)} %collective-permute-done.13.refs_2_, ...), custom_call_target="tpu_custom_call" | custom-call | flops 134217728 | bytes 8388608 | tf_op jit(solution)/shard_map/pallas_call | solution.py:106
  70.0 3.4 %collective-permute-start.15 = (bf16[4,16512]{1,0:T(4,128)(2,1)S(1)}, bf16[4,16512]{1,0:T(4,128)(2,1)S(1)}, u32[]{:S(2)}, u32[]{:S(2)}) collective-permute-start(bf16[4,16512]{1,0:T(4,128)(2,1)S(1)} %get-tuple-element.18), channel_id=1, source_target_pairs={{0,4},{4,8},{8,12},{12,0},{1,5},{5,9},{9,13},{13,1},{2,6},{6,10},{... | collective-permute-start | bytes 396296 | tf_op jit(solution)/shard_map/ppermute | solution.py:26
  73.4 2.1 %collective-permute-start.16 = (bf16[4,16512]{1,0:T(4,128)(2,1)S(1)}, bf16[4,16512]{1,0:T(4,128)(2,1)S(1)}, u32[]{:S(2)}, u32[]{:S(2)}) collective-permute-start(bf16[4,16512]{1,0:T(4,128)(2,1)S(1)} %get-tuple-element.19), channel_id=1, source_target_pairs={{0,8},{4,12},{8,0},{12,4},{1,9},{5,13},{9,1},{13,5},{2,10},{6,14},... | collective-permute-start | bytes 396296 | tf_op jit(solution)/shard_map/ppermute | solution.py:26
  75.5 0.3 collective-permute-start.17
  75.9 3.6 %collective-permute-done.15.refs_1_ = bf16[4,16512]{1,0:T(4,128)(2,1)S(1)} collective-permute-done((bf16[4,16512]{1,0:T(4,128)(2,1)S(1)}, bf16[4,16512]{1,0:T(4,128)(2,1)S(1)}, u32[]{:S(2)}, u32[]{:S(2)}) %collective-permute-start.15) | collective-permute-done | bytes 132128 | tf_op jit(solution)/shard_map/ppermute | solution.py:26
  79.5 4.4 %collective-permute-done.16.refs_2_ = bf16[4,16512]{1,0:T(4,128)(2,1)S(1)} collective-permute-done((bf16[4,16512]{1,0:T(4,128)(2,1)S(1)}, bf16[4,16512]{1,0:T(4,128)(2,1)S(1)}, u32[]{:S(2)}, u32[]{:S(2)}) %collective-permute-start.16) | collective-permute-done | bytes 132128 | tf_op jit(solution)/shard_map/ppermute | solution.py:26
  83.9 0.0 collective-permute-done.17.refs_3_
  83.9 0.9 %shard_map.51 = f32[4,16384]{1,0:T(4,128)} custom-call(bf16[4,16512]{1,0:T(4,128)(2,1)S(1)} %get-tuple-element.17.refs_0_, bf16[4,16512]{1,0:T(4,128)(2,1)S(1)} %collective-permute-done.15.refs_1_, bf16[4,16512]{1,0:T(4,128)(2,1)S(1)} %collective-permute-done.16.refs_2_, bf16[4,16512]{1,0:T(4,128)(2,1)S(1)} %collective-permute-done.17.refs_3_, ...), custom_call_target="tpu_custom_call" | custom-call | flops 524288 | bytes 786432 | tf_op jit(solution)/shard_map/pallas_call | solution.py:137
Async XLA Ops:
  0.0 24.3 %copy-start.3 = (f32[4096]{0:T(1024)S(1)}, f32[4096]{0:T(1024)}, u32[]{:S(2)}) copy-start(f32[4096]{0:T(1024)} %param.6) | copy-start | bytes 49156
  1.0 9.5 %collective-permute-start.2 = (bf16[4,16384]{1,0:T(4,128)(2,1)S(1)}, bf16[4,16384]{1,0:T(4,128)(2,1)S(1)}, u32[]{:S(2)}, u32[]{:S(2)}) collective-permute-start(bf16[4,16384]{1,0:T(4,128)(2,1)S(1)} %convert_element_type.3.refs_0_.refs_4_), channel_id=1, source_target_pairs={{0,4},{4,8},{8,12},{12,0},{1,5},{5,9},{9,13},{13,1},{2,6},{6,10},{... | collective-permute-start | bytes 393224 | tf_op jit(solution)/shard_map/ppermute | solution.py:26
  4.1 11.2 %collective-permute-start.1 = (bf16[4,16384]{1,0:T(4,128)(2,1)S(1)}, bf16[4,16384]{1,0:T(4,128)(2,1)S(1)}, u32[]{:S(2)}, u32[]{:S(2)}) collective-permute-start(bf16[4,16384]{1,0:T(4,128)(2,1)S(1)} %convert_element_type.3.refs_0_.refs_4_), channel_id=1, source_target_pairs={{0,8},{4,12},{8,0},{12,4},{1,9},{5,13},{9,1},{13,5},{2,10},{6,14},... | collective-permute-start | bytes 393224 | tf_op jit(solution)/shard_map/ppermute | solution.py:26
  6.7 8.6 %collective-permute-start = (bf16[4,16384]{1,0:T(4,128)(2,1)S(1)}, bf16[4,16384]{1,0:T(4,128)(2,1)S(1)}, u32[]{:S(2)}, u32[]{:S(2)}) collective-permute-start(bf16[4,16384]{1,0:T(4,128)(2,1)S(1)} %convert_element_type.3.refs_0_.refs_4_), channel_id=1, source_target_pairs={{0,12},{4,0},{8,4},{12,8},{1,13},{5,1},{9,5},{13,9},{2,14},{6,2},{... | collective-permute-start | bytes 393224 | tf_op jit(solution)/shard_map/ppermute | solution.py:26
  15.3 3.4 %copy-start = (bf16[256,16384]{1,0:T(8,128)(2,1)S(1)}, bf16[256,16384]{1,0:T(8,128)(2,1)}, u32[]{:S(2)}) copy-start(bf16[256,16384]{1,0:T(8,128)(2,1)} %refs_5_.3) | copy-start | bytes 25165828
  22.4 3.3 %collective-permute-start.5 = (f32[16,256]{1,0:T(8,128)S(1)}, f32[16,256]{1,0:T(8,128)S(1)}, u32[]{:S(2)}, u32[]{:S(2)}) collective-permute-start(f32[16,256]{1,0:T(8,128)S(1)} %shard_map.46.refs_0_), channel_id=1, source_target_pairs={{0,3},{1,2},{2,1},{3,0},{4,7},{5,6},{6,5},{7,4},{8,11},{9,10},{10,... | collective-permute-start | bytes 49160 | tf_op jit(solution)/shard_map/ppermute | solution.py:34
  23.4 3.7 %collective-permute-start.4 = (f32[16,256]{1,0:T(8,128)S(1)}, f32[16,256]{1,0:T(8,128)S(1)}, u32[]{:S(2)}, u32[]{:S(2)}) collective-permute-start(f32[16,256]{1,0:T(8,128)S(1)} %shard_map.46.refs_0_), channel_id=1, source_target_pairs={{0,2},{1,3},{2,0},{3,1},{4,6},{5,7},{6,4},{7,5},{8,10},{9,11},{10,... | collective-permute-start | bytes 49160 | tf_op jit(solution)/shard_map/ppermute | solution.py:34
  24.0 3.2 %collective-permute-start.3 = (f32[16,256]{1,0:T(8,128)S(1)}, f32[16,256]{1,0:T(8,128)S(1)}, u32[]{:S(2)}, u32[]{:S(2)}) collective-permute-start(f32[16,256]{1,0:T(8,128)S(1)} %shard_map.46.refs_0_), channel_id=1, source_target_pairs={{0,1},{1,0},{2,3},{3,2},{4,5},{5,4},{6,7},{7,6},{8,9},{9,8},{10,11... | collective-permute-start | bytes 49160 | tf_op jit(solution)/shard_map/ppermute | solution.py:34
  27.2 3.4 %copy-start.1 = (bf16[256,16384]{1,0:T(8,128)(2,1)S(1)}, bf16[256,16384]{1,0:T(8,128)(2,1)}, u32[]{:S(2)}) copy-start(bf16[256,16384]{1,0:T(8,128)(2,1)} %refs_5_.3) | copy-start | bytes 25165828
  30.6 29.1 %copy-start.2 = (bf16[256,16384]{1,0:T(8,128)(2,1)S(1)}, bf16[256,16384]{1,0:T(8,128)(2,1)}, u32[]{:S(2)}) copy-start(bf16[256,16384]{1,0:T(8,128)(2,1)} %refs_5_.3) | copy-start | bytes 25165828
  33.3 8.3 %collective-permute-start.6 = (bf16[4,16512]{1,0:T(4,128)(2,1)S(1)}, bf16[4,16512]{1,0:T(4,128)(2,1)S(1)}, u32[]{:S(2)}, u32[]{:S(2)}) collective-permute-start(bf16[4,16512]{1,0:T(4,128)(2,1)S(1)} %get-tuple-element.14), channel_id=1, source_target_pairs={{0,4},{4,8},{8,12},{12,0},{1,5},{5,9},{9,13},{13,1},{2,6},{6,10},{... | collective-permute-start | bytes 396296 | tf_op jit(solution)/shard_map/ppermute | solution.py:26
  36.7 9.8 %collective-permute-start.7 = (bf16[4,16512]{1,0:T(4,128)(2,1)S(1)}, bf16[4,16512]{1,0:T(4,128)(2,1)S(1)}, u32[]{:S(2)}, u32[]{:S(2)}) collective-permute-start(bf16[4,16512]{1,0:T(4,128)(2,1)S(1)} %get-tuple-element.15), channel_id=1, source_target_pairs={{0,8},{4,12},{8,0},{12,4},{1,9},{5,13},{9,1},{13,5},{2,10},{6,14},... | collective-permute-start | bytes 396296 | tf_op jit(solution)/shard_map/ppermute | solution.py:26
  37.3 9.2 %collective-permute-start.8 = (bf16[4,16512]{1,0:T(4,128)(2,1)S(1)}, bf16[4,16512]{1,0:T(4,128)(2,1)S(1)}, u32[]{:S(2)}, u32[]{:S(2)}) collective-permute-start(bf16[4,16512]{1,0:T(4,128)(2,1)S(1)} %get-tuple-element.16), channel_id=1, source_target_pairs={{0,12},{4,0},{8,4},{12,8},{1,13},{5,1},{9,5},{13,9},{2,14},{6,2},{... | collective-permute-start | bytes 396296 | tf_op jit(solution)/shard_map/ppermute | solution.py:26
  46.8 8.1 %collective-permute-start.11 = (bf16[4,16384]{1,0:T(4,128)(2,1)S(1)}, bf16[4,16384]{1,0:T(4,128)(2,1)S(1)}, u32[]{:S(2)}, u32[]{:S(2)}) collective-permute-start(bf16[4,16384]{1,0:T(4,128)(2,1)S(1)} %shard_map.48.refs_0_.refs_4_), channel_id=1, source_target_pairs={{0,4},{4,8},{8,12},{12,0},{1,5},{5,9},{9,13},{13,1},{2,6},{6,10},{... | collective-permute-start | bytes 393224 | tf_op jit(solution)/shard_map/ppermute | solution.py:26
  50.2 9.5 %collective-permute-start.10 = (bf16[4,16384]{1,0:T(4,128)(2,1)S(1)}, bf16[4,16384]{1,0:T(4,128)(2,1)S(1)}, u32[]{:S(2)}, u32[]{:S(2)}) collective-permute-start(bf16[4,16384]{1,0:T(4,128)(2,1)S(1)} %shard_map.48.refs_0_.refs_4_), channel_id=1, source_target_pairs={{0,8},{4,12},{8,0},{12,4},{1,9},{5,13},{9,1},{13,5},{2,10},{6,14},... | collective-permute-start | bytes 393224 | tf_op jit(solution)/shard_map/ppermute | solution.py:26
  51.5 8.2 %collective-permute-start.9 = (bf16[4,16384]{1,0:T(4,128)(2,1)S(1)}, bf16[4,16384]{1,0:T(4,128)(2,1)S(1)}, u32[]{:S(2)}, u32[]{:S(2)}) collective-permute-start(bf16[4,16384]{1,0:T(4,128)(2,1)S(1)} %shard_map.48.refs_0_.refs_4_), channel_id=1, source_target_pairs={{0,12},{4,0},{8,4},{12,8},{1,13},{5,1},{9,5},{13,9},{2,14},{6,2},{... | collective-permute-start | bytes 393224 | tf_op jit(solution)/shard_map/ppermute | solution.py:26
  63.4 3.3 %collective-permute-start.14 = (f32[16,256]{1,0:T(8,128)S(1)}, f32[16,256]{1,0:T(8,128)S(1)}, u32[]{:S(2)}, u32[]{:S(2)}) collective-permute-start(f32[16,256]{1,0:T(8,128)S(1)} %shard_map.49.refs_0_), channel_id=1, source_target_pairs={{0,3},{1,2},{2,1},{3,0},{4,7},{5,6},{6,5},{7,4},{8,11},{9,10},{10,... | collective-permute-start | bytes 49160 | tf_op jit(solution)/shard_map/ppermute | solution.py:34
  63.5 3.7 %collective-permute-start.13 = (f32[16,256]{1,0:T(8,128)S(1)}, f32[16,256]{1,0:T(8,128)S(1)}, u32[]{:S(2)}, u32[]{:S(2)}) collective-permute-start(f32[16,256]{1,0:T(8,128)S(1)} %shard_map.49.refs_0_), channel_id=1, source_target_pairs={{0,2},{1,3},{2,0},{3,1},{4,6},{5,7},{6,4},{7,5},{8,10},{9,11},{10,... | collective-permute-start | bytes 49160 | tf_op jit(solution)/shard_map/ppermute | solution.py:34
  65.0 2.3 %collective-permute-start.12 = (f32[16,256]{1,0:T(8,128)S(1)}, f32[16,256]{1,0:T(8,128)S(1)}, u32[]{:S(2)}, u32[]{:S(2)}) collective-permute-start(f32[16,256]{1,0:T(8,128)S(1)} %shard_map.49.refs_0_), channel_id=1, source_target_pairs={{0,1},{1,0},{2,3},{3,2},{4,5},{5,4},{6,7},{7,6},{8,9},{9,8},{10,11... | collective-permute-start | bytes 49160 | tf_op jit(solution)/shard_map/ppermute | solution.py:34
  70.0 9.5 %collective-permute-start.15 = (bf16[4,16512]{1,0:T(4,128)(2,1)S(1)}, bf16[4,16512]{1,0:T(4,128)(2,1)S(1)}, u32[]{:S(2)}, u32[]{:S(2)}) collective-permute-start(bf16[4,16512]{1,0:T(4,128)(2,1)S(1)} %get-tuple-element.18), channel_id=1, source_target_pairs={{0,4},{4,8},{8,12},{12,0},{1,5},{5,9},{9,13},{13,1},{2,6},{6,10},{... | collective-permute-start | bytes 396296 | tf_op jit(solution)/shard_map/ppermute | solution.py:26
  73.4 10.4 %collective-permute-start.16 = (bf16[4,16512]{1,0:T(4,128)(2,1)S(1)}, bf16[4,16512]{1,0:T(4,128)(2,1)S(1)}, u32[]{:S(2)}, u32[]{:S(2)}) collective-permute-start(bf16[4,16512]{1,0:T(4,128)(2,1)S(1)} %get-tuple-element.19), channel_id=1, source_target_pairs={{0,8},{4,12},{8,0},{12,4},{1,9},{5,13},{9,1},{13,5},{2,10},{6,14},... | collective-permute-start | bytes 396296 | tf_op jit(solution)/shard_map/ppermute | solution.py:26
  75.5 8.3 %collective-permute-start.17 = (bf16[4,16512]{1,0:T(4,128)(2,1)S(1)}, bf16[4,16512]{1,0:T(4,128)(2,1)S(1)}, u32[]{:S(2)}, u32[]{:S(2)}) collective-permute-start(bf16[4,16512]{1,0:T(4,128)(2,1)S(1)} %get-tuple-element.20), channel_id=1, source_target_pairs={{0,12},{4,0},{8,4},{12,8},{1,13},{5,1},{9,5},{13,9},{2,14},{6,2},{... | collective-permute-start | bytes 396296 | tf_op jit(solution)/shard_map/ppermute | solution.py:26

commit v2 on v0

v2 whole, which is shorter than its diff:
```python
import functools
import math

import jax
import jax.numpy as jnp
from jax import lax
from jax.experimental import pallas as pl
from jax.experimental.pallas import tpu as pltpu
from jax.sharding import PartitionSpec as P

PIX = 65536
ITERS = 2
TAIL = 128
VMEM_BYTES = 40 * 1024 * 1024
IN_VMEM = pl.BlockSpec(memory_space=pltpu.VMEM)


def params():
    return pltpu.CompilerParams(vmem_limit_bytes=VMEM_BYTES)


def tree_sum(terms):
    while len(terms) > 1:
        terms = [a + b for a, b in zip(terms[::2], terms[1::2])] + terms[len(terms) & ~1 :]
    return terms[0]


def chunks(size, most):
    step = math.gcd(size, most)
    return [pl.ds(at, step) for at in range(0, size, step)]


def rotate_rows(value, by):
    return value if by == 0 else jnp.concatenate([value[by:], value[:by]], axis=0)


def from_others(block, axis, size):
    return [lax.ppermute(block, axis, [((i + k) % size, i) for i in range(size)]) for k in range(1, size)]


def to_others(blocks, axis, size):
    return [lax.ppermute(blocks[k], axis, [(i, (i + k) % size) for i in range(size)]) for k in range(1, size)]


def exchange_all(part, axes, size):
    if size & (size - 1):
        return [lax.psum(part, axes)]
    return [part] + [lax.ppermute(part, axes, [(i, i ^ k) for i in range(size)]) for k in range(1, size)]


def load_kernel(frames_ref, here_ref, turned_ref, sems):
    pieces = chunks(frames_ref.shape[1], 2048)
    copies = [
        pltpu.make_async_copy(frames_ref.at[:, piece], here_ref.at[:, piece], sems.at[i])
        for i, piece in enumerate(pieces)
    ]
    for copy in copies:
        copy.start()
    for copy, piece in zip(copies, pieces):
        copy.wait()
        turned_ref[piece, :] = here_ref[:, piece].T


def load_frames(frames):
    rows, pix = frames.shape
    return pl.pallas_call(
        load_kernel,
        in_specs=[pl.BlockSpec(memory_space=pl.ANY)],
        out_specs=[IN_VMEM, IN_VMEM],
        out_shape=[pltpu.VMEM((rows, pix), frames.dtype), pltpu.VMEM((pix, rows), frames.dtype)],
        scratch_shapes=[pltpu.SemaphoreType.DMA((len(chunks(pix, 2048)),))],
        compiler_params=params(),
        cost_estimate=pl.CostEstimate(flops=0, bytes_accessed=6 * rows * pix, transcendentals=0),
        name="load_frames",
    )(pltpu.with_memory_space_constraint(frames, pltpu.HBM))


def score_kernel(n, *refs):
    blocks, turned_ref, out_ref = refs[:n], refs[n], refs[n + 1]
    raw, squares = [], []
    for piece in chunks(turned_ref.shape[0], 512):
        model = jnp.concatenate([ref[:, piece] for ref in blocks], axis=0)
        raw.append(jnp.dot(model, turned_ref[piece, :], preferred_element_type=jnp.float32))
        wide = model.astype(jnp.float32)
        squares.append(tree_sum([jnp.square(wide[:, at : at + 128]) for at in range(0, wide.shape[1], 128)]))
        if len(raw) > 4:
            raw, squares = [raw[0] + raw[4], *raw[1:4]], [squares[0] + squares[4], *squares[1:4]]
            raw, squares = raw[1:] + raw[:1], squares[1:] + squares[:1]
    out_ref[...] = tree_sum(raw) - 0.5 * jnp.sum(tree_sum(squares), axis=1, keepdims=True)


def score_parts(blocks, turned):
    pix, rows = turned.shape
    many = sum(b.shape[0] for b in blocks)
    return pl.pallas_call(
        functools.partial(score_kernel, len(blocks)),
        in_specs=[IN_VMEM] * (len(blocks) + 1),
        out_specs=IN_VMEM,
        out_shape=jax.ShapeDtypeStruct((many, rows), jnp.float32),
        compiler_params=params(),
        cost_estimate=pl.CostEstimate(flops=2 * rows * pix * many, bytes_accessed=2 * rows * pix, transcendentals=0),
        name="score_parts",
    )(*blocks, pltpu.with_memory_space_constraint(turned, pltpu.VMEM))


def weigh(parts, prior_ref):
    raw = tree_sum([ref[...] for ref in parts])
    scores = (3.0 / math.sqrt(PIX)) * raw + prior_ref[...]
    up = jnp.exp(scores - jnp.max(scores, axis=0, keepdims=True))
    weights = (up / jnp.sum(up, axis=0, keepdims=True)).astype(jnp.bfloat16).astype(jnp.float32)
    counts = jnp.sum(weights, axis=1, keepdims=True)
    high = counts.astype(jnp.bfloat16).astype(jnp.float32)
    lane = lax.broadcasted_iota(jnp.int32, (counts.shape[0], TAIL), 1)
    return weights, jnp.where(lane < TAIL // 2, high, counts - high)


def plain_totals_kernel(n, *refs):
    parts, prior_ref, frames_ref, out_ref = refs[:n], refs[n], refs[n + 1], refs[n + 2]
    weights, tail = weigh(parts, prior_ref)
    weights = weights.astype(jnp.bfloat16)
    pix = frames_ref.shape[1]
    for piece in chunks(pix, 512):
        total = jnp.dot(weights, frames_ref[:, piece], preferred_element_type=jnp.float32)
        out_ref[:, piece] = total.astype(jnp.bfloat16)
    out_ref[:, pix:] = tail.astype(jnp.bfloat16)


def dense_totals_kernel(n, *refs):
    parts, prior_ref, frames_ref, outs = refs[:n], refs[n], refs[n + 1], refs[n + 2 :]
    weights, tail = weigh(parts, prior_ref)
    turned = [rotate_rows(weights, (-4 * q) % 16).astype(jnp.bfloat16) for q in range(4)]
    quarter = frames_ref.shape[1] // 4
    for piece in chunks(quarter, 512):
        totals = [
            jnp.dot(
                turned[q], frames_ref[:, pl.ds(q * quarter + piece.start, piece.size)], preferred_element_type=jnp.float32
            )
            for q in range(4)
        ]
        upper = lax.broadcasted_iota(jnp.int32, (8, piece.size), 0) < 4
        for k, out_ref in enumerate(outs):
            first = jnp.where(upper, totals[-k % 4][:8], totals[(1 - k) % 4][:8])
            second = jnp.where(upper, totals[(2 - k) % 4][8:], totals[(3 - k) % 4][8:])
            out_ref[:, piece] = jnp.concatenate([first, second], axis=0).astype(jnp.bfloat16)
    for k, out_ref in enumerate(outs):
        out_ref[:, quarter:] = jnp.concatenate([tail[4 * k : 4 * k + 4]] * 4, axis=0).astype(jnp.bfloat16)


def block_totals(parts, prior, frames, dense):
    rows, pix = frames.shape
    many = prior.shape[0]
    if dense:
        kernel, shapes = dense_totals_kernel, [(16, pix // 4 + TAIL)] * 4
    else:
        kernel, shapes = plain_totals_kernel, [(many, pix + TAIL)]
    return pl.pallas_call(
        functools.partial(kernel, len(parts)),
        in_specs=[IN_VMEM] * (len(parts) + 2),
        out_specs=[IN_VMEM] * len(shapes),
        out_shape=[jax.ShapeDtypeStruct(shape, jnp.bfloat16) for shape in shapes],
        compiler_params=params(),
        cost_estimate=pl.CostEstimate(
            flops=2 * rows * pix * many, bytes_accessed=2 * rows * pix, transcendentals=rows * many
        ),
        name="block_totals",
    )(*parts, prior, pltpu.with_memory_space_constraint(frames, pltpu.VMEM))


def plain_update_kernel(terms_ref, owned_ref, out_ref):
    pix = owned_ref.shape[1]
    tail = jnp.sum(terms_ref[:, :, pix:].astype(jnp.float32), axis=0)
    counts = tail[:, :1] + tail[:, TAIL // 2 : TAIL // 2 + 1]
    for piece in chunks(pix, 512):
        total = jnp.sum(terms_ref[:, :, piece].astype(jnp.float32), axis=0)
        out_ref[:, piece] = ((total + owned_ref[:, piece].astype(jnp.float32)) / (counts + 1.0)).astype(out_ref.dtype)


def dense_update_kernel(*refs):
    terms, owned_ref, out_ref = refs[:4], refs[4], refs[5]
    quarter = owned_ref.shape[1] // 4

    def total(piece):
        return tree_sum([rotate_rows(ref[:, piece].astype(jnp.float32), 4 * k) for k, ref in enumerate(terms)])

    tail = total(pl.ds(quarter, TAIL))
    scale = tail[:, :1] + tail[:, TAIL // 2 : TAIL // 2 + 1] + 1.0
    for piece in chunks(quarter, 512):
        spots = [pl.ds(q * quarter + piece.start, piece.size) for q in range(4)]
        owned = jnp.concatenate([owned_ref[:, spot].astype(jnp.float32) for spot in spots], axis=0)
        new = (total(piece) + owned) / scale
        for q, spot in enumerate(spots):
            out_ref[:, spot] = new[4 * q : 4 * q + 4].astype(out_ref.dtype)


def update(terms, owned, dtype):
    return pl.pallas_call(
        dense_update_kernel if len(terms) == 4 else plain_update_kernel,
        in_specs=[IN_VMEM] * (len(terms) + 1),
        out_specs=IN_VMEM,
        out_shape=jax.ShapeDtypeStruct(owned.shape, dtype),
        compiler_params=params(),
        cost_estimate=pl.CostEstimate(flops=8 * owned.size, bytes_accessed=12 * owned.size, transcendentals=0),
        name="update",
    )(*terms, owned)


def local(sizes, frames, slices, log_prior, orient):
    along, across = sizes
    owned, pix = slices.shape
    dense = along == 4 and owned == 4 and pix % 512 == 0
    if dense:
        first = lax.axis_index("frame") * owned
        orient = lax.dynamic_slice_in_dim(jnp.concatenate([orient, orient]), first, orient.shape[0], 0)
    matches = orient[:, None] == jnp.arange(log_prior.shape[0], dtype=jnp.int32)[None, :]
    prior = jnp.sum(jnp.where(matches, log_prior[None, :], 0.0), axis=1, keepdims=True)
    owned_b = slices.astype(jnp.bfloat16)
    here, turned = load_frames(frames)
    for step in range(ITERS):
        if dense:
            blocks = [owned_b] + from_others(owned_b, "frame", along)
        else:
            blocks = [lax.all_gather(owned_b, "frame", axis=0, tiled=True)]
        parts = exchange_all(score_parts(blocks, turned), ("panel", "sub"), across)
        totals = block_totals(parts, prior, here, dense)
        if dense:
            terms = [totals[0]] + to_others(totals, "frame", along)
        else:
            whole = totals[0].reshape(along, owned, totals[0].shape[1])
            terms = [lax.all_to_all(whole, "frame", split_axis=0, concat_axis=0, tiled=False)]
        owned_b = update(terms, owned_b, jnp.bfloat16 if step + 1 < ITERS else jnp.float32)
    return owned_b


def solution(mesh):
    in_specs = (
        P(("groups", "frame"), ("panel", "sub")),
        P(("groups", "frame"), ("panel", "sub")),
        P(),
        P("groups"),
    )
    out_specs = P(("groups", "frame"), ("panel", "sub"))
    sizes = (mesh.shape["frame"], mesh.shape["panel"] * mesh.shape["sub"])
    return jax.shard_map(
        functools.partial(local, sizes), mesh=mesh, in_specs=in_specs, out_specs=out_specs, check_vma=False
    )
```

time: 174 us -> 83.1 us (0.48)
  blocking collectives: 77.1 us -> 0 us
  waiting for transfers between devices: 54.2 us -> 28.3 us
  starting transfers between devices: 0.04 us -> 25.8 us
  matrix products: 22.2 us -> 0 us
  local copies, waits for them, and re-layouts: 0.85 us -> 16.8 us
  between operations: 14.1 us -> 0.08 us
  Pallas kernels: 0 us -> 9.99 us
  other arithmetic: 5.48 us -> 1.31 us
    unnamed x4 -> x0, waiting for transfers between devices: 54.2 us -> none
    psum x4 -> x0, blocking collectives: 43.6 us -> none  [the longest x2 23.3 us: local(): counts = lax.psum(jnp.sum(weights.astype(jnp.float32), axis=0), 'frame')]
    all_gather x2 -> x0, blocking collectives: 33.5 us -> none  [fetch_slices(): return lax.all_gather(owned_b, 'frame', axis=0, tiled=True)]
    ppermute x0 -> x18, waiting for transfers between devices: none -> 28.3 us  [the longest x6 17.6 us: to_others(): lax.ppermute(blocks[k], axis, [(i, (i + k) % size) for i in range(size)])]
    ppermute x0 -> x18, starting transfers between devices: none -> 25.8 us  [the longest x6 12.4 us: from_others(): lax.ppermute(block, axis, [((i + k) % size, i) for i in range(size)])]
    dot_general x4 -> x0, matrix products: 22.2 us -> none  [the longest x2 11.3 us: local(): jnp.einsum('fp,mp->fm', frames, gathered, preferred_element_type=jnp.floa...]
    unnamed x11 -> x18, local copies, waits for them, and re-layouts: 0.85 us -> 16.6 us
    pallas_call x0 -> x7, Pallas kernels: none -> 9.99 us  [the longest x1 3.92 us: load_frames(): pl.pallas_call(load_kernel, in_specs=[pl.BlockSpec(memory_space=pl.ANY)],...]
  transfers between devices with their start and end apart: 2 -> 18, of which waited for: 2 -> 10; matrix products, arithmetic and copies ran while one was open for 0% -> 1% of each run, Pallas kernels for 0% -> 5%
where the time goes in v2:
time: 83.1 us; the launch traced here: 82.3 us
  waiting for transfers between devices  28.3 us (34%)
  starting transfers between devices  25.8 us (31%)
  local copies, waits for them, and re-layouts  16.8 us (20%)
  Pallas kernels  9.99 us (12%)
  other arithmetic  1.31 us (2%)
    ppermute x6, waiting for transfers between devices, to_others(): lax.ppermute(blocks[k], axis, [(i, (i + k) % size) for i in range(size)])  17.6 us
    unnamed x18, local copies, waits for them, and re-layouts  16.6 us
    ppermute x6, starting transfers between devices, from_others(): lax.ppermute(block, axis, [((i + k) % size, i) for i in range(size)])  12.4 us
    ppermute x6, starting transfers between devices, to_others(): lax.ppermute(blocks[k], axis, [(i, (i + k) % size) for i in range(size)])  9.68 us
    ppermute x6, waiting for transfers between devices, from_others(): lax.ppermute(block, axis, [((i + k) % size, i) for i in range(size)])  7.13 us
    pallas_call x1, Pallas kernels, load_frames(): pl.pallas_call(load_kernel, in_specs=[pl.BlockSpec(memory_space=pl.ANY)],...  3.92 us
    ppermute x6, starting transfers between devices, exchange_all(): lax.ppermute(part, axes, [(i, i ^ k) for i in range(size)])  3.74 us
    ppermute x6, waiting for transfers between devices, exchange_all(): lax.ppermute(part, axes, [(i, i ^ k) for i in range(size)])  3.58 us
  transfers between devices with their start and end apart: 18, of which 10 were waited for; matrix products, arithmetic and copies ran while one was open for 1% of the time, Pallas kernels for 5%

profile of v2, /device:TPU:0, one launch (start us, length us, event | category | flops | bytes accessed | tf_op | source)
XLA Modules:
  0.0 82.3 jit_solution(428064057022001973)
XLA Ops:
  0.0 0.0 copy-start.6
  0.0 1.0 %convert_element_type.3.refs_0_.refs_4_ = bf16[4,16384]{1,0:T(4,128)(2,1)S(1)} convert(f32[4,16384]{1,0:T(4,128)} %param.5) | non-fusion elementwise | flops 65536 | bytes 393216 | tf_op jit(solution)/shard_map/convert_element_type | solution.py:216
  1.0 3.1 %collective-permute-start.2 = (bf16[4,16384]{1,0:T(4,128)(2,1)S(1)}, bf16[4,16384]{1,0:T(4,128)(2,1)S(1)}, u32[]{:S(2)}, u32[]{:S(2)}) collective-permute-start(bf16[4,16384]{1,0:T(4,128)(2,1)S(1)} %convert_element_type.3.refs_0_.refs_4_), channel_id=1, source_target_pairs={{12,0},{0,4},{4,8},{8,12},{13,1},{1,5},{5,9},{9,13},{14,2},{2,6},{... | collective-permute-start | bytes 393224 | tf_op jit(solution)/shard_map/ppermute | solution.py:38
  4.1 2.6 %collective-permute-start.1 = (bf16[4,16384]{1,0:T(4,128)(2,1)S(1)}, bf16[4,16384]{1,0:T(4,128)(2,1)S(1)}, u32[]{:S(2)}, u32[]{:S(2)}) collective-permute-start(bf16[4,16384]{1,0:T(4,128)(2,1)S(1)} %convert_element_type.3.refs_0_.refs_4_), channel_id=1, source_target_pairs={{8,0},{12,4},{0,8},{4,12},{9,1},{13,5},{1,9},{5,13},{10,2},{14,6},... | collective-permute-start | bytes 393224 | tf_op jit(solution)/shard_map/ppermute | solution.py:38
  6.7 1.3 %collective-permute-start = (bf16[4,16384]{1,0:T(4,128)(2,1)S(1)}, bf16[4,16384]{1,0:T(4,128)(2,1)S(1)}, u32[]{:S(2)}, u32[]{:S(2)}) collective-permute-start(bf16[4,16384]{1,0:T(4,128)(2,1)S(1)} %convert_element_type.3.refs_0_.refs_4_), channel_id=1, source_target_pairs={{4,0},{8,4},{12,8},{0,12},{5,1},{9,5},{13,9},{1,13},{6,2},{10,6},{... | collective-permute-start | bytes 393224 | tf_op jit(solution)/shard_map/ppermute | solution.py:38
  8.0 0.0 copy-start.5
  8.0 3.9 %load_frames.1 = (bf16[256,16384]{1,0:T(8,128)(2,1)S(1)}, bf16[16384,256]{1,0:T(8,128)(2,1)S(1)}) custom-call(bf16[256,16384]{1,0:T(8,128)(2,1)} %frames_ref.1), custom_call_target="tpu_custom_call" | custom-call | bytes 25165824 | tf_op jit(solution)/shard_map/load_frames/pallas_call | solution.py:66
  12.0 0.0 copy-start
  12.0 3.3 %copy-done = bf16[256,16384]{1,0:T(8,128)(2,1)} copy-done((bf16[256,16384]{1,0:T(8,128)(2,1)}, bf16[256,16384]{1,0:T(8,128)(2,1)S(1)}, u32[]{:S(2)}) %copy-start) | copy-done | bytes 8388632
  15.2 0.0 copy-start.2
  15.2 3.2 %copy-done.2 = bf16[16384,256]{1,0:T(8,128)(2,1)} copy-done((bf16[16384,256]{1,0:T(8,128)(2,1)}, bf16[16384,256]{1,0:T(8,128)(2,1)S(1)}, u32[]{:S(2)}) %copy-start.2) | copy-done | bytes 8388632
  18.5 0.0 copy-done.6
  18.5 0.1 pad_add_fusion
  18.5 0.1 dynamic_slice.3
  18.6 0.0 collective-permute-done.2.refs_3_
  18.6 0.0 collective-permute-done.1.refs_2_
  18.6 0.0 collective-permute-done.refs_1_
  18.6 0.0 copy-start.3
  18.6 3.4 %copy-done.3 = bf16[16384,256]{1,0:T(8,128)(2,1)S(1)} copy-done((bf16[16384,256]{1,0:T(8,128)(2,1)S(1)}, bf16[16384,256]{1,0:T(8,128)(2,1)}, u32[]{:S(2)}) %copy-start.3) | copy-done | bytes 8388632
  22.0 1.2 %score_parts.2.refs_0_ = f32[16,256]{1,0:T(8,128)S(1)} custom-call(bf16[4,16384]{1,0:T(4,128)(2,1)S(1)} %convert_element_type.3.refs_0_.refs_4_, bf16[4,16384]{1,0:T(4,128)(2,1)S(1)} %collective-permute-done.refs_1_, bf16[4,16384]{1,0:T(4,128)(2,1)S(1)} %collective-permute-done.1.refs_2_, bf16[4,16384]{1,0:T(4,128)(2,1)S(1)} %collective-permute-done.2.refs_3_, ...), custom_call_target="tpu_custom_call" | custom-call | flops 134217728 | bytes 8388608 | tf_op jit(solution)/shard_map/score_parts/pallas_call | solution.py:95
  23.2 0.1 collective-permute-start.5
  23.3 1.4 %collective-permute-start.4 = (f32[16,256]{1,0:T(8,128)S(1)}, f32[16,256]{1,0:T(8,128)S(1)}, u32[]{:S(2)}, u32[]{:S(2)}) collective-permute-start(f32[16,256]{1,0:T(8,128)S(1)} %score_parts.2.refs_0_), channel_id=1, source_target_pairs={{0,2},{1,3},{2,0},{3,1},{4,6},{5,7},{6,4},{7,5},{8,10},{9,11},{10,... | collective-permute-start | bytes 49160 | tf_op jit(solution)/shard_map/ppermute | solution.py:48
  24.7 0.3 collective-permute-start.3
  25.1 0.0 copy-done.5
  25.1 0.2 select_reduce_fusion
  25.3 0.1 copy.7.refs_4_
  25.4 1.1 %collective-permute-done.5.refs_3_ = f32[16,256]{1,0:T(8,128)S(1)} collective-permute-done((f32[16,256]{1,0:T(8,128)S(1)}, f32[16,256]{1,0:T(8,128)S(1)}, u32[]{:S(2)}, u32[]{:S(2)}) %collective-permute-start.5) | collective-permute-done | bytes 16416 | tf_op jit(solution)/shard_map/ppermute | solution.py:48
  26.5 0.5 collective-permute-done.4.refs_2_
  27.0 0.0 collective-permute-done.3.refs_1_
  27.0 0.0 copy-start.1
  27.0 3.4 %copy-done.1 = bf16[256,16384]{1,0:T(8,128)(2,1)S(1)} copy-done((bf16[256,16384]{1,0:T(8,128)(2,1)S(1)}, bf16[256,16384]{1,0:T(8,128)(2,1)}, u32[]{:S(2)}) %copy-start.1) | copy-done | bytes 8388632
  30.4 0.0 slice-start
  30.4 1.3 %block_totals.2 = (bf16[16,4224]{1,0:T(8,128)(2,1)S(1)}, bf16[16,4224]{1,0:T(8,128)(2,1)S(1)}, bf16[16,4224]{1,0:T(8,128)(2,1)S(1)}, bf16[16,4224]{1,0:T(8,128)(2,1)S(1)}) custom-call(f32[16,256]{1,0:T(8,128)S(1)} %score_parts.2.refs_0_, f32[16,256]{1,0:T(8,128)S(1)} %collective-permute-done.3.refs_1_, f32[16,256]{1,0:T(8,128)S(1)} %collective-permute-done.4.refs_2_, ...), custom_call_target="tpu_custom_call" | custom-call | flops 134217728 | bytes 8388608 | tf_op jit(solution)/shard_map/block_totals/pallas_call | solution.py:156
  31.7 1.0 %collective-permute-start.6 = (bf16[16,4224]{1,0:T(8,128)(2,1)S(1)}, bf16[16,4224]{1,0:T(8,128)(2,1)S(1)}, u32[]{:S(2)}, u32[]{:S(2)}) collective-permute-start(bf16[16,4224]{1,0:T(8,128)(2,1)S(1)} %get-tuple-element.18), channel_id=1, source_target_pairs={{0,4},{4,8},{8,12},{12,0},{1,5},{5,9},{9,13},{13,1},{2,6},{6,10},{... | collective-permute-start | bytes 405512 | tf_op jit(solution)/shard_map/ppermute | solution.py:42
  32.7 0.6 collective-permute-start.7
  33.3 2.3 %collective-permute-start.8 = (bf16[16,4224]{1,0:T(8,128)(2,1)S(1)}, bf16[16,4224]{1,0:T(8,128)(2,1)S(1)}, u32[]{:S(2)}, u32[]{:S(2)}) collective-permute-start(bf16[16,4224]{1,0:T(8,128)(2,1)S(1)} %get-tuple-element.20), channel_id=1, source_target_pairs={{0,12},{4,0},{8,4},{12,8},{1,13},{5,1},{9,5},{13,9},{2,14},{6,2},{... | collective-permute-start | bytes 405512 | tf_op jit(solution)/shard_map/ppermute | solution.py:42
  35.6 4.5 %collective-permute-done.6.refs_1_ = bf16[16,4224]{1,0:T(8,128)(2,1)S(1)} collective-permute-done((bf16[16,4224]{1,0:T(8,128)(2,1)S(1)}, bf16[16,4224]{1,0:T(8,128)(2,1)S(1)}, u32[]{:S(2)}, u32[]{:S(2)}) %collective-permute-start.6) | collective-permute-done | bytes 135200 | tf_op jit(solution)/shard_map/ppermute | solution.py:42
  40.1 5.2 %collective-permute-done.7.refs_2_ = bf16[16,4224]{1,0:T(8,128)(2,1)S(1)} collective-permute-done((bf16[16,4224]{1,0:T(8,128)(2,1)S(1)}, bf16[16,4224]{1,0:T(8,128)(2,1)S(1)}, u32[]{:S(2)}, u32[]{:S(2)}) %collective-permute-start.7) | collective-permute-done | bytes 135200 | tf_op jit(solution)/shard_map/ppermute | solution.py:42
  45.3 0.0 collective-permute-done.8.refs_3_
  45.3 0.2 update.2.refs_0_.refs_4_
  45.6 3.0 %collective-permute-start.11 = (bf16[4,16384]{1,0:T(4,128)(2,1)S(1)}, bf16[4,16384]{1,0:T(4,128)(2,1)S(1)}, u32[]{:S(2)}, u32[]{:S(2)}) collective-permute-start(bf16[4,16384]{1,0:T(4,128)(2,1)S(1)} %update.2.refs_0_.refs_4_), channel_id=1, source_target_pairs={{12,0},{0,4},{4,8},{8,12},{13,1},{1,5},{5,9},{9,13},{14,2},{2,6},{... | collective-permute-start | bytes 393224 | tf_op jit(solution)/shard_map/ppermute | solution.py:38
  48.5 0.1 collective-permute-start.10
  48.7 2.3 %collective-permute-start.9 = (bf16[4,16384]{1,0:T(4,128)(2,1)S(1)}, bf16[4,16384]{1,0:T(4,128)(2,1)S(1)}, u32[]{:S(2)}, u32[]{:S(2)}) collective-permute-start(bf16[4,16384]{1,0:T(4,128)(2,1)S(1)} %update.2.refs_0_.refs_4_), channel_id=1, source_target_pairs={{4,0},{8,4},{12,8},{0,12},{5,1},{9,5},{13,9},{1,13},{6,2},{10,6},{... | collective-permute-start | bytes 393224 | tf_op jit(solution)/shard_map/ppermute | solution.py:38
  51.0 2.8 %collective-permute-done.11.refs_3_ = bf16[4,16384]{1,0:T(4,128)(2,1)S(1)} collective-permute-done((bf16[4,16384]{1,0:T(4,128)(2,1)S(1)}, bf16[4,16384]{1,0:T(4,128)(2,1)S(1)}, u32[]{:S(2)}, u32[]{:S(2)}) %collective-permute-start.11) | collective-permute-done | bytes 131104 | tf_op jit(solution)/shard_map/ppermute | solution.py:38
  53.8 4.3 %collective-permute-done.10.refs_2_ = bf16[4,16384]{1,0:T(4,128)(2,1)S(1)} collective-permute-done((bf16[4,16384]{1,0:T(4,128)(2,1)S(1)}, bf16[4,16384]{1,0:T(4,128)(2,1)S(1)}, u32[]{:S(2)}, u32[]{:S(2)}) %collective-permute-start.10) | collective-permute-done | bytes 131104 | tf_op jit(solution)/shard_map/ppermute | solution.py:38
  58.1 0.0 collective-permute-done.9.refs_1_
  58.1 3.4 %copy-done.4 = bf16[16384,256]{1,0:T(8,128)(2,1)S(1)} copy-done((bf16[16384,256]{1,0:T(8,128)(2,1)S(1)}, bf16[16384,256]{1,0:T(8,128)(2,1)}, u32[]{:S(2)}) %copy-start.4) | copy-done | bytes 8388632
  61.5 1.2 %score_parts.3.refs_0_ = f32[16,256]{1,0:T(8,128)S(1)} custom-call(bf16[4,16384]{1,0:T(4,128)(2,1)S(1)} %update.2.refs_0_.refs_4_, bf16[4,16384]{1,0:T(4,128)(2,1)S(1)} %collective-permute-done.9.refs_1_, bf16[4,16384]{1,0:T(4,128)(2,1)S(1)} %collective-permute-done.10.refs_2_, bf16[4,16384]{1,0:T(4,128)(2,1)S(1)} %collective-permute-done.11.refs_3_, ...), custom_call_target="tpu_custom_call" | custom-call | flops 134217728 | bytes 8388608 | tf_op jit(solution)/shard_map/score_parts/pallas_call | solution.py:95
  62.7 0.0 collective-permute-start.14
  62.7 1.6 %collective-permute-start.13 = (f32[16,256]{1,0:T(8,128)S(1)}, f32[16,256]{1,0:T(8,128)S(1)}, u32[]{:S(2)}, u32[]{:S(2)}) collective-permute-start(f32[16,256]{1,0:T(8,128)S(1)} %score_parts.3.refs_0_), channel_id=1, source_target_pairs={{0,2},{1,3},{2,0},{3,1},{4,6},{5,7},{6,4},{7,5},{8,10},{9,11},{10,... | collective-permute-start | bytes 49160 | tf_op jit(solution)/shard_map/ppermute | solution.py:48
  64.3 0.3 collective-permute-start.12
  64.6 1.4 %collective-permute-done.14.refs_3_ = f32[16,256]{1,0:T(8,128)S(1)} collective-permute-done((f32[16,256]{1,0:T(8,128)S(1)}, f32[16,256]{1,0:T(8,128)S(1)}, u32[]{:S(2)}, u32[]{:S(2)}) %collective-permute-start.14) | collective-permute-done | bytes 16416 | tf_op jit(solution)/shard_map/ppermute | solution.py:48
  65.9 0.6 collective-permute-done.13.refs_2_
  66.5 0.0 collective-permute-done.12.refs_1_
  66.5 0.0 slice-done
  66.5 0.0 slice-done.1
  66.5 1.3 %block_totals.3 = (bf16[16,4224]{1,0:T(8,128)(2,1)S(1)}, bf16[16,4224]{1,0:T(8,128)(2,1)S(1)}, bf16[16,4224]{1,0:T(8,128)(2,1)S(1)}, bf16[16,4224]{1,0:T(8,128)(2,1)S(1)}) custom-call(f32[16,256]{1,0:T(8,128)S(1)} %score_parts.3.refs_0_, f32[16,256]{1,0:T(8,128)S(1)} %collective-permute-done.12.refs_1_, f32[16,256]{1,0:T(8,128)S(1)} %collective-permute-done.13.refs_2_, ...), custom_call_target="tpu_custom_call" | custom-call | flops 134217728 | bytes 8388608 | tf_op jit(solution)/shard_map/block_totals/pallas_call | solution.py:156
  67.8 3.4 %collective-permute-start.15 = (bf16[16,4224]{1,0:T(8,128)(2,1)S(1)}, bf16[16,4224]{1,0:T(8,128)(2,1)S(1)}, u32[]{:S(2)}, u32[]{:S(2)}) collective-permute-start(bf16[16,4224]{1,0:T(8,128)(2,1)S(1)} %get-tuple-element.22), channel_id=1, source_target_pairs={{0,4},{4,8},{8,12},{12,0},{1,5},{5,9},{9,13},{13,1},{2,6},{6,10},{... | collective-permute-start | bytes 405512 | tf_op jit(solution)/shard_map/ppermute | solution.py:42
  71.1 1.7 %collective-permute-start.16 = (bf16[16,4224]{1,0:T(8,128)(2,1)S(1)}, bf16[16,4224]{1,0:T(8,128)(2,1)S(1)}, u32[]{:S(2)}, u32[]{:S(2)}) collective-permute-start(bf16[16,4224]{1,0:T(8,128)(2,1)S(1)} %get-tuple-element.23), channel_id=1, source_target_pairs={{0,8},{4,12},{8,0},{12,4},{1,9},{5,13},{9,1},{13,5},{2,10},{6,14},... | collective-permute-start | bytes 405512 | tf_op jit(solution)/shard_map/ppermute | solution.py:42
  72.8 0.7 collective-permute-start.17
  73.6 3.3 %collective-permute-done.15.refs_1_ = bf16[16,4224]{1,0:T(8,128)(2,1)S(1)} collective-permute-done((bf16[16,4224]{1,0:T(8,128)(2,1)S(1)}, bf16[16,4224]{1,0:T(8,128)(2,1)S(1)}, u32[]{:S(2)}, u32[]{:S(2)}) %collective-permute-start.15) | collective-permute-done | bytes 135200 | tf_op jit(solution)/shard_map/ppermute | solution.py:42
  76.8 4.6 %collective-permute-done.16.refs_2_ = bf16[16,4224]{1,0:T(8,128)(2,1)S(1)} collective-permute-done((bf16[16,4224]{1,0:T(8,128)(2,1)S(1)}, bf16[16,4224]{1,0:T(8,128)(2,1)S(1)}, u32[]{:S(2)}, u32[]{:S(2)}) %collective-permute-start.16) | collective-permute-done | bytes 135200 | tf_op jit(solution)/shard_map/ppermute | solution.py:42
  81.4 0.0 collective-permute-done.17.refs_3_
  81.4 0.9 %update.3 = f32[4,16384]{1,0:T(4,128)} custom-call(bf16[16,4224]{1,0:T(8,128)(2,1)S(1)} %get-tuple-element.21.refs_0_, bf16[16,4224]{1,0:T(8,128)(2,1)S(1)} %collective-permute-done.15.refs_1_, bf16[16,4224]{1,0:T(8,128)(2,1)S(1)} %collective-permute-done.16.refs_2_, bf16[16,4224]{1,0:T(8,128)(2,1)S(1)} %collective-permute-done.17.refs_3_, ...), custom_call_target="tpu_custom_call" | custom-call | flops 524288 | bytes 786432 | tf_op jit(solution)/shard_map/update/pallas_call | solution.py:196
  (3 shorter events, 0.0 us)
Async XLA Ops:
  0.0 18.5 %copy-start.6 = (s32[16]{0:T(128)S(1)}, s32[16]{0:T(128)}, u32[]{:S(2)}) copy-start(s32[16]{0:T(128)} %param.7) | copy-start | bytes 196
  1.0 17.6 %collective-permute-start.2 = (bf16[4,16384]{1,0:T(4,128)(2,1)S(1)}, bf16[4,16384]{1,0:T(4,128)(2,1)S(1)}, u32[]{:S(2)}, u32[]{:S(2)}) collective-permute-start(bf16[4,16384]{1,0:T(4,128)(2,1)S(1)} %convert_element_type.3.refs_0_.refs_4_), channel_id=1, source_target_pairs={{12,0},{0,4},{4,8},{8,12},{13,1},{1,5},{5,9},{9,13},{14,2},{2,6},{... | collective-permute-start | bytes 393224 | tf_op jit(solution)/shard_map/ppermute | solution.py:38
  4.1 14.5 %collective-permute-start.1 = (bf16[4,16384]{1,0:T(4,128)(2,1)S(1)}, bf16[4,16384]{1,0:T(4,128)(2,1)S(1)}, u32[]{:S(2)}, u32[]{:S(2)}) collective-permute-start(bf16[4,16384]{1,0:T(4,128)(2,1)S(1)} %convert_element_type.3.refs_0_.refs_4_), channel_id=1, source_target_pairs={{8,0},{12,4},{0,8},{4,12},{9,1},{13,5},{1,9},{5,13},{10,2},{14,6},... | collective-permute-start | bytes 393224 | tf_op jit(solution)/shard_map/ppermute | solution.py:38
  6.7 11.9 %collective-permute-start = (bf16[4,16384]{1,0:T(4,128)(2,1)S(1)}, bf16[4,16384]{1,0:T(4,128)(2,1)S(1)}, u32[]{:S(2)}, u32[]{:S(2)}) collective-permute-start(bf16[4,16384]{1,0:T(4,128)(2,1)S(1)} %convert_element_type.3.refs_0_.refs_4_), channel_id=1, source_target_pairs={{4,0},{8,4},{12,8},{0,12},{5,1},{9,5},{13,9},{1,13},{6,2},{10,6},{... | collective-permute-start | bytes 393224 | tf_op jit(solution)/shard_map/ppermute | solution.py:38
  8.0 17.0 %copy-start.5 = (f32[4096]{0:T(1024)S(1)}, f32[4096]{0:T(1024)}, u32[]{:S(2)}) copy-start(f32[4096]{0:T(1024)} %param.6) | copy-start | bytes 49156
  12.0 3.3 %copy-start = (bf16[256,16384]{1,0:T(8,128)(2,1)}, bf16[256,16384]{1,0:T(8,128)(2,1)S(1)}, u32[]{:S(2)}) copy-start(bf16[256,16384]{1,0:T(8,128)(2,1)S(1)} %get-tuple-element.16.refs_5_) | copy-start | bytes 25165828
  15.2 3.2 %copy-start.2 = (bf16[16384,256]{1,0:T(8,128)(2,1)}, bf16[16384,256]{1,0:T(8,128)(2,1)S(1)}, u32[]{:S(2)}) copy-start(bf16[16384,256]{1,0:T(8,128)(2,1)S(1)} %get-tuple-element.15.refs_4_) | copy-start | bytes 25165828
  18.6 3.4 %copy-start.3 = (bf16[16384,256]{1,0:T(8,128)(2,1)S(1)}, bf16[16384,256]{1,0:T(8,128)(2,1)}, u32[]{:S(2)}) copy-start(bf16[16384,256]{1,0:T(8,128)(2,1)} %copy-done.2) | copy-start | bytes 25165828
  23.2 3.3 %collective-permute-start.5 = (f32[16,256]{1,0:T(8,128)S(1)}, f32[16,256]{1,0:T(8,128)S(1)}, u32[]{:S(2)}, u32[]{:S(2)}) collective-permute-start(f32[16,256]{1,0:T(8,128)S(1)} %score_parts.2.refs_0_), channel_id=1, source_target_pairs={{0,3},{1,2},{2,1},{3,0},{4,7},{5,6},{6,5},{7,4},{8,11},{9,10},{10,... | collective-permute-start | bytes 49160 | tf_op jit(solution)/shard_map/ppermute | solution.py:48
  23.3 3.7 %collective-permute-start.4 = (f32[16,256]{1,0:T(8,128)S(1)}, f32[16,256]{1,0:T(8,128)S(1)}, u32[]{:S(2)}, u32[]{:S(2)}) collective-permute-start(f32[16,256]{1,0:T(8,128)S(1)} %score_parts.2.refs_0_), channel_id=1, source_target_pairs={{0,2},{1,3},{2,0},{3,1},{4,6},{5,7},{6,4},{7,5},{8,10},{9,11},{10,... | collective-permute-start | bytes 49160 | tf_op jit(solution)/shard_map/ppermute | solution.py:48
  24.7 2.3 %collective-permute-start.3 = (f32[16,256]{1,0:T(8,128)S(1)}, f32[16,256]{1,0:T(8,128)S(1)}, u32[]{:S(2)}, u32[]{:S(2)}) collective-permute-start(f32[16,256]{1,0:T(8,128)S(1)} %score_parts.2.refs_0_), channel_id=1, source_target_pairs={{0,1},{1,0},{2,3},{3,2},{4,5},{5,4},{6,7},{7,6},{8,9},{9,8},{10,11... | collective-permute-start | bytes 49160 | tf_op jit(solution)/shard_map/ppermute | solution.py:48
  27.0 3.4 %copy-start.1 = (bf16[256,16384]{1,0:T(8,128)(2,1)S(1)}, bf16[256,16384]{1,0:T(8,128)(2,1)}, u32[]{:S(2)}) copy-start(bf16[256,16384]{1,0:T(8,128)(2,1)} %copy-done) | copy-start | bytes 25165828
  30.4 36.1 %slice-start = ((s8[8388608]{0:T(1024)(128)(4,1)}), s8[4194304]{0:T(1024)(128)(4,1)S(1)}, s32[]{:S(2)}) async-start(s8[8388608]{0:T(1024)(128)(4,1)} %bitcast.1), calls=%async_computation | async-start | bytes 8388608
  31.7 8.4 %collective-permute-start.6 = (bf16[16,4224]{1,0:T(8,128)(2,1)S(1)}, bf16[16,4224]{1,0:T(8,128)(2,1)S(1)}, u32[]{:S(2)}, u32[]{:S(2)}) collective-permute-start(bf16[16,4224]{1,0:T(8,128)(2,1)S(1)} %get-tuple-element.18), channel_id=1, source_target_pairs={{0,4},{4,8},{8,12},{12,0},{1,5},{5,9},{9,13},{13,1},{2,6},{6,10},{... | collective-permute-start | bytes 405512 | tf_op jit(solution)/shard_map/ppermute | solution.py:42
  32.7 12.6 %collective-permute-start.7 = (bf16[16,4224]{1,0:T(8,128)(2,1)S(1)}, bf16[16,4224]{1,0:T(8,128)(2,1)S(1)}, u32[]{:S(2)}, u32[]{:S(2)}) collective-permute-start(bf16[16,4224]{1,0:T(8,128)(2,1)S(1)} %get-tuple-element.19), channel_id=1, source_target_pairs={{0,8},{4,12},{8,0},{12,4},{1,9},{5,13},{9,1},{13,5},{2,10},{6,14},... | collective-permute-start | bytes 405512 | tf_op jit(solution)/shard_map/ppermute | solution.py:42
  33.3 12.0 %collective-permute-start.8 = (bf16[16,4224]{1,0:T(8,128)(2,1)S(1)}, bf16[16,4224]{1,0:T(8,128)(2,1)S(1)}, u32[]{:S(2)}, u32[]{:S(2)}) collective-permute-start(bf16[16,4224]{1,0:T(8,128)(2,1)S(1)} %get-tuple-element.20), channel_id=1, source_target_pairs={{0,12},{4,0},{8,4},{12,8},{1,13},{5,1},{9,5},{13,9},{2,14},{6,2},{... | collective-permute-start | bytes 405512 | tf_op jit(solution)/shard_map/ppermute | solution.py:42
  45.3 21.2 %slice-start.1 = ((s8[8388608]{0:T(1024)(128)(4,1)}), s8[4194304]{0:T(1024)(128)(4,1)S(1)}, s32[]{:S(2)}) async-start(s8[8388608]{0:T(1024)(128)(4,1)} %bitcast.1), calls=%async_computation.1 | async-start | bytes 8388608
  45.6 8.2 %collective-permute-start.11 = (bf16[4,16384]{1,0:T(4,128)(2,1)S(1)}, bf16[4,16384]{1,0:T(4,128)(2,1)S(1)}, u32[]{:S(2)}, u32[]{:S(2)}) collective-permute-start(bf16[4,16384]{1,0:T(4,128)(2,1)S(1)} %update.2.refs_0_.refs_4_), channel_id=1, source_target_pairs={{12,0},{0,4},{4,8},{8,12},{13,1},{1,5},{5,9},{9,13},{14,2},{2,6},{... | collective-permute-start | bytes 393224 | tf_op jit(solution)/shard_map/ppermute | solution.py:38
  48.5 9.6 %collective-permute-start.10 = (bf16[4,16384]{1,0:T(4,128)(2,1)S(1)}, bf16[4,16384]{1,0:T(4,128)(2,1)S(1)}, u32[]{:S(2)}, u32[]{:S(2)}) collective-permute-start(bf16[4,16384]{1,0:T(4,128)(2,1)S(1)} %update.2.refs_0_.refs_4_), channel_id=1, source_target_pairs={{8,0},{12,4},{0,8},{4,12},{9,1},{13,5},{1,9},{5,13},{10,2},{14,6},... | collective-permute-start | bytes 393224 | tf_op jit(solution)/shard_map/ppermute | solution.py:38
  48.7 9.4 %collective-permute-start.9 = (bf16[4,16384]{1,0:T(4,128)(2,1)S(1)}, bf16[4,16384]{1,0:T(4,128)(2,1)S(1)}, u32[]{:S(2)}, u32[]{:S(2)}) collective-permute-start(bf16[4,16384]{1,0:T(4,128)(2,1)S(1)} %update.2.refs_0_.refs_4_), channel_id=1, source_target_pairs={{4,0},{8,4},{12,8},{0,12},{5,1},{9,5},{13,9},{1,13},{6,2},{10,6},{... | collective-permute-start | bytes 393224 | tf_op jit(solution)/shard_map/ppermute | solution.py:38
  58.1 3.4 %copy-start.4 = (bf16[16384,256]{1,0:T(8,128)(2,1)S(1)}, bf16[16384,256]{1,0:T(8,128)(2,1)}, u32[]{:S(2)}) copy-start(bf16[16384,256]{1,0:T(8,128)(2,1)} %copy-done.2) | copy-start | bytes 25165828
  62.7 3.2 %collective-permute-start.14 = (f32[16,256]{1,0:T(8,128)S(1)}, f32[16,256]{1,0:T(8,128)S(1)}, u32[]{:S(2)}, u32[]{:S(2)}) collective-permute-start(f32[16,256]{1,0:T(8,128)S(1)} %score_parts.3.refs_0_), channel_id=1, source_target_pairs={{0,3},{1,2},{2,1},{3,0},{4,7},{5,6},{6,5},{7,4},{8,11},{9,10},{10,... | collective-permute-start | bytes 49160 | tf_op jit(solution)/shard_map/ppermute | solution.py:48
  62.7 3.8 %collective-permute-start.13 = (f32[16,256]{1,0:T(8,128)S(1)}, f32[16,256]{1,0:T(8,128)S(1)}, u32[]{:S(2)}, u32[]{:S(2)}) collective-permute-start(f32[16,256]{1,0:T(8,128)S(1)} %score_parts.3.refs_0_), channel_id=1, source_target_pairs={{0,2},{1,3},{2,0},{3,1},{4,6},{5,7},{6,4},{7,5},{8,10},{9,11},{10,... | collective-permute-start | bytes 49160 | tf_op jit(solution)/shard_map/ppermute | solution.py:48
  64.3 2.2 %collective-permute-start.12 = (f32[16,256]{1,0:T(8,128)S(1)}, f32[16,256]{1,0:T(8,128)S(1)}, u32[]{:S(2)}, u32[]{:S(2)}) collective-permute-start(f32[16,256]{1,0:T(8,128)S(1)} %score_parts.3.refs_0_), channel_id=1, source_target_pairs={{0,1},{1,0},{2,3},{3,2},{4,5},{5,4},{6,7},{7,6},{8,9},{9,8},{10,11... | collective-permute-start | bytes 49160 | tf_op jit(solution)/shard_map/ppermute | solution.py:48
  67.8 9.1 %collective-permute-start.15 = (bf16[16,4224]{1,0:T(8,128)(2,1)S(1)}, bf16[16,4224]{1,0:T(8,128)(2,1)S(1)}, u32[]{:S(2)}, u32[]{:S(2)}) collective-permute-start(bf16[16,4224]{1,0:T(8,128)(2,1)S(1)} %get-tuple-element.22), channel_id=1, source_target_pairs={{0,4},{4,8},{8,12},{12,0},{1,5},{5,9},{9,13},{13,1},{2,6},{6,10},{... | collective-permute-start | bytes 405512 | tf_op jit(solution)/shard_map/ppermute | solution.py:42
  71.1 10.3 %collective-permute-start.16 = (bf16[16,4224]{1,0:T(8,128)(2,1)S(1)}, bf16[16,4224]{1,0:T(8,128)(2,1)S(1)}, u32[]{:S(2)}, u32[]{:S(2)}) collective-permute-start(bf16[16,4224]{1,0:T(8,128)(2,1)S(1)} %get-tuple-element.23), channel_id=1, source_target_pairs={{0,8},{4,12},{8,0},{12,4},{1,9},{5,13},{9,1},{13,5},{2,10},{6,14},... | collective-permute-start | bytes 405512 | tf_op jit(solution)/shard_map/ppermute | solution.py:42
  72.8 8.6 %collective-permute-start.17 = (bf16[16,4224]{1,0:T(8,128)(2,1)S(1)}, bf16[16,4224]{1,0:T(8,128)(2,1)S(1)}, u32[]{:S(2)}, u32[]{:S(2)}) collective-permute-start(bf16[16,4224]{1,0:T(8,128)(2,1)S(1)} %get-tuple-element.24), channel_id=1, source_target_pairs={{0,12},{4,0},{8,4},{12,8},{1,13},{5,1},{9,5},{13,9},{2,14},{6,2},{... | collective-permute-start | bytes 405512 | tf_op jit(solution)/shard_map/ppermute | solution.py:42

commit v3 on v2

--- a/solution.py
+++ b/solution.py
@@ -11,7 +11,7 @@
 PIX = 65536
 ITERS = 2
 TAIL = 128
-VMEM_BYTES = 40 * 1024 * 1024
+VMEM_BYTES = 12 * 1024 * 1024
 IN_VMEM = pl.BlockSpec(memory_space=pltpu.VMEM)
 
 
@@ -46,6 +46,26 @@
     if size & (size - 1):
         return [lax.psum(part, axes)]
     return [part] + [lax.ppermute(part, axes, [(i, i ^ k) for i in range(size)]) for k in range(1, size)]
+
+
+def prior_kernel(turn, orient_ref, log_prior_ref, out_ref):
+    many, columns = out_ref.shape
+    first = lax.axis_index("frame") * turn
+    for row in range(many):
+        entry = log_prior_ref[orient_ref[lax.rem(first + row, many)]]
+        out_ref[row : row + 1, :] = jnp.full((1, columns), entry, jnp.float32)
+
+
+def slice_priors(orient, log_prior, turn, columns):
+    return pl.pallas_call(
+        functools.partial(prior_kernel, turn),
+        in_specs=[pl.BlockSpec(memory_space=pltpu.SMEM)] * 2,
+        out_specs=IN_VMEM,
+        out_shape=jax.ShapeDtypeStruct((orient.shape[0], columns), jnp.float32),
+        compiler_params=params(),
+        cost_estimate=pl.CostEstimate(flops=0, bytes_accessed=4 * log_prior.size, transcendentals=0),
+        name="slice_priors",
+    )(orient, log_prior)
 
 
 def load_kernel(frames_ref, here_ref, turned_ref, sems):
@@ -208,12 +228,9 @@
     along, across = sizes
     owned, pix = slices.shape
     dense = along == 4 and owned == 4 and pix % 512 == 0
-    if dense:
-        first = lax.axis_index("frame") * owned
-        orient = lax.dynamic_slice_in_dim(jnp.concatenate([orient, orient]), first, orient.shape[0], 0)
-    matches = orient[:, None] == jnp.arange(log_prior.shape[0], dtype=jnp.int32)[None, :]
-    prior = jnp.sum(jnp.where(matches, log_prior[None, :], 0.0), axis=1, keepdims=True)
+    prior = slice_priors(orient, log_prior, owned if dense else 0, frames.shape[0])
     owned_b = slices.astype(jnp.bfloat16)
+    frames, prior = lax.optimization_barrier((frames, prior))
     here, turned = load_frames(frames)
     for step in range(ITERS):
         if dense:

time: 83.1 us -> 71.5 us (0.86)
  local copies, waits for them, and re-layouts: 16.8 us -> 1.37 us
  starting transfers between devices: 25.8 us -> 28.3 us
    unnamed x18 -> x4, local copies, waits for them, and re-layouts: 16.6 us -> 1.37 us
    ppermute x6, starting transfers between devices: 9.68 us -> 11.7 us  [to_others(): lax.ppermute(blocks[k], axis, [(i, (i + k) % size) for i in range(size)])]
    ppermute x6, waiting for transfers between devices: 17.6 us -> 15.9 us  [to_others(): lax.ppermute(blocks[k], axis, [(i, (i + k) % size) for i in range(size)])]
    ppermute x6, waiting for transfers between devices: 3.58 us -> 4.88 us  [exchange_all(): lax.ppermute(part, axes, [(i, i ^ k) for i in range(size)])]
    ppermute x6, waiting for transfers between devices: 7.13 us -> 8.17 us  [from_others(): lax.ppermute(block, axis, [((i + k) % size, i) for i in range(size)])]
    pallas_call x0 -> x1, Pallas kernels: none -> 0.85 us  [slice_priors(): pl.pallas_call(functools.partial(prior_kernel, turn), in_specs=[pl.BlockS...]
  transfers between devices with their start and end apart: 18 -> 18, of which waited for: 10 -> 11; matrix products, arithmetic and copies ran while one was open for 1% -> 0% of each run, Pallas kernels for 5% -> 7%
where the time goes in v3:
time: 71.5 us; the launch traced here: 70.4 us
  waiting for transfers between devices  28.9 us (40%)
  starting transfers between devices  28.3 us (40%)
  Pallas kernels  10.7 us (15%)
  local copies, waits for them, and re-layouts  1.37 us (2%)
  other arithmetic  1 us (1%)
    ppermute x6, waiting for transfers between devices, to_others(): lax.ppermute(blocks[k], axis, [(i, (i + k) % size) for i in range(size)])  15.9 us
    ppermute x6, starting transfers between devices, from_others(): lax.ppermute(block, axis, [((i + k) % size, i) for i in range(size)])  12.9 us
    ppermute x6, starting transfers between devices, to_others(): lax.ppermute(blocks[k], axis, [(i, (i + k) % size) for i in range(size)])  11.7 us
    ppermute x6, waiting for transfers between devices, from_others(): lax.ppermute(block, axis, [((i + k) % size, i) for i in range(size)])  8.17 us
    ppermute x6, waiting for transfers between devices, exchange_all(): lax.ppermute(part, axes, [(i, i ^ k) for i in range(size)])  4.88 us
    pallas_call x1, Pallas kernels, load_frames(): pl.pallas_call(load_kernel, in_specs=[pl.BlockSpec(memory_space=pl.ANY)],...  3.91 us
    ppermute x6, starting transfers between devices, exchange_all(): lax.ppermute(part, axes, [(i, i ^ k) for i in range(size)])  3.74 us
    pallas_call x2, Pallas kernels, block_totals(): pl.pallas_call(functools.partial(kernel, len(parts)), in_specs=[IN_VMEM]...  2.41 us
  transfers between devices with their start and end apart: 18, of which 11 were waited for; matrix products, arithmetic and copies ran while one was open for 0% of the time, Pallas kernels for 7%

profile of v3, /device:TPU:0, one launch (start us, length us, event | category | flops | bytes accessed | tf_op | source)
XLA Modules:
  0.0 70.4 jit_solution(9978800071919677498)
XLA Ops:
  0.0 1.0 %convert_element_type.3.refs_0_.refs_4_ = bf16[4,16384]{1,0:T(4,128)(2,1)S(1)} convert(f32[4,16384]{1,0:T(4,128)} %param.5) | non-fusion elementwise | flops 65536 | bytes 393216 | tf_op jit(solution)/shard_map/convert_element_type | solution.py:232
  1.0 3.1 %collective-permute-start.2 = (bf16[4,16384]{1,0:T(4,128)(2,1)S(1)}, bf16[4,16384]{1,0:T(4,128)(2,1)S(1)}, u32[]{:S(2)}, u32[]{:S(2)}) collective-permute-start(bf16[4,16384]{1,0:T(4,128)(2,1)S(1)} %convert_element_type.3.refs_0_.refs_4_), channel_id=1, source_target_pairs={{12,0},{0,4},{4,8},{8,12},{13,1},{1,5},{5,9},{9,13},{14,2},{2,6},{... | collective-permute-start | bytes 393224 | tf_op jit(solution)/shard_map/ppermute | solution.py:38
  4.1 2.6 %collective-permute-start.1 = (bf16[4,16384]{1,0:T(4,128)(2,1)S(1)}, bf16[4,16384]{1,0:T(4,128)(2,1)S(1)}, u32[]{:S(2)}, u32[]{:S(2)}) collective-permute-start(bf16[4,16384]{1,0:T(4,128)(2,1)S(1)} %convert_element_type.3.refs_0_.refs_4_), channel_id=1, source_target_pairs={{8,0},{12,4},{0,8},{4,12},{9,1},{13,5},{1,9},{5,13},{10,2},{14,6},... | collective-permute-start | bytes 393224 | tf_op jit(solution)/shard_map/ppermute | solution.py:38
  6.7 1.3 %collective-permute-start = (bf16[4,16384]{1,0:T(4,128)(2,1)S(1)}, bf16[4,16384]{1,0:T(4,128)(2,1)S(1)}, u32[]{:S(2)}, u32[]{:S(2)}) collective-permute-start(bf16[4,16384]{1,0:T(4,128)(2,1)S(1)} %convert_element_type.3.refs_0_.refs_4_), channel_id=1, source_target_pairs={{4,0},{8,4},{12,8},{0,12},{5,1},{9,5},{13,9},{1,13},{6,2},{10,6},{... | collective-permute-start | bytes 393224 | tf_op jit(solution)/shard_map/ppermute | solution.py:38
  8.0 0.0 copy-start
  8.0 0.7 %copy-done = f32[4096]{0:T(1024)S(1)} copy-done((f32[4096]{0:T(1024)S(1)}, f32[4096]{0:T(1024)}, u32[]{:S(2)}) %copy-start) | copy-done | bytes 16408
  8.7 0.0 copy-start.1
  8.7 0.7 copy-done.1
  9.4 0.9 %slice_priors.1.refs_4_ = f32[16,256]{1,0:T(8,128)S(1)} custom-call(s32[16]{0:T(128)S(1)} %copy-done.1, f32[4096]{0:T(1024)S(1)} %copy-done), custom_call_target="tpu_custom_call" | custom-call | bytes 16384 | tf_op jit(solution)/shard_map/slice_priors/pallas_call | solution.py:60
  10.2 3.9 %load_frames.1 = (bf16[256,16384]{1,0:T(8,128)(2,1)S(1)}, bf16[16384,256]{1,0:T(8,128)(2,1)S(1)}) custom-call(bf16[256,16384]{1,0:T(8,128)(2,1)} %frames_ref), custom_call_target="tpu_custom_call" | custom-call | bytes 25165824 | tf_op jit(solution)/shard_map/load_frames/pallas_call | solution.py:86
  14.2 0.0 collective-permute-done.2.refs_3_
  14.2 1.1 %collective-permute-done.1.refs_2_ = bf16[4,16384]{1,0:T(4,128)(2,1)S(1)} collective-permute-done((bf16[4,16384]{1,0:T(4,128)(2,1)S(1)}, bf16[4,16384]{1,0:T(4,128)(2,1)S(1)}, u32[]{:S(2)}, u32[]{:S(2)}) %collective-permute-start.1) | collective-permute-done | bytes 131104 | tf_op jit(solution)/shard_map/ppermute | solution.py:38
  15.3 0.0 collective-permute-done.refs_1_
  15.3 1.2 %score_parts.2.refs_0_ = f32[16,256]{1,0:T(8,128)S(1)} custom-call(bf16[4,16384]{1,0:T(4,128)(2,1)S(1)} %convert_element_type.3.refs_0_.refs_4_, bf16[4,16384]{1,0:T(4,128)(2,1)S(1)} %collective-permute-done.refs_1_, bf16[4,16384]{1,0:T(4,128)(2,1)S(1)} %collective-permute-done.1.refs_2_, bf16[4,16384]{1,0:T(4,128)(2,1)S(1)} %collective-permute-done.2.refs_3_, ...), custom_call_target="tpu_custom_call" | custom-call | flops 134217728 | bytes 8388608 | tf_op jit(solution)/shard_map/score_parts/pallas_call | solution.py:115
  16.5 1.0 %collective-permute-start.5 = (f32[16,256]{1,0:T(8,128)S(1)}, f32[16,256]{1,0:T(8,128)S(1)}, u32[]{:S(2)}, u32[]{:S(2)}) collective-permute-start(f32[16,256]{1,0:T(8,128)S(1)} %score_parts.2.refs_0_), channel_id=1, source_target_pairs={{0,3},{1,2},{2,1},{3,0},{4,7},{5,6},{6,5},{7,4},{8,11},{9,10},{10,... | collective-permute-start | bytes 49160 | tf_op jit(solution)/shard_map/ppermute | solution.py:48
  17.5 0.5 collective-permute-start.4
  18.1 0.3 collective-permute-start.3
  18.4 1.4 %collective-permute-done.5.refs_3_ = f32[16,256]{1,0:T(8,128)S(1)} collective-permute-done((f32[16,256]{1,0:T(8,128)S(1)}, f32[16,256]{1,0:T(8,128)S(1)}, u32[]{:S(2)}, u32[]{:S(2)}) %collective-permute-start.5) | collective-permute-done | bytes 16416 | tf_op jit(solution)/shard_map/ppermute | solution.py:48
  19.7 1.5 %collective-permute-done.4.refs_2_ = f32[16,256]{1,0:T(8,128)S(1)} collective-permute-done((f32[16,256]{1,0:T(8,128)S(1)}, f32[16,256]{1,0:T(8,128)S(1)}, u32[]{:S(2)}, u32[]{:S(2)}) %collective-permute-start.4) | collective-permute-done | bytes 16416 | tf_op jit(solution)/shard_map/ppermute | solution.py:48
  21.3 0.0 collective-permute-done.3.refs_1_
  21.3 1.2 %block_totals.2 = (bf16[16,4224]{1,0:T(8,128)(2,1)S(1)}, bf16[16,4224]{1,0:T(8,128)(2,1)S(1)}, bf16[16,4224]{1,0:T(8,128)(2,1)S(1)}, bf16[16,4224]{1,0:T(8,128)(2,1)S(1)}) custom-call(f32[16,256]{1,0:T(8,128)S(1)} %score_parts.2.refs_0_, f32[16,256]{1,0:T(8,128)S(1)} %collective-permute-done.3.refs_1_, f32[16,256]{1,0:T(8,128)S(1)} %collective-permute-done.4.refs_2_, ...), custom_call_target="tpu_custom_call" | custom-call | flops 134217728 | bytes 8388608 | tf_op jit(solution)/shard_map/block_totals/pallas_call | solution.py:176
  22.5 3.4 %collective-permute-start.6 = (bf16[16,4224]{1,0:T(8,128)(2,1)S(1)}, bf16[16,4224]{1,0:T(8,128)(2,1)S(1)}, u32[]{:S(2)}, u32[]{:S(2)}) collective-permute-start(bf16[16,4224]{1,0:T(8,128)(2,1)S(1)} %get-tuple-element.22), channel_id=1, source_target_pairs={{0,4},{4,8},{8,12},{12,0},{1,5},{5,9},{9,13},{13,1},{2,6},{6,10},{... | collective-permute-start | bytes 405512 | tf_op jit(solution)/shard_map/ppermute | solution.py:42
  25.9 0.6 collective-permute-start.7
  26.5 1.9 %collective-permute-start.8 = (bf16[16,4224]{1,0:T(8,128)(2,1)S(1)}, bf16[16,4224]{1,0:T(8,128)(2,1)S(1)}, u32[]{:S(2)}, u32[]{:S(2)}) collective-permute-start(bf16[16,4224]{1,0:T(8,128)(2,1)S(1)} %get-tuple-element.24), channel_id=1, source_target_pairs={{0,12},{4,0},{8,4},{12,8},{1,13},{5,1},{9,5},{13,9},{2,14},{6,2},{... | collective-permute-start | bytes 405512 | tf_op jit(solution)/shard_map/ppermute | solution.py:42
  28.3 2.5 %collective-permute-done.6.refs_1_ = bf16[16,4224]{1,0:T(8,128)(2,1)S(1)} collective-permute-done((bf16[16,4224]{1,0:T(8,128)(2,1)S(1)}, bf16[16,4224]{1,0:T(8,128)(2,1)S(1)}, u32[]{:S(2)}, u32[]{:S(2)}) %collective-permute-start.6) | collective-permute-done | bytes 135200 | tf_op jit(solution)/shard_map/ppermute | solution.py:42
  30.8 5.1 %collective-permute-done.7.refs_2_ = bf16[16,4224]{1,0:T(8,128)(2,1)S(1)} collective-permute-done((bf16[16,4224]{1,0:T(8,128)(2,1)S(1)}, bf16[16,4224]{1,0:T(8,128)(2,1)S(1)}, u32[]{:S(2)}, u32[]{:S(2)}) %collective-permute-start.7) | collective-permute-done | bytes 135200 | tf_op jit(solution)/shard_map/ppermute | solution.py:42
  35.9 0.0 collective-permute-done.8.refs_3_
  35.9 0.2 update.2.refs_0_.refs_4_
  36.2 3.4 %collective-permute-start.11 = (bf16[4,16384]{1,0:T(4,128)(2,1)S(1)}, bf16[4,16384]{1,0:T(4,128)(2,1)S(1)}, u32[]{:S(2)}, u32[]{:S(2)}) collective-permute-start(bf16[4,16384]{1,0:T(4,128)(2,1)S(1)} %update.2.refs_0_.refs_4_), channel_id=1, source_target_pairs={{12,0},{0,4},{4,8},{8,12},{13,1},{1,5},{5,9},{9,13},{14,2},{2,6},{... | collective-permute-start | bytes 393224 | tf_op jit(solution)/shard_map/ppermute | solution.py:38
  39.6 1.3 %collective-permute-start.10 = (bf16[4,16384]{1,0:T(4,128)(2,1)S(1)}, bf16[4,16384]{1,0:T(4,128)(2,1)S(1)}, u32[]{:S(2)}, u32[]{:S(2)}) collective-permute-start(bf16[4,16384]{1,0:T(4,128)(2,1)S(1)} %update.2.refs_0_.refs_4_), channel_id=1, source_target_pairs={{8,0},{12,4},{0,8},{4,12},{9,1},{13,5},{1,9},{5,13},{10,2},{14,6},... | collective-permute-start | bytes 393224 | tf_op jit(solution)/shard_map/ppermute | solution.py:38
  40.9 1.1 %collective-permute-start.9 = (bf16[4,16384]{1,0:T(4,128)(2,1)S(1)}, bf16[4,16384]{1,0:T(4,128)(2,1)S(1)}, u32[]{:S(2)}, u32[]{:S(2)}) collective-permute-start(bf16[4,16384]{1,0:T(4,128)(2,1)S(1)} %update.2.refs_0_.refs_4_), channel_id=1, source_target_pairs={{4,0},{8,4},{12,8},{0,12},{5,1},{9,5},{13,9},{1,13},{6,2},{10,6},{... | collective-permute-start | bytes 393224 | tf_op jit(solution)/shard_map/ppermute | solution.py:38
  42.0 2.2 %collective-permute-done.11.refs_3_ = bf16[4,16384]{1,0:T(4,128)(2,1)S(1)} collective-permute-done((bf16[4,16384]{1,0:T(4,128)(2,1)S(1)}, bf16[4,16384]{1,0:T(4,128)(2,1)S(1)}, u32[]{:S(2)}, u32[]{:S(2)}) %collective-permute-start.11) | collective-permute-done | bytes 131104 | tf_op jit(solution)/shard_map/ppermute | solution.py:38
  44.2 4.8 %collective-permute-done.10.refs_2_ = bf16[4,16384]{1,0:T(4,128)(2,1)S(1)} collective-permute-done((bf16[4,16384]{1,0:T(4,128)(2,1)S(1)}, bf16[4,16384]{1,0:T(4,128)(2,1)S(1)}, u32[]{:S(2)}, u32[]{:S(2)}) %collective-permute-start.10) | collective-permute-done | bytes 131104 | tf_op jit(solution)/shard_map/ppermute | solution.py:38
  49.1 0.0 collective-permute-done.9.refs_1_
  49.1 1.2 %score_parts.3.refs_0_ = f32[16,256]{1,0:T(8,128)S(1)} custom-call(bf16[4,16384]{1,0:T(4,128)(2,1)S(1)} %update.2.refs_0_.refs_4_, bf16[4,16384]{1,0:T(4,128)(2,1)S(1)} %collective-permute-done.9.refs_1_, bf16[4,16384]{1,0:T(4,128)(2,1)S(1)} %collective-permute-done.10.refs_2_, bf16[4,16384]{1,0:T(4,128)(2,1)S(1)} %collective-permute-done.11.refs_3_, ...), custom_call_target="tpu_custom_call" | custom-call | flops 134217728 | bytes 8388608 | tf_op jit(solution)/shard_map/score_parts/pallas_call | solution.py:115
  50.3 0.1 collective-permute-start.14
  50.4 1.5 %collective-permute-start.13 = (f32[16,256]{1,0:T(8,128)S(1)}, f32[16,256]{1,0:T(8,128)S(1)}, u32[]{:S(2)}, u32[]{:S(2)}) collective-permute-start(f32[16,256]{1,0:T(8,128)S(1)} %score_parts.3.refs_0_), channel_id=1, source_target_pairs={{0,2},{1,3},{2,0},{3,1},{4,6},{5,7},{6,4},{7,5},{8,10},{9,11},{10,... | collective-permute-start | bytes 49160 | tf_op jit(solution)/shard_map/ppermute | solution.py:48
  51.8 0.3 collective-permute-start.12
  52.1 1.4 %collective-permute-done.14.refs_3_ = f32[16,256]{1,0:T(8,128)S(1)} collective-permute-done((f32[16,256]{1,0:T(8,128)S(1)}, f32[16,256]{1,0:T(8,128)S(1)}, u32[]{:S(2)}, u32[]{:S(2)}) %collective-permute-start.14) | collective-permute-done | bytes 16416 | tf_op jit(solution)/shard_map/ppermute | solution.py:48
  53.5 0.6 collective-permute-done.13.refs_2_
  54.1 0.0 collective-permute-done.12.refs_1_
  54.1 1.2 %block_totals.3 = (bf16[16,4224]{1,0:T(8,128)(2,1)S(1)}, bf16[16,4224]{1,0:T(8,128)(2,1)S(1)}, bf16[16,4224]{1,0:T(8,128)(2,1)S(1)}, bf16[16,4224]{1,0:T(8,128)(2,1)S(1)}) custom-call(f32[16,256]{1,0:T(8,128)S(1)} %score_parts.3.refs_0_, f32[16,256]{1,0:T(8,128)S(1)} %collective-permute-done.12.refs_1_, f32[16,256]{1,0:T(8,128)S(1)} %collective-permute-done.13.refs_2_, ...), custom_call_target="tpu_custom_call" | custom-call | flops 134217728 | bytes 8388608 | tf_op jit(solution)/shard_map/block_totals/pallas_call | solution.py:176
  55.3 3.4 %collective-permute-start.15 = (bf16[16,4224]{1,0:T(8,128)(2,1)S(1)}, bf16[16,4224]{1,0:T(8,128)(2,1)S(1)}, u32[]{:S(2)}, u32[]{:S(2)}) collective-permute-start(bf16[16,4224]{1,0:T(8,128)(2,1)S(1)} %get-tuple-element.26), channel_id=1, source_target_pairs={{0,4},{4,8},{8,12},{12,0},{1,5},{5,9},{9,13},{13,1},{2,6},{6,10},{... | collective-permute-start | bytes 405512 | tf_op jit(solution)/shard_map/ppermute | solution.py:42
  58.7 2.1 %collective-permute-start.16 = (bf16[16,4224]{1,0:T(8,128)(2,1)S(1)}, bf16[16,4224]{1,0:T(8,128)(2,1)S(1)}, u32[]{:S(2)}, u32[]{:S(2)}) collective-permute-start(bf16[16,4224]{1,0:T(8,128)(2,1)S(1)} %get-tuple-element.27), channel_id=1, source_target_pairs={{0,8},{4,12},{8,0},{12,4},{1,9},{5,13},{9,1},{13,5},{2,10},{6,14},... | collective-permute-start | bytes 405512 | tf_op jit(solution)/shard_map/ppermute | solution.py:42
  60.9 0.3 collective-permute-start.17
  61.2 3.7 %collective-permute-done.15.refs_1_ = bf16[16,4224]{1,0:T(8,128)(2,1)S(1)} collective-permute-done((bf16[16,4224]{1,0:T(8,128)(2,1)S(1)}, bf16[16,4224]{1,0:T(8,128)(2,1)S(1)}, u32[]{:S(2)}, u32[]{:S(2)}) %collective-permute-start.15) | collective-permute-done | bytes 135200 | tf_op jit(solution)/shard_map/ppermute | solution.py:42
  64.9 4.6 %collective-permute-done.16.refs_2_ = bf16[16,4224]{1,0:T(8,128)(2,1)S(1)} collective-permute-done((bf16[16,4224]{1,0:T(8,128)(2,1)S(1)}, bf16[16,4224]{1,0:T(8,128)(2,1)S(1)}, u32[]{:S(2)}, u32[]{:S(2)}) %collective-permute-start.16) | collective-permute-done | bytes 135200 | tf_op jit(solution)/shard_map/ppermute | solution.py:42
  69.4 0.0 collective-permute-done.17.refs_3_
  69.4 0.9 %update.3 = f32[4,16384]{1,0:T(4,128)} custom-call(bf16[16,4224]{1,0:T(8,128)(2,1)S(1)} %get-tuple-element.25.refs_0_, bf16[16,4224]{1,0:T(8,128)(2,1)S(1)} %collective-permute-done.15.refs_1_, bf16[16,4224]{1,0:T(8,128)(2,1)S(1)} %collective-permute-done.16.refs_2_, bf16[16,4224]{1,0:T(8,128)(2,1)S(1)} %collective-permute-done.17.refs_3_, ...), custom_call_target="tpu_custom_call" | custom-call | flops 524288 | bytes 786432 | tf_op jit(solution)/shard_map/update/pallas_call | solution.py:216
Async XLA Ops:
  1.0 13.2 %collective-permute-start.2 = (bf16[4,16384]{1,0:T(4,128)(2,1)S(1)}, bf16[4,16384]{1,0:T(4,128)(2,1)S(1)}, u32[]{:S(2)}, u32[]{:S(2)}) collective-permute-start(bf16[4,16384]{1,0:T(4,128)(2,1)S(1)} %convert_element_type.3.refs_0_.refs_4_), channel_id=1, source_target_pairs={{12,0},{0,4},{4,8},{8,12},{13,1},{1,5},{5,9},{9,13},{14,2},{2,6},{... | collective-permute-start | bytes 393224 | tf_op jit(solution)/shard_map/ppermute | solution.py:38
  4.1 11.2 %collective-permute-start.1 = (bf16[4,16384]{1,0:T(4,128)(2,1)S(1)}, bf16[4,16384]{1,0:T(4,128)(2,1)S(1)}, u32[]{:S(2)}, u32[]{:S(2)}) collective-permute-start(bf16[4,16384]{1,0:T(4,128)(2,1)S(1)} %convert_element_type.3.refs_0_.refs_4_), channel_id=1, source_target_pairs={{8,0},{12,4},{0,8},{4,12},{9,1},{13,5},{1,9},{5,13},{10,2},{14,6},... | collective-permute-start | bytes 393224 | tf_op jit(solution)/shard_map/ppermute | solution.py:38
  6.7 8.6 %collective-permute-start = (bf16[4,16384]{1,0:T(4,128)(2,1)S(1)}, bf16[4,16384]{1,0:T(4,128)(2,1)S(1)}, u32[]{:S(2)}, u32[]{:S(2)}) collective-permute-start(bf16[4,16384]{1,0:T(4,128)(2,1)S(1)} %convert_element_type.3.refs_0_.refs_4_), channel_id=1, source_target_pairs={{4,0},{8,4},{12,8},{0,12},{5,1},{9,5},{13,9},{1,13},{6,2},{10,6},{... | collective-permute-start | bytes 393224 | tf_op jit(solution)/shard_map/ppermute | solution.py:38
  8.0 0.7 %copy-start = (f32[4096]{0:T(1024)S(1)}, f32[4096]{0:T(1024)}, u32[]{:S(2)}) copy-start(f32[4096]{0:T(1024)} %log_prior_ref.1) | copy-start | bytes 49156
  8.7 0.7 copy-start.1
  16.5 3.2 %collective-permute-start.5 = (f32[16,256]{1,0:T(8,128)S(1)}, f32[16,256]{1,0:T(8,128)S(1)}, u32[]{:S(2)}, u32[]{:S(2)}) collective-permute-start(f32[16,256]{1,0:T(8,128)S(1)} %score_parts.2.refs_0_), channel_id=1, source_target_pairs={{0,3},{1,2},{2,1},{3,0},{4,7},{5,6},{6,5},{7,4},{8,11},{9,10},{10,... | collective-permute-start | bytes 49160 | tf_op jit(solution)/shard_map/ppermute | solution.py:48
  17.5 3.7 %collective-permute-start.4 = (f32[16,256]{1,0:T(8,128)S(1)}, f32[16,256]{1,0:T(8,128)S(1)}, u32[]{:S(2)}, u32[]{:S(2)}) collective-permute-start(f32[16,256]{1,0:T(8,128)S(1)} %score_parts.2.refs_0_), channel_id=1, source_target_pairs={{0,2},{1,3},{2,0},{3,1},{4,6},{5,7},{6,4},{7,5},{8,10},{9,11},{10,... | collective-permute-start | bytes 49160 | tf_op jit(solution)/shard_map/ppermute | solution.py:48
  18.1 3.2 %collective-permute-start.3 = (f32[16,256]{1,0:T(8,128)S(1)}, f32[16,256]{1,0:T(8,128)S(1)}, u32[]{:S(2)}, u32[]{:S(2)}) collective-permute-start(f32[16,256]{1,0:T(8,128)S(1)} %score_parts.2.refs_0_), channel_id=1, source_target_pairs={{0,1},{1,0},{2,3},{3,2},{4,5},{5,4},{6,7},{7,6},{8,9},{9,8},{10,11... | collective-permute-start | bytes 49160 | tf_op jit(solution)/shard_map/ppermute | solution.py:48
  22.5 8.4 %collective-permute-start.6 = (bf16[16,4224]{1,0:T(8,128)(2,1)S(1)}, bf16[16,4224]{1,0:T(8,128)(2,1)S(1)}, u32[]{:S(2)}, u32[]{:S(2)}) collective-permute-start(bf16[16,4224]{1,0:T(8,128)(2,1)S(1)} %get-tuple-element.22), channel_id=1, source_target_pairs={{0,4},{4,8},{8,12},{12,0},{1,5},{5,9},{9,13},{13,1},{2,6},{6,10},{... | collective-permute-start | bytes 405512 | tf_op jit(solution)/shard_map/ppermute | solution.py:42
  25.9 10.0 %collective-permute-start.7 = (bf16[16,4224]{1,0:T(8,128)(2,1)S(1)}, bf16[16,4224]{1,0:T(8,128)(2,1)S(1)}, u32[]{:S(2)}, u32[]{:S(2)}) collective-permute-start(bf16[16,4224]{1,0:T(8,128)(2,1)S(1)} %get-tuple-element.23), channel_id=1, source_target_pairs={{0,8},{4,12},{8,0},{12,4},{1,9},{5,13},{9,1},{13,5},{2,10},{6,14},... | collective-permute-start | bytes 405512 | tf_op jit(solution)/shard_map/ppermute | solution.py:42
  26.5 9.5 %collective-permute-start.8 = (bf16[16,4224]{1,0:T(8,128)(2,1)S(1)}, bf16[16,4224]{1,0:T(8,128)(2,1)S(1)}, u32[]{:S(2)}, u32[]{:S(2)}) collective-permute-start(bf16[16,4224]{1,0:T(8,128)(2,1)S(1)} %get-tuple-element.24), channel_id=1, source_target_pairs={{0,12},{4,0},{8,4},{12,8},{1,13},{5,1},{9,5},{13,9},{2,14},{6,2},{... | collective-permute-start | bytes 405512 | tf_op jit(solution)/shard_map/ppermute | solution.py:42
  36.2 8.0 %collective-permute-start.11 = (bf16[4,16384]{1,0:T(4,128)(2,1)S(1)}, bf16[4,16384]{1,0:T(4,128)(2,1)S(1)}, u32[]{:S(2)}, u32[]{:S(2)}) collective-permute-start(bf16[4,16384]{1,0:T(4,128)(2,1)S(1)} %update.2.refs_0_.refs_4_), channel_id=1, source_target_pairs={{12,0},{0,4},{4,8},{8,12},{13,1},{1,5},{5,9},{9,13},{14,2},{2,6},{... | collective-permute-start | bytes 393224 | tf_op jit(solution)/shard_map/ppermute | solution.py:38
  39.6 9.5 %collective-permute-start.10 = (bf16[4,16384]{1,0:T(4,128)(2,1)S(1)}, bf16[4,16384]{1,0:T(4,128)(2,1)S(1)}, u32[]{:S(2)}, u32[]{:S(2)}) collective-permute-start(bf16[4,16384]{1,0:T(4,128)(2,1)S(1)} %update.2.refs_0_.refs_4_), channel_id=1, source_target_pairs={{8,0},{12,4},{0,8},{4,12},{9,1},{13,5},{1,9},{5,13},{10,2},{14,6},... | collective-permute-start | bytes 393224 | tf_op jit(solution)/shard_map/ppermute | solution.py:38
  40.9 8.2 %collective-permute-start.9 = (bf16[4,16384]{1,0:T(4,128)(2,1)S(1)}, bf16[4,16384]{1,0:T(4,128)(2,1)S(1)}, u32[]{:S(2)}, u32[]{:S(2)}) collective-permute-start(bf16[4,16384]{1,0:T(4,128)(2,1)S(1)} %update.2.refs_0_.refs_4_), channel_id=1, source_target_pairs={{4,0},{8,4},{12,8},{0,12},{5,1},{9,5},{13,9},{1,13},{6,2},{10,6},{... | collective-permute-start | bytes 393224 | tf_op jit(solution)/shard_map/ppermute | solution.py:38
  50.3 3.2 %collective-permute-start.14 = (f32[16,256]{1,0:T(8,128)S(1)}, f32[16,256]{1,0:T(8,128)S(1)}, u32[]{:S(2)}, u32[]{:S(2)}) collective-permute-start(f32[16,256]{1,0:T(8,128)S(1)} %score_parts.3.refs_0_), channel_id=1, source_target_pairs={{0,3},{1,2},{2,1},{3,0},{4,7},{5,6},{6,5},{7,4},{8,11},{9,10},{10,... | collective-permute-start | bytes 49160 | tf_op jit(solution)/shard_map/ppermute | solution.py:48
  50.4 3.7 %collective-permute-start.13 = (f32[16,256]{1,0:T(8,128)S(1)}, f32[16,256]{1,0:T(8,128)S(1)}, u32[]{:S(2)}, u32[]{:S(2)}) collective-permute-start(f32[16,256]{1,0:T(8,128)S(1)} %score_parts.3.refs_0_), channel_id=1, source_target_pairs={{0,2},{1,3},{2,0},{3,1},{4,6},{5,7},{6,4},{7,5},{8,10},{9,11},{10,... | collective-permute-start | bytes 49160 | tf_op jit(solution)/shard_map/ppermute | solution.py:48
  51.8 2.3 %collective-permute-start.12 = (f32[16,256]{1,0:T(8,128)S(1)}, f32[16,256]{1,0:T(8,128)S(1)}, u32[]{:S(2)}, u32[]{:S(2)}) collective-permute-start(f32[16,256]{1,0:T(8,128)S(1)} %score_parts.3.refs_0_), channel_id=1, source_target_pairs={{0,1},{1,0},{2,3},{3,2},{4,5},{5,4},{6,7},{7,6},{8,9},{9,8},{10,11... | collective-permute-start | bytes 49160 | tf_op jit(solution)/shard_map/ppermute | solution.py:48
  55.3 9.5 %collective-permute-start.15 = (bf16[16,4224]{1,0:T(8,128)(2,1)S(1)}, bf16[16,4224]{1,0:T(8,128)(2,1)S(1)}, u32[]{:S(2)}, u32[]{:S(2)}) collective-permute-start(bf16[16,4224]{1,0:T(8,128)(2,1)S(1)} %get-tuple-element.26), channel_id=1, source_target_pairs={{0,4},{4,8},{8,12},{12,0},{1,5},{5,9},{9,13},{13,1},{2,6},{6,10},{... | collective-permute-start | bytes 405512 | tf_op jit(solution)/shard_map/ppermute | solution.py:42
  58.7 10.7 %collective-permute-start.16 = (bf16[16,4224]{1,0:T(8,128)(2,1)S(1)}, bf16[16,4224]{1,0:T(8,128)(2,1)S(1)}, u32[]{:S(2)}, u32[]{:S(2)}) collective-permute-start(bf16[16,4224]{1,0:T(8,128)(2,1)S(1)} %get-tuple-element.27), channel_id=1, source_target_pairs={{0,8},{4,12},{8,0},{12,4},{1,9},{5,13},{9,1},{13,5},{2,10},{6,14},... | collective-permute-start | bytes 405512 | tf_op jit(solution)/shard_map/ppermute | solution.py:42
  60.9 8.6 %collective-permute-start.17 = (bf16[16,4224]{1,0:T(8,128)(2,1)S(1)}, bf16[16,4224]{1,0:T(8,128)(2,1)S(1)}, u32[]{:S(2)}, u32[]{:S(2)}) collective-permute-start(bf16[16,4224]{1,0:T(8,128)(2,1)S(1)} %get-tuple-element.28), channel_id=1, source_target_pairs={{0,12},{4,0},{8,4},{12,8},{1,13},{5,1},{9,5},{13,9},{2,14},{6,2},{... | collective-permute-start | bytes 405512 | tf_op jit(solution)/shard_map/ppermute | solution.py:42

commit v4 on v2

v4 whole, which is shorter than its diff:
```python
import functools
import math

import jax
import jax.numpy as jnp
from jax import lax
from jax.experimental import pallas as pl
from jax.experimental.pallas import tpu as pltpu
from jax.sharding import PartitionSpec as P

PIX = 65536
ITERS = 2
GATHER_ORDER = (0, 1, 2, 3, 4, 5)
SCATTER_ORDER = (0, 1, 2, 3, 4)
TAIL = 128
VMEM_BYTES = 12 * 1024 * 1024
IN_VMEM = pl.BlockSpec(memory_space=pltpu.VMEM)


def params():
    return pltpu.CompilerParams(vmem_limit_bytes=VMEM_BYTES)


def tree_sum(terms):
    while len(terms) > 1:
        terms = [a + b for a, b in zip(terms[::2], terms[1::2])] + terms[len(terms) & ~1 :]
    return terms[0]


def chunks(size, most):
    step = math.gcd(size, most)
    return [pl.ds(at, step) for at in range(0, size, step)]


def rotate_rows(value, by):
    return value if by == 0 else jnp.concatenate([value[by:], value[:by]], axis=0)


def early(value, flops):
    return pl.pallas_call(
        lambda in_ref, out_ref: None,
        in_specs=[pl.BlockSpec(memory_space=pl.ANY)],
        out_specs=pl.BlockSpec(memory_space=pl.ANY),
        out_shape=jax.ShapeDtypeStruct(value.shape, value.dtype),
        input_output_aliases={0: 0},
        compiler_params=params(),
        cost_estimate=pl.CostEstimate(flops=flops, bytes_accessed=0, transcendentals=0),
        name="early",
    )(value)


def swap(value, distance):
    return lax.ppermute(value, "frame", [(i, i ^ distance) for i in range(4)])


def gather_line(whole, relayed, direct):
    over = swap(relayed, 2)
    direct_2 = swap(direct, 2)
    direct_3 = swap(direct, 3)
    near = swap(whole, 1)
    return [whole, near, over, direct_2, swap(over, 1), direct_3], over


def round_kernel(slices_ref, whole_ref, first_ref, second_ref, held_ref, sems):
    pix = slices_ref.shape[1]
    quarter, half = pix // 4, pix // 8
    copies = [
        pltpu.make_async_copy(
            slices_ref.at[:, pl.ds(q * quarter, quarter)], held_ref.at[:, pl.ds(q * quarter, quarter)], sems.at[q]
        )
        for q in range(4)
    ]
    for copy in copies:
        copy.start()
    for q, copy in enumerate(copies):
        copy.wait()
        for part, out_ref in enumerate((first_ref, second_ref)):
            there = pl.ds(q * quarter + part * half, half)
            value = held_ref[:, there].astype(jnp.bfloat16)
            whole_ref[:, there] = value
            out_ref[:, pl.ds(q * half, half)] = value


def round_slices(slices):
    owned, pix = slices.shape
    return pl.pallas_call(
        round_kernel,
        in_specs=[pl.BlockSpec(memory_space=pl.ANY)],
        out_specs=[IN_VMEM] * 3,
        out_shape=[jax.ShapeDtypeStruct((owned, size), jnp.bfloat16) for size in (pix, pix // 2, pix // 2)],
        scratch_shapes=[pltpu.VMEM((owned, pix), slices.dtype), pltpu.SemaphoreType.DMA((4,))],
        compiler_params=params(),
        cost_estimate=pl.CostEstimate(flops=0, bytes_accessed=8 * slices.size, transcendentals=0),
        name="round_slices",
    )(pltpu.with_memory_space_constraint(slices, pltpu.HBM))


def relay_kernel(came_ref, own_ref, out_ref):
    for piece in chunks(own_ref.shape[1], 512):
        came = rotate_rows(came_ref[:, piece].astype(jnp.float32), 4)
        out_ref[:, piece] = (came + own_ref[:, piece].astype(jnp.float32)).astype(jnp.bfloat16)


def scatter_line(own, near, relayed_2, direct_2, relayed_3, direct_3):
    came = swap(relayed_3, 1)
    joined = pl.pallas_call(
        relay_kernel,
        in_specs=[IN_VMEM] * 2,
        out_specs=IN_VMEM,
        out_shape=jax.ShapeDtypeStruct(came.shape, came.dtype),
        compiler_params=params(),
        cost_estimate=pl.CostEstimate(flops=2 * came.size, bytes_accessed=6 * came.size, transcendentals=0),
        name="relay",
    )(came, relayed_2)
    joined = swap(joined, 2)
    direct_3 = early(swap(direct_3, 3), 10**9)
    direct_2 = early(swap(direct_2, 2), 10**9)
    near = swap(near, 1)
    return [own, near, joined, direct_2, direct_3]


def exchange_all(part, axes, size):
    if size & (size - 1):
        return [lax.psum(part, axes)]
    return [part] + [lax.ppermute(part, axes, [(i, i ^ k) for i in range(size)]) for k in range(1, size)]


def load_kernel(
    dense, frames_ref, orient_in_ref, log_prior_in_ref, here_ref, turned_ref, prior_ref, orient_ref, log_prior_ref, sems
):
    pieces = chunks(frames_ref.shape[1], 2048)
    tables = [
        pltpu.make_async_copy(orient_in_ref, orient_ref, sems.at[len(pieces)]),
        pltpu.make_async_copy(log_prior_in_ref, log_prior_ref, sems.at[len(pieces) + 1]),
    ]
    for copy in tables:
        copy.start()
    copies = [
        pltpu.make_async_copy(frames_ref.at[:, piece], here_ref.at[:, piece], sems.at[i])
        for i, piece in enumerate(pieces)
    ]
    for copy in copies:
        copy.start()
    for i, (copy, piece) in enumerate(zip(copies, pieces)):
        copy.wait()
        turned_ref[piece, :] = here_ref[:, piece].T
        if i == len(pieces) // 2:
            for table in tables:
                table.wait()
            many, columns = prior_ref.shape
            place = lax.axis_index("frame")
            for row in range(many):
                spot = 4 * (place ^ (row // 4)) + row % 4 if dense else row
                prior_ref[row : row + 1, :] = jnp.full((1, columns), log_prior_ref[orient_ref[spot]], jnp.float32)


def load_frames(frames, orient, log_prior, dense):
    rows, pix = frames.shape
    return pl.pallas_call(
        functools.partial(load_kernel, dense),
        in_specs=[pl.BlockSpec(memory_space=pl.ANY)] * 3,
        out_specs=[IN_VMEM] * 3,
        out_shape=[
            pltpu.VMEM((rows, pix), frames.dtype),
            pltpu.VMEM((pix, rows), frames.dtype),
            jax.ShapeDtypeStruct((orient.shape[0], rows), jnp.float32),
        ],
        scratch_shapes=[
            pltpu.SMEM(orient.shape, orient.dtype),
            pltpu.SMEM(log_prior.shape, log_prior.dtype),
            pltpu.SemaphoreType.DMA((len(chunks(pix, 2048)) + 2,)),
        ],
        compiler_params=params(),
        cost_estimate=pl.CostEstimate(flops=0, bytes_accessed=6 * rows * pix, transcendentals=0),
        name="load_frames",
    )(*(pltpu.with_memory_space_constraint(x, pltpu.HBM) for x in (frames, orient, log_prior)))


def score_kernel(pieces, order, *refs):
    turned_ref, out_ref = refs[-2:]
    raw, squares = [], []
    for first, size, rows in pieces:
        model = jnp.concatenate([refs[order.index(ref)][:, pl.ds(column, size)] for ref, column in rows], axis=0)
        raw.append(jnp.dot(model, turned_ref[pl.ds(first, size), :], preferred_element_type=jnp.float32))
        wide = model.astype(jnp.float32)
        squares.append(tree_sum([jnp.square(wide[:, at : at + 128]) for at in range(0, wide.shape[1], 128)]))
        if len(raw) > 4:
            raw, squares = raw[1:4] + [raw[0] + raw[4]], squares[1:4] + [squares[0] + squares[4]]
    out_ref[...] = tree_sum(raw) - 0.5 * jnp.sum(tree_sum(squares), axis=1, keepdims=True)


def score_parts(blocks, pieces, many, turned):
    pix, rows = turned.shape
    order = GATHER_ORDER if len(blocks) > 1 else (0,)
    return pl.pallas_call(
        functools.partial(score_kernel, pieces, order),
        in_specs=[IN_VMEM] * (len(blocks) + 1),
        out_specs=IN_VMEM,
        out_shape=jax.ShapeDtypeStruct((many, rows), jnp.float32),
        compiler_params=params(),
        cost_estimate=pl.CostEstimate(flops=2 * rows * pix * many, bytes_accessed=2 * rows * pix, transcendentals=0),
        name="score_parts",
    )(*[blocks[i] for i in order], pltpu.with_memory_space_constraint(turned, pltpu.VMEM))


def gathered_pieces(pix):
    quarter = pix // 4
    half = quarter // 2
    pieces = []
    for part in range(2):
        for q in range(4):
            for at in range(0, half, math.gcd(half, 512)):
                there, here = q * quarter + part * half + at, q * half + at
                rows = [(0, there), (1, there), (2 + part, here), (4 + part, here)]
                pieces.append((there, math.gcd(half, 512), rows))
    return pieces


def weigh(parts, prior_ref):
    raw = tree_sum([ref[...] for ref in parts])
    scores = (3.0 / math.sqrt(PIX)) * raw + prior_ref[...]
    up = jnp.exp(scores - jnp.max(scores, axis=0, keepdims=True))
    weights = (up / jnp.sum(up, axis=0, keepdims=True)).astype(jnp.bfloat16).astype(jnp.float32)
    counts = jnp.sum(weights, axis=1, keepdims=True)
    high = counts.astype(jnp.bfloat16).astype(jnp.float32)
    lane = lax.broadcasted_iota(jnp.int32, (counts.shape[0], TAIL), 1)
    return weights, jnp.where(lane < TAIL // 2, high, counts - high)


def plain_totals_kernel(n, *refs):
    parts, prior_ref, frames_ref, out_ref = refs[:n], refs[n], refs[n + 1], refs[n + 2]
    weights, tail = weigh(parts, prior_ref)
    weights = weights.astype(jnp.bfloat16)
    pix = frames_ref.shape[1]
    for piece in chunks(pix, 512):
        total = jnp.dot(weights, frames_ref[:, piece], preferred_element_type=jnp.float32)
        out_ref[:, piece] = total.astype(jnp.bfloat16)
    out_ref[:, pix:] = tail.astype(jnp.bfloat16)


def dense_totals_kernel(n, *refs):
    parts, prior_ref, frames_ref, outs = refs[:n], refs[n], refs[n + 1], refs[n + 2 :]
    weights, tail = weigh(parts, prior_ref)
    quarter = frames_ref.shape[1] // 4
    half = quarter // 2
    for k, out_ref in enumerate([outs[0], outs[1], outs[3], outs[5]]):
        rows = jnp.concatenate([tail[4 * k : 4 * k + 4]] * 4, axis=0)
        out_ref[:, out_ref.shape[1] - TAIL :] = rows.astype(jnp.bfloat16)
    turned = [rotate_rows(weights, (-4 * q) % 16).astype(jnp.bfloat16) for q in range(4)]
    for part in range(2):
        for piece in chunks(half, 512):
            totals = [
                jnp.dot(
                    turned[q],
                    frames_ref[:, pl.ds(q * quarter + part * half + piece.start, piece.size)],
                    preferred_element_type=jnp.float32,
                )
                for q in range(4)
            ]
            upper = lax.broadcasted_iota(jnp.int32, (8, piece.size), 0) < 4
            whole = pl.ds(part * half + piece.start, piece.size)
            spots = [(outs[0], whole), (outs[1], whole), (outs[2 + part], piece), (outs[4 + part], piece)]
            for k, (out_ref, spot) in enumerate(spots):
                first = jnp.where(upper, totals[-k % 4][:8], totals[(1 - k) % 4][:8])
                second = jnp.where(upper, totals[(2 - k) % 4][8:], totals[(3 - k) % 4][8:])
                out_ref[:, spot] = jnp.concatenate([first, second], axis=0).astype(jnp.bfloat16)


def block_totals(parts, prior, frames, dense):
    rows, pix = frames.shape
    many = prior.shape[0]
    if dense:
        half = pix // 8
        kernel = dense_totals_kernel
        shapes = [(16, 2 * half + TAIL)] * 2 + [(16, half), (16, half + TAIL)] * 2
    else:
        kernel, shapes = plain_totals_kernel, [(many, pix + TAIL)]
    return pl.pallas_call(
        functools.partial(kernel, len(parts)),
        in_specs=[IN_VMEM] * (len(parts) + 2),
        out_specs=[IN_VMEM] * len(shapes),
        out_shape=[jax.ShapeDtypeStruct(shape, jnp.bfloat16) for shape in shapes],
        compiler_params=params(),
        cost_estimate=pl.CostEstimate(
            flops=2 * rows * pix * many, bytes_accessed=2 * rows * pix, transcendentals=rows * many
        ),
        name="block_totals",
    )(*parts, prior, pltpu.with_memory_space_constraint(frames, pltpu.VMEM))


def plain_update_kernel(terms_ref, owned_ref, out_ref):
    pix = owned_ref.shape[1]
    tail = jnp.sum(terms_ref[:, :, pix:].astype(jnp.float32), axis=0)
    counts = tail[:, :1] + tail[:, TAIL // 2 : TAIL // 2 + 1]
    for piece in chunks(pix, 512):
        total = jnp.sum(terms_ref[:, :, piece].astype(jnp.float32), axis=0)
        out_ref[:, piece] = ((total + owned_ref[:, piece].astype(jnp.float32)) / (counts + 1.0)).astype(out_ref.dtype)


def dense_update_kernel(*refs):
    own_ref, near_ref, joined_ref, direct_2_ref, direct_3_ref = (refs[SCATTER_ORDER.index(i)] for i in range(5))
    owned_ref, out_ref = refs[5:7]
    quarter = owned_ref.shape[1] // 4
    half = quarter // 2

    def total(terms):
        return tree_sum([rotate_rows(ref[:, spot].astype(jnp.float32), 4 * k) for k, ref, spot in terms])

    behind, behind_half = pl.ds(quarter, TAIL), pl.ds(half, TAIL)
    tail = total(
        [(0, own_ref, behind), (1, near_ref, behind), (2, direct_2_ref, behind_half), (3, direct_3_ref, behind_half)]
    )
    scale = tail[:, :1] + tail[:, TAIL // 2 : TAIL // 2 + 1] + 1.0
    for part in range(2):
        for piece in chunks(half, 512):
            whole = pl.ds(part * half + piece.start, piece.size)
            terms = [(0, own_ref, whole), (1, near_ref, whole)]
            terms += [(2, direct_2_ref, piece), (3, direct_3_ref, piece)] if part else [(2, joined_ref, piece)]
            spots = [pl.ds(q * quarter + whole.start, whole.size) for q in range(4)]
            owned = jnp.concatenate([owned_ref[:, spot].astype(jnp.float32) for spot in spots], axis=0)
            new = ((total(terms) + owned) / scale).astype(out_ref.dtype)
            for q, spot in enumerate(spots):
                out_ref[:, spot] = new[4 * q : 4 * q + 4]
                if len(refs) > 7:
                    refs[7 + part][:, pl.ds(q * half + piece.start, piece.size)] = new[4 * q : 4 * q + 4]


def update(terms, owned, dtype, halves):
    shapes = [owned.shape] + ([(owned.shape[0], owned.shape[1] // 2)] * 2 if halves else [])
    return pl.pallas_call(
        plain_update_kernel if len(terms) == 1 else dense_update_kernel,
        in_specs=[IN_VMEM] * (len(terms) + 1),
        out_specs=[IN_VMEM] * len(shapes),
        out_shape=[jax.ShapeDtypeStruct(shape, dtype) for shape in shapes],
        compiler_params=params(),
        cost_estimate=pl.CostEstimate(flops=8 * owned.size, bytes_accessed=12 * owned.size, transcendentals=0),
        name="update",
    )(*([terms[i] for i in SCATTER_ORDER] if len(terms) > 1 else terms), owned)


def local(sizes, frames, slices, log_prior, orient):
    along, across = sizes
    owned, pix = slices.shape
    dense = along == 4 and owned == 4 and pix % 2048 == 0
    owned_b = round_slices(slices) if dense else [slices.astype(jnp.bfloat16)]
    if not dense:
        here, turned, prior = load_frames(frames, orient, log_prior, dense)
    for step in range(ITERS):
        last = step + 1 == ITERS
        if dense:
            blocks, over = gather_line(*owned_b)
            if step == 0:
                frames, over = lax.optimization_barrier((frames, over))
                here, turned, prior = load_frames(frames, orient, log_prior, dense)
            pieces = gathered_pieces(pix)
        else:
            blocks = [lax.all_gather(owned_b[0], "frame", axis=0, tiled=True)]
            pieces = [(piece.start, piece.size, [(0, piece.start)]) for piece in chunks(pix, 512)]
        parts = exchange_all(
            score_parts(blocks, pieces, along * owned, turned), ("panel", "sub"), across
        )
        totals = block_totals(parts, prior, here, dense)
        if dense:
            terms = scatter_line(*totals)
        else:
            whole = totals[0].reshape(along, owned, totals[0].shape[1])
            terms = [lax.all_to_all(whole, "frame", split_axis=0, concat_axis=0, tiled=False)]
        owned_b = update(terms, owned_b[0], jnp.float32 if last else jnp.bfloat16, dense and not last)
    return owned_b[0]


def solution(mesh):
    in_specs = (
        P(("groups", "frame"), ("panel", "sub")),
        P(("groups", "frame"), ("panel", "sub")),
        P(),
        P("groups"),
    )
    out_specs = P(("groups", "frame"), ("panel", "sub"))
    sizes = (mesh.shape["frame"], mesh.shape["panel"] * mesh.shape["sub"])
    return jax.shard_map(
        functools.partial(local, sizes), mesh=mesh, in_specs=in_specs, out_specs=out_specs, check_vma=False
    )
```

time: 83.1 us -> 66.4 us (0.80)
  local copies, waits for them, and re-layouts: 16.8 us -> 0 us
  starting transfers between devices: 25.8 us -> 35.4 us
  waiting for transfers between devices: 28.3 us -> 19.8 us
  other arithmetic: 1.31 us -> 0 us
  Pallas kernels: 9.99 us -> 10.9 us
    unnamed x18 -> x0, local copies, waits for them, and re-layouts: 16.6 us -> none
    ppermute x12 -> x20, starting transfers between devices: 22.1 us -> 31.1 us  [swap(): return lax.ppermute(value, 'frame', [(i, i ^ distance) for i in range(4)])]
    ppermute x12 -> x20, waiting for transfers between devices: 24.7 us -> 15.9 us  [swap(): return lax.ppermute(value, 'frame', [(i, i ^ distance) for i in range(4)])]
    pallas_call x5 -> x12, Pallas kernels: 7.46 us -> 8.52 us  [the longest x1 3.98 us: load_frames(): pl.pallas_call(functools.partial(load_kernel, dense), in_specs=[pl.BlockS...]
    convert_element_type x1 -> x0, other arithmetic: 1.01 us -> none  [local(): owned_b = slices.astype(jnp.bfloat16)]
  transfers between devices with their start and end apart: 18 -> 26, of which waited for: 10 -> 15; matrix products, arithmetic and copies ran while one was open for 1% -> 0% of each run, Pallas kernels for 5% -> 6%
where the time goes in v4:
time: 66.4 us; the launch traced here: 66.2 us
  starting transfers between devices  35.4 us (53%)
  waiting for transfers between devices  19.8 us (30%)
  Pallas kernels  10.9 us (16%)
    ppermute x20, starting transfers between devices, swap(): return lax.ppermute(value, 'frame', [(i, i ^ distance) for i in range(4)])  31.1 us
    ppermute x20, waiting for transfers between devices, swap(): return lax.ppermute(value, 'frame', [(i, i ^ distance) for i in range(4)])  15.9 us
    ppermute x6, starting transfers between devices, exchange_all(): lax.ppermute(part, axes, [(i, i ^ k) for i in range(size)])  4.31 us
    pallas_call x1, Pallas kernels, load_frames(): pl.pallas_call(functools.partial(load_kernel, dense), in_specs=[pl.BlockS...  3.98 us
    ppermute x6, waiting for transfers between devices, exchange_all(): lax.ppermute(part, axes, [(i, i ^ k) for i in range(size)])  3.89 us
    pallas_call x2, Pallas kernels, block_totals(): pl.pallas_call(functools.partial(kernel, len(parts)), in_specs=[IN_VMEM]...  2.42 us
    pallas_call x2, Pallas kernels, score_parts(): pl.pallas_call(functools.partial(score_kernel, pieces, order), in_specs=[...  2.38 us
  transfers between devices with their start and end apart: 26, of which 15 were waited for; matrix products, arithmetic and copies ran while one was open for 0% of the time, Pallas kernels for 6%

profile of v4, /device:TPU:0, one launch (start us, length us, event | category | flops | bytes accessed | tf_op | source)
XLA Modules:
  0.0 66.2 jit_solution(1624018440715626590)
XLA Ops:
  0.0 1.0 %round_slices.1 = (bf16[4,16384]{1,0:T(4,128)(2,1)S(1)}, bf16[4,8192]{1,0:T(4,128)(2,1)S(1)}, bf16[4,8192]{1,0:T(4,128)(2,1)S(1)}) custom-call(f32[4,16384]{1,0:T(4,128)} %slices_ref.1), custom_call_target="tpu_custom_call" | custom-call | bytes 524288 | tf_op jit(solution)/shard_map/round_slices/pallas_call | solution.py:86
  1.0 4.1 %collective-permute-start.1 = (bf16[4,8192]{1,0:T(4,128)(2,1)S(1)}, bf16[4,8192]{1,0:T(4,128)(2,1)S(1)}, u32[]{:S(2)}, u32[]{:S(2)}) collective-permute-start(bf16[4,8192]{1,0:T(4,128)(2,1)S(1)} %get-tuple-element.28), channel_id=1, source_target_pairs={{0,8},{4,12},{8,0},{12,4},{1,9},{5,13},{9,1},{13,5},{2,10},{6,14},... | collective-permute-start | bytes 196616 | tf_op jit(solution)/shard_map/ppermute | solution.py:53
  5.1 1.6 %collective-permute-start = (bf16[4,16384]{1,0:T(4,128)(2,1)S(1)}, bf16[4,16384]{1,0:T(4,128)(2,1)S(1)}, u32[]{:S(2)}, u32[]{:S(2)}) collective-permute-start(bf16[4,16384]{1,0:T(4,128)(2,1)S(1)} %get-tuple-element.27.refs_0_.refs_5_), channel_id=1, source_target_pairs={{0,4},{4,0},{8,12},{12,8},{1,5},{5,1},{9,13},{13,9},{2,6},{6,2},{1... | collective-permute-start | bytes 393224 | tf_op jit(solution)/shard_map/ppermute | solution.py:53
  6.7 0.0 collective-permute-start.4
  6.7 1.9 %collective-permute-start.2 = (bf16[4,8192]{1,0:T(4,128)(2,1)S(1)}, bf16[4,8192]{1,0:T(4,128)(2,1)S(1)}, u32[]{:S(2)}, u32[]{:S(2)}) collective-permute-start(bf16[4,8192]{1,0:T(4,128)(2,1)S(1)} %get-tuple-element.29), channel_id=1, source_target_pairs={{0,8},{4,12},{8,0},{12,4},{1,9},{5,13},{9,1},{13,5},{2,10},{6,14},... | collective-permute-start | bytes 196616 | tf_op jit(solution)/shard_map/ppermute | solution.py:53
  8.6 0.0 collective-permute-done.1.refs_2_
  8.6 2.5 %collective-permute-start.3 = (bf16[4,8192]{1,0:T(4,128)(2,1)S(1)}, bf16[4,8192]{1,0:T(4,128)(2,1)S(1)}, u32[]{:S(2)}, u32[]{:S(2)}) collective-permute-start(bf16[4,8192]{1,0:T(4,128)(2,1)S(1)} %collective-permute-done.1.refs_2_), channel_id=1, source_target_pairs={{0,4},{4,0},{8,12},{12,8},{1,5},{5,1},{9,13},{13,9},{2,6},{6,2},{1... | collective-permute-start | bytes 196616 | tf_op jit(solution)/shard_map/ppermute | solution.py:53
  11.1 4.0 %load_frames.1 = (bf16[256,16384]{1,0:T(8,128)(2,1)S(1)}, bf16[16384,256]{1,0:T(8,128)(2,1)S(1)}, f32[16,256]{1,0:T(8,128)S(1)}) custom-call(bf16[256,16384]{1,0:T(8,128)(2,1)} %frames_ref, s32[16]{0:T(128)} %orient_in_ref.1, f32[4096]{0:T(1024)} %log_prior_in_ref.1), custom_call_target="tpu_custom_call" | custom-call | bytes 25165824 | tf_op jit(solution)/shard_map/load_frames/pallas_call | solution.py:159
  15.0 0.0 collective-permute-done.4.refs_5_
  15.1 0.0 collective-permute-done.2.refs_3_
  15.1 0.0 collective-permute-done.3.refs_4_
  15.1 0.0 collective-permute-done.refs_1_
  15.1 1.2 %score_parts.2.refs_0_ = f32[16,256]{1,0:T(8,128)S(1)} custom-call(bf16[4,16384]{1,0:T(4,128)(2,1)S(1)} %get-tuple-element.27.refs_0_.refs_5_, bf16[4,16384]{1,0:T(4,128)(2,1)S(1)} %collective-permute-done.refs_1_, bf16[4,8192]{1,0:T(4,128)(2,1)S(1)} %collective-permute-done.1.refs_2_, bf16[4,8192]{1,0:T(4,128)(2,1)S(1)} %collective-permute-done.2.refs_3_, ...), custom_call_target="tpu_custom_call" | custom-call | flops 134217728 | bytes 8388608 | tf_op jit(solution)/shard_map/score_parts/pallas_call | solution.py:195
  16.3 0.2 collective-permute-start.7
  16.5 1.3 %collective-permute-start.6 = (f32[16,256]{1,0:T(8,128)S(1)}, f32[16,256]{1,0:T(8,128)S(1)}, u32[]{:S(2)}, u32[]{:S(2)}) collective-permute-start(f32[16,256]{1,0:T(8,128)S(1)} %score_parts.2.refs_0_), channel_id=1, source_target_pairs={{0,2},{1,3},{2,0},{3,1},{4,6},{5,7},{6,4},{7,5},{8,10},{9,11},{10,... | collective-permute-start | bytes 49160 | tf_op jit(solution)/shard_map/ppermute | solution.py:125
  17.8 0.3 collective-permute-start.5
  18.1 1.4 %collective-permute-done.7.refs_3_ = f32[16,256]{1,0:T(8,128)S(1)} collective-permute-done((f32[16,256]{1,0:T(8,128)S(1)}, f32[16,256]{1,0:T(8,128)S(1)}, u32[]{:S(2)}, u32[]{:S(2)}) %collective-permute-start.7) | collective-permute-done | bytes 16416 | tf_op jit(solution)/shard_map/ppermute | solution.py:125
  19.6 0.7 %collective-permute-done.6.refs_2_ = f32[16,256]{1,0:T(8,128)S(1)} collective-permute-done((f32[16,256]{1,0:T(8,128)S(1)}, f32[16,256]{1,0:T(8,128)S(1)}, u32[]{:S(2)}, u32[]{:S(2)}) %collective-permute-start.6) | collective-permute-done | bytes 16416 | tf_op jit(solution)/shard_map/ppermute | solution.py:125
  20.3 0.0 collective-permute-done.5.refs_1_
  20.3 1.2 %block_totals.2 = (bf16[16,4224]{1,0:T(8,128)(2,1)S(1)}, bf16[16,4224]{1,0:T(8,128)(2,1)S(1)}, bf16[16,2048]{1,0:T(8,128)(2,1)S(1)}, bf16[16,2176]{1,0:T(8,128)(...) custom-call(f32[16,256]{1,0:T(8,128)S(1)} %score_parts.2.refs_0_, ...), custom_call_target="tpu_custom_call" | custom-call | flops 134217728 | bytes 8388608 | tf_op jit(solution)/shard_map/block_totals/pallas_call | solution.py:278
  21.5 1.9 %collective-permute-start.11 = (bf16[16,2176]{1,0:T(8,128)(2,1)S(1)}, bf16[16,2176]{1,0:T(8,128)(2,1)S(1)}, u32[]{:S(2)}, u32[]{:S(2)}) collective-permute-start(bf16[16,2176]{1,0:T(8,128)(2,1)S(1)} %get-tuple-element.38), channel_id=1, source_target_pairs={{0,8},{4,12},{8,0},{12,4},{1,9},{5,13},{9,1},{13,5},{2,10},{6,14},... | collective-permute-start | bytes 208904 | tf_op jit(solution)/shard_map/ppermute | solution.py:53
  23.4 1.2 %collective-permute-start.9 = (bf16[16,2048]{1,0:T(8,128)(2,1)S(1)}, bf16[16,2048]{1,0:T(8,128)(2,1)S(1)}, u32[]{:S(2)}, u32[]{:S(2)}) collective-permute-start(bf16[16,2048]{1,0:T(8,128)(2,1)S(1)} %get-tuple-element.36), channel_id=1, source_target_pairs={{0,4},{4,0},{8,12},{12,8},{1,5},{5,1},{9,13},{13,9},{2,6},{6,2},{1... | collective-permute-start | bytes 196616 | tf_op jit(solution)/shard_map/ppermute | solution.py:53
  24.6 1.3 %collective-permute-start.12 = (bf16[16,2176]{1,0:T(8,128)(2,1)S(1)}, bf16[16,2176]{1,0:T(8,128)(2,1)S(1)}, u32[]{:S(2)}, u32[]{:S(2)}) collective-permute-start(bf16[16,2176]{1,0:T(8,128)(2,1)S(1)} %get-tuple-element.39), channel_id=1, source_target_pairs={{0,12},{4,8},{8,4},{12,0},{1,13},{5,9},{9,5},{13,1},{2,14},{6,10},... | collective-permute-start | bytes 208904 | tf_op jit(solution)/shard_map/ppermute | solution.py:53
  25.9 0.2 collective-permute-start.8
  26.2 1.7 %collective-permute-done.9.came_ref = bf16[16,2048]{1,0:T(8,128)(2,1)S(1)} collective-permute-done((bf16[16,2048]{1,0:T(8,128)(2,1)S(1)}, bf16[16,2048]{1,0:T(8,128)(2,1)S(1)}, u32[]{:S(2)}, u32[]{:S(2)}) %collective-permute-start.9) | collective-permute-done | bytes 65568 | tf_op jit(solution)/shard_map/ppermute | solution.py:53
  27.9 1.8 %collective-permute-start.10 = (bf16[16,2048]{1,0:T(8,128)(2,1)S(1)}, bf16[16,2048]{1,0:T(8,128)(2,1)S(1)}, u32[]{:S(2)}, u32[]{:S(2)}) collective-permute-start(bf16[16,2048]{1,0:T(8,128)(2,1)S(1)} %relay.2), channel_id=1, source_target_pairs={{0,8},{4,12},{8,0},{12,4},{1,9},{5,13},{9,1},{13,5},{2,10},{6,14},... | collective-permute-start | bytes 196616 | tf_op jit(solution)/shard_map/ppermute | solution.py:53
  29.7 0.0 collective-permute-done.11.in_ref
  29.7 1.8 %collective-permute-done.12.in_ref = bf16[16,2176]{1,0:T(8,128)(2,1)S(1)} collective-permute-done((bf16[16,2176]{1,0:T(8,128)(2,1)S(1)}, bf16[16,2176]{1,0:T(8,128)(2,1)S(1)}, u32[]{:S(2)}, u32[]{:S(2)}) %collective-permute-start.12) | collective-permute-done | bytes 69664 | tf_op jit(solution)/shard_map/ppermute | solution.py:53
  31.6 2.3 %collective-permute-done.10.refs_2_ = bf16[16,2048]{1,0:T(8,128)(2,1)S(1)} collective-permute-done((bf16[16,2048]{1,0:T(8,128)(2,1)S(1)}, bf16[16,2048]{1,0:T(8,128)(2,1)S(1)}, u32[]{:S(2)}, u32[]{:S(2)}) %collective-permute-start.10) | collective-permute-done | bytes 65568 | tf_op jit(solution)/shard_map/ppermute | solution.py:53
  33.9 0.2 collective-permute-done.8.refs_1_
  34.1 0.2 update.2
  34.3 2.0 %collective-permute-start.14 = (bf16[4,8192]{1,0:T(4,128)(2,1)S(1)}, bf16[4,8192]{1,0:T(4,128)(2,1)S(1)}, u32[]{:S(2)}, u32[]{:S(2)}) collective-permute-start(bf16[4,8192]{1,0:T(4,128)(2,1)S(1)} %get-tuple-element.41), channel_id=1, source_target_pairs={{0,8},{4,12},{8,0},{12,4},{1,9},{5,13},{9,1},{13,5},{2,10},{6,14},... | collective-permute-start | bytes 196616 | tf_op jit(solution)/shard_map/ppermute | solution.py:53
  36.4 1.2 %collective-permute-start.13 = (bf16[4,16384]{1,0:T(4,128)(2,1)S(1)}, bf16[4,16384]{1,0:T(4,128)(2,1)S(1)}, u32[]{:S(2)}, u32[]{:S(2)}) collective-permute-start(bf16[4,16384]{1,0:T(4,128)(2,1)S(1)} %get-tuple-element.40.refs_0_.refs_5_), channel_id=1, source_target_pairs={{0,4},{4,0},{8,12},{12,8},{1,5},{5,1},{9,13},{13,9},{2,6},{6,2},{1... | collective-permute-start | bytes 393224 | tf_op jit(solution)/shard_map/ppermute | solution.py:53
  37.6 1.2 %collective-permute-start.17 = (bf16[4,8192]{1,0:T(4,128)(2,1)S(1)}, bf16[4,8192]{1,0:T(4,128)(2,1)S(1)}, u32[]{:S(2)}, u32[]{:S(2)}) collective-permute-start(bf16[4,8192]{1,0:T(4,128)(2,1)S(1)} %get-tuple-element.42), channel_id=1, source_target_pairs={{0,12},{4,8},{8,4},{12,0},{1,13},{5,9},{9,5},{13,1},{2,14},{6,10},... | collective-permute-start | bytes 196616 | tf_op jit(solution)/shard_map/ppermute | solution.py:53
  38.8 1.1 %collective-permute-start.15 = (bf16[4,8192]{1,0:T(4,128)(2,1)S(1)}, bf16[4,8192]{1,0:T(4,128)(2,1)S(1)}, u32[]{:S(2)}, u32[]{:S(2)}) collective-permute-start(bf16[4,8192]{1,0:T(4,128)(2,1)S(1)} %get-tuple-element.42), channel_id=1, source_target_pairs={{0,8},{4,12},{8,0},{12,4},{1,9},{5,13},{9,1},{13,5},{2,10},{6,14},... | collective-permute-start | bytes 196616 | tf_op jit(solution)/shard_map/ppermute | solution.py:53
  39.9 0.0 collective-permute-done.14.refs_2_
  39.9 2.1 %collective-permute-start.16 = (bf16[4,8192]{1,0:T(4,128)(2,1)S(1)}, bf16[4,8192]{1,0:T(4,128)(2,1)S(1)}, u32[]{:S(2)}, u32[]{:S(2)}) collective-permute-start(bf16[4,8192]{1,0:T(4,128)(2,1)S(1)} %collective-permute-done.14.refs_2_), channel_id=1, source_target_pairs={{0,4},{4,0},{8,12},{12,8},{1,5},{5,1},{9,13},{13,9},{2,6},{6,2},{1... | collective-permute-start | bytes 196616 | tf_op jit(solution)/shard_map/ppermute | solution.py:53
  42.0 2.5 %collective-permute-done.17.refs_5_ = bf16[4,8192]{1,0:T(4,128)(2,1)S(1)} collective-permute-done((bf16[4,8192]{1,0:T(4,128)(2,1)S(1)}, bf16[4,8192]{1,0:T(4,128)(2,1)S(1)}, u32[]{:S(2)}, u32[]{:S(2)}) %collective-permute-start.17) | collective-permute-done | bytes 65568 | tf_op jit(solution)/shard_map/ppermute | solution.py:53
  44.4 1.6 %collective-permute-done.15.refs_3_ = bf16[4,8192]{1,0:T(4,128)(2,1)S(1)} collective-permute-done((bf16[4,8192]{1,0:T(4,128)(2,1)S(1)}, bf16[4,8192]{1,0:T(4,128)(2,1)S(1)}, u32[]{:S(2)}, u32[]{:S(2)}) %collective-permute-start.15) | collective-permute-done | bytes 65568 | tf_op jit(solution)/shard_map/ppermute | solution.py:53
  46.0 0.1 collective-permute-done.16.refs_4_
  46.0 0.0 collective-permute-done.13.refs_1_
  46.0 1.2 %score_parts.3.refs_0_ = f32[16,256]{1,0:T(8,128)S(1)} custom-call(bf16[4,16384]{1,0:T(4,128)(2,1)S(1)} %get-tuple-element.40.refs_0_.refs_5_, bf16[4,16384]{1,0:T(4,128)(2,1)S(1)} %collective-permute-done.13.refs_1_, bf16[4,8192]{1,0:T(4,128)(2,1)S(1)} %collective-permute-done.14.refs_2_, bf16[4,8192]{1,0:T(4,128)(2,1)S(1)} %collective-permute-done.15.refs_3_, ...), custom_call_target="tpu_custom_call" | custom-call | flops 134217728 | bytes 8388608 | tf_op jit(solution)/shard_map/score_parts/pallas_call | solution.py:195
  47.2 0.0 collective-permute-start.20
  47.2 2.4 %collective-permute-start.19 = (f32[16,256]{1,0:T(8,128)S(1)}, f32[16,256]{1,0:T(8,128)S(1)}, u32[]{:S(2)}, u32[]{:S(2)}) collective-permute-start(f32[16,256]{1,0:T(8,128)S(1)} %score_parts.3.refs_0_), channel_id=1, source_target_pairs={{0,2},{1,3},{2,0},{3,1},{4,6},{5,7},{6,4},{7,5},{8,10},{9,11},{10,... | collective-permute-start | bytes 49160 | tf_op jit(solution)/shard_map/ppermute | solution.py:125
  49.6 0.1 collective-permute-start.18
  49.7 0.7 %collective-permute-done.20.refs_3_ = f32[16,256]{1,0:T(8,128)S(1)} collective-permute-done((f32[16,256]{1,0:T(8,128)S(1)}, f32[16,256]{1,0:T(8,128)S(1)}, u32[]{:S(2)}, u32[]{:S(2)}) %collective-permute-start.20) | collective-permute-done | bytes 16416 | tf_op jit(solution)/shard_map/ppermute | solution.py:125
  50.4 1.0 %collective-permute-done.19.refs_2_ = f32[16,256]{1,0:T(8,128)S(1)} collective-permute-done((f32[16,256]{1,0:T(8,128)S(1)}, f32[16,256]{1,0:T(8,128)S(1)}, u32[]{:S(2)}, u32[]{:S(2)}) %collective-permute-start.19) | collective-permute-done | bytes 16416 | tf_op jit(solution)/shard_map/ppermute | solution.py:125
  51.5 0.0 collective-permute-done.18.refs_1_
  51.5 1.2 %block_totals.3 = (bf16[16,4224]{1,0:T(8,128)(2,1)S(1)}, bf16[16,4224]{1,0:T(8,128)(2,1)S(1)}, bf16[16,2048]{1,0:T(8,128)(2,1)S(1)}, bf16[16,2176]{1,0:T(8,128)(...) custom-call(f32[16,256]{1,0:T(8,128)S(1)} %score_parts.3.refs_0_, ...), custom_call_target="tpu_custom_call" | custom-call | flops 134217728 | bytes 8388608 | tf_op jit(solution)/shard_map/block_totals/pallas_call | solution.py:278
  52.7 1.0 %collective-permute-start.24 = (bf16[16,2176]{1,0:T(8,128)(2,1)S(1)}, bf16[16,2176]{1,0:T(8,128)(2,1)S(1)}, u32[]{:S(2)}, u32[]{:S(2)}) collective-permute-start(bf16[16,2176]{1,0:T(8,128)(2,1)S(1)} %get-tuple-element.47), channel_id=1, source_target_pairs={{0,8},{4,12},{8,0},{12,4},{1,9},{5,13},{9,1},{13,5},{2,10},{6,14},... | collective-permute-start | bytes 208904 | tf_op jit(solution)/shard_map/ppermute | solution.py:53
  53.7 1.7 %collective-permute-start.22 = (bf16[16,2048]{1,0:T(8,128)(2,1)S(1)}, bf16[16,2048]{1,0:T(8,128)(2,1)S(1)}, u32[]{:S(2)}, u32[]{:S(2)}) collective-permute-start(bf16[16,2048]{1,0:T(8,128)(2,1)S(1)} %get-tuple-element.45), channel_id=1, source_target_pairs={{0,4},{4,0},{8,12},{12,8},{1,5},{5,1},{9,13},{13,9},{2,6},{6,2},{1... | collective-permute-start | bytes 196616 | tf_op jit(solution)/shard_map/ppermute | solution.py:53
  55.4 1.7 %collective-permute-start.25 = (bf16[16,2176]{1,0:T(8,128)(2,1)S(1)}, bf16[16,2176]{1,0:T(8,128)(2,1)S(1)}, u32[]{:S(2)}, u32[]{:S(2)}) collective-permute-start(bf16[16,2176]{1,0:T(8,128)(2,1)S(1)} %get-tuple-element.48), channel_id=1, source_target_pairs={{0,12},{4,8},{8,4},{12,0},{1,13},{5,9},{9,5},{13,1},{2,14},{6,10},... | collective-permute-start | bytes 208904 | tf_op jit(solution)/shard_map/ppermute | solution.py:53
  57.1 0.0 collective-permute-start.21
  57.1 1.0 %collective-permute-done.22.came_ref = bf16[16,2048]{1,0:T(8,128)(2,1)S(1)} collective-permute-done((bf16[16,2048]{1,0:T(8,128)(2,1)S(1)}, bf16[16,2048]{1,0:T(8,128)(2,1)S(1)}, u32[]{:S(2)}, u32[]{:S(2)}) %collective-permute-start.22) | collective-permute-done | bytes 65568 | tf_op jit(solution)/shard_map/ppermute | solution.py:53
  58.1 2.5 %collective-permute-start.23 = (bf16[16,2048]{1,0:T(8,128)(2,1)S(1)}, bf16[16,2048]{1,0:T(8,128)(2,1)S(1)}, u32[]{:S(2)}, u32[]{:S(2)}) collective-permute-start(bf16[16,2048]{1,0:T(8,128)(2,1)S(1)} %relay.3), channel_id=1, source_target_pairs={{0,8},{4,12},{8,0},{12,4},{1,9},{5,13},{9,1},{13,5},{2,10},{6,14},... | collective-permute-start | bytes 196616 | tf_op jit(solution)/shard_map/ppermute | solution.py:53
  60.6 0.0 collective-permute-done.24.in_ref
  60.6 1.7 %collective-permute-done.25.in_ref = bf16[16,2176]{1,0:T(8,128)(2,1)S(1)} collective-permute-done((bf16[16,2176]{1,0:T(8,128)(2,1)S(1)}, bf16[16,2176]{1,0:T(8,128)(2,1)S(1)}, u32[]{:S(2)}, u32[]{:S(2)}) %collective-permute-start.25) | collective-permute-done | bytes 69664 | tf_op jit(solution)/shard_map/ppermute | solution.py:53
  62.3 2.4 %collective-permute-done.23.refs_2_ = bf16[16,2048]{1,0:T(8,128)(2,1)S(1)} collective-permute-done((bf16[16,2048]{1,0:T(8,128)(2,1)S(1)}, bf16[16,2048]{1,0:T(8,128)(2,1)S(1)}, u32[]{:S(2)}, u32[]{:S(2)}) %collective-permute-start.23) | collective-permute-done | bytes 65568 | tf_op jit(solution)/shard_map/ppermute | solution.py:53
  64.7 0.7 collective-permute-done.21.refs_1_
  65.3 0.9 %update.3 = f32[4,16384]{1,0:T(4,128)} custom-call(bf16[16,4224]{1,0:T(8,128)(2,1)S(1)} %get-tuple-element.43.refs_0_, bf16[16,4224]{1,0:T(8,128)(2,1)S(1)} %collective-permute-done.21.refs_1_, bf16[16,2048]{1,0:T(8,128)(2,1)S(1)} %collective-permute-done.23.refs_2_, bf16[16,2176]{1,0:T(8,128)(2,1)S(1)} %early.6.refs_3_, bf16[16,2176]{1,0:T(8,128)(2,1)S(1)} %early.7.refs_4_, ...), custom_call_target="tpu_custom_call" | custom-call | flops 524288 | bytes 786432 | tf_op jit(solution)/shard_map/update/pallas_call | solution.py:330
  (6 shorter events, 0.1 us)
Async XLA Ops:
  1.0 7.6 %collective-permute-start.1 = (bf16[4,8192]{1,0:T(4,128)(2,1)S(1)}, bf16[4,8192]{1,0:T(4,128)(2,1)S(1)}, u32[]{:S(2)}, u32[]{:S(2)}) collective-permute-start(bf16[4,8192]{1,0:T(4,128)(2,1)S(1)} %get-tuple-element.28), channel_id=1, source_target_pairs={{0,8},{4,12},{8,0},{12,4},{1,9},{5,13},{9,1},{13,5},{2,10},{6,14},... | collective-permute-start | bytes 196616 | tf_op jit(solution)/shard_map/ppermute | solution.py:53
  5.1 10.0 %collective-permute-start = (bf16[4,16384]{1,0:T(4,128)(2,1)S(1)}, bf16[4,16384]{1,0:T(4,128)(2,1)S(1)}, u32[]{:S(2)}, u32[]{:S(2)}) collective-permute-start(bf16[4,16384]{1,0:T(4,128)(2,1)S(1)} %get-tuple-element.27.refs_0_.refs_5_), channel_id=1, source_target_pairs={{0,4},{4,0},{8,12},{12,8},{1,5},{5,1},{9,13},{13,9},{2,6},{6,2},{1... | collective-permute-start | bytes 393224 | tf_op jit(solution)/shard_map/ppermute | solution.py:53
  6.7 8.4 %collective-permute-start.4 = (bf16[4,8192]{1,0:T(4,128)(2,1)S(1)}, bf16[4,8192]{1,0:T(4,128)(2,1)S(1)}, u32[]{:S(2)}, u32[]{:S(2)}) collective-permute-start(bf16[4,8192]{1,0:T(4,128)(2,1)S(1)} %get-tuple-element.29), channel_id=1, source_target_pairs={{0,12},{4,8},{8,4},{12,0},{1,13},{5,9},{9,5},{13,1},{2,14},{6,10},... | collective-permute-start | bytes 196616 | tf_op jit(solution)/shard_map/ppermute | solution.py:53
  6.7 8.4 %collective-permute-start.2 = (bf16[4,8192]{1,0:T(4,128)(2,1)S(1)}, bf16[4,8192]{1,0:T(4,128)(2,1)S(1)}, u32[]{:S(2)}, u32[]{:S(2)}) collective-permute-start(bf16[4,8192]{1,0:T(4,128)(2,1)S(1)} %get-tuple-element.29), channel_id=1, source_target_pairs={{0,8},{4,12},{8,0},{12,4},{1,9},{5,13},{9,1},{13,5},{2,10},{6,14},... | collective-permute-start | bytes 196616 | tf_op jit(solution)/shard_map/ppermute | solution.py:53
  8.6 6.5 %collective-permute-start.3 = (bf16[4,8192]{1,0:T(4,128)(2,1)S(1)}, bf16[4,8192]{1,0:T(4,128)(2,1)S(1)}, u32[]{:S(2)}, u32[]{:S(2)}) collective-permute-start(bf16[4,8192]{1,0:T(4,128)(2,1)S(1)} %collective-permute-done.1.refs_2_), channel_id=1, source_target_pairs={{0,4},{4,0},{8,12},{12,8},{1,5},{5,1},{9,13},{13,9},{2,6},{6,2},{1... | collective-permute-start | bytes 196616 | tf_op jit(solution)/shard_map/ppermute | solution.py:53
  16.3 3.3 %collective-permute-start.7 = (f32[16,256]{1,0:T(8,128)S(1)}, f32[16,256]{1,0:T(8,128)S(1)}, u32[]{:S(2)}, u32[]{:S(2)}) collective-permute-start(f32[16,256]{1,0:T(8,128)S(1)} %score_parts.2.refs_0_), channel_id=1, source_target_pairs={{0,3},{1,2},{2,1},{3,0},{4,7},{5,6},{6,5},{7,4},{8,11},{9,10},{10,... | collective-permute-start | bytes 49160 | tf_op jit(solution)/shard_map/ppermute | solution.py:125
  16.5 3.7 %collective-permute-start.6 = (f32[16,256]{1,0:T(8,128)S(1)}, f32[16,256]{1,0:T(8,128)S(1)}, u32[]{:S(2)}, u32[]{:S(2)}) collective-permute-start(f32[16,256]{1,0:T(8,128)S(1)} %score_parts.2.refs_0_), channel_id=1, source_target_pairs={{0,2},{1,3},{2,0},{3,1},{4,6},{5,7},{6,4},{7,5},{8,10},{9,11},{10,... | collective-permute-start | bytes 49160 | tf_op jit(solution)/shard_map/ppermute | solution.py:125
  17.8 2.4 %collective-permute-start.5 = (f32[16,256]{1,0:T(8,128)S(1)}, f32[16,256]{1,0:T(8,128)S(1)}, u32[]{:S(2)}, u32[]{:S(2)}) collective-permute-start(f32[16,256]{1,0:T(8,128)S(1)} %score_parts.2.refs_0_), channel_id=1, source_target_pairs={{0,1},{1,0},{2,3},{3,2},{4,5},{5,4},{6,7},{7,6},{8,9},{9,8},{10,11... | collective-permute-start | bytes 49160 | tf_op jit(solution)/shard_map/ppermute | solution.py:125
  21.5 8.2 %collective-permute-start.11 = (bf16[16,2176]{1,0:T(8,128)(2,1)S(1)}, bf16[16,2176]{1,0:T(8,128)(2,1)S(1)}, u32[]{:S(2)}, u32[]{:S(2)}) collective-permute-start(bf16[16,2176]{1,0:T(8,128)(2,1)S(1)} %get-tuple-element.38), channel_id=1, source_target_pairs={{0,8},{4,12},{8,0},{12,4},{1,9},{5,13},{9,1},{13,5},{2,10},{6,14},... | collective-permute-start | bytes 208904 | tf_op jit(solution)/shard_map/ppermute | solution.py:53
  23.4 4.5 %collective-permute-start.9 = (bf16[16,2048]{1,0:T(8,128)(2,1)S(1)}, bf16[16,2048]{1,0:T(8,128)(2,1)S(1)}, u32[]{:S(2)}, u32[]{:S(2)}) collective-permute-start(bf16[16,2048]{1,0:T(8,128)(2,1)S(1)} %get-tuple-element.36), channel_id=1, source_target_pairs={{0,4},{4,0},{8,12},{12,8},{1,5},{5,1},{9,13},{13,9},{2,6},{6,2},{1... | collective-permute-start | bytes 196616 | tf_op jit(solution)/shard_map/ppermute | solution.py:53
  24.6 6.9 %collective-permute-start.12 = (bf16[16,2176]{1,0:T(8,128)(2,1)S(1)}, bf16[16,2176]{1,0:T(8,128)(2,1)S(1)}, u32[]{:S(2)}, u32[]{:S(2)}) collective-permute-start(bf16[16,2176]{1,0:T(8,128)(2,1)S(1)} %get-tuple-element.39), channel_id=1, source_target_pairs={{0,12},{4,8},{8,4},{12,0},{1,13},{5,9},{9,5},{13,1},{2,14},{6,10},... | collective-permute-start | bytes 208904 | tf_op jit(solution)/shard_map/ppermute | solution.py:53
  25.9 8.2 %collective-permute-start.8 = (bf16[16,4224]{1,0:T(8,128)(2,1)S(1)}, bf16[16,4224]{1,0:T(8,128)(2,1)S(1)}, u32[]{:S(2)}, u32[]{:S(2)}) collective-permute-start(bf16[16,4224]{1,0:T(8,128)(2,1)S(1)} %get-tuple-element.35), channel_id=1, source_target_pairs={{0,4},{4,0},{8,12},{12,8},{1,5},{5,1},{9,13},{13,9},{2,6},{6,2},{1... | collective-permute-start | bytes 405512 | tf_op jit(solution)/shard_map/ppermute | solution.py:53
  27.9 6.0 %collective-permute-start.10 = (bf16[16,2048]{1,0:T(8,128)(2,1)S(1)}, bf16[16,2048]{1,0:T(8,128)(2,1)S(1)}, u32[]{:S(2)}, u32[]{:S(2)}) collective-permute-start(bf16[16,2048]{1,0:T(8,128)(2,1)S(1)} %relay.2), channel_id=1, source_target_pairs={{0,8},{4,12},{8,0},{12,4},{1,9},{5,13},{9,1},{13,5},{2,10},{6,14},... | collective-permute-start | bytes 196616 | tf_op jit(solution)/shard_map/ppermute | solution.py:53
  34.3 5.5 %collective-permute-start.14 = (bf16[4,8192]{1,0:T(4,128)(2,1)S(1)}, bf16[4,8192]{1,0:T(4,128)(2,1)S(1)}, u32[]{:S(2)}, u32[]{:S(2)}) collective-permute-start(bf16[4,8192]{1,0:T(4,128)(2,1)S(1)} %get-tuple-element.41), channel_id=1, source_target_pairs={{0,8},{4,12},{8,0},{12,4},{1,9},{5,13},{9,1},{13,5},{2,10},{6,14},... | collective-permute-start | bytes 196616 | tf_op jit(solution)/shard_map/ppermute | solution.py:53
  36.4 9.7 %collective-permute-start.13 = (bf16[4,16384]{1,0:T(4,128)(2,1)S(1)}, bf16[4,16384]{1,0:T(4,128)(2,1)S(1)}, u32[]{:S(2)}, u32[]{:S(2)}) collective-permute-start(bf16[4,16384]{1,0:T(4,128)(2,1)S(1)} %get-tuple-element.40.refs_0_.refs_5_), channel_id=1, source_target_pairs={{0,4},{4,0},{8,12},{12,8},{1,5},{5,1},{9,13},{13,9},{2,6},{6,2},{1... | collective-permute-start | bytes 393224 | tf_op jit(solution)/shard_map/ppermute | solution.py:53
  37.6 6.8 %collective-permute-start.17 = (bf16[4,8192]{1,0:T(4,128)(2,1)S(1)}, bf16[4,8192]{1,0:T(4,128)(2,1)S(1)}, u32[]{:S(2)}, u32[]{:S(2)}) collective-permute-start(bf16[4,8192]{1,0:T(4,128)(2,1)S(1)} %get-tuple-element.42), channel_id=1, source_target_pairs={{0,12},{4,8},{8,4},{12,0},{1,13},{5,9},{9,5},{13,1},{2,14},{6,10},... | collective-permute-start | bytes 196616 | tf_op jit(solution)/shard_map/ppermute | solution.py:53
  38.8 7.2 %collective-permute-start.15 = (bf16[4,8192]{1,0:T(4,128)(2,1)S(1)}, bf16[4,8192]{1,0:T(4,128)(2,1)S(1)}, u32[]{:S(2)}, u32[]{:S(2)}) collective-permute-start(bf16[4,8192]{1,0:T(4,128)(2,1)S(1)} %get-tuple-element.42), channel_id=1, source_target_pairs={{0,8},{4,12},{8,0},{12,4},{1,9},{5,13},{9,1},{13,5},{2,10},{6,14},... | collective-permute-start | bytes 196616 | tf_op jit(solution)/shard_map/ppermute | solution.py:53
  39.9 6.2 %collective-permute-start.16 = (bf16[4,8192]{1,0:T(4,128)(2,1)S(1)}, bf16[4,8192]{1,0:T(4,128)(2,1)S(1)}, u32[]{:S(2)}, u32[]{:S(2)}) collective-permute-start(bf16[4,8192]{1,0:T(4,128)(2,1)S(1)} %collective-permute-done.14.refs_2_), channel_id=1, source_target_pairs={{0,4},{4,0},{8,12},{12,8},{1,5},{5,1},{9,13},{13,9},{2,6},{6,2},{1... | collective-permute-start | bytes 196616 | tf_op jit(solution)/shard_map/ppermute | solution.py:53
  47.2 3.2 %collective-permute-start.20 = (f32[16,256]{1,0:T(8,128)S(1)}, f32[16,256]{1,0:T(8,128)S(1)}, u32[]{:S(2)}, u32[]{:S(2)}) collective-permute-start(f32[16,256]{1,0:T(8,128)S(1)} %score_parts.3.refs_0_), channel_id=1, source_target_pairs={{0,3},{1,2},{2,1},{3,0},{4,7},{5,6},{6,5},{7,4},{8,11},{9,10},{10,... | collective-permute-start | bytes 49160 | tf_op jit(solution)/shard_map/ppermute | solution.py:125
  47.2 4.2 %collective-permute-start.19 = (f32[16,256]{1,0:T(8,128)S(1)}, f32[16,256]{1,0:T(8,128)S(1)}, u32[]{:S(2)}, u32[]{:S(2)}) collective-permute-start(f32[16,256]{1,0:T(8,128)S(1)} %score_parts.3.refs_0_), channel_id=1, source_target_pairs={{0,2},{1,3},{2,0},{3,1},{4,6},{5,7},{6,4},{7,5},{8,10},{9,11},{10,... | collective-permute-start | bytes 49160 | tf_op jit(solution)/shard_map/ppermute | solution.py:125
  49.6 1.8 %collective-permute-start.18 = (f32[16,256]{1,0:T(8,128)S(1)}, f32[16,256]{1,0:T(8,128)S(1)}, u32[]{:S(2)}, u32[]{:S(2)}) collective-permute-start(f32[16,256]{1,0:T(8,128)S(1)} %score_parts.3.refs_0_), channel_id=1, source_target_pairs={{0,1},{1,0},{2,3},{3,2},{4,5},{5,4},{6,7},{7,6},{8,9},{9,8},{10,11... | collective-permute-start | bytes 49160 | tf_op jit(solution)/shard_map/ppermute | solution.py:125
  52.7 7.9 %collective-permute-start.24 = (bf16[16,2176]{1,0:T(8,128)(2,1)S(1)}, bf16[16,2176]{1,0:T(8,128)(2,1)S(1)}, u32[]{:S(2)}, u32[]{:S(2)}) collective-permute-start(bf16[16,2176]{1,0:T(8,128)(2,1)S(1)} %get-tuple-element.47), channel_id=1, source_target_pairs={{0,8},{4,12},{8,0},{12,4},{1,9},{5,13},{9,1},{13,5},{2,10},{6,14},... | collective-permute-start | bytes 208904 | tf_op jit(solution)/shard_map/ppermute | solution.py:53
  53.7 4.4 %collective-permute-start.22 = (bf16[16,2048]{1,0:T(8,128)(2,1)S(1)}, bf16[16,2048]{1,0:T(8,128)(2,1)S(1)}, u32[]{:S(2)}, u32[]{:S(2)}) collective-permute-start(bf16[16,2048]{1,0:T(8,128)(2,1)S(1)} %get-tuple-element.45), channel_id=1, source_target_pairs={{0,4},{4,0},{8,12},{12,8},{1,5},{5,1},{9,13},{13,9},{2,6},{6,2},{1... | collective-permute-start | bytes 196616 | tf_op jit(solution)/shard_map/ppermute | solution.py:53
  55.4 6.9 %collective-permute-start.25 = (bf16[16,2176]{1,0:T(8,128)(2,1)S(1)}, bf16[16,2176]{1,0:T(8,128)(2,1)S(1)}, u32[]{:S(2)}, u32[]{:S(2)}) collective-permute-start(bf16[16,2176]{1,0:T(8,128)(2,1)S(1)} %get-tuple-element.48), channel_id=1, source_target_pairs={{0,12},{4,8},{8,4},{12,0},{1,13},{5,9},{9,5},{13,1},{2,14},{6,10},... | collective-permute-start | bytes 208904 | tf_op jit(solution)/shard_map/ppermute | solution.py:53
  57.1 8.2 %collective-permute-start.21 = (bf16[16,4224]{1,0:T(8,128)(2,1)S(1)}, bf16[16,4224]{1,0:T(8,128)(2,1)S(1)}, u32[]{:S(2)}, u32[]{:S(2)}) collective-permute-start(bf16[16,4224]{1,0:T(8,128)(2,1)S(1)} %get-tuple-element.44), channel_id=1, source_target_pairs={{0,4},{4,0},{8,12},{12,8},{1,5},{5,1},{9,13},{13,9},{2,6},{6,2},{1... | collective-permute-start | bytes 405512 | tf_op jit(solution)/shard_map/ppermute | solution.py:53
  58.1 6.6 %collective-permute-start.23 = (bf16[16,2048]{1,0:T(8,128)(2,1)S(1)}, bf16[16,2048]{1,0:T(8,128)(2,1)S(1)}, u32[]{:S(2)}, u32[]{:S(2)}) collective-permute-start(bf16[16,2048]{1,0:T(8,128)(2,1)S(1)} %relay.3), channel_id=1, source_target_pairs={{0,8},{4,12},{8,0},{12,4},{1,9},{5,13},{9,1},{13,5},{2,10},{6,14},... | collective-permute-start | bytes 196616 | tf_op jit(solution)/shard_map/ppermute | solution.py:53

commit v5 on v4

--- a/solution.py
+++ b/solution.py
@@ -203,7 +203,7 @@
     )(*[blocks[i] for i in order], pltpu.with_memory_space_constraint(turned, pltpu.VMEM))
 
 
-def gathered_pieces(pix):
+def gathered_pieces(pix, relayed):
     quarter = pix // 4
     half = quarter // 2
     pieces = []
@@ -211,7 +211,8 @@
         for q in range(4):
             for at in range(0, half, math.gcd(half, 512)):
                 there, here = q * quarter + part * half + at, q * half + at
-                rows = [(0, there), (1, there), (2 + part, here), (4 + part, here)]
+                direct = part != relayed
+                rows = [(0, there), (1, there), (2 + direct, here), (4 + direct, here)]
                 pieces.append((there, math.gcd(half, 512), rows))
     return pieces
 
@@ -297,9 +298,11 @@
         out_ref[:, piece] = ((total + owned_ref[:, piece].astype(jnp.float32)) / (counts + 1.0)).astype(out_ref.dtype)
 
 
-def dense_update_kernel(*refs):
-    own_ref, near_ref, joined_ref, direct_2_ref, direct_3_ref = (refs[SCATTER_ORDER.index(i)] for i in range(5))
-    owned_ref, out_ref = refs[5:7]
+def dense_update_kernel(parts, *refs):
+    own_ref, near_ref, joined_ref, direct_2_ref, direct_3_ref, owned_ref = refs[:6]
+    out_ref, half_refs = refs[-1], refs[-2:-1]
+    if len(refs) < 8:
+        half_refs = []
     quarter = owned_ref.shape[1] // 4
     half = quarter // 2
 
@@ -311,7 +314,7 @@
         [(0, own_ref, behind), (1, near_ref, behind), (2, direct_2_ref, behind_half), (3, direct_3_ref, behind_half)]
     )
     scale = tail[:, :1] + tail[:, TAIL // 2 : TAIL // 2 + 1] + 1.0
-    for part in range(2):
+    for part in parts:
         for piece in chunks(half, 512):
             whole = pl.ds(part * half + piece.start, piece.size)
             terms = [(0, own_ref, whole), (1, near_ref, whole)]
@@ -321,21 +324,38 @@
             new = ((total(terms) + owned) / scale).astype(out_ref.dtype)
             for q, spot in enumerate(spots):
                 out_ref[:, spot] = new[4 * q : 4 * q + 4]
-                if len(refs) > 7:
-                    refs[7 + part][:, pl.ds(q * half + piece.start, piece.size)] = new[4 * q : 4 * q + 4]
-
-
-def update(terms, owned, dtype, halves):
-    shapes = [owned.shape] + ([(owned.shape[0], owned.shape[1] // 2)] * 2 if halves else [])
-    return pl.pallas_call(
-        plain_update_kernel if len(terms) == 1 else dense_update_kernel,
-        in_specs=[IN_VMEM] * (len(terms) + 1),
+                for half_ref in half_refs:
+                    half_ref[:, pl.ds(q * half + piece.start, piece.size)] = new[4 * q : 4 * q + 4]
+
+
+def update_call(kernel, operands, shapes, aliases={}):
+    size = operands[0].size
+    return pl.pallas_call(
+        kernel,
+        in_specs=[IN_VMEM] * len(operands),
         out_specs=[IN_VMEM] * len(shapes),
-        out_shape=[jax.ShapeDtypeStruct(shape, dtype) for shape in shapes],
-        compiler_params=params(),
-        cost_estimate=pl.CostEstimate(flops=8 * owned.size, bytes_accessed=12 * owned.size, transcendentals=0),
+        out_shape=shapes,
+        input_output_aliases=aliases,
+        compiler_params=params(),
+        cost_estimate=pl.CostEstimate(flops=8 * size, bytes_accessed=12 * size, transcendentals=0),
         name="update",
-    )(*([terms[i] for i in SCATTER_ORDER] if len(terms) > 1 else terms), owned)
+    )(*operands)
+
+
+def update_in_parts(terms, owned):
+    own, near, joined, direct_2, direct_3 = terms
+    many, pix = owned.shape
+    half, whole = (jax.ShapeDtypeStruct((many, size), jnp.bfloat16) for size in (pix // 2, pix))
+
+    def second(own_ref, near_ref, direct_2_ref, direct_3_ref, owned_ref, *outs):
+        dense_update_kernel((1,), own_ref, near_ref, None, direct_2_ref, direct_3_ref, owned_ref, *outs)
+
+    def first(own_ref, near_ref, joined_ref, direct_2_ref, direct_3_ref, owned_ref, _, *outs):
+        dense_update_kernel((0,), own_ref, near_ref, joined_ref, direct_2_ref, direct_3_ref, owned_ref, *outs)
+
+    part_1, begun = update_call(second, (own, near, direct_2, direct_3, owned), [half, whole])
+    part_0, done = update_call(first, (*terms, owned, begun), [half, whole], {6: 1})
+    return [done, part_1, part_0]
 
 
 def local(sizes, frames, slices, log_prior, orient):
@@ -352,7 +372,7 @@
             if step == 0:
                 frames, over = lax.optimization_barrier((frames, over))
                 here, turned, prior = load_frames(frames, orient, log_prior, dense)
-            pieces = gathered_pieces(pix)
+            pieces = gathered_pieces(pix, step % 2)
         else:
             blocks = [lax.all_gather(owned_b[0], "frame", axis=0, tiled=True)]
             pieces = [(piece.start, piece.size, [(0, piece.start)]) for piece in chunks(pix, 512)]
@@ -365,7 +385,12 @@
         else:
             whole = totals[0].reshape(along, owned, totals[0].shape[1])
             terms = [lax.all_to_all(whole, "frame", split_axis=0, concat_axis=0, tiled=False)]
-        owned_b = update(terms, owned_b[0], jnp.float32 if last else jnp.bfloat16, dense and not last)
+        if dense and not last:
+            owned_b = update_in_parts(terms, owned_b[0])
+        else:
+            kernel = functools.partial(dense_update_kernel, (0, 1)) if dense else plain_update_kernel
+            shape = jax.ShapeDtypeStruct(slices.shape, jnp.float32 if last else jnp.bfloat16)
+            owned_b = update_call(kernel, (*terms, owned_b[0]), [shape])
     return owned_b[0]
 
 

time: 66.4 us -> 65 us (0.979)
  starting transfers between devices: 35.4 us -> 33.3 us
    ppermute x20, starting transfers between devices: 31.1 us -> 29.6 us  [swap(): return lax.ppermute(value, 'frame', [(i, i ^ distance) for i in range(4)])]
  transfers between devices with their start and end apart: 26 -> 26, of which waited for: 15 -> 14; matrix products, arithmetic and copies ran while one was open for 0% -> 0% of each run, Pallas kernels for 6% -> 7%
where the time goes in v5:
time: 65 us; the launch traced here: 64.9 us
  starting transfers between devices  33.3 us (51%)
  waiting for transfers between devices  20.4 us (31%)
  Pallas kernels  11.1 us (17%)
    ppermute x20, starting transfers between devices, swap(): return lax.ppermute(value, 'frame', [(i, i ^ distance) for i in range(4)])  29.6 us
    ppermute x20, waiting for transfers between devices, swap(): return lax.ppermute(value, 'frame', [(i, i ^ distance) for i in range(4)])  16.3 us
    ppermute x6, waiting for transfers between devices, exchange_all(): lax.ppermute(part, axes, [(i, i ^ k) for i in range(size)])  4.05 us
    pallas_call x1, Pallas kernels, load_frames(): pl.pallas_call(functools.partial(load_kernel, dense), in_specs=[pl.BlockS...  3.98 us
    ppermute x6, starting transfers between devices, exchange_all(): lax.ppermute(part, axes, [(i, i ^ k) for i in range(size)])  3.74 us
    pallas_call x2, Pallas kernels, block_totals(): pl.pallas_call(functools.partial(kernel, len(parts)), in_specs=[IN_VMEM]...  2.41 us
    pallas_call x2, Pallas kernels, score_parts(): pl.pallas_call(functools.partial(score_kernel, pieces, order), in_specs=[...  2.38 us
  transfers between devices with their start and end apart: 26, of which 14 were waited for; matrix products, arithmetic and copies ran while one was open for 0% of the time, Pallas kernels for 7%

profile of v5, /device:TPU:0, one launch (start us, length us, event | category | flops | bytes accessed | tf_op | source)
XLA Modules:
  0.0 64.9 jit_solution(11947334629969466563)
XLA Ops:
  0.0 1.0 %round_slices.1 = (bf16[4,16384]{1,0:T(4,128)(2,1)S(1)}, bf16[4,8192]{1,0:T(4,128)(2,1)S(1)}, bf16[4,8192]{1,0:T(4,128)(2,1)S(1)}) custom-call(f32[4,16384]{1,0:T(4,128)} %slices_ref.1), custom_call_target="tpu_custom_call" | custom-call | bytes 524288 | tf_op jit(solution)/shard_map/round_slices/pallas_call | solution.py:86
  1.0 4.1 %collective-permute-start.1 = (bf16[4,8192]{1,0:T(4,128)(2,1)S(1)}, bf16[4,8192]{1,0:T(4,128)(2,1)S(1)}, u32[]{:S(2)}, u32[]{:S(2)}) collective-permute-start(bf16[4,8192]{1,0:T(4,128)(2,1)S(1)} %get-tuple-element.29), channel_id=1, source_target_pairs={{0,8},{4,12},{8,0},{12,4},{1,9},{5,13},{9,1},{13,5},{2,10},{6,14},... | collective-permute-start | bytes 196616 | tf_op jit(solution)/shard_map/ppermute | solution.py:53
  5.1 1.6 %collective-permute-start = (bf16[4,16384]{1,0:T(4,128)(2,1)S(1)}, bf16[4,16384]{1,0:T(4,128)(2,1)S(1)}, u32[]{:S(2)}, u32[]{:S(2)}) collective-permute-start(bf16[4,16384]{1,0:T(4,128)(2,1)S(1)} %get-tuple-element.28.refs_0_.owned_ref), channel_id=1, source_target_pairs={{0,4},{4,0},{8,12},{12,8},{1,5},{5,1},{9,13},{13,9},{2,6},{6,2},{1... | collective-permute-start | bytes 393224 | tf_op jit(solution)/shard_map/ppermute | solution.py:53
  6.7 0.0 collective-permute-start.4
  6.7 1.9 %collective-permute-start.2 = (bf16[4,8192]{1,0:T(4,128)(2,1)S(1)}, bf16[4,8192]{1,0:T(4,128)(2,1)S(1)}, u32[]{:S(2)}, u32[]{:S(2)}) collective-permute-start(bf16[4,8192]{1,0:T(4,128)(2,1)S(1)} %get-tuple-element.30), channel_id=1, source_target_pairs={{0,8},{4,12},{8,0},{12,4},{1,9},{5,13},{9,1},{13,5},{2,10},{6,14},... | collective-permute-start | bytes 196616 | tf_op jit(solution)/shard_map/ppermute | solution.py:53
  8.6 0.0 collective-permute-done.1.refs_2_
  8.6 2.5 %collective-permute-start.3 = (bf16[4,8192]{1,0:T(4,128)(2,1)S(1)}, bf16[4,8192]{1,0:T(4,128)(2,1)S(1)}, u32[]{:S(2)}, u32[]{:S(2)}) collective-permute-start(bf16[4,8192]{1,0:T(4,128)(2,1)S(1)} %collective-permute-done.1.refs_2_), channel_id=1, source_target_pairs={{0,4},{4,0},{8,12},{12,8},{1,5},{5,1},{9,13},{13,9},{2,6},{6,2},{1... | collective-permute-start | bytes 196616 | tf_op jit(solution)/shard_map/ppermute | solution.py:53
  11.1 4.0 %load_frames.1 = (bf16[256,16384]{1,0:T(8,128)(2,1)S(1)}, bf16[16384,256]{1,0:T(8,128)(2,1)S(1)}, f32[16,256]{1,0:T(8,128)S(1)}) custom-call(bf16[256,16384]{1,0:T(8,128)(2,1)} %frames_ref, s32[16]{0:T(128)} %orient_in_ref.1, f32[4096]{0:T(1024)} %log_prior_in_ref.1), custom_call_target="tpu_custom_call" | custom-call | bytes 25165824 | tf_op jit(solution)/shard_map/load_frames/pallas_call | solution.py:159
  15.0 0.0 collective-permute-done.4.refs_5_
  15.1 0.0 collective-permute-done.2.refs_3_
  15.1 0.0 collective-permute-done.3.refs_4_
  15.1 0.0 collective-permute-done.refs_1_
  15.1 1.2 %score_parts.2.refs_0_ = f32[16,256]{1,0:T(8,128)S(1)} custom-call(bf16[4,16384]{1,0:T(4,128)(2,1)S(1)} %get-tuple-element.28.refs_0_.owned_ref, bf16[4,16384]{1,0:T(4,128)(2,1)S(1)} %collective-permute-done.refs_1_, bf16[4,8192]{1,0:T(4,128)(2,1)S(1)} %collective-permute-done.1.refs_2_, bf16[4,8192]{1,0:T(4,128)(2,1)S(1)} %collective-permute-done.2.refs_3_, ...), custom_call_target="tpu_custom_call" | custom-call | flops 134217728 | bytes 8388608 | tf_op jit(solution)/shard_map/score_parts/pallas_call | solution.py:195
  16.3 0.2 collective-permute-start.7
  16.5 1.3 %collective-permute-start.6 = (f32[16,256]{1,0:T(8,128)S(1)}, f32[16,256]{1,0:T(8,128)S(1)}, u32[]{:S(2)}, u32[]{:S(2)}) collective-permute-start(f32[16,256]{1,0:T(8,128)S(1)} %score_parts.2.refs_0_), channel_id=1, source_target_pairs={{0,2},{1,3},{2,0},{3,1},{4,6},{5,7},{6,4},{7,5},{8,10},{9,11},{10,... | collective-permute-start | bytes 49160 | tf_op jit(solution)/shard_map/ppermute | solution.py:125
  17.8 0.3 collective-permute-start.5
  18.1 1.4 %collective-permute-done.7.refs_3_ = f32[16,256]{1,0:T(8,128)S(1)} collective-permute-done((f32[16,256]{1,0:T(8,128)S(1)}, f32[16,256]{1,0:T(8,128)S(1)}, u32[]{:S(2)}, u32[]{:S(2)}) %collective-permute-start.7) | collective-permute-done | bytes 16416 | tf_op jit(solution)/shard_map/ppermute | solution.py:125
  19.6 0.7 %collective-permute-done.6.refs_2_ = f32[16,256]{1,0:T(8,128)S(1)} collective-permute-done((f32[16,256]{1,0:T(8,128)S(1)}, f32[16,256]{1,0:T(8,128)S(1)}, u32[]{:S(2)}, u32[]{:S(2)}) %collective-permute-start.6) | collective-permute-done | bytes 16416 | tf_op jit(solution)/shard_map/ppermute | solution.py:125
  20.3 0.0 collective-permute-done.5.refs_1_
  20.3 1.2 %block_totals.2 = (bf16[16,4224]{1,0:T(8,128)(2,1)S(1)}, bf16[16,4224]{1,0:T(8,128)(2,1)S(1)}, bf16[16,2048]{1,0:T(8,128)(2,1)S(1)}, bf16[16,2176]{1,0:T(8,128)(...) custom-call(f32[16,256]{1,0:T(8,128)S(1)} %score_parts.2.refs_0_, ...), custom_call_target="tpu_custom_call" | custom-call | flops 134217728 | bytes 8388608 | tf_op jit(solution)/shard_map/block_totals/pallas_call | solution.py:279
  21.5 1.9 %collective-permute-start.11 = (bf16[16,2176]{1,0:T(8,128)(2,1)S(1)}, bf16[16,2176]{1,0:T(8,128)(2,1)S(1)}, u32[]{:S(2)}, u32[]{:S(2)}) collective-permute-start(bf16[16,2176]{1,0:T(8,128)(2,1)S(1)} %get-tuple-element.39), channel_id=1, source_target_pairs={{0,8},{4,12},{8,0},{12,4},{1,9},{5,13},{9,1},{13,5},{2,10},{6,14},... | collective-permute-start | bytes 208904 | tf_op jit(solution)/shard_map/ppermute | solution.py:53
  23.4 1.2 %collective-permute-start.9 = (bf16[16,2048]{1,0:T(8,128)(2,1)S(1)}, bf16[16,2048]{1,0:T(8,128)(2,1)S(1)}, u32[]{:S(2)}, u32[]{:S(2)}) collective-permute-start(bf16[16,2048]{1,0:T(8,128)(2,1)S(1)} %get-tuple-element.37), channel_id=1, source_target_pairs={{0,4},{4,0},{8,12},{12,8},{1,5},{5,1},{9,13},{13,9},{2,6},{6,2},{1... | collective-permute-start | bytes 196616 | tf_op jit(solution)/shard_map/ppermute | solution.py:53
  24.6 1.3 %collective-permute-start.12 = (bf16[16,2176]{1,0:T(8,128)(2,1)S(1)}, bf16[16,2176]{1,0:T(8,128)(2,1)S(1)}, u32[]{:S(2)}, u32[]{:S(2)}) collective-permute-start(bf16[16,2176]{1,0:T(8,128)(2,1)S(1)} %get-tuple-element.40), channel_id=1, source_target_pairs={{0,12},{4,8},{8,4},{12,0},{1,13},{5,9},{9,5},{13,1},{2,14},{6,10},... | collective-permute-start | bytes 208904 | tf_op jit(solution)/shard_map/ppermute | solution.py:53
  25.9 0.2 collective-permute-start.8
  26.2 1.7 %collective-permute-done.9.came_ref = bf16[16,2048]{1,0:T(8,128)(2,1)S(1)} collective-permute-done((bf16[16,2048]{1,0:T(8,128)(2,1)S(1)}, bf16[16,2048]{1,0:T(8,128)(2,1)S(1)}, u32[]{:S(2)}, u32[]{:S(2)}) %collective-permute-start.9) | collective-permute-done | bytes 65568 | tf_op jit(solution)/shard_map/ppermute | solution.py:53
  27.9 1.8 %collective-permute-start.10 = (bf16[16,2048]{1,0:T(8,128)(2,1)S(1)}, bf16[16,2048]{1,0:T(8,128)(2,1)S(1)}, u32[]{:S(2)}, u32[]{:S(2)}) collective-permute-start(bf16[16,2048]{1,0:T(8,128)(2,1)S(1)} %relay.2), channel_id=1, source_target_pairs={{0,8},{4,12},{8,0},{12,4},{1,9},{5,13},{9,1},{13,5},{2,10},{6,14},... | collective-permute-start | bytes 196616 | tf_op jit(solution)/shard_map/ppermute | solution.py:53
  29.7 0.0 collective-permute-done.11.in_ref
  29.7 1.8 %collective-permute-done.12.in_ref = bf16[16,2176]{1,0:T(8,128)(2,1)S(1)} collective-permute-done((bf16[16,2176]{1,0:T(8,128)(2,1)S(1)}, bf16[16,2176]{1,0:T(8,128)(2,1)S(1)}, u32[]{:S(2)}, u32[]{:S(2)}) %collective-permute-start.12) | collective-permute-done | bytes 69664 | tf_op jit(solution)/shard_map/ppermute | solution.py:53
  31.5 2.5 %collective-permute-done.8.near_ref = bf16[16,4224]{1,0:T(8,128)(2,1)S(1)} collective-permute-done((bf16[16,4224]{1,0:T(8,128)(2,1)S(1)}, bf16[16,4224]{1,0:T(8,128)(2,1)S(1)}, u32[]{:S(2)}, u32[]{:S(2)}) %collective-permute-start.8) | collective-permute-done | bytes 135200 | tf_op jit(solution)/shard_map/ppermute | solution.py:53
  34.1 0.2 update.3
  34.3 0.8 %collective-permute-start.14 = (bf16[4,8192]{1,0:T(4,128)(2,1)S(1)}, bf16[4,8192]{1,0:T(4,128)(2,1)S(1)}, u32[]{:S(2)}, u32[]{:S(2)}) collective-permute-start(bf16[4,8192]{1,0:T(4,128)(2,1)S(1)} %get-tuple-element.43), channel_id=1, source_target_pairs={{0,8},{4,12},{8,0},{12,4},{1,9},{5,13},{9,1},{13,5},{2,10},{6,14},... | collective-permute-start | bytes 196616 | tf_op jit(solution)/shard_map/ppermute | solution.py:53
  35.0 0.0 collective-permute-done.10.joined_ref
  35.0 0.2 update.4
  35.2 2.5 %collective-permute-start.13 = (bf16[4,16384]{1,0:T(4,128)(2,1)S(1)}, bf16[4,16384]{1,0:T(4,128)(2,1)S(1)}, u32[]{:S(2)}, u32[]{:S(2)}) collective-permute-start(bf16[4,16384]{1,0:T(4,128)(2,1)S(1)} %get-tuple-element.42.refs_0_.refs_5_), channel_id=1, source_target_pairs={{0,4},{4,0},{8,12},{12,8},{1,5},{5,1},{9,13},{13,9},{2,6},{6,2},{1... | collective-permute-start | bytes 393224 | tf_op jit(solution)/shard_map/ppermute | solution.py:53
  37.8 1.2 %collective-permute-start.17 = (bf16[4,8192]{1,0:T(4,128)(2,1)S(1)}, bf16[4,8192]{1,0:T(4,128)(2,1)S(1)}, u32[]{:S(2)}, u32[]{:S(2)}) collective-permute-start(bf16[4,8192]{1,0:T(4,128)(2,1)S(1)} %get-tuple-element.44), channel_id=1, source_target_pairs={{0,12},{4,8},{8,4},{12,0},{1,13},{5,9},{9,5},{13,1},{2,14},{6,10},... | collective-permute-start | bytes 196616 | tf_op jit(solution)/shard_map/ppermute | solution.py:53
  39.0 0.3 collective-permute-start.15
  39.3 1.2 %collective-permute-done.14.refs_2_ = bf16[4,8192]{1,0:T(4,128)(2,1)S(1)} collective-permute-done((bf16[4,8192]{1,0:T(4,128)(2,1)S(1)}, bf16[4,8192]{1,0:T(4,128)(2,1)S(1)}, u32[]{:S(2)}, u32[]{:S(2)}) %collective-permute-start.14) | collective-permute-done | bytes 65568 | tf_op jit(solution)/shard_map/ppermute | solution.py:53
  40.5 1.6 %collective-permute-start.16 = (bf16[4,8192]{1,0:T(4,128)(2,1)S(1)}, bf16[4,8192]{1,0:T(4,128)(2,1)S(1)}, u32[]{:S(2)}, u32[]{:S(2)}) collective-permute-start(bf16[4,8192]{1,0:T(4,128)(2,1)S(1)} %collective-permute-done.14.refs_2_), channel_id=1, source_target_pairs={{0,4},{4,0},{8,12},{12,8},{1,5},{5,1},{9,13},{13,9},{2,6},{6,2},{1... | collective-permute-start | bytes 196616 | tf_op jit(solution)/shard_map/ppermute | solution.py:53
  42.2 2.5 %collective-permute-done.17.refs_5_ = bf16[4,8192]{1,0:T(4,128)(2,1)S(1)} collective-permute-done((bf16[4,8192]{1,0:T(4,128)(2,1)S(1)}, bf16[4,8192]{1,0:T(4,128)(2,1)S(1)}, u32[]{:S(2)}, u32[]{:S(2)}) %collective-permute-start.17) | collective-permute-done | bytes 65568 | tf_op jit(solution)/shard_map/ppermute | solution.py:53
  44.6 1.1 %collective-permute-done.15.refs_3_ = bf16[4,8192]{1,0:T(4,128)(2,1)S(1)} collective-permute-done((bf16[4,8192]{1,0:T(4,128)(2,1)S(1)}, bf16[4,8192]{1,0:T(4,128)(2,1)S(1)}, u32[]{:S(2)}, u32[]{:S(2)}) %collective-permute-start.15) | collective-permute-done | bytes 65568 | tf_op jit(solution)/shard_map/ppermute | solution.py:53
  45.7 0.0 collective-permute-done.16.refs_4_
  45.7 0.0 collective-permute-done.13.refs_1_
  45.7 1.2 %score_parts.3.refs_0_ = f32[16,256]{1,0:T(8,128)S(1)} custom-call(bf16[4,16384]{1,0:T(4,128)(2,1)S(1)} %get-tuple-element.42.refs_0_.refs_5_, bf16[4,16384]{1,0:T(4,128)(2,1)S(1)} %collective-permute-done.13.refs_1_, bf16[4,8192]{1,0:T(4,128)(2,1)S(1)} %collective-permute-done.14.refs_2_, bf16[4,8192]{1,0:T(4,128)(2,1)S(1)} %collective-permute-done.15.refs_3_, ...), custom_call_target="tpu_custom_call" | custom-call | flops 134217728 | bytes 8388608 | tf_op jit(solution)/shard_map/score_parts/pallas_call | solution.py:195
  46.9 0.0 collective-permute-start.20
  46.9 0.7 %collective-permute-start.19 = (f32[16,256]{1,0:T(8,128)S(1)}, f32[16,256]{1,0:T(8,128)S(1)}, u32[]{:S(2)}, u32[]{:S(2)}) collective-permute-start(f32[16,256]{1,0:T(8,128)S(1)} %score_parts.3.refs_0_), channel_id=1, source_target_pairs={{0,2},{1,3},{2,0},{3,1},{4,6},{5,7},{6,4},{7,5},{8,10},{9,11},{10,... | collective-permute-start | bytes 49160 | tf_op jit(solution)/shard_map/ppermute | solution.py:125
  47.6 1.1 %collective-permute-start.18 = (f32[16,256]{1,0:T(8,128)S(1)}, f32[16,256]{1,0:T(8,128)S(1)}, u32[]{:S(2)}, u32[]{:S(2)}) collective-permute-start(f32[16,256]{1,0:T(8,128)S(1)} %score_parts.3.refs_0_), channel_id=1, source_target_pairs={{0,1},{1,0},{2,3},{3,2},{4,5},{5,4},{6,7},{7,6},{8,9},{9,8},{10,11... | collective-permute-start | bytes 49160 | tf_op jit(solution)/shard_map/ppermute | solution.py:125
  48.8 1.3 %collective-permute-done.20.refs_3_ = f32[16,256]{1,0:T(8,128)S(1)} collective-permute-done((f32[16,256]{1,0:T(8,128)S(1)}, f32[16,256]{1,0:T(8,128)S(1)}, u32[]{:S(2)}, u32[]{:S(2)}) %collective-permute-start.20) | collective-permute-done | bytes 16416 | tf_op jit(solution)/shard_map/ppermute | solution.py:125
  50.1 0.6 collective-permute-done.19.refs_2_
  50.7 0.0 collective-permute-done.18.refs_1_
  50.7 1.2 %block_totals.3 = (bf16[16,4224]{1,0:T(8,128)(2,1)S(1)}, bf16[16,4224]{1,0:T(8,128)(2,1)S(1)}, bf16[16,2048]{1,0:T(8,128)(2,1)S(1)}, bf16[16,2176]{1,0:T(8,128)(...) custom-call(f32[16,256]{1,0:T(8,128)S(1)} %score_parts.3.refs_0_, ...), custom_call_target="tpu_custom_call" | custom-call | flops 134217728 | bytes 8388608 | tf_op jit(solution)/shard_map/block_totals/pallas_call | solution.py:279
  51.9 1.4 %collective-permute-start.24 = (bf16[16,2176]{1,0:T(8,128)(2,1)S(1)}, bf16[16,2176]{1,0:T(8,128)(2,1)S(1)}, u32[]{:S(2)}, u32[]{:S(2)}) collective-permute-start(bf16[16,2176]{1,0:T(8,128)(2,1)S(1)} %get-tuple-element.49), channel_id=1, source_target_pairs={{0,8},{4,12},{8,0},{12,4},{1,9},{5,13},{9,1},{13,5},{2,10},{6,14},... | collective-permute-start | bytes 208904 | tf_op jit(solution)/shard_map/ppermute | solution.py:53
  53.3 1.6 %collective-permute-start.22 = (bf16[16,2048]{1,0:T(8,128)(2,1)S(1)}, bf16[16,2048]{1,0:T(8,128)(2,1)S(1)}, u32[]{:S(2)}, u32[]{:S(2)}) collective-permute-start(bf16[16,2048]{1,0:T(8,128)(2,1)S(1)} %get-tuple-element.47), channel_id=1, source_target_pairs={{0,4},{4,0},{8,12},{12,8},{1,5},{5,1},{9,13},{13,9},{2,6},{6,2},{1... | collective-permute-start | bytes 196616 | tf_op jit(solution)/shard_map/ppermute | solution.py:53
  55.0 1.4 %collective-permute-start.25 = (bf16[16,2176]{1,0:T(8,128)(2,1)S(1)}, bf16[16,2176]{1,0:T(8,128)(2,1)S(1)}, u32[]{:S(2)}, u32[]{:S(2)}) collective-permute-start(bf16[16,2176]{1,0:T(8,128)(2,1)S(1)} %get-tuple-element.50), channel_id=1, source_target_pairs={{0,12},{4,8},{8,4},{12,0},{1,13},{5,9},{9,5},{13,1},{2,14},{6,10},... | collective-permute-start | bytes 208904 | tf_op jit(solution)/shard_map/ppermute | solution.py:53
  56.4 0.1 collective-permute-start.21
  56.5 1.1 %collective-permute-done.22.came_ref = bf16[16,2048]{1,0:T(8,128)(2,1)S(1)} collective-permute-done((bf16[16,2048]{1,0:T(8,128)(2,1)S(1)}, bf16[16,2048]{1,0:T(8,128)(2,1)S(1)}, u32[]{:S(2)}, u32[]{:S(2)}) %collective-permute-start.22) | collective-permute-done | bytes 65568 | tf_op jit(solution)/shard_map/ppermute | solution.py:53
  57.7 2.0 %collective-permute-start.23 = (bf16[16,2048]{1,0:T(8,128)(2,1)S(1)}, bf16[16,2048]{1,0:T(8,128)(2,1)S(1)}, u32[]{:S(2)}, u32[]{:S(2)}) collective-permute-start(bf16[16,2048]{1,0:T(8,128)(2,1)S(1)} %relay.3), channel_id=1, source_target_pairs={{0,8},{4,12},{8,0},{12,4},{1,9},{5,13},{9,1},{13,5},{2,10},{6,14},... | collective-permute-start | bytes 196616 | tf_op jit(solution)/shard_map/ppermute | solution.py:53
  59.7 0.0 collective-permute-done.24.in_ref
  59.7 2.3 %collective-permute-done.25.in_ref = bf16[16,2176]{1,0:T(8,128)(2,1)S(1)} collective-permute-done((bf16[16,2176]{1,0:T(8,128)(2,1)S(1)}, bf16[16,2176]{1,0:T(8,128)(2,1)S(1)}, u32[]{:S(2)}, u32[]{:S(2)}) %collective-permute-start.25) | collective-permute-done | bytes 69664 | tf_op jit(solution)/shard_map/ppermute | solution.py:53
  62.0 1.2 %collective-permute-done.23.refs_2_ = bf16[16,2048]{1,0:T(8,128)(2,1)S(1)} collective-permute-done((bf16[16,2048]{1,0:T(8,128)(2,1)S(1)}, bf16[16,2048]{1,0:T(8,128)(2,1)S(1)}, u32[]{:S(2)}, u32[]{:S(2)}) %collective-permute-start.23) | collective-permute-done | bytes 65568 | tf_op jit(solution)/shard_map/ppermute | solution.py:53
  63.2 0.8 %collective-permute-done.21.refs_1_ = bf16[16,4224]{1,0:T(8,128)(2,1)S(1)} collective-permute-done((bf16[16,4224]{1,0:T(8,128)(2,1)S(1)}, bf16[16,4224]{1,0:T(8,128)(2,1)S(1)}, u32[]{:S(2)}, u32[]{:S(2)}) %collective-permute-start.21) | collective-permute-done | bytes 135200 | tf_op jit(solution)/shard_map/ppermute | solution.py:53
  64.0 0.9 %update.5 = f32[4,16384]{1,0:T(4,128)} custom-call(bf16[16,4224]{1,0:T(8,128)(2,1)S(1)} %get-tuple-element.45.refs_0_, bf16[16,4224]{1,0:T(8,128)(2,1)S(1)} %collective-permute-done.21.refs_1_, bf16[16,2048]{1,0:T(8,128)(2,1)S(1)} %collective-permute-done.23.refs_2_, bf16[16,2176]{1,0:T(8,128)(2,1)S(1)} %early.6.refs_3_, bf16[16,2176]{1,0:T(8,128)(2,1)S(1)} %early.7.refs_4_, ...), custom_call_target="tpu_custom_call" | custom-call | flops 540672 | bytes 811008 | tf_op jit(solution)/shard_map/update/pallas_call | solution.py:333
  (6 shorter events, 0.1 us)
Async XLA Ops:
  1.0 7.6 %collective-permute-start.1 = (bf16[4,8192]{1,0:T(4,128)(2,1)S(1)}, bf16[4,8192]{1,0:T(4,128)(2,1)S(1)}, u32[]{:S(2)}, u32[]{:S(2)}) collective-permute-start(bf16[4,8192]{1,0:T(4,128)(2,1)S(1)} %get-tuple-element.29), channel_id=1, source_target_pairs={{0,8},{4,12},{8,0},{12,4},{1,9},{5,13},{9,1},{13,5},{2,10},{6,14},... | collective-permute-start | bytes 196616 | tf_op jit(solution)/shard_map/ppermute | solution.py:53
  5.1 10.0 %collective-permute-start = (bf16[4,16384]{1,0:T(4,128)(2,1)S(1)}, bf16[4,16384]{1,0:T(4,128)(2,1)S(1)}, u32[]{:S(2)}, u32[]{:S(2)}) collective-permute-start(bf16[4,16384]{1,0:T(4,128)(2,1)S(1)} %get-tuple-element.28.refs_0_.owned_ref), channel_id=1, source_target_pairs={{0,4},{4,0},{8,12},{12,8},{1,5},{5,1},{9,13},{13,9},{2,6},{6,2},{1... | collective-permute-start | bytes 393224 | tf_op jit(solution)/shard_map/ppermute | solution.py:53
  6.7 8.4 %collective-permute-start.4 = (bf16[4,8192]{1,0:T(4,128)(2,1)S(1)}, bf16[4,8192]{1,0:T(4,128)(2,1)S(1)}, u32[]{:S(2)}, u32[]{:S(2)}) collective-permute-start(bf16[4,8192]{1,0:T(4,128)(2,1)S(1)} %get-tuple-element.30), channel_id=1, source_target_pairs={{0,12},{4,8},{8,4},{12,0},{1,13},{5,9},{9,5},{13,1},{2,14},{6,10},... | collective-permute-start | bytes 196616 | tf_op jit(solution)/shard_map/ppermute | solution.py:53
  6.7 8.4 %collective-permute-start.2 = (bf16[4,8192]{1,0:T(4,128)(2,1)S(1)}, bf16[4,8192]{1,0:T(4,128)(2,1)S(1)}, u32[]{:S(2)}, u32[]{:S(2)}) collective-permute-start(bf16[4,8192]{1,0:T(4,128)(2,1)S(1)} %get-tuple-element.30), channel_id=1, source_target_pairs={{0,8},{4,12},{8,0},{12,4},{1,9},{5,13},{9,1},{13,5},{2,10},{6,14},... | collective-permute-start | bytes 196616 | tf_op jit(solution)/shard_map/ppermute | solution.py:53
  8.6 6.5 %collective-permute-start.3 = (bf16[4,8192]{1,0:T(4,128)(2,1)S(1)}, bf16[4,8192]{1,0:T(4,128)(2,1)S(1)}, u32[]{:S(2)}, u32[]{:S(2)}) collective-permute-start(bf16[4,8192]{1,0:T(4,128)(2,1)S(1)} %collective-permute-done.1.refs_2_), channel_id=1, source_target_pairs={{0,4},{4,0},{8,12},{12,8},{1,5},{5,1},{9,13},{13,9},{2,6},{6,2},{1... | collective-permute-start | bytes 196616 | tf_op jit(solution)/shard_map/ppermute | solution.py:53
  16.3 3.3 %collective-permute-start.7 = (f32[16,256]{1,0:T(8,128)S(1)}, f32[16,256]{1,0:T(8,128)S(1)}, u32[]{:S(2)}, u32[]{:S(2)}) collective-permute-start(f32[16,256]{1,0:T(8,128)S(1)} %score_parts.2.refs_0_), channel_id=1, source_target_pairs={{0,3},{1,2},{2,1},{3,0},{4,7},{5,6},{6,5},{7,4},{8,11},{9,10},{10,... | collective-permute-start | bytes 49160 | tf_op jit(solution)/shard_map/ppermute | solution.py:125
  16.5 3.7 %collective-permute-start.6 = (f32[16,256]{1,0:T(8,128)S(1)}, f32[16,256]{1,0:T(8,128)S(1)}, u32[]{:S(2)}, u32[]{:S(2)}) collective-permute-start(f32[16,256]{1,0:T(8,128)S(1)} %score_parts.2.refs_0_), channel_id=1, source_target_pairs={{0,2},{1,3},{2,0},{3,1},{4,6},{5,7},{6,4},{7,5},{8,10},{9,11},{10,... | collective-permute-start | bytes 49160 | tf_op jit(solution)/shard_map/ppermute | solution.py:125
  17.8 2.4 %collective-permute-start.5 = (f32[16,256]{1,0:T(8,128)S(1)}, f32[16,256]{1,0:T(8,128)S(1)}, u32[]{:S(2)}, u32[]{:S(2)}) collective-permute-start(f32[16,256]{1,0:T(8,128)S(1)} %score_parts.2.refs_0_), channel_id=1, source_target_pairs={{0,1},{1,0},{2,3},{3,2},{4,5},{5,4},{6,7},{7,6},{8,9},{9,8},{10,11... | collective-permute-start | bytes 49160 | tf_op jit(solution)/shard_map/ppermute | solution.py:125
  21.5 8.2 %collective-permute-start.11 = (bf16[16,2176]{1,0:T(8,128)(2,1)S(1)}, bf16[16,2176]{1,0:T(8,128)(2,1)S(1)}, u32[]{:S(2)}, u32[]{:S(2)}) collective-permute-start(bf16[16,2176]{1,0:T(8,128)(2,1)S(1)} %get-tuple-element.39), channel_id=1, source_target_pairs={{0,8},{4,12},{8,0},{12,4},{1,9},{5,13},{9,1},{13,5},{2,10},{6,14},... | collective-permute-start | bytes 208904 | tf_op jit(solution)/shard_map/ppermute | solution.py:53
  23.4 4.5 %collective-permute-start.9 = (bf16[16,2048]{1,0:T(8,128)(2,1)S(1)}, bf16[16,2048]{1,0:T(8,128)(2,1)S(1)}, u32[]{:S(2)}, u32[]{:S(2)}) collective-permute-start(bf16[16,2048]{1,0:T(8,128)(2,1)S(1)} %get-tuple-element.37), channel_id=1, source_target_pairs={{0,4},{4,0},{8,12},{12,8},{1,5},{5,1},{9,13},{13,9},{2,6},{6,2},{1... | collective-permute-start | bytes 196616 | tf_op jit(solution)/shard_map/ppermute | solution.py:53
  24.6 6.9 %collective-permute-start.12 = (bf16[16,2176]{1,0:T(8,128)(2,1)S(1)}, bf16[16,2176]{1,0:T(8,128)(2,1)S(1)}, u32[]{:S(2)}, u32[]{:S(2)}) collective-permute-start(bf16[16,2176]{1,0:T(8,128)(2,1)S(1)} %get-tuple-element.40), channel_id=1, source_target_pairs={{0,12},{4,8},{8,4},{12,0},{1,13},{5,9},{9,5},{13,1},{2,14},{6,10},... | collective-permute-start | bytes 208904 | tf_op jit(solution)/shard_map/ppermute | solution.py:53
  25.9 8.2 %collective-permute-start.8 = (bf16[16,4224]{1,0:T(8,128)(2,1)S(1)}, bf16[16,4224]{1,0:T(8,128)(2,1)S(1)}, u32[]{:S(2)}, u32[]{:S(2)}) collective-permute-start(bf16[16,4224]{1,0:T(8,128)(2,1)S(1)} %get-tuple-element.36), channel_id=1, source_target_pairs={{0,4},{4,0},{8,12},{12,8},{1,5},{5,1},{9,13},{13,9},{2,6},{6,2},{1... | collective-permute-start | bytes 405512 | tf_op jit(solution)/shard_map/ppermute | solution.py:53
  27.9 7.1 %collective-permute-start.10 = (bf16[16,2048]{1,0:T(8,128)(2,1)S(1)}, bf16[16,2048]{1,0:T(8,128)(2,1)S(1)}, u32[]{:S(2)}, u32[]{:S(2)}) collective-permute-start(bf16[16,2048]{1,0:T(8,128)(2,1)S(1)} %relay.2), channel_id=1, source_target_pairs={{0,8},{4,12},{8,0},{12,4},{1,9},{5,13},{9,1},{13,5},{2,10},{6,14},... | collective-permute-start | bytes 196616 | tf_op jit(solution)/shard_map/ppermute | solution.py:53
  34.3 6.3 %collective-permute-start.14 = (bf16[4,8192]{1,0:T(4,128)(2,1)S(1)}, bf16[4,8192]{1,0:T(4,128)(2,1)S(1)}, u32[]{:S(2)}, u32[]{:S(2)}) collective-permute-start(bf16[4,8192]{1,0:T(4,128)(2,1)S(1)} %get-tuple-element.43), channel_id=1, source_target_pairs={{0,8},{4,12},{8,0},{12,4},{1,9},{5,13},{9,1},{13,5},{2,10},{6,14},... | collective-permute-start | bytes 196616 | tf_op jit(solution)/shard_map/ppermute | solution.py:53
  35.2 10.5 %collective-permute-start.13 = (bf16[4,16384]{1,0:T(4,128)(2,1)S(1)}, bf16[4,16384]{1,0:T(4,128)(2,1)S(1)}, u32[]{:S(2)}, u32[]{:S(2)}) collective-permute-start(bf16[4,16384]{1,0:T(4,128)(2,1)S(1)} %get-tuple-element.42.refs_0_.refs_5_), channel_id=1, source_target_pairs={{0,4},{4,0},{8,12},{12,8},{1,5},{5,1},{9,13},{13,9},{2,6},{6,2},{1... | collective-permute-start | bytes 393224 | tf_op jit(solution)/shard_map/ppermute | solution.py:53
  37.8 6.9 %collective-permute-start.17 = (bf16[4,8192]{1,0:T(4,128)(2,1)S(1)}, bf16[4,8192]{1,0:T(4,128)(2,1)S(1)}, u32[]{:S(2)}, u32[]{:S(2)}) collective-permute-start(bf16[4,8192]{1,0:T(4,128)(2,1)S(1)} %get-tuple-element.44), channel_id=1, source_target_pairs={{0,12},{4,8},{8,4},{12,0},{1,13},{5,9},{9,5},{13,1},{2,14},{6,10},... | collective-permute-start | bytes 196616 | tf_op jit(solution)/shard_map/ppermute | solution.py:53
  39.0 6.7 %collective-permute-start.15 = (bf16[4,8192]{1,0:T(4,128)(2,1)S(1)}, bf16[4,8192]{1,0:T(4,128)(2,1)S(1)}, u32[]{:S(2)}, u32[]{:S(2)}) collective-permute-start(bf16[4,8192]{1,0:T(4,128)(2,1)S(1)} %get-tuple-element.44), channel_id=1, source_target_pairs={{0,8},{4,12},{8,0},{12,4},{1,9},{5,13},{9,1},{13,5},{2,10},{6,14},... | collective-permute-start | bytes 196616 | tf_op jit(solution)/shard_map/ppermute | solution.py:53
  40.5 5.2 %collective-permute-start.16 = (bf16[4,8192]{1,0:T(4,128)(2,1)S(1)}, bf16[4,8192]{1,0:T(4,128)(2,1)S(1)}, u32[]{:S(2)}, u32[]{:S(2)}) collective-permute-start(bf16[4,8192]{1,0:T(4,128)(2,1)S(1)} %collective-permute-done.14.refs_2_), channel_id=1, source_target_pairs={{0,4},{4,0},{8,12},{12,8},{1,5},{5,1},{9,13},{13,9},{2,6},{6,2},{1... | collective-permute-start | bytes 196616 | tf_op jit(solution)/shard_map/ppermute | solution.py:53
  46.9 3.2 %collective-permute-start.20 = (f32[16,256]{1,0:T(8,128)S(1)}, f32[16,256]{1,0:T(8,128)S(1)}, u32[]{:S(2)}, u32[]{:S(2)}) collective-permute-start(f32[16,256]{1,0:T(8,128)S(1)} %score_parts.3.refs_0_), channel_id=1, source_target_pairs={{0,3},{1,2},{2,1},{3,0},{4,7},{5,6},{6,5},{7,4},{8,11},{9,10},{10,... | collective-permute-start | bytes 49160 | tf_op jit(solution)/shard_map/ppermute | solution.py:125
  46.9 3.8 %collective-permute-start.19 = (f32[16,256]{1,0:T(8,128)S(1)}, f32[16,256]{1,0:T(8,128)S(1)}, u32[]{:S(2)}, u32[]{:S(2)}) collective-permute-start(f32[16,256]{1,0:T(8,128)S(1)} %score_parts.3.refs_0_), channel_id=1, source_target_pairs={{0,2},{1,3},{2,0},{3,1},{4,6},{5,7},{6,4},{7,5},{8,10},{9,11},{10,... | collective-permute-start | bytes 49160 | tf_op jit(solution)/shard_map/ppermute | solution.py:125
  47.6 3.1 %collective-permute-start.18 = (f32[16,256]{1,0:T(8,128)S(1)}, f32[16,256]{1,0:T(8,128)S(1)}, u32[]{:S(2)}, u32[]{:S(2)}) collective-permute-start(f32[16,256]{1,0:T(8,128)S(1)} %score_parts.3.refs_0_), channel_id=1, source_target_pairs={{0,1},{1,0},{2,3},{3,2},{4,5},{5,4},{6,7},{7,6},{8,9},{9,8},{10,11... | collective-permute-start | bytes 49160 | tf_op jit(solution)/shard_map/ppermute | solution.py:125
  51.9 7.8 %collective-permute-start.24 = (bf16[16,2176]{1,0:T(8,128)(2,1)S(1)}, bf16[16,2176]{1,0:T(8,128)(2,1)S(1)}, u32[]{:S(2)}, u32[]{:S(2)}) collective-permute-start(bf16[16,2176]{1,0:T(8,128)(2,1)S(1)} %get-tuple-element.49), channel_id=1, source_target_pairs={{0,8},{4,12},{8,0},{12,4},{1,9},{5,13},{9,1},{13,5},{2,10},{6,14},... | collective-permute-start | bytes 208904 | tf_op jit(solution)/shard_map/ppermute | solution.py:53
  53.3 4.3 %collective-permute-start.22 = (bf16[16,2048]{1,0:T(8,128)(2,1)S(1)}, bf16[16,2048]{1,0:T(8,128)(2,1)S(1)}, u32[]{:S(2)}, u32[]{:S(2)}) collective-permute-start(bf16[16,2048]{1,0:T(8,128)(2,1)S(1)} %get-tuple-element.47), channel_id=1, source_target_pairs={{0,4},{4,0},{8,12},{12,8},{1,5},{5,1},{9,13},{13,9},{2,6},{6,2},{1... | collective-permute-start | bytes 196616 | tf_op jit(solution)/shard_map/ppermute | solution.py:53
  55.0 7.0 %collective-permute-start.25 = (bf16[16,2176]{1,0:T(8,128)(2,1)S(1)}, bf16[16,2176]{1,0:T(8,128)(2,1)S(1)}, u32[]{:S(2)}, u32[]{:S(2)}) collective-permute-start(bf16[16,2176]{1,0:T(8,128)(2,1)S(1)} %get-tuple-element.50), channel_id=1, source_target_pairs={{0,12},{4,8},{8,4},{12,0},{1,13},{5,9},{9,5},{13,1},{2,14},{6,10},... | collective-permute-start | bytes 208904 | tf_op jit(solution)/shard_map/ppermute | solution.py:53
  56.4 7.6 %collective-permute-start.21 = (bf16[16,4224]{1,0:T(8,128)(2,1)S(1)}, bf16[16,4224]{1,0:T(8,128)(2,1)S(1)}, u32[]{:S(2)}, u32[]{:S(2)}) collective-permute-start(bf16[16,4224]{1,0:T(8,128)(2,1)S(1)} %get-tuple-element.46), channel_id=1, source_target_pairs={{0,4},{4,0},{8,12},{12,8},{1,5},{5,1},{9,13},{13,9},{2,6},{6,2},{1... | collective-permute-start | bytes 405512 | tf_op jit(solution)/shard_map/ppermute | solution.py:53
  57.7 5.5 %collective-permute-start.23 = (bf16[16,2048]{1,0:T(8,128)(2,1)S(1)}, bf16[16,2048]{1,0:T(8,128)(2,1)S(1)}, u32[]{:S(2)}, u32[]{:S(2)}) collective-permute-start(bf16[16,2048]{1,0:T(8,128)(2,1)S(1)} %relay.3), channel_id=1, source_target_pairs={{0,8},{4,12},{8,0},{12,4},{1,9},{5,13},{9,1},{13,5},{2,10},{6,14},... | collective-permute-start | bytes 196616 | tf_op jit(solution)/shard_map/ppermute | solution.py:53

commit v6 on v5

--- a/solution.py
+++ b/solution.py
@@ -10,8 +10,6 @@
 
 PIX = 65536
 ITERS = 2
-GATHER_ORDER = (0, 1, 2, 3, 4, 5)
-SCATTER_ORDER = (0, 1, 2, 3, 4)
 TAIL = 128
 VMEM_BYTES = 12 * 1024 * 1024
 IN_VMEM = pl.BlockSpec(memory_space=pltpu.VMEM)
@@ -90,7 +88,7 @@
         out_shape=[jax.ShapeDtypeStruct((owned, size), jnp.bfloat16) for size in (pix, pix // 2, pix // 2)],
         scratch_shapes=[pltpu.VMEM((owned, pix), slices.dtype), pltpu.SemaphoreType.DMA((4,))],
         compiler_params=params(),
-        cost_estimate=pl.CostEstimate(flops=0, bytes_accessed=8 * slices.size, transcendentals=0),
+        cost_estimate=pl.CostEstimate(flops=5 * 10**9, bytes_accessed=8 * slices.size, transcendentals=0),
         name="round_slices",
     )(pltpu.with_memory_space_constraint(slices, pltpu.HBM))
 
@@ -101,7 +99,8 @@
         out_ref[:, piece] = (came + own_ref[:, piece].astype(jnp.float32)).astype(jnp.bfloat16)
 
 
-def scatter_line(own, near, relayed_2, direct_2, relayed_3, direct_3):
+def scatter_line(own, *others):
+    *near, relayed_2, direct_2, relayed_3, direct_3 = others
     came = swap(relayed_3, 1)
     joined = pl.pallas_call(
         relay_kernel,
@@ -115,7 +114,11 @@
     joined = swap(joined, 2)
     direct_3 = early(swap(direct_3, 3), 10**9)
     direct_2 = early(swap(direct_2, 2), 10**9)
-    near = swap(near, 1)
+    if len(near) > 1:
+        direct_2, near_0 = lax.optimization_barrier((direct_2, near[0]))
+        near = [swap(near_0, 1), swap(near[1], 1)]
+    else:
+        near = [swap(near[0], 1)]
     return [own, near, joined, direct_2, direct_3]
 
 
@@ -125,62 +128,52 @@
     return [part] + [lax.ppermute(part, axes, [(i, i ^ k) for i in range(size)]) for k in range(1, size)]
 
 
-def load_kernel(
-    dense, frames_ref, orient_in_ref, log_prior_in_ref, here_ref, turned_ref, prior_ref, orient_ref, log_prior_ref, sems
-):
-    pieces = chunks(frames_ref.shape[1], 2048)
+def load_kernel(dense, here_ref, orient_in_ref, log_prior_in_ref, turned_ref, prior_ref, orient_ref, log_prior_ref, sems):
     tables = [
-        pltpu.make_async_copy(orient_in_ref, orient_ref, sems.at[len(pieces)]),
-        pltpu.make_async_copy(log_prior_in_ref, log_prior_ref, sems.at[len(pieces) + 1]),
+        pltpu.make_async_copy(orient_in_ref, orient_ref, sems.at[0]),
+        pltpu.make_async_copy(log_prior_in_ref, log_prior_ref, sems.at[1]),
     ]
     for copy in tables:
         copy.start()
-    copies = [
-        pltpu.make_async_copy(frames_ref.at[:, piece], here_ref.at[:, piece], sems.at[i])
-        for i, piece in enumerate(pieces)
-    ]
-    for copy in copies:
-        copy.start()
-    for i, (copy, piece) in enumerate(zip(copies, pieces)):
-        copy.wait()
+    for piece in chunks(here_ref.shape[1], 512):
         turned_ref[piece, :] = here_ref[:, piece].T
-        if i == len(pieces) // 2:
-            for table in tables:
-                table.wait()
-            many, columns = prior_ref.shape
-            place = lax.axis_index("frame")
-            for row in range(many):
-                spot = 4 * (place ^ (row // 4)) + row % 4 if dense else row
-                prior_ref[row : row + 1, :] = jnp.full((1, columns), log_prior_ref[orient_ref[spot]], jnp.float32)
+    for table in tables:
+        table.wait()
+    many, columns = prior_ref.shape
+    place = lax.axis_index("frame")
+    for row in range(many):
+        spot = 4 * (place ^ (row // 4)) + row % 4 if dense else row
+        prior_ref[row : row + 1, :] = jnp.full((1, columns), log_prior_ref[orient_ref[spot]], jnp.float32)
 
 
 def load_frames(frames, orient, log_prior, dense):
     rows, pix = frames.shape
-    return pl.pallas_call(
+    here = pltpu.with_memory_space_constraint(frames, pltpu.VMEM)
+    turned, prior = pl.pallas_call(
         functools.partial(load_kernel, dense),
-        in_specs=[pl.BlockSpec(memory_space=pl.ANY)] * 3,
-        out_specs=[IN_VMEM] * 3,
+        in_specs=[IN_VMEM] + [pl.BlockSpec(memory_space=pl.ANY)] * 2,
+        out_specs=[IN_VMEM] * 2,
         out_shape=[
-            pltpu.VMEM((rows, pix), frames.dtype),
             pltpu.VMEM((pix, rows), frames.dtype),
             jax.ShapeDtypeStruct((orient.shape[0], rows), jnp.float32),
         ],
         scratch_shapes=[
             pltpu.SMEM(orient.shape, orient.dtype),
             pltpu.SMEM(log_prior.shape, log_prior.dtype),
-            pltpu.SemaphoreType.DMA((len(chunks(pix, 2048)) + 2,)),
+            pltpu.SemaphoreType.DMA((2,)),
         ],
         compiler_params=params(),
         cost_estimate=pl.CostEstimate(flops=0, bytes_accessed=6 * rows * pix, transcendentals=0),
         name="load_frames",
-    )(*(pltpu.with_memory_space_constraint(x, pltpu.HBM) for x in (frames, orient, log_prior)))
-
-
-def score_kernel(pieces, order, *refs):
+    )(here, *(pltpu.with_memory_space_constraint(x, pltpu.HBM) for x in (orient, log_prior)))
+    return frames, turned, prior
+
+
+def score_kernel(pieces, *refs):
     turned_ref, out_ref = refs[-2:]
     raw, squares = [], []
     for first, size, rows in pieces:
-        model = jnp.concatenate([refs[order.index(ref)][:, pl.ds(column, size)] for ref, column in rows], axis=0)
+        model = jnp.concatenate([refs[ref][:, pl.ds(column, size)] for ref, column in rows], axis=0)
         raw.append(jnp.dot(model, turned_ref[pl.ds(first, size), :], preferred_element_type=jnp.float32))
         wide = model.astype(jnp.float32)
         squares.append(tree_sum([jnp.square(wide[:, at : at + 128]) for at in range(0, wide.shape[1], 128)]))
@@ -191,16 +184,15 @@
 
 def score_parts(blocks, pieces, many, turned):
     pix, rows = turned.shape
-    order = GATHER_ORDER if len(blocks) > 1 else (0,)
     return pl.pallas_call(
-        functools.partial(score_kernel, pieces, order),
+        functools.partial(score_kernel, pieces),
         in_specs=[IN_VMEM] * (len(blocks) + 1),
         out_specs=IN_VMEM,
         out_shape=jax.ShapeDtypeStruct((many, rows), jnp.float32),
         compiler_params=params(),
         cost_estimate=pl.CostEstimate(flops=2 * rows * pix * many, bytes_accessed=2 * rows * pix, transcendentals=0),
         name="score_parts",
-    )(*[blocks[i] for i in order], pltpu.with_memory_space_constraint(turned, pltpu.VMEM))
+    )(*blocks, pltpu.with_memory_space_constraint(turned, pltpu.VMEM))
 
 
 def gathered_pieces(pix, relayed):
@@ -244,7 +236,9 @@
     weights, tail = weigh(parts, prior_ref)
     quarter = frames_ref.shape[1] // 4
     half = quarter // 2
-    for k, out_ref in enumerate([outs[0], outs[1], outs[3], outs[5]]):
+    own_ref, *near_refs = outs[:-4]
+    two_refs, three_refs = outs[-4:-2], outs[-2:]
+    for k, out_ref in enumerate([own_ref, near_refs[-1], two_refs[1], three_refs[1]]):
         rows = jnp.concatenate([tail[4 * k : 4 * k + 4]] * 4, axis=0)
         out_ref[:, out_ref.shape[1] - TAIL :] = rows.astype(jnp.bfloat16)
     turned = [rotate_rows(weights, (-4 * q) % 16).astype(jnp.bfloat16) for q in range(4)]
@@ -260,20 +254,22 @@
             ]
             upper = lax.broadcasted_iota(jnp.int32, (8, piece.size), 0) < 4
             whole = pl.ds(part * half + piece.start, piece.size)
-            spots = [(outs[0], whole), (outs[1], whole), (outs[2 + part], piece), (outs[4 + part], piece)]
+            near = (near_refs[part], piece) if len(near_refs) > 1 else (near_refs[0], whole)
+            spots = [(own_ref, whole), near, (two_refs[part], piece), (three_refs[part], piece)]
             for k, (out_ref, spot) in enumerate(spots):
                 first = jnp.where(upper, totals[-k % 4][:8], totals[(1 - k) % 4][:8])
                 second = jnp.where(upper, totals[(2 - k) % 4][8:], totals[(3 - k) % 4][8:])
                 out_ref[:, spot] = jnp.concatenate([first, second], axis=0).astype(jnp.bfloat16)
 
 
-def block_totals(parts, prior, frames, dense):
+def block_totals(parts, prior, frames, dense, near_halves):
     rows, pix = frames.shape
     many = prior.shape[0]
     if dense:
         half = pix // 8
         kernel = dense_totals_kernel
-        shapes = [(16, 2 * half + TAIL)] * 2 + [(16, half), (16, half + TAIL)] * 2
+        whole, halves = [(16, 2 * half + TAIL)], [(16, half), (16, half + TAIL)]
+        shapes = whole + (halves if near_halves else whole) + 2 * halves
     else:
         kernel, shapes = plain_totals_kernel, [(many, pix + TAIL)]
     return pl.pallas_call(
@@ -299,7 +295,7 @@
 
 
 def dense_update_kernel(parts, *refs):
-    own_ref, near_ref, joined_ref, direct_2_ref, direct_3_ref, owned_ref = refs[:6]
+    own_ref, near_refs, joined_ref, direct_2_ref, direct_3_ref, owned_ref = refs[:6]
     out_ref, half_refs = refs[-1], refs[-2:-1]
     if len(refs) < 8:
         half_refs = []
@@ -311,13 +307,19 @@
 
     behind, behind_half = pl.ds(quarter, TAIL), pl.ds(half, TAIL)
     tail = total(
-        [(0, own_ref, behind), (1, near_ref, behind), (2, direct_2_ref, behind_half), (3, direct_3_ref, behind_half)]
+        [
+            (0, own_ref, behind),
+            (1, near_refs[-1], behind_half if len(near_refs) > 1 else behind),
+            (2, direct_2_ref, behind_half),
+            (3, direct_3_ref, behind_half),
+        ]
     )
     scale = tail[:, :1] + tail[:, TAIL // 2 : TAIL // 2 + 1] + 1.0
     for part in parts:
         for piece in chunks(half, 512):
             whole = pl.ds(part * half + piece.start, piece.size)
-            terms = [(0, own_ref, whole), (1, near_ref, whole)]
+            terms = [(0, own_ref, whole)]
+            terms += [(1, near_refs[part], piece) if len(near_refs) > 1 else (1, near_refs[0], whole)]
             terms += [(2, direct_2_ref, piece), (3, direct_3_ref, piece)] if part else [(2, joined_ref, piece)]
             spots = [pl.ds(q * quarter + whole.start, whole.size) for q in range(4)]
             owned = jnp.concatenate([owned_ref[:, spot].astype(jnp.float32) for spot in spots], axis=0)
@@ -328,6 +330,10 @@
                     half_ref[:, pl.ds(q * half + piece.start, piece.size)] = new[4 * q : 4 * q + 4]
 
 
+def last_update_kernel(own_ref, near_ref, *refs):
+    dense_update_kernel((0, 1), own_ref, (near_ref,), *refs)
+
+
 def update_call(kernel, operands, shapes, aliases={}):
     size = operands[0].size
     return pl.pallas_call(
@@ -347,14 +353,16 @@
     many, pix = owned.shape
     half, whole = (jax.ShapeDtypeStruct((many, size), jnp.bfloat16) for size in (pix // 2, pix))
 
-    def second(own_ref, near_ref, direct_2_ref, direct_3_ref, owned_ref, *outs):
-        dense_update_kernel((1,), own_ref, near_ref, None, direct_2_ref, direct_3_ref, owned_ref, *outs)
-
-    def first(own_ref, near_ref, joined_ref, direct_2_ref, direct_3_ref, owned_ref, _, *outs):
-        dense_update_kernel((0,), own_ref, near_ref, joined_ref, direct_2_ref, direct_3_ref, owned_ref, *outs)
-
-    part_1, begun = update_call(second, (own, near, direct_2, direct_3, owned), [half, whole])
-    part_0, done = update_call(first, (*terms, owned, begun), [half, whole], {6: 1})
+    def second(own_ref, near_1_ref, direct_2_ref, direct_3_ref, owned_ref, *outs):
+        dense_update_kernel((1,), own_ref, (None, near_1_ref), None, direct_2_ref, direct_3_ref, owned_ref, *outs)
+
+    def first(own_ref, near_0_ref, near_1_ref, joined_ref, direct_2_ref, direct_3_ref, owned_ref, _, *outs):
+        near_refs = (near_0_ref, near_1_ref)
+        dense_update_kernel((0,), own_ref, near_refs, joined_ref, direct_2_ref, direct_3_ref, owned_ref, *outs)
+
+    part_1, begun = update_call(second, (own, near[1], direct_2, direct_3, owned), [half, whole])
+    operands = (own, *near, joined, direct_2, direct_3, owned, begun)
+    part_0, done = update_call(first, operands, [half, whole], {7: 1})
     return [done, part_1, part_0]
 
 
@@ -379,7 +387,7 @@
         parts = exchange_all(
             score_parts(blocks, pieces, along * owned, turned), ("panel", "sub"), across
         )
-        totals = block_totals(parts, prior, here, dense)
+        totals = block_totals(parts, prior, here, dense, not last)
         if dense:
             terms = scatter_line(*totals)
         else:
@@ -388,7 +396,9 @@
         if dense and not last:
             owned_b = update_in_parts(terms, owned_b[0])
         else:
-            kernel = functools.partial(dense_update_kernel, (0, 1)) if dense else plain_update_kernel
+            kernel = last_update_kernel if dense else plain_update_kernel
+            if dense:
+                terms[1:2] = terms[1]
             shape = jax.ShapeDtypeStruct(slices.shape, jnp.float32 if last else jnp.bfloat16)
             owned_b = update_call(kernel, (*terms, owned_b[0]), [shape])
     return owned_b[0]

time: 65 us -> 64.2 us (0.988)
  starting transfers between devices: 33.3 us -> 35.2 us
  Pallas kernels: 11.1 us -> 9.51 us
  waiting for transfers between devices: 20.4 us -> 19.3 us
    ppermute x20 -> x21, starting transfers between devices: 29.6 us -> 31.4 us  [swap(): return lax.ppermute(value, 'frame', [(i, i ^ distance) for i in range(4)])]
    pallas_call x3, Pallas kernels: 6.36 us -> 4.66 us  [the longest x2 2.38 us: score_parts(): pl.pallas_call(functools.partial(score_kernel, pieces), in_specs=[IN_VMEM...]
    ppermute x20 -> x21, waiting for transfers between devices: 16.3 us -> 14.9 us  [swap(): return lax.ppermute(value, 'frame', [(i, i ^ distance) for i in range(4)])]
  transfers between devices with their start and end apart: 26 -> 27, of which waited for: 14 -> 16; matrix products, arithmetic and copies ran while one was open for 0% -> 0% of each run, Pallas kernels for 7% -> 4%
where the time goes in v6:
time: 64.2 us; the launch traced here: 64.1 us
  starting transfers between devices  35.2 us (55%)
  waiting for transfers between devices  19.3 us (30%)
  Pallas kernels  9.51 us (15%)
    ppermute x21, starting transfers between devices, swap(): return lax.ppermute(value, 'frame', [(i, i ^ distance) for i in range(4)])  31.4 us
    ppermute x21, waiting for transfers between devices, swap(): return lax.ppermute(value, 'frame', [(i, i ^ distance) for i in range(4)])  14.9 us
    ppermute x6, waiting for transfers between devices, exchange_all(): lax.ppermute(part, axes, [(i, i ^ k) for i in range(size)])  4.43 us
    ppermute x6, starting transfers between devices, exchange_all(): lax.ppermute(part, axes, [(i, i ^ k) for i in range(size)])  3.79 us
    pallas_call x2, Pallas kernels, block_totals(): pl.pallas_call(functools.partial(kernel, len(parts)), in_specs=[IN_VMEM]...  2.41 us
    pallas_call x2, Pallas kernels, score_parts(): pl.pallas_call(functools.partial(score_kernel, pieces), in_specs=[IN_VMEM...  2.38 us
    pallas_call x1, Pallas kernels, load_frames(): pl.pallas_call(functools.partial(load_kernel, dense), in_specs=[IN_VMEM]...  2.28 us
  transfers between devices with their start and end apart: 27, of which 16 were waited for; matrix products, arithmetic and copies ran while one was open for 0% of the time, Pallas kernels for 4%

profile of v6, /device:TPU:0, one launch (start us, length us, event | category | flops | bytes accessed | tf_op | source)
XLA Modules:
  0.0 64.1 jit_solution(7551406699098752525)
XLA Ops:
  0.0 1.1 %round_slices.1 = (bf16[4,16384]{1,0:T(4,128)(2,1)S(1)}, bf16[4,8192]{1,0:T(4,128)(2,1)S(1)}, bf16[4,8192]{1,0:T(4,128)(2,1)S(1)}) custom-call(f32[4,16384]{1,0:T(4,128)} %slices_ref.1), custom_call_target="tpu_custom_call" | custom-call | flops 5000000000 | bytes 524288 | tf_op jit(solution)/shard_map/round_slices/pallas_call | solution.py:84
  1.1 4.1 %collective-permute-start.1 = (bf16[4,8192]{1,0:T(4,128)(2,1)S(1)}, bf16[4,8192]{1,0:T(4,128)(2,1)S(1)}, u32[]{:S(2)}, u32[]{:S(2)}) collective-permute-start(bf16[4,8192]{1,0:T(4,128)(2,1)S(1)} %get-tuple-element.31), channel_id=1, source_target_pairs={{0,8},{4,12},{8,0},{12,4},{1,9},{5,13},{9,1},{13,5},{2,10},{6,14},... | collective-permute-start | bytes 196616 | tf_op jit(solution)/shard_map/ppermute | solution.py:51
  5.2 1.6 %collective-permute-start = (bf16[4,16384]{1,0:T(4,128)(2,1)S(1)}, bf16[4,16384]{1,0:T(4,128)(2,1)S(1)}, u32[]{:S(2)}, u32[]{:S(2)}) collective-permute-start(bf16[4,16384]{1,0:T(4,128)(2,1)S(1)} %get-tuple-element.30.refs_0_.owned_ref), channel_id=1, source_target_pairs={{0,4},{4,0},{8,12},{12,8},{1,5},{5,1},{9,13},{13,9},{2,6},{6,2},{1... | collective-permute-start | bytes 393224 | tf_op jit(solution)/shard_map/ppermute | solution.py:51
  6.8 0.0 collective-permute-start.4
  6.8 1.9 %collective-permute-start.2 = (bf16[4,8192]{1,0:T(4,128)(2,1)S(1)}, bf16[4,8192]{1,0:T(4,128)(2,1)S(1)}, u32[]{:S(2)}, u32[]{:S(2)}) collective-permute-start(bf16[4,8192]{1,0:T(4,128)(2,1)S(1)} %get-tuple-element.32), channel_id=1, source_target_pairs={{0,8},{4,12},{8,0},{12,4},{1,9},{5,13},{9,1},{13,5},{2,10},{6,14},... | collective-permute-start | bytes 196616 | tf_op jit(solution)/shard_map/ppermute | solution.py:51
  8.7 0.0 collective-permute-done.1.refs_2_
  8.7 2.5 %collective-permute-start.3 = (bf16[4,8192]{1,0:T(4,128)(2,1)S(1)}, bf16[4,8192]{1,0:T(4,128)(2,1)S(1)}, u32[]{:S(2)}, u32[]{:S(2)}) collective-permute-start(bf16[4,8192]{1,0:T(4,128)(2,1)S(1)} %collective-permute-done.1.refs_2_), channel_id=1, source_target_pairs={{0,4},{4,0},{8,12},{12,8},{1,5},{5,1},{9,13},{13,9},{2,6},{6,2},{1... | collective-permute-start | bytes 196616 | tf_op jit(solution)/shard_map/ppermute | solution.py:51
  11.2 0.0 copy-done
  11.2 2.3 %load_frames.1 = (bf16[16384,256]{1,0:T(8,128)(2,1)S(1)}, f32[16,256]{1,0:T(8,128)S(1)}) custom-call(bf16[256,16384]{1,0:T(8,128)(2,1)S(1)} %copy-done, s32[16]{0:T(128)} %orient_in_ref.1, f32[4096]{0:T(1024)} %log_prior_in_ref.1), custom_call_target="tpu_custom_call" | custom-call | bytes 25165824 | tf_op jit(solution)/shard_map/load_frames/pallas_call | solution.py:152
  13.5 0.2 collective-permute-done.4.refs_5_
  13.7 0.5 collective-permute-done.2.refs_3_
  14.3 0.5 collective-permute-done.3.refs_4_
  14.8 0.0 collective-permute-done.refs_1_
  14.8 1.2 %score_parts.2.refs_0_ = f32[16,256]{1,0:T(8,128)S(1)} custom-call(bf16[4,16384]{1,0:T(4,128)(2,1)S(1)} %get-tuple-element.30.refs_0_.owned_ref, bf16[4,16384]{1,0:T(4,128)(2,1)S(1)} %collective-permute-done.refs_1_, bf16[4,8192]{1,0:T(4,128)(2,1)S(1)} %collective-permute-done.1.refs_2_, bf16[4,8192]{1,0:T(4,128)(2,1)S(1)} %collective-permute-done.2.refs_3_, ...), custom_call_target="tpu_custom_call" | custom-call | flops 134217728 | bytes 8388608 | tf_op jit(solution)/shard_map/score_parts/pallas_call | solution.py:187
  16.0 0.7 %collective-permute-start.7 = (f32[16,256]{1,0:T(8,128)S(1)}, f32[16,256]{1,0:T(8,128)S(1)}, u32[]{:S(2)}, u32[]{:S(2)}) collective-permute-start(f32[16,256]{1,0:T(8,128)S(1)} %score_parts.2.refs_0_), channel_id=1, source_target_pairs={{0,3},{1,2},{2,1},{3,0},{4,7},{5,6},{6,5},{7,4},{8,11},{9,10},{10,... | collective-permute-start | bytes 49160 | tf_op jit(solution)/shard_map/ppermute | solution.py:128
  16.7 1.2 %collective-permute-start.6 = (f32[16,256]{1,0:T(8,128)S(1)}, f32[16,256]{1,0:T(8,128)S(1)}, u32[]{:S(2)}, u32[]{:S(2)}) collective-permute-start(f32[16,256]{1,0:T(8,128)S(1)} %score_parts.2.refs_0_), channel_id=1, source_target_pairs={{0,2},{1,3},{2,0},{3,1},{4,6},{5,7},{6,4},{7,5},{8,10},{9,11},{10,... | collective-permute-start | bytes 49160 | tf_op jit(solution)/shard_map/ppermute | solution.py:128
  17.8 0.1 collective-permute-start.5
  17.9 1.3 %collective-permute-done.7.refs_3_ = f32[16,256]{1,0:T(8,128)S(1)} collective-permute-done((f32[16,256]{1,0:T(8,128)S(1)}, f32[16,256]{1,0:T(8,128)S(1)}, u32[]{:S(2)}, u32[]{:S(2)}) %collective-permute-start.7) | collective-permute-done | bytes 16416 | tf_op jit(solution)/shard_map/ppermute | solution.py:128
  19.2 1.2 %collective-permute-done.6.refs_2_ = f32[16,256]{1,0:T(8,128)S(1)} collective-permute-done((f32[16,256]{1,0:T(8,128)S(1)}, f32[16,256]{1,0:T(8,128)S(1)}, u32[]{:S(2)}, u32[]{:S(2)}) %collective-permute-start.6) | collective-permute-done | bytes 16416 | tf_op jit(solution)/shard_map/ppermute | solution.py:128
  20.4 0.0 collective-permute-done.5.refs_1_
  20.4 1.2 %block_totals.2 = (bf16[16,4224]{1,0:T(8,128)(2,1)S(1)}, bf16[16,2048]{1,0:T(8,128)(2,1)S(1)}, bf16[16,2176]{1,0:T(8,128)(2,1)S(1)}, bf16[16,2048]{1,0:T(8,128)(...) custom-call(f32[16,256]{1,0:T(8,128)S(1)} %score_parts.2.refs_0_, ...), custom_call_target="tpu_custom_call" | custom-call | flops 134217728 | bytes 8388608 | tf_op jit(solution)/shard_map/block_totals/pallas_call | solution.py:275
  21.6 1.4 %collective-permute-start.8 = (bf16[16,2176]{1,0:T(8,128)(2,1)S(1)}, bf16[16,2176]{1,0:T(8,128)(2,1)S(1)}, u32[]{:S(2)}, u32[]{:S(2)}) collective-permute-start(bf16[16,2176]{1,0:T(8,128)(2,1)S(1)} %get-tuple-element.37), channel_id=1, source_target_pairs={{0,8},{4,12},{8,0},{12,4},{1,9},{5,13},{9,1},{13,5},{2,10},{6,14},... | collective-permute-start | bytes 208904 | tf_op jit(solution)/shard_map/ppermute | solution.py:51
  23.0 1.8 %collective-permute-start.11 = (bf16[16,2048]{1,0:T(8,128)(2,1)S(1)}, bf16[16,2048]{1,0:T(8,128)(2,1)S(1)}, u32[]{:S(2)}, u32[]{:S(2)}) collective-permute-start(bf16[16,2048]{1,0:T(8,128)(2,1)S(1)} %get-tuple-element.41), channel_id=1, source_target_pairs={{0,4},{4,0},{8,12},{12,8},{1,5},{5,1},{9,13},{13,9},{2,6},{6,2},{1... | collective-permute-start | bytes 196616 | tf_op jit(solution)/shard_map/ppermute | solution.py:51
  24.8 0.3 collective-permute-start.10
  25.0 2.2 %collective-permute-start.13 = (bf16[16,2176]{1,0:T(8,128)(2,1)S(1)}, bf16[16,2176]{1,0:T(8,128)(2,1)S(1)}, u32[]{:S(2)}, u32[]{:S(2)}) collective-permute-start(bf16[16,2176]{1,0:T(8,128)(2,1)S(1)} %get-tuple-element.44), channel_id=1, source_target_pairs={{0,12},{4,8},{8,4},{12,0},{1,13},{5,9},{9,5},{13,1},{2,14},{6,10},... | collective-permute-start | bytes 208904 | tf_op jit(solution)/shard_map/ppermute | solution.py:51
  27.2 1.4 %collective-permute-done.11.came_ref = bf16[16,2048]{1,0:T(8,128)(2,1)S(1)} collective-permute-done((bf16[16,2048]{1,0:T(8,128)(2,1)S(1)}, bf16[16,2048]{1,0:T(8,128)(2,1)S(1)}, u32[]{:S(2)}, u32[]{:S(2)}) %collective-permute-start.11) | collective-permute-done | bytes 65568 | tf_op jit(solution)/shard_map/ppermute | solution.py:51
  28.6 1.6 %collective-permute-start.12 = (bf16[16,2048]{1,0:T(8,128)(2,1)S(1)}, bf16[16,2048]{1,0:T(8,128)(2,1)S(1)}, u32[]{:S(2)}, u32[]{:S(2)}) collective-permute-start(bf16[16,2048]{1,0:T(8,128)(2,1)S(1)} %relay.2), channel_id=1, source_target_pairs={{0,8},{4,12},{8,0},{12,4},{1,9},{5,13},{9,1},{13,5},{2,10},{6,14},... | collective-permute-start | bytes 196616 | tf_op jit(solution)/shard_map/ppermute | solution.py:51
  30.2 0.0 collective-permute-done.8.in_ref
  30.2 2.1 %collective-permute-start.9 = (bf16[16,2048]{1,0:T(8,128)(2,1)S(1)}, bf16[16,2048]{1,0:T(8,128)(2,1)S(1)}, u32[]{:S(2)}, u32[]{:S(2)}) collective-permute-start(bf16[16,2048]{1,0:T(8,128)(2,1)S(1)} %get-tuple-element.39), channel_id=1, source_target_pairs={{0,4},{4,0},{8,12},{12,8},{1,5},{5,1},{9,13},{13,9},{2,6},{6,2},{1... | collective-permute-start | bytes 196616 | tf_op jit(solution)/shard_map/ppermute | solution.py:51
  32.3 0.4 collective-permute-done.13.in_ref
  32.7 0.0 collective-permute-done.10.near_1_ref
  32.7 0.2 update.3
  32.8 1.3 %collective-permute-start.15 = (bf16[4,8192]{1,0:T(4,128)(2,1)S(1)}, bf16[4,8192]{1,0:T(4,128)(2,1)S(1)}, u32[]{:S(2)}, u32[]{:S(2)}) collective-permute-start(bf16[4,8192]{1,0:T(4,128)(2,1)S(1)} %get-tuple-element.47), channel_id=1, source_target_pairs={{0,8},{4,12},{8,0},{12,4},{1,9},{5,13},{9,1},{13,5},{2,10},{6,14},... | collective-permute-start | bytes 196616 | tf_op jit(solution)/shard_map/ppermute | solution.py:51
  34.2 1.4 %collective-permute-done.12.joined_ref = bf16[16,2048]{1,0:T(8,128)(2,1)S(1)} collective-permute-done((bf16[16,2048]{1,0:T(8,128)(2,1)S(1)}, bf16[16,2048]{1,0:T(8,128)(2,1)S(1)}, u32[]{:S(2)}, u32[]{:S(2)}) %collective-permute-start.12) | collective-permute-done | bytes 65568 | tf_op jit(solution)/shard_map/ppermute | solution.py:51
  35.6 0.0 collective-permute-done.9.near_0_ref
  35.6 0.2 update.4
  35.8 1.1 %collective-permute-start.14 = (bf16[4,16384]{1,0:T(4,128)(2,1)S(1)}, bf16[4,16384]{1,0:T(4,128)(2,1)S(1)}, u32[]{:S(2)}, u32[]{:S(2)}) collective-permute-start(bf16[4,16384]{1,0:T(4,128)(2,1)S(1)} %get-tuple-element.46.refs_0_.refs_3_), channel_id=1, source_target_pairs={{0,4},{4,0},{8,12},{12,8},{1,5},{5,1},{9,13},{13,9},{2,6},{6,2},{1... | collective-permute-start | bytes 393224 | tf_op jit(solution)/shard_map/ppermute | solution.py:51
  36.8 1.7 %collective-permute-start.18 = (bf16[4,8192]{1,0:T(4,128)(2,1)S(1)}, bf16[4,8192]{1,0:T(4,128)(2,1)S(1)}, u32[]{:S(2)}, u32[]{:S(2)}) collective-permute-start(bf16[4,8192]{1,0:T(4,128)(2,1)S(1)} %get-tuple-element.48), channel_id=1, source_target_pairs={{0,12},{4,8},{8,4},{12,0},{1,13},{5,9},{9,5},{13,1},{2,14},{6,10},... | collective-permute-start | bytes 196616 | tf_op jit(solution)/shard_map/ppermute | solution.py:51
  38.6 0.7 %collective-permute-start.16 = (bf16[4,8192]{1,0:T(4,128)(2,1)S(1)}, bf16[4,8192]{1,0:T(4,128)(2,1)S(1)}, u32[]{:S(2)}, u32[]{:S(2)}) collective-permute-start(bf16[4,8192]{1,0:T(4,128)(2,1)S(1)} %get-tuple-element.48), channel_id=1, source_target_pairs={{0,8},{4,12},{8,0},{12,4},{1,9},{5,13},{9,1},{13,5},{2,10},{6,14},... | collective-permute-start | bytes 196616 | tf_op jit(solution)/shard_map/ppermute | solution.py:51
  39.3 0.0 collective-permute-done.15.refs_2_
  39.3 1.9 %collective-permute-start.17 = (bf16[4,8192]{1,0:T(4,128)(2,1)S(1)}, bf16[4,8192]{1,0:T(4,128)(2,1)S(1)}, u32[]{:S(2)}, u32[]{:S(2)}) collective-permute-start(bf16[4,8192]{1,0:T(4,128)(2,1)S(1)} %collective-permute-done.15.refs_2_), channel_id=1, source_target_pairs={{0,4},{4,0},{8,12},{12,8},{1,5},{5,1},{9,13},{13,9},{2,6},{6,2},{1... | collective-permute-start | bytes 196616 | tf_op jit(solution)/shard_map/ppermute | solution.py:51
  41.2 1.8 %collective-permute-done.18.refs_5_ = bf16[4,8192]{1,0:T(4,128)(2,1)S(1)} collective-permute-done((bf16[4,8192]{1,0:T(4,128)(2,1)S(1)}, bf16[4,8192]{1,0:T(4,128)(2,1)S(1)}, u32[]{:S(2)}, u32[]{:S(2)}) %collective-permute-start.18) | collective-permute-done | bytes 65568 | tf_op jit(solution)/shard_map/ppermute | solution.py:51
  43.0 1.4 %collective-permute-done.16.refs_3_ = bf16[4,8192]{1,0:T(4,128)(2,1)S(1)} collective-permute-done((bf16[4,8192]{1,0:T(4,128)(2,1)S(1)}, bf16[4,8192]{1,0:T(4,128)(2,1)S(1)}, u32[]{:S(2)}, u32[]{:S(2)}) %collective-permute-start.16) | collective-permute-done | bytes 65568 | tf_op jit(solution)/shard_map/ppermute | solution.py:51
  44.4 0.0 collective-permute-done.17.refs_4_
  44.4 0.0 collective-permute-done.14.refs_1_
  44.4 1.2 %score_parts.3.refs_0_ = f32[16,256]{1,0:T(8,128)S(1)} custom-call(bf16[4,16384]{1,0:T(4,128)(2,1)S(1)} %get-tuple-element.46.refs_0_.refs_3_, bf16[4,16384]{1,0:T(4,128)(2,1)S(1)} %collective-permute-done.14.refs_1_, bf16[4,8192]{1,0:T(4,128)(2,1)S(1)} %collective-permute-done.15.refs_2_, bf16[4,8192]{1,0:T(4,128)(2,1)S(1)} %collective-permute-done.16.refs_3_, ...), custom_call_target="tpu_custom_call" | custom-call | flops 134217728 | bytes 8388608 | tf_op jit(solution)/shard_map/score_parts/pallas_call | solution.py:187
  45.6 0.0 collective-permute-start.21
  45.6 1.2 %collective-permute-start.20 = (f32[16,256]{1,0:T(8,128)S(1)}, f32[16,256]{1,0:T(8,128)S(1)}, u32[]{:S(2)}, u32[]{:S(2)}) collective-permute-start(f32[16,256]{1,0:T(8,128)S(1)} %score_parts.3.refs_0_), channel_id=1, source_target_pairs={{0,2},{1,3},{2,0},{3,1},{4,6},{5,7},{6,4},{7,5},{8,10},{9,11},{10,... | collective-permute-start | bytes 49160 | tf_op jit(solution)/shard_map/ppermute | solution.py:128
  46.9 0.6 collective-permute-start.19
  47.5 1.3 %collective-permute-done.21.refs_3_ = f32[16,256]{1,0:T(8,128)S(1)} collective-permute-done((f32[16,256]{1,0:T(8,128)S(1)}, f32[16,256]{1,0:T(8,128)S(1)}, u32[]{:S(2)}, u32[]{:S(2)}) %collective-permute-start.21) | collective-permute-done | bytes 16416 | tf_op jit(solution)/shard_map/ppermute | solution.py:128
  48.8 0.6 collective-permute-done.20.refs_2_
  49.4 0.0 collective-permute-done.19.refs_1_
  49.4 1.2 %block_totals.3 = (bf16[16,4224]{1,0:T(8,128)(2,1)S(1)}, bf16[16,4224]{1,0:T(8,128)(2,1)S(1)}, bf16[16,2048]{1,0:T(8,128)(2,1)S(1)}, bf16[16,2176]{1,0:T(8,128)(...) custom-call(f32[16,256]{1,0:T(8,128)S(1)} %score_parts.3.refs_0_, ...), custom_call_target="tpu_custom_call" | custom-call | flops 134217728 | bytes 8388608 | tf_op jit(solution)/shard_map/block_totals/pallas_call | solution.py:275
  50.6 1.4 %collective-permute-start.25 = (bf16[16,2176]{1,0:T(8,128)(2,1)S(1)}, bf16[16,2176]{1,0:T(8,128)(2,1)S(1)}, u32[]{:S(2)}, u32[]{:S(2)}) collective-permute-start(bf16[16,2176]{1,0:T(8,128)(2,1)S(1)} %get-tuple-element.53), channel_id=1, source_target_pairs={{0,8},{4,12},{8,0},{12,4},{1,9},{5,13},{9,1},{13,5},{2,10},{6,14},... | collective-permute-start | bytes 208904 | tf_op jit(solution)/shard_map/ppermute | solution.py:51
  52.1 1.7 %collective-permute-start.23 = (bf16[16,2048]{1,0:T(8,128)(2,1)S(1)}, bf16[16,2048]{1,0:T(8,128)(2,1)S(1)}, u32[]{:S(2)}, u32[]{:S(2)}) collective-permute-start(bf16[16,2048]{1,0:T(8,128)(2,1)S(1)} %get-tuple-element.51), channel_id=1, source_target_pairs={{0,4},{4,0},{8,12},{12,8},{1,5},{5,1},{9,13},{13,9},{2,6},{6,2},{1... | collective-permute-start | bytes 196616 | tf_op jit(solution)/shard_map/ppermute | solution.py:51
  53.7 1.4 %collective-permute-start.26 = (bf16[16,2176]{1,0:T(8,128)(2,1)S(1)}, bf16[16,2176]{1,0:T(8,128)(2,1)S(1)}, u32[]{:S(2)}, u32[]{:S(2)}) collective-permute-start(bf16[16,2176]{1,0:T(8,128)(2,1)S(1)} %get-tuple-element.54), channel_id=1, source_target_pairs={{0,12},{4,8},{8,4},{12,0},{1,13},{5,9},{9,5},{13,1},{2,14},{6,10},... | collective-permute-start | bytes 208904 | tf_op jit(solution)/shard_map/ppermute | solution.py:51
  55.1 0.1 collective-permute-start.22
  55.2 2.3 %collective-permute-done.23.came_ref = bf16[16,2048]{1,0:T(8,128)(2,1)S(1)} collective-permute-done((bf16[16,2048]{1,0:T(8,128)(2,1)S(1)}, bf16[16,2048]{1,0:T(8,128)(2,1)S(1)}, u32[]{:S(2)}, u32[]{:S(2)}) %collective-permute-start.23) | collective-permute-done | bytes 65568 | tf_op jit(solution)/shard_map/ppermute | solution.py:51
  57.6 0.7 %collective-permute-start.24 = (bf16[16,2048]{1,0:T(8,128)(2,1)S(1)}, bf16[16,2048]{1,0:T(8,128)(2,1)S(1)}, u32[]{:S(2)}, u32[]{:S(2)}) collective-permute-start(bf16[16,2048]{1,0:T(8,128)(2,1)S(1)} %relay.3), channel_id=1, source_target_pairs={{0,8},{4,12},{8,0},{12,4},{1,9},{5,13},{9,1},{13,5},{2,10},{6,14},... | collective-permute-start | bytes 196616 | tf_op jit(solution)/shard_map/ppermute | solution.py:51
  58.3 0.0 collective-permute-done.25.in_ref
  58.3 2.4 %collective-permute-done.26.in_ref = bf16[16,2176]{1,0:T(8,128)(2,1)S(1)} collective-permute-done((bf16[16,2176]{1,0:T(8,128)(2,1)S(1)}, bf16[16,2176]{1,0:T(8,128)(2,1)S(1)}, u32[]{:S(2)}, u32[]{:S(2)}) %collective-permute-start.26) | collective-permute-done | bytes 69664 | tf_op jit(solution)/shard_map/ppermute | solution.py:51
  60.7 2.2 %collective-permute-done.24.refs_0_ = bf16[16,2048]{1,0:T(8,128)(2,1)S(1)} collective-permute-done((bf16[16,2048]{1,0:T(8,128)(2,1)S(1)}, bf16[16,2048]{1,0:T(8,128)(2,1)S(1)}, u32[]{:S(2)}, u32[]{:S(2)}) %collective-permute-start.24) | collective-permute-done | bytes 65568 | tf_op jit(solution)/shard_map/ppermute | solution.py:51
  62.9 0.2 collective-permute-done.22.near_ref
  63.2 0.9 %update.5 = f32[4,16384]{1,0:T(4,128)} custom-call(bf16[16,4224]{1,0:T(8,128)(2,1)S(1)} %get-tuple-element.49.own_ref, bf16[16,4224]{1,0:T(8,128)(2,1)S(1)} %collective-permute-done.22.near_ref, bf16[16,2048]{1,0:T(8,128)(2,1)S(1)} %collective-permute-done.24.refs_0_, bf16[16,2176]{1,0:T(8,128)(2,1)S(1)} %early.6.refs_1_, ...), custom_call_target="tpu_custom_call" | custom-call | flops 540672 | bytes 811008 | tf_op jit(solution)/shard_map/update/pallas_call | solution.py:339
  (7 shorter events, 0.1 us)
Async XLA Ops:
  0.0 11.2 %copy-start = (bf16[256,16384]{1,0:T(8,128)(2,1)S(1)}, bf16[256,16384]{1,0:T(8,128)(2,1)}, u32[]{:S(2)}) copy-start(bf16[256,16384]{1,0:T(8,128)(2,1)} %refs_5_.1) | copy-start | bytes 25165828
  1.1 7.6 %collective-permute-start.1 = (bf16[4,8192]{1,0:T(4,128)(2,1)S(1)}, bf16[4,8192]{1,0:T(4,128)(2,1)S(1)}, u32[]{:S(2)}, u32[]{:S(2)}) collective-permute-start(bf16[4,8192]{1,0:T(4,128)(2,1)S(1)} %get-tuple-element.31), channel_id=1, source_target_pairs={{0,8},{4,12},{8,0},{12,4},{1,9},{5,13},{9,1},{13,5},{2,10},{6,14},... | collective-permute-start | bytes 196616 | tf_op jit(solution)/shard_map/ppermute | solution.py:51
  5.2 9.6 %collective-permute-start = (bf16[4,16384]{1,0:T(4,128)(2,1)S(1)}, bf16[4,16384]{1,0:T(4,128)(2,1)S(1)}, u32[]{:S(2)}, u32[]{:S(2)}) collective-permute-start(bf16[4,16384]{1,0:T(4,128)(2,1)S(1)} %get-tuple-element.30.refs_0_.owned_ref), channel_id=1, source_target_pairs={{0,4},{4,0},{8,12},{12,8},{1,5},{5,1},{9,13},{13,9},{2,6},{6,2},{1... | collective-permute-start | bytes 393224 | tf_op jit(solution)/shard_map/ppermute | solution.py:51
  6.8 6.9 %collective-permute-start.4 = (bf16[4,8192]{1,0:T(4,128)(2,1)S(1)}, bf16[4,8192]{1,0:T(4,128)(2,1)S(1)}, u32[]{:S(2)}, u32[]{:S(2)}) collective-permute-start(bf16[4,8192]{1,0:T(4,128)(2,1)S(1)} %get-tuple-element.32), channel_id=1, source_target_pairs={{0,12},{4,8},{8,4},{12,0},{1,13},{5,9},{9,5},{13,1},{2,14},{6,10},... | collective-permute-start | bytes 196616 | tf_op jit(solution)/shard_map/ppermute | solution.py:51
  6.8 7.4 %collective-permute-start.2 = (bf16[4,8192]{1,0:T(4,128)(2,1)S(1)}, bf16[4,8192]{1,0:T(4,128)(2,1)S(1)}, u32[]{:S(2)}, u32[]{:S(2)}) collective-permute-start(bf16[4,8192]{1,0:T(4,128)(2,1)S(1)} %get-tuple-element.32), channel_id=1, source_target_pairs={{0,8},{4,12},{8,0},{12,4},{1,9},{5,13},{9,1},{13,5},{2,10},{6,14},... | collective-permute-start | bytes 196616 | tf_op jit(solution)/shard_map/ppermute | solution.py:51
  8.7 6.1 %collective-permute-start.3 = (bf16[4,8192]{1,0:T(4,128)(2,1)S(1)}, bf16[4,8192]{1,0:T(4,128)(2,1)S(1)}, u32[]{:S(2)}, u32[]{:S(2)}) collective-permute-start(bf16[4,8192]{1,0:T(4,128)(2,1)S(1)} %collective-permute-done.1.refs_2_), channel_id=1, source_target_pairs={{0,4},{4,0},{8,12},{12,8},{1,5},{5,1},{9,13},{13,9},{2,6},{6,2},{1... | collective-permute-start | bytes 196616 | tf_op jit(solution)/shard_map/ppermute | solution.py:51
  16.0 3.2 %collective-permute-start.7 = (f32[16,256]{1,0:T(8,128)S(1)}, f32[16,256]{1,0:T(8,128)S(1)}, u32[]{:S(2)}, u32[]{:S(2)}) collective-permute-start(f32[16,256]{1,0:T(8,128)S(1)} %score_parts.2.refs_0_), channel_id=1, source_target_pairs={{0,3},{1,2},{2,1},{3,0},{4,7},{5,6},{6,5},{7,4},{8,11},{9,10},{10,... | collective-permute-start | bytes 49160 | tf_op jit(solution)/shard_map/ppermute | solution.py:128
  16.7 3.7 %collective-permute-start.6 = (f32[16,256]{1,0:T(8,128)S(1)}, f32[16,256]{1,0:T(8,128)S(1)}, u32[]{:S(2)}, u32[]{:S(2)}) collective-permute-start(f32[16,256]{1,0:T(8,128)S(1)} %score_parts.2.refs_0_), channel_id=1, source_target_pairs={{0,2},{1,3},{2,0},{3,1},{4,6},{5,7},{6,4},{7,5},{8,10},{9,11},{10,... | collective-permute-start | bytes 49160 | tf_op jit(solution)/shard_map/ppermute | solution.py:128
  17.8 2.6 %collective-permute-start.5 = (f32[16,256]{1,0:T(8,128)S(1)}, f32[16,256]{1,0:T(8,128)S(1)}, u32[]{:S(2)}, u32[]{:S(2)}) collective-permute-start(f32[16,256]{1,0:T(8,128)S(1)} %score_parts.2.refs_0_), channel_id=1, source_target_pairs={{0,1},{1,0},{2,3},{3,2},{4,5},{5,4},{6,7},{7,6},{8,9},{9,8},{10,11... | collective-permute-start | bytes 49160 | tf_op jit(solution)/shard_map/ppermute | solution.py:128
  21.6 8.6 %collective-permute-start.8 = (bf16[16,2176]{1,0:T(8,128)(2,1)S(1)}, bf16[16,2176]{1,0:T(8,128)(2,1)S(1)}, u32[]{:S(2)}, u32[]{:S(2)}) collective-permute-start(bf16[16,2176]{1,0:T(8,128)(2,1)S(1)} %get-tuple-element.37), channel_id=1, source_target_pairs={{0,8},{4,12},{8,0},{12,4},{1,9},{5,13},{9,1},{13,5},{2,10},{6,14},... | collective-permute-start | bytes 208904 | tf_op jit(solution)/shard_map/ppermute | solution.py:51
  23.0 5.6 %collective-permute-start.11 = (bf16[16,2048]{1,0:T(8,128)(2,1)S(1)}, bf16[16,2048]{1,0:T(8,128)(2,1)S(1)}, u32[]{:S(2)}, u32[]{:S(2)}) collective-permute-start(bf16[16,2048]{1,0:T(8,128)(2,1)S(1)} %get-tuple-element.41), channel_id=1, source_target_pairs={{0,4},{4,0},{8,12},{12,8},{1,5},{5,1},{9,13},{13,9},{2,6},{6,2},{1... | collective-permute-start | bytes 196616 | tf_op jit(solution)/shard_map/ppermute | solution.py:51
  24.8 7.9 %collective-permute-start.10 = (bf16[16,2176]{1,0:T(8,128)(2,1)S(1)}, bf16[16,2176]{1,0:T(8,128)(2,1)S(1)}, u32[]{:S(2)}, u32[]{:S(2)}) collective-permute-start(bf16[16,2176]{1,0:T(8,128)(2,1)S(1)} %get-tuple-element.40), channel_id=1, source_target_pairs={{0,4},{4,0},{8,12},{12,8},{1,5},{5,1},{9,13},{13,9},{2,6},{6,2},{1... | collective-permute-start | bytes 208904 | tf_op jit(solution)/shard_map/ppermute | solution.py:51
  25.0 7.6 %collective-permute-start.13 = (bf16[16,2176]{1,0:T(8,128)(2,1)S(1)}, bf16[16,2176]{1,0:T(8,128)(2,1)S(1)}, u32[]{:S(2)}, u32[]{:S(2)}) collective-permute-start(bf16[16,2176]{1,0:T(8,128)(2,1)S(1)} %get-tuple-element.44), channel_id=1, source_target_pairs={{0,12},{4,8},{8,4},{12,0},{1,13},{5,9},{9,5},{13,1},{2,14},{6,10},... | collective-permute-start | bytes 208904 | tf_op jit(solution)/shard_map/ppermute | solution.py:51
  28.6 7.0 %collective-permute-start.12 = (bf16[16,2048]{1,0:T(8,128)(2,1)S(1)}, bf16[16,2048]{1,0:T(8,128)(2,1)S(1)}, u32[]{:S(2)}, u32[]{:S(2)}) collective-permute-start(bf16[16,2048]{1,0:T(8,128)(2,1)S(1)} %relay.2), channel_id=1, source_target_pairs={{0,8},{4,12},{8,0},{12,4},{1,9},{5,13},{9,1},{13,5},{2,10},{6,14},... | collective-permute-start | bytes 196616 | tf_op jit(solution)/shard_map/ppermute | solution.py:51
  30.2 5.3 %collective-permute-start.9 = (bf16[16,2048]{1,0:T(8,128)(2,1)S(1)}, bf16[16,2048]{1,0:T(8,128)(2,1)S(1)}, u32[]{:S(2)}, u32[]{:S(2)}) collective-permute-start(bf16[16,2048]{1,0:T(8,128)(2,1)S(1)} %get-tuple-element.39), channel_id=1, source_target_pairs={{0,4},{4,0},{8,12},{12,8},{1,5},{5,1},{9,13},{13,9},{2,6},{6,2},{1... | collective-permute-start | bytes 196616 | tf_op jit(solution)/shard_map/ppermute | solution.py:51
  32.8 6.5 %collective-permute-start.15 = (bf16[4,8192]{1,0:T(4,128)(2,1)S(1)}, bf16[4,8192]{1,0:T(4,128)(2,1)S(1)}, u32[]{:S(2)}, u32[]{:S(2)}) collective-permute-start(bf16[4,8192]{1,0:T(4,128)(2,1)S(1)} %get-tuple-element.47), channel_id=1, source_target_pairs={{0,8},{4,12},{8,0},{12,4},{1,9},{5,13},{9,1},{13,5},{2,10},{6,14},... | collective-permute-start | bytes 196616 | tf_op jit(solution)/shard_map/ppermute | solution.py:51
  35.8 8.7 %collective-permute-start.14 = (bf16[4,16384]{1,0:T(4,128)(2,1)S(1)}, bf16[4,16384]{1,0:T(4,128)(2,1)S(1)}, u32[]{:S(2)}, u32[]{:S(2)}) collective-permute-start(bf16[4,16384]{1,0:T(4,128)(2,1)S(1)} %get-tuple-element.46.refs_0_.refs_3_), channel_id=1, source_target_pairs={{0,4},{4,0},{8,12},{12,8},{1,5},{5,1},{9,13},{13,9},{2,6},{6,2},{1... | collective-permute-start | bytes 393224 | tf_op jit(solution)/shard_map/ppermute | solution.py:51
  36.8 6.2 %collective-permute-start.18 = (bf16[4,8192]{1,0:T(4,128)(2,1)S(1)}, bf16[4,8192]{1,0:T(4,128)(2,1)S(1)}, u32[]{:S(2)}, u32[]{:S(2)}) collective-permute-start(bf16[4,8192]{1,0:T(4,128)(2,1)S(1)} %get-tuple-element.48), channel_id=1, source_target_pairs={{0,12},{4,8},{8,4},{12,0},{1,13},{5,9},{9,5},{13,1},{2,14},{6,10},... | collective-permute-start | bytes 196616 | tf_op jit(solution)/shard_map/ppermute | solution.py:51
  38.6 5.9 %collective-permute-start.16 = (bf16[4,8192]{1,0:T(4,128)(2,1)S(1)}, bf16[4,8192]{1,0:T(4,128)(2,1)S(1)}, u32[]{:S(2)}, u32[]{:S(2)}) collective-permute-start(bf16[4,8192]{1,0:T(4,128)(2,1)S(1)} %get-tuple-element.48), channel_id=1, source_target_pairs={{0,8},{4,12},{8,0},{12,4},{1,9},{5,13},{9,1},{13,5},{2,10},{6,14},... | collective-permute-start | bytes 196616 | tf_op jit(solution)/shard_map/ppermute | solution.py:51
  39.3 5.1 %collective-permute-start.17 = (bf16[4,8192]{1,0:T(4,128)(2,1)S(1)}, bf16[4,8192]{1,0:T(4,128)(2,1)S(1)}, u32[]{:S(2)}, u32[]{:S(2)}) collective-permute-start(bf16[4,8192]{1,0:T(4,128)(2,1)S(1)} %collective-permute-done.15.refs_2_), channel_id=1, source_target_pairs={{0,4},{4,0},{8,12},{12,8},{1,5},{5,1},{9,13},{13,9},{2,6},{6,2},{1... | collective-permute-start | bytes 196616 | tf_op jit(solution)/shard_map/ppermute | solution.py:51
  45.6 3.2 %collective-permute-start.21 = (f32[16,256]{1,0:T(8,128)S(1)}, f32[16,256]{1,0:T(8,128)S(1)}, u32[]{:S(2)}, u32[]{:S(2)}) collective-permute-start(f32[16,256]{1,0:T(8,128)S(1)} %score_parts.3.refs_0_), channel_id=1, source_target_pairs={{0,3},{1,2},{2,1},{3,0},{4,7},{5,6},{6,5},{7,4},{8,11},{9,10},{10,... | collective-permute-start | bytes 49160 | tf_op jit(solution)/shard_map/ppermute | solution.py:128
  45.6 3.8 %collective-permute-start.20 = (f32[16,256]{1,0:T(8,128)S(1)}, f32[16,256]{1,0:T(8,128)S(1)}, u32[]{:S(2)}, u32[]{:S(2)}) collective-permute-start(f32[16,256]{1,0:T(8,128)S(1)} %score_parts.3.refs_0_), channel_id=1, source_target_pairs={{0,2},{1,3},{2,0},{3,1},{4,6},{5,7},{6,4},{7,5},{8,10},{9,11},{10,... | collective-permute-start | bytes 49160 | tf_op jit(solution)/shard_map/ppermute | solution.py:128
  46.9 2.6 %collective-permute-start.19 = (f32[16,256]{1,0:T(8,128)S(1)}, f32[16,256]{1,0:T(8,128)S(1)}, u32[]{:S(2)}, u32[]{:S(2)}) collective-permute-start(f32[16,256]{1,0:T(8,128)S(1)} %score_parts.3.refs_0_), channel_id=1, source_target_pairs={{0,1},{1,0},{2,3},{3,2},{4,5},{5,4},{6,7},{7,6},{8,9},{9,8},{10,11... | collective-permute-start | bytes 49160 | tf_op jit(solution)/shard_map/ppermute | solution.py:128
  50.6 7.7 %collective-permute-start.25 = (bf16[16,2176]{1,0:T(8,128)(2,1)S(1)}, bf16[16,2176]{1,0:T(8,128)(2,1)S(1)}, u32[]{:S(2)}, u32[]{:S(2)}) collective-permute-start(bf16[16,2176]{1,0:T(8,128)(2,1)S(1)} %get-tuple-element.53), channel_id=1, source_target_pairs={{0,8},{4,12},{8,0},{12,4},{1,9},{5,13},{9,1},{13,5},{2,10},{6,14},... | collective-permute-start | bytes 208904 | tf_op jit(solution)/shard_map/ppermute | solution.py:51
  52.1 5.5 %collective-permute-start.23 = (bf16[16,2048]{1,0:T(8,128)(2,1)S(1)}, bf16[16,2048]{1,0:T(8,128)(2,1)S(1)}, u32[]{:S(2)}, u32[]{:S(2)}) collective-permute-start(bf16[16,2048]{1,0:T(8,128)(2,1)S(1)} %get-tuple-element.51), channel_id=1, source_target_pairs={{0,4},{4,0},{8,12},{12,8},{1,5},{5,1},{9,13},{13,9},{2,6},{6,2},{1... | collective-permute-start | bytes 196616 | tf_op jit(solution)/shard_map/ppermute | solution.py:51
  53.7 7.0 %collective-permute-start.26 = (bf16[16,2176]{1,0:T(8,128)(2,1)S(1)}, bf16[16,2176]{1,0:T(8,128)(2,1)S(1)}, u32[]{:S(2)}, u32[]{:S(2)}) collective-permute-start(bf16[16,2176]{1,0:T(8,128)(2,1)S(1)} %get-tuple-element.54), channel_id=1, source_target_pairs={{0,12},{4,8},{8,4},{12,0},{1,13},{5,9},{9,5},{13,1},{2,14},{6,10},... | collective-permute-start | bytes 208904 | tf_op jit(solution)/shard_map/ppermute | solution.py:51
  55.1 8.1 %collective-permute-start.22 = (bf16[16,4224]{1,0:T(8,128)(2,1)S(1)}, bf16[16,4224]{1,0:T(8,128)(2,1)S(1)}, u32[]{:S(2)}, u32[]{:S(2)}) collective-permute-start(bf16[16,4224]{1,0:T(8,128)(2,1)S(1)} %get-tuple-element.50), channel_id=1, source_target_pairs={{0,4},{4,0},{8,12},{12,8},{1,5},{5,1},{9,13},{13,9},{2,6},{6,2},{1... | collective-permute-start | bytes 405512 | tf_op jit(solution)/shard_map/ppermute | solution.py:51
  57.6 5.3 %collective-permute-start.24 = (bf16[16,2048]{1,0:T(8,128)(2,1)S(1)}, bf16[16,2048]{1,0:T(8,128)(2,1)S(1)}, u32[]{:S(2)}, u32[]{:S(2)}) collective-permute-start(bf16[16,2048]{1,0:T(8,128)(2,1)S(1)} %relay.3), channel_id=1, source_target_pairs={{0,8},{4,12},{8,0},{12,4},{1,9},{5,13},{9,1},{13,5},{2,10},{6,14},... | collective-permute-start | bytes 196616 | tf_op jit(solution)/shard_map/ppermute | solution.py:51

commit v7 on v6

--- a/solution.py
+++ b/solution.py
@@ -10,6 +10,7 @@
 
 PIX = 65536
 ITERS = 2
+LEAD = 1
 TAIL = 128
 VMEM_BYTES = 12 * 1024 * 1024
 IN_VMEM = pl.BlockSpec(memory_space=pltpu.VMEM)
@@ -209,15 +210,19 @@
     return pieces
 
 
+def split(counts):
+    high = counts.astype(jnp.bfloat16).astype(jnp.float32)
+    lane = lax.broadcasted_iota(jnp.int32, (counts.shape[0], TAIL), 1)
+    return jnp.where(lane < TAIL // 2, high, counts - high)
+
+
 def weigh(parts, prior_ref):
     raw = tree_sum([ref[...] for ref in parts])
     scores = (3.0 / math.sqrt(PIX)) * raw + prior_ref[...]
     up = jnp.exp(scores - jnp.max(scores, axis=0, keepdims=True))
     weights = (up / jnp.sum(up, axis=0, keepdims=True)).astype(jnp.bfloat16).astype(jnp.float32)
     counts = jnp.sum(weights, axis=1, keepdims=True)
-    high = counts.astype(jnp.bfloat16).astype(jnp.float32)
-    lane = lax.broadcasted_iota(jnp.int32, (counts.shape[0], TAIL), 1)
-    return weights, jnp.where(lane < TAIL // 2, high, counts - high)
+    return weights, split(counts)
 
 
 def plain_totals_kernel(n, *refs):
@@ -231,58 +236,111 @@
     out_ref[:, pix:] = tail.astype(jnp.bfloat16)
 
 
-def dense_totals_kernel(n, *refs):
-    parts, prior_ref, frames_ref, outs = refs[:n], refs[n], refs[n + 1], refs[n + 2 :]
-    weights, tail = weigh(parts, prior_ref)
+def dense_totals_kernel(part, weights, frames_ref, own_ref, near_ref, two_ref, three_ref):
     quarter = frames_ref.shape[1] // 4
     half = quarter // 2
-    own_ref, *near_refs = outs[:-4]
-    two_refs, three_refs = outs[-4:-2], outs[-2:]
-    for k, out_ref in enumerate([own_ref, near_refs[-1], two_refs[1], three_refs[1]]):
+    turned = [rotate_rows(weights, (-4 * q) % 16).astype(jnp.bfloat16) for q in range(4)]
+    for piece in chunks(half, 512):
+        totals = [
+            jnp.dot(
+                turned[q],
+                frames_ref[:, pl.ds(q * quarter + part * half + piece.start, piece.size)],
+                preferred_element_type=jnp.float32,
+            )
+            for q in range(4)
+        ]
+        upper = lax.broadcasted_iota(jnp.int32, (8, piece.size), 0) < 4
+        whole = pl.ds(part * half + piece.start, piece.size)
+        near = whole if near_ref.shape[1] > quarter else piece
+        spots = [(own_ref, whole), (near_ref, near), (two_ref, piece), (three_ref, piece)]
+        for k, (out_ref, spot) in enumerate(spots):
+            first = jnp.where(upper, totals[-k % 4][:8], totals[(1 - k) % 4][:8])
+            second = jnp.where(upper, totals[(2 - k) % 4][8:], totals[(3 - k) % 4][8:])
+            out_ref[:, spot] = jnp.concatenate([first, second], axis=0).astype(jnp.bfloat16)
+
+
+def put_counts(tail, outs):
+    for k, out_ref in outs:
         rows = jnp.concatenate([tail[4 * k : 4 * k + 4]] * 4, axis=0)
         out_ref[:, out_ref.shape[1] - TAIL :] = rows.astype(jnp.bfloat16)
-    turned = [rotate_rows(weights, (-4 * q) % 16).astype(jnp.bfloat16) for q in range(4)]
-    for part in range(2):
-        for piece in chunks(half, 512):
-            totals = [
-                jnp.dot(
-                    turned[q],
-                    frames_ref[:, pl.ds(q * quarter + part * half + piece.start, piece.size)],
-                    preferred_element_type=jnp.float32,
-                )
-                for q in range(4)
-            ]
-            upper = lax.broadcasted_iota(jnp.int32, (8, piece.size), 0) < 4
-            whole = pl.ds(part * half + piece.start, piece.size)
-            near = (near_refs[part], piece) if len(near_refs) > 1 else (near_refs[0], whole)
-            spots = [(own_ref, whole), near, (two_refs[part], piece), (three_refs[part], piece)]
-            for k, (out_ref, spot) in enumerate(spots):
-                first = jnp.where(upper, totals[-k % 4][:8], totals[(1 - k) % 4][:8])
-                second = jnp.where(upper, totals[(2 - k) % 4][8:], totals[(3 - k) % 4][8:])
-                out_ref[:, spot] = jnp.concatenate([first, second], axis=0).astype(jnp.bfloat16)
+
+
+def whole_totals_kernel(n, *refs):
+    parts, prior_ref, frames_ref = refs[:n], refs[n], refs[n + 1]
+    own_ref, near_0_ref, near_1_ref, two_0_ref, two_1_ref, three_0_ref, three_1_ref = refs[n + 2 :]
+    weights, tail = weigh(parts, prior_ref)
+    put_counts(tail, ((0, own_ref), (1, near_1_ref), (2, two_1_ref), (3, three_1_ref)))
+    dense_totals_kernel(0, weights, frames_ref, own_ref, near_0_ref, two_0_ref, three_0_ref)
+    dense_totals_kernel(1, weights, frames_ref, own_ref, near_1_ref, two_1_ref, three_1_ref)
+
+
+def first_totals_kernel(n, part, *refs):
+    parts, prior_ref, frames_ref, outs, weights_ref = refs[:n], refs[n], refs[n + 1], refs[n + 2 : n + 6], refs[n + 6]
+    weights, tail = weigh(parts, prior_ref)
+    weights_ref[...] = weights
+    put_counts(tail, list(enumerate(outs)) if part else list(enumerate(outs[:2])))
+    dense_totals_kernel(part, weights, frames_ref, *outs)
+
+
+def second_totals_kernel(part, weights_ref, frames_ref, _own_ref, _near_ref, *outs):
+    weights = weights_ref[...]
+    if part:
+        put_counts(split(jnp.sum(weights, axis=1, keepdims=True)), ((2, outs[2]), (3, outs[3])))
+    dense_totals_kernel(part, weights, frames_ref, *outs)
+
+
+def totals_call(kernel, operands, shapes, frames, aliases={}):
+    rows, pix = frames.shape
+    many = 16
+    return pl.pallas_call(
+        kernel,
+        in_specs=[IN_VMEM] * len(operands),
+        out_specs=[IN_VMEM] * len(shapes),
+        out_shape=shapes,
+        input_output_aliases=aliases,
+        compiler_params=params(),
+        cost_estimate=pl.CostEstimate(
+            flops=rows * pix * many, bytes_accessed=rows * pix, transcendentals=rows * many
+        ),
+        name="block_totals",
+    )(*operands)
 
 
 def block_totals(parts, prior, frames, dense, near_halves):
     rows, pix = frames.shape
     many = prior.shape[0]
-    if dense:
-        half = pix // 8
-        kernel = dense_totals_kernel
-        whole, halves = [(16, 2 * half + TAIL)], [(16, half), (16, half + TAIL)]
-        shapes = whole + (halves if near_halves else whole) + 2 * halves
-    else:
-        kernel, shapes = plain_totals_kernel, [(many, pix + TAIL)]
-    return pl.pallas_call(
-        functools.partial(kernel, len(parts)),
-        in_specs=[IN_VMEM] * (len(parts) + 2),
-        out_specs=[IN_VMEM] * len(shapes),
-        out_shape=[jax.ShapeDtypeStruct(shape, jnp.bfloat16) for shape in shapes],
-        compiler_params=params(),
-        cost_estimate=pl.CostEstimate(
-            flops=2 * rows * pix * many, bytes_accessed=2 * rows * pix, transcendentals=rows * many
-        ),
-        name="block_totals",
-    )(*parts, prior, pltpu.with_memory_space_constraint(frames, pltpu.VMEM))
+    frames = pltpu.with_memory_space_constraint(frames, pltpu.VMEM)
+    if not dense:
+        whole = jax.ShapeDtypeStruct((many, pix + TAIL), jnp.bfloat16)
+        return totals_call(
+            functools.partial(plain_totals_kernel, len(parts)), (*parts, prior, frames), [whole], frames
+        )
+    whole, half, half_tail = (
+        jax.ShapeDtypeStruct((16, size), jnp.bfloat16) for size in (pix // 4 + TAIL, pix // 8, pix // 8 + TAIL)
+    )
+    if near_halves:
+        return totals_call(
+            functools.partial(whole_totals_kernel, len(parts)),
+            (*parts, prior, frames),
+            [whole, half, half_tail, half, half_tail, half, half_tail],
+            frames,
+        )
+    sizes = (half, half_tail)
+    own, near, two, three, weights = totals_call(
+        functools.partial(first_totals_kernel, len(parts), LEAD),
+        (*parts, prior, frames),
+        [whole, whole, sizes[LEAD], sizes[LEAD], jax.ShapeDtypeStruct((many, rows), jnp.float32)],
+        frames,
+    )
+    own, near, *other = totals_call(
+        functools.partial(second_totals_kernel, 1 - LEAD),
+        (weights, frames, own, near),
+        [whole, whole, sizes[1 - LEAD], sizes[1 - LEAD]],
+        frames,
+        {2: 0, 3: 1},
+    )
+    twos, threes = (two, other[0]), (three, other[1])
+    return own, near, twos[LEAD], twos[1 - LEAD], threes[LEAD], threes[1 - LEAD]
 
 
 def plain_update_kernel(terms_ref, owned_ref, out_ref):

time: 64.2 us -> 64.1 us (level)
  waiting for transfers between devices: 19.3 us -> 18.6 us
    ppermute x21, waiting for transfers between devices: 14.9 us -> 14.2 us  [swap(): return lax.ppermute(value, 'frame', [(i, i ^ distance) for i in range(4)])]
    pallas_call x2 -> x3, Pallas kernels: 2.41 us -> 2.51 us  [totals_call(): pl.pallas_call(kernel, in_specs=[IN_VMEM] * len(operands), out_specs=[IN_...]
  transfers between devices with their start and end apart: 27 -> 27, of which waited for: 16 -> 16; matrix products, arithmetic and copies ran while one was open for 0% -> 0% of each run, Pallas kernels for 4% -> 5%
where the time goes in v7:
time: 64.1 us; the launch traced here: 64 us
  starting transfers between devices  35.7 us (56%)
  waiting for transfers between devices  18.6 us (29%)
  Pallas kernels  9.61 us (15%)
    ppermute x21, starting transfers between devices, swap(): return lax.ppermute(value, 'frame', [(i, i ^ distance) for i in range(4)])  31.9 us
    ppermute x21, waiting for transfers between devices, swap(): return lax.ppermute(value, 'frame', [(i, i ^ distance) for i in range(4)])  14.2 us
    ppermute x6, waiting for transfers between devices, exchange_all(): lax.ppermute(part, axes, [(i, i ^ k) for i in range(size)])  4.43 us
    ppermute x6, starting transfers between devices, exchange_all(): lax.ppermute(part, axes, [(i, i ^ k) for i in range(size)])  3.79 us
    pallas_call x3, Pallas kernels, totals_call(): pl.pallas_call(kernel, in_specs=[IN_VMEM] * len(operands), out_specs=[IN_...  2.51 us
    pallas_call x2, Pallas kernels, score_parts(): pl.pallas_call(functools.partial(score_kernel, pieces), in_specs=[IN_VMEM...  2.38 us
    pallas_call x1, Pallas kernels, load_frames(): pl.pallas_call(functools.partial(load_kernel, dense), in_specs=[IN_VMEM]...  2.28 us
  transfers between devices with their start and end apart: 27, of which 16 were waited for; matrix products, arithmetic and copies ran while one was open for 0% of the time, Pallas kernels for 5%

profile of v7, /device:TPU:0, one launch (start us, length us, event | category | flops | bytes accessed | tf_op | source)
XLA Modules:
  0.0 64.0 jit_solution(17833189072927102555)
XLA Ops:
  0.0 1.1 %round_slices.1 = (bf16[4,16384]{1,0:T(4,128)(2,1)S(1)}, bf16[4,8192]{1,0:T(4,128)(2,1)S(1)}, bf16[4,8192]{1,0:T(4,128)(2,1)S(1)}) custom-call(f32[4,16384]{1,0:T(4,128)} %slices_ref.1), custom_call_target="tpu_custom_call" | custom-call | flops 5000000000 | bytes 524288 | tf_op jit(solution)/shard_map/round_slices/pallas_call | solution.py:85
  1.1 4.1 %collective-permute-start.1 = (bf16[4,8192]{1,0:T(4,128)(2,1)S(1)}, bf16[4,8192]{1,0:T(4,128)(2,1)S(1)}, u32[]{:S(2)}, u32[]{:S(2)}) collective-permute-start(bf16[4,8192]{1,0:T(4,128)(2,1)S(1)} %get-tuple-element.34), channel_id=1, source_target_pairs={{0,8},{4,12},{8,0},{12,4},{1,9},{5,13},{9,1},{13,5},{2,10},{6,14},... | collective-permute-start | bytes 196616 | tf_op jit(solution)/shard_map/ppermute | solution.py:52
  5.2 1.6 %collective-permute-start = (bf16[4,16384]{1,0:T(4,128)(2,1)S(1)}, bf16[4,16384]{1,0:T(4,128)(2,1)S(1)}, u32[]{:S(2)}, u32[]{:S(2)}) collective-permute-start(bf16[4,16384]{1,0:T(4,128)(2,1)S(1)} %get-tuple-element.33.refs_0_.owned_ref), channel_id=1, source_target_pairs={{0,4},{4,0},{8,12},{12,8},{1,5},{5,1},{9,13},{13,9},{2,6},{6,2},{1... | collective-permute-start | bytes 393224 | tf_op jit(solution)/shard_map/ppermute | solution.py:52
  6.8 0.0 collective-permute-start.4
  6.8 1.9 %collective-permute-start.2 = (bf16[4,8192]{1,0:T(4,128)(2,1)S(1)}, bf16[4,8192]{1,0:T(4,128)(2,1)S(1)}, u32[]{:S(2)}, u32[]{:S(2)}) collective-permute-start(bf16[4,8192]{1,0:T(4,128)(2,1)S(1)} %get-tuple-element.35), channel_id=1, source_target_pairs={{0,8},{4,12},{8,0},{12,4},{1,9},{5,13},{9,1},{13,5},{2,10},{6,14},... | collective-permute-start | bytes 196616 | tf_op jit(solution)/shard_map/ppermute | solution.py:52
  8.7 0.0 collective-permute-done.1.refs_2_
  8.7 2.5 %collective-permute-start.3 = (bf16[4,8192]{1,0:T(4,128)(2,1)S(1)}, bf16[4,8192]{1,0:T(4,128)(2,1)S(1)}, u32[]{:S(2)}, u32[]{:S(2)}) collective-permute-start(bf16[4,8192]{1,0:T(4,128)(2,1)S(1)} %collective-permute-done.1.refs_2_), channel_id=1, source_target_pairs={{0,4},{4,0},{8,12},{12,8},{1,5},{5,1},{9,13},{13,9},{2,6},{6,2},{1... | collective-permute-start | bytes 196616 | tf_op jit(solution)/shard_map/ppermute | solution.py:52
  11.2 2.3 %load_frames.1 = (bf16[16384,256]{1,0:T(8,128)(2,1)S(1)}, f32[16,256]{1,0:T(8,128)S(1)}) custom-call(bf16[256,16384]{1,0:T(8,128)(2,1)S(1)} %copy-done, s32[16]{0:T(128)} %orient_in_ref.1, f32[4096]{0:T(1024)} %log_prior_in_ref.1), custom_call_target="tpu_custom_call" | custom-call | bytes 25165824 | tf_op jit(solution)/shard_map/load_frames/pallas_call | solution.py:153
  13.5 0.2 collective-permute-done.4.refs_5_
  13.7 0.5 collective-permute-done.2.refs_3_
  14.3 0.5 collective-permute-done.3.refs_4_
  14.8 0.0 collective-permute-done.refs_1_
  14.8 1.2 %score_parts.2.refs_0_ = f32[16,256]{1,0:T(8,128)S(1)} custom-call(bf16[4,16384]{1,0:T(4,128)(2,1)S(1)} %get-tuple-element.33.refs_0_.owned_ref, bf16[4,16384]{1,0:T(4,128)(2,1)S(1)} %collective-permute-done.refs_1_, bf16[4,8192]{1,0:T(4,128)(2,1)S(1)} %collective-permute-done.1.refs_2_, bf16[4,8192]{1,0:T(4,128)(2,1)S(1)} %collective-permute-done.2.refs_3_, ...), custom_call_target="tpu_custom_call" | custom-call | flops 134217728 | bytes 8388608 | tf_op jit(solution)/shard_map/score_parts/pallas_call | solution.py:188
  16.0 0.7 %collective-permute-start.7 = (f32[16,256]{1,0:T(8,128)S(1)}, f32[16,256]{1,0:T(8,128)S(1)}, u32[]{:S(2)}, u32[]{:S(2)}) collective-permute-start(f32[16,256]{1,0:T(8,128)S(1)} %score_parts.2.refs_0_), channel_id=1, source_target_pairs={{0,3},{1,2},{2,1},{3,0},{4,7},{5,6},{6,5},{7,4},{8,11},{9,10},{10,... | collective-permute-start | bytes 49160 | tf_op jit(solution)/shard_map/ppermute | solution.py:129
  16.7 1.2 %collective-permute-start.6 = (f32[16,256]{1,0:T(8,128)S(1)}, f32[16,256]{1,0:T(8,128)S(1)}, u32[]{:S(2)}, u32[]{:S(2)}) collective-permute-start(f32[16,256]{1,0:T(8,128)S(1)} %score_parts.2.refs_0_), channel_id=1, source_target_pairs={{0,2},{1,3},{2,0},{3,1},{4,6},{5,7},{6,4},{7,5},{8,10},{9,11},{10,... | collective-permute-start | bytes 49160 | tf_op jit(solution)/shard_map/ppermute | solution.py:129
  17.8 0.1 collective-permute-start.5
  17.9 1.3 %collective-permute-done.7.refs_3_ = f32[16,256]{1,0:T(8,128)S(1)} collective-permute-done((f32[16,256]{1,0:T(8,128)S(1)}, f32[16,256]{1,0:T(8,128)S(1)}, u32[]{:S(2)}, u32[]{:S(2)}) %collective-permute-start.7) | collective-permute-done | bytes 16416 | tf_op jit(solution)/shard_map/ppermute | solution.py:129
  19.2 1.2 %collective-permute-done.6.refs_2_ = f32[16,256]{1,0:T(8,128)S(1)} collective-permute-done((f32[16,256]{1,0:T(8,128)S(1)}, f32[16,256]{1,0:T(8,128)S(1)}, u32[]{:S(2)}, u32[]{:S(2)}) %collective-permute-start.6) | collective-permute-done | bytes 16416 | tf_op jit(solution)/shard_map/ppermute | solution.py:129
  20.4 0.0 collective-permute-done.5.refs_1_
  20.4 1.2 %block_totals.3 = (bf16[16,4224]{1,0:T(8,128)(2,1)S(1)}, bf16[16,2048]{1,0:T(8,128)(2,1)S(1)}, bf16[16,2176]{1,0:T(8,128)(2,1)S(1)}, bf16[16,2048]{1,0:T(8,128)(...) custom-call(f32[16,256]{1,0:T(8,128)S(1)} %score_parts.2.refs_0_, ...), custom_call_target="tpu_custom_call" | custom-call | flops 67108864 | bytes 4194304 | tf_op jit(solution)/shard_map/block_totals/pallas_call | solution.py:295
  21.6 1.4 %collective-permute-start.8 = (bf16[16,2176]{1,0:T(8,128)(2,1)S(1)}, bf16[16,2176]{1,0:T(8,128)(2,1)S(1)}, u32[]{:S(2)}, u32[]{:S(2)}) collective-permute-start(bf16[16,2176]{1,0:T(8,128)(2,1)S(1)} %get-tuple-element.40), channel_id=1, source_target_pairs={{0,8},{4,12},{8,0},{12,4},{1,9},{5,13},{9,1},{13,5},{2,10},{6,14},... | collective-permute-start | bytes 208904 | tf_op jit(solution)/shard_map/ppermute | solution.py:52
  23.0 1.8 %collective-permute-start.11 = (bf16[16,2048]{1,0:T(8,128)(2,1)S(1)}, bf16[16,2048]{1,0:T(8,128)(2,1)S(1)}, u32[]{:S(2)}, u32[]{:S(2)}) collective-permute-start(bf16[16,2048]{1,0:T(8,128)(2,1)S(1)} %get-tuple-element.44), channel_id=1, source_target_pairs={{0,4},{4,0},{8,12},{12,8},{1,5},{5,1},{9,13},{13,9},{2,6},{6,2},{1... | collective-permute-start | bytes 196616 | tf_op jit(solution)/shard_map/ppermute | solution.py:52
  24.8 0.3 collective-permute-start.10
  25.0 2.2 %collective-permute-start.13 = (bf16[16,2176]{1,0:T(8,128)(2,1)S(1)}, bf16[16,2176]{1,0:T(8,128)(2,1)S(1)}, u32[]{:S(2)}, u32[]{:S(2)}) collective-permute-start(bf16[16,2176]{1,0:T(8,128)(2,1)S(1)} %get-tuple-element.47), channel_id=1, source_target_pairs={{0,12},{4,8},{8,4},{12,0},{1,13},{5,9},{9,5},{13,1},{2,14},{6,10},... | collective-permute-start | bytes 208904 | tf_op jit(solution)/shard_map/ppermute | solution.py:52
  27.2 1.4 %collective-permute-done.11.came_ref = bf16[16,2048]{1,0:T(8,128)(2,1)S(1)} collective-permute-done((bf16[16,2048]{1,0:T(8,128)(2,1)S(1)}, bf16[16,2048]{1,0:T(8,128)(2,1)S(1)}, u32[]{:S(2)}, u32[]{:S(2)}) %collective-permute-start.11) | collective-permute-done | bytes 65568 | tf_op jit(solution)/shard_map/ppermute | solution.py:52
  28.6 1.6 %collective-permute-start.12 = (bf16[16,2048]{1,0:T(8,128)(2,1)S(1)}, bf16[16,2048]{1,0:T(8,128)(2,1)S(1)}, u32[]{:S(2)}, u32[]{:S(2)}) collective-permute-start(bf16[16,2048]{1,0:T(8,128)(2,1)S(1)} %relay.2), channel_id=1, source_target_pairs={{0,8},{4,12},{8,0},{12,4},{1,9},{5,13},{9,1},{13,5},{2,10},{6,14},... | collective-permute-start | bytes 196616 | tf_op jit(solution)/shard_map/ppermute | solution.py:52
  30.2 0.0 collective-permute-done.8.in_ref
  30.2 2.1 %collective-permute-start.9 = (bf16[16,2048]{1,0:T(8,128)(2,1)S(1)}, bf16[16,2048]{1,0:T(8,128)(2,1)S(1)}, u32[]{:S(2)}, u32[]{:S(2)}) collective-permute-start(bf16[16,2048]{1,0:T(8,128)(2,1)S(1)} %get-tuple-element.42), channel_id=1, source_target_pairs={{0,4},{4,0},{8,12},{12,8},{1,5},{5,1},{9,13},{13,9},{2,6},{6,2},{1... | collective-permute-start | bytes 196616 | tf_op jit(solution)/shard_map/ppermute | solution.py:52
  32.3 0.4 collective-permute-done.13.in_ref
  32.7 0.0 collective-permute-done.10.near_1_ref
  32.7 0.2 update.3
  32.8 1.3 %collective-permute-start.15 = (bf16[4,8192]{1,0:T(4,128)(2,1)S(1)}, bf16[4,8192]{1,0:T(4,128)(2,1)S(1)}, u32[]{:S(2)}, u32[]{:S(2)}) collective-permute-start(bf16[4,8192]{1,0:T(4,128)(2,1)S(1)} %get-tuple-element.50), channel_id=1, source_target_pairs={{0,8},{4,12},{8,0},{12,4},{1,9},{5,13},{9,1},{13,5},{2,10},{6,14},... | collective-permute-start | bytes 196616 | tf_op jit(solution)/shard_map/ppermute | solution.py:52
  34.2 1.4 %collective-permute-done.12.joined_ref = bf16[16,2048]{1,0:T(8,128)(2,1)S(1)} collective-permute-done((bf16[16,2048]{1,0:T(8,128)(2,1)S(1)}, bf16[16,2048]{1,0:T(8,128)(2,1)S(1)}, u32[]{:S(2)}, u32[]{:S(2)}) %collective-permute-start.12) | collective-permute-done | bytes 65568 | tf_op jit(solution)/shard_map/ppermute | solution.py:52
  35.6 0.0 collective-permute-done.9.near_0_ref
  35.6 0.2 update.4
  35.8 1.1 %collective-permute-start.14 = (bf16[4,16384]{1,0:T(4,128)(2,1)S(1)}, bf16[4,16384]{1,0:T(4,128)(2,1)S(1)}, u32[]{:S(2)}, u32[]{:S(2)}) collective-permute-start(bf16[4,16384]{1,0:T(4,128)(2,1)S(1)} %get-tuple-element.49.refs_0_.refs_3_), channel_id=1, source_target_pairs={{0,4},{4,0},{8,12},{12,8},{1,5},{5,1},{9,13},{13,9},{2,6},{6,2},{1... | collective-permute-start | bytes 393224 | tf_op jit(solution)/shard_map/ppermute | solution.py:52
  36.8 1.7 %collective-permute-start.18 = (bf16[4,8192]{1,0:T(4,128)(2,1)S(1)}, bf16[4,8192]{1,0:T(4,128)(2,1)S(1)}, u32[]{:S(2)}, u32[]{:S(2)}) collective-permute-start(bf16[4,8192]{1,0:T(4,128)(2,1)S(1)} %get-tuple-element.51), channel_id=1, source_target_pairs={{0,12},{4,8},{8,4},{12,0},{1,13},{5,9},{9,5},{13,1},{2,14},{6,10},... | collective-permute-start | bytes 196616 | tf_op jit(solution)/shard_map/ppermute | solution.py:52
  38.6 0.7 %collective-permute-start.16 = (bf16[4,8192]{1,0:T(4,128)(2,1)S(1)}, bf16[4,8192]{1,0:T(4,128)(2,1)S(1)}, u32[]{:S(2)}, u32[]{:S(2)}) collective-permute-start(bf16[4,8192]{1,0:T(4,128)(2,1)S(1)} %get-tuple-element.51), channel_id=1, source_target_pairs={{0,8},{4,12},{8,0},{12,4},{1,9},{5,13},{9,1},{13,5},{2,10},{6,14},... | collective-permute-start | bytes 196616 | tf_op jit(solution)/shard_map/ppermute | solution.py:52
  39.3 0.0 collective-permute-done.15.refs_2_
  39.3 1.9 %collective-permute-start.17 = (bf16[4,8192]{1,0:T(4,128)(2,1)S(1)}, bf16[4,8192]{1,0:T(4,128)(2,1)S(1)}, u32[]{:S(2)}, u32[]{:S(2)}) collective-permute-start(bf16[4,8192]{1,0:T(4,128)(2,1)S(1)} %collective-permute-done.15.refs_2_), channel_id=1, source_target_pairs={{0,4},{4,0},{8,12},{12,8},{1,5},{5,1},{9,13},{13,9},{2,6},{6,2},{1... | collective-permute-start | bytes 196616 | tf_op jit(solution)/shard_map/ppermute | solution.py:52
  41.2 1.8 %collective-permute-done.18.refs_5_ = bf16[4,8192]{1,0:T(4,128)(2,1)S(1)} collective-permute-done((bf16[4,8192]{1,0:T(4,128)(2,1)S(1)}, bf16[4,8192]{1,0:T(4,128)(2,1)S(1)}, u32[]{:S(2)}, u32[]{:S(2)}) %collective-permute-start.18) | collective-permute-done | bytes 65568 | tf_op jit(solution)/shard_map/ppermute | solution.py:52
  43.0 1.4 %collective-permute-done.16.refs_3_ = bf16[4,8192]{1,0:T(4,128)(2,1)S(1)} collective-permute-done((bf16[4,8192]{1,0:T(4,128)(2,1)S(1)}, bf16[4,8192]{1,0:T(4,128)(2,1)S(1)}, u32[]{:S(2)}, u32[]{:S(2)}) %collective-permute-start.16) | collective-permute-done | bytes 65568 | tf_op jit(solution)/shard_map/ppermute | solution.py:52
  44.4 0.0 collective-permute-done.17.refs_4_
  44.4 0.0 collective-permute-done.14.refs_1_
  44.4 1.2 %score_parts.3.refs_0_ = f32[16,256]{1,0:T(8,128)S(1)} custom-call(bf16[4,16384]{1,0:T(4,128)(2,1)S(1)} %get-tuple-element.49.refs_0_.refs_3_, bf16[4,16384]{1,0:T(4,128)(2,1)S(1)} %collective-permute-done.14.refs_1_, bf16[4,8192]{1,0:T(4,128)(2,1)S(1)} %collective-permute-done.15.refs_2_, bf16[4,8192]{1,0:T(4,128)(2,1)S(1)} %collective-permute-done.16.refs_3_, ...), custom_call_target="tpu_custom_call" | custom-call | flops 134217728 | bytes 8388608 | tf_op jit(solution)/shard_map/score_parts/pallas_call | solution.py:188
  45.6 0.0 collective-permute-start.21
  45.6 1.2 %collective-permute-start.20 = (f32[16,256]{1,0:T(8,128)S(1)}, f32[16,256]{1,0:T(8,128)S(1)}, u32[]{:S(2)}, u32[]{:S(2)}) collective-permute-start(f32[16,256]{1,0:T(8,128)S(1)} %score_parts.3.refs_0_), channel_id=1, source_target_pairs={{0,2},{1,3},{2,0},{3,1},{4,6},{5,7},{6,4},{7,5},{8,10},{9,11},{10,... | collective-permute-start | bytes 49160 | tf_op jit(solution)/shard_map/ppermute | solution.py:129
  46.9 0.6 collective-permute-start.19
  47.5 1.3 %collective-permute-done.21.refs_3_ = f32[16,256]{1,0:T(8,128)S(1)} collective-permute-done((f32[16,256]{1,0:T(8,128)S(1)}, f32[16,256]{1,0:T(8,128)S(1)}, u32[]{:S(2)}, u32[]{:S(2)}) %collective-permute-start.21) | collective-permute-done | bytes 16416 | tf_op jit(solution)/shard_map/ppermute | solution.py:129
  48.8 0.6 collective-permute-done.20.refs_2_
  49.4 0.0 collective-permute-done.19.refs_1_
  49.4 0.7 %block_totals.4 = (bf16[16,4224]{1,0:T(8,128)(2,1)S(1)}, bf16[16,4224]{1,0:T(8,128)(2,1)S(1)}, bf16[16,2176]{1,0:T(8,128)(2,1)S(1)}, bf16[16,2176]{1,0:T(8,128)(2,1)S(1)}, f32[16,256]{1,0:T(8,128)S(1)}) custom-call(f32[16,256]{1,0:T(8,128)S(1)} %score_parts.3.refs_0_, f32[16,256]{1,0:T(8,128)S(1)} %collective-permute-done.19.refs_1_, ...), custom_call_target="tpu_custom_call" | custom-call | flops 67108864 | bytes 4194304 | tf_op jit(solution)/shard_map/block_totals/pallas_call | solution.py:295
  50.1 1.4 %collective-permute-start.25 = (bf16[16,2176]{1,0:T(8,128)(2,1)S(1)}, bf16[16,2176]{1,0:T(8,128)(2,1)S(1)}, u32[]{:S(2)}, u32[]{:S(2)}) collective-permute-start(bf16[16,2176]{1,0:T(8,128)(2,1)S(1)} %get-tuple-element.59), channel_id=1, source_target_pairs={{0,8},{4,12},{8,0},{12,4},{1,9},{5,13},{9,1},{13,5},{2,10},{6,14},... | collective-permute-start | bytes 208904 | tf_op jit(solution)/shard_map/ppermute | solution.py:52
  51.5 0.6 %block_totals.5 = (bf16[16,4224]{1,0:T(8,128)(2,1)S(1)}, bf16[16,4224]{1,0:T(8,128)(2,1)S(1)}, bf16[16,2048]{1,0:T(8,128)(2,1)S(1)}, bf16[16,2048]{1,0:T(8,128)(2,1)S(1)}) custom-call(f32[16,256]{1,0:T(8,128)S(1)} %get-tuple-element.52.weights_ref, bf16[256,16384]{1,0:T(8,128)(2,1)S(1)} %copy-done, ...), custom_call_target="tpu_custom_call", output_to_operand_aliasing={{0}: (2, {}), {1}: (3, {})} | custom-call | flops 67108864 | bytes 4194304 | tf_op jit(solution)/shard_map/block_totals/pallas_call | solution.py:295
  52.2 1.7 %collective-permute-start.23 = (bf16[16,2048]{1,0:T(8,128)(2,1)S(1)}, bf16[16,2048]{1,0:T(8,128)(2,1)S(1)}, u32[]{:S(2)}, u32[]{:S(2)}) collective-permute-start(bf16[16,2048]{1,0:T(8,128)(2,1)S(1)} %get-tuple-element.57), channel_id=1, source_target_pairs={{0,4},{4,0},{8,12},{12,8},{1,5},{5,1},{9,13},{13,9},{2,6},{6,2},{1... | collective-permute-start | bytes 196616 | tf_op jit(solution)/shard_map/ppermute | solution.py:52
  53.9 1.4 %collective-permute-start.26 = (bf16[16,2176]{1,0:T(8,128)(2,1)S(1)}, bf16[16,2176]{1,0:T(8,128)(2,1)S(1)}, u32[]{:S(2)}, u32[]{:S(2)}) collective-permute-start(bf16[16,2176]{1,0:T(8,128)(2,1)S(1)} %get-tuple-element.60), channel_id=1, source_target_pairs={{0,12},{4,8},{8,4},{12,0},{1,13},{5,9},{9,5},{13,1},{2,14},{6,10},... | collective-permute-start | bytes 208904 | tf_op jit(solution)/shard_map/ppermute | solution.py:52
  55.2 0.1 collective-permute-start.22
  55.4 2.0 %collective-permute-done.23.came_ref = bf16[16,2048]{1,0:T(8,128)(2,1)S(1)} collective-permute-done((bf16[16,2048]{1,0:T(8,128)(2,1)S(1)}, bf16[16,2048]{1,0:T(8,128)(2,1)S(1)}, u32[]{:S(2)}, u32[]{:S(2)}) %collective-permute-start.23) | collective-permute-done | bytes 65568 | tf_op jit(solution)/shard_map/ppermute | solution.py:52
  57.4 1.1 %collective-permute-start.24 = (bf16[16,2048]{1,0:T(8,128)(2,1)S(1)}, bf16[16,2048]{1,0:T(8,128)(2,1)S(1)}, u32[]{:S(2)}, u32[]{:S(2)}) collective-permute-start(bf16[16,2048]{1,0:T(8,128)(2,1)S(1)} %relay.3), channel_id=1, source_target_pairs={{0,8},{4,12},{8,0},{12,4},{1,9},{5,13},{9,1},{13,5},{2,10},{6,14},... | collective-permute-start | bytes 196616 | tf_op jit(solution)/shard_map/ppermute | solution.py:52
  58.5 0.0 collective-permute-done.25.in_ref
  58.5 2.4 %collective-permute-done.26.in_ref = bf16[16,2176]{1,0:T(8,128)(2,1)S(1)} collective-permute-done((bf16[16,2176]{1,0:T(8,128)(2,1)S(1)}, bf16[16,2176]{1,0:T(8,128)(2,1)S(1)}, u32[]{:S(2)}, u32[]{:S(2)}) %collective-permute-start.26) | collective-permute-done | bytes 69664 | tf_op jit(solution)/shard_map/ppermute | solution.py:52
  60.9 2.0 %collective-permute-done.24.refs_0_ = bf16[16,2048]{1,0:T(8,128)(2,1)S(1)} collective-permute-done((bf16[16,2048]{1,0:T(8,128)(2,1)S(1)}, bf16[16,2048]{1,0:T(8,128)(2,1)S(1)}, u32[]{:S(2)}, u32[]{:S(2)}) %collective-permute-start.24) | collective-permute-done | bytes 65568 | tf_op jit(solution)/shard_map/ppermute | solution.py:52
  62.9 0.2 collective-permute-done.22.near_ref
  63.1 0.9 %update.5 = f32[4,16384]{1,0:T(4,128)} custom-call(bf16[16,4224]{1,0:T(8,128)(2,1)S(1)} %get-tuple-element.55.own_ref, bf16[16,4224]{1,0:T(8,128)(2,1)S(1)} %collective-permute-done.22.near_ref, bf16[16,2048]{1,0:T(8,128)(2,1)S(1)} %collective-permute-done.24.refs_0_, bf16[16,2176]{1,0:T(8,128)(2,1)S(1)} %early.6.refs_1_, ...), custom_call_target="tpu_custom_call" | custom-call | flops 540672 | bytes 811008 | tf_op jit(solution)/shard_map/update/pallas_call | solution.py:397
  (8 shorter events, 0.1 us)
Async XLA Ops:
  0.0 11.2 %copy-start = (bf16[256,16384]{1,0:T(8,128)(2,1)S(1)}, bf16[256,16384]{1,0:T(8,128)(2,1)}, u32[]{:S(2)}) copy-start(bf16[256,16384]{1,0:T(8,128)(2,1)} %frames_ref) | copy-start | bytes 25165828
  1.1 7.6 %collective-permute-start.1 = (bf16[4,8192]{1,0:T(4,128)(2,1)S(1)}, bf16[4,8192]{1,0:T(4,128)(2,1)S(1)}, u32[]{:S(2)}, u32[]{:S(2)}) collective-permute-start(bf16[4,8192]{1,0:T(4,128)(2,1)S(1)} %get-tuple-element.34), channel_id=1, source_target_pairs={{0,8},{4,12},{8,0},{12,4},{1,9},{5,13},{9,1},{13,5},{2,10},{6,14},... | collective-permute-start | bytes 196616 | tf_op jit(solution)/shard_map/ppermute | solution.py:52
  5.2 9.6 %collective-permute-start = (bf16[4,16384]{1,0:T(4,128)(2,1)S(1)}, bf16[4,16384]{1,0:T(4,128)(2,1)S(1)}, u32[]{:S(2)}, u32[]{:S(2)}) collective-permute-start(bf16[4,16384]{1,0:T(4,128)(2,1)S(1)} %get-tuple-element.33.refs_0_.owned_ref), channel_id=1, source_target_pairs={{0,4},{4,0},{8,12},{12,8},{1,5},{5,1},{9,13},{13,9},{2,6},{6,2},{1... | collective-permute-start | bytes 393224 | tf_op jit(solution)/shard_map/ppermute | solution.py:52
  6.8 6.9 %collective-permute-start.4 = (bf16[4,8192]{1,0:T(4,128)(2,1)S(1)}, bf16[4,8192]{1,0:T(4,128)(2,1)S(1)}, u32[]{:S(2)}, u32[]{:S(2)}) collective-permute-start(bf16[4,8192]{1,0:T(4,128)(2,1)S(1)} %get-tuple-element.35), channel_id=1, source_target_pairs={{0,12},{4,8},{8,4},{12,0},{1,13},{5,9},{9,5},{13,1},{2,14},{6,10},... | collective-permute-start | bytes 196616 | tf_op jit(solution)/shard_map/ppermute | solution.py:52
  6.8 7.4 %collective-permute-start.2 = (bf16[4,8192]{1,0:T(4,128)(2,1)S(1)}, bf16[4,8192]{1,0:T(4,128)(2,1)S(1)}, u32[]{:S(2)}, u32[]{:S(2)}) collective-permute-start(bf16[4,8192]{1,0:T(4,128)(2,1)S(1)} %get-tuple-element.35), channel_id=1, source_target_pairs={{0,8},{4,12},{8,0},{12,4},{1,9},{5,13},{9,1},{13,5},{2,10},{6,14},... | collective-permute-start | bytes 196616 | tf_op jit(solution)/shard_map/ppermute | solution.py:52
  8.7 6.1 %collective-permute-start.3 = (bf16[4,8192]{1,0:T(4,128)(2,1)S(1)}, bf16[4,8192]{1,0:T(4,128)(2,1)S(1)}, u32[]{:S(2)}, u32[]{:S(2)}) collective-permute-start(bf16[4,8192]{1,0:T(4,128)(2,1)S(1)} %collective-permute-done.1.refs_2_), channel_id=1, source_target_pairs={{0,4},{4,0},{8,12},{12,8},{1,5},{5,1},{9,13},{13,9},{2,6},{6,2},{1... | collective-permute-start | bytes 196616 | tf_op jit(solution)/shard_map/ppermute | solution.py:52
  16.0 3.2 %collective-permute-start.7 = (f32[16,256]{1,0:T(8,128)S(1)}, f32[16,256]{1,0:T(8,128)S(1)}, u32[]{:S(2)}, u32[]{:S(2)}) collective-permute-start(f32[16,256]{1,0:T(8,128)S(1)} %score_parts.2.refs_0_), channel_id=1, source_target_pairs={{0,3},{1,2},{2,1},{3,0},{4,7},{5,6},{6,5},{7,4},{8,11},{9,10},{10,... | collective-permute-start | bytes 49160 | tf_op jit(solution)/shard_map/ppermute | solution.py:129
  16.7 3.7 %collective-permute-start.6 = (f32[16,256]{1,0:T(8,128)S(1)}, f32[16,256]{1,0:T(8,128)S(1)}, u32[]{:S(2)}, u32[]{:S(2)}) collective-permute-start(f32[16,256]{1,0:T(8,128)S(1)} %score_parts.2.refs_0_), channel_id=1, source_target_pairs={{0,2},{1,3},{2,0},{3,1},{4,6},{5,7},{6,4},{7,5},{8,10},{9,11},{10,... | collective-permute-start | bytes 49160 | tf_op jit(solution)/shard_map/ppermute | solution.py:129
  17.8 2.6 %collective-permute-start.5 = (f32[16,256]{1,0:T(8,128)S(1)}, f32[16,256]{1,0:T(8,128)S(1)}, u32[]{:S(2)}, u32[]{:S(2)}) collective-permute-start(f32[16,256]{1,0:T(8,128)S(1)} %score_parts.2.refs_0_), channel_id=1, source_target_pairs={{0,1},{1,0},{2,3},{3,2},{4,5},{5,4},{6,7},{7,6},{8,9},{9,8},{10,11... | collective-permute-start | bytes 49160 | tf_op jit(solution)/shard_map/ppermute | solution.py:129
  21.6 8.6 %collective-permute-start.8 = (bf16[16,2176]{1,0:T(8,128)(2,1)S(1)}, bf16[16,2176]{1,0:T(8,128)(2,1)S(1)}, u32[]{:S(2)}, u32[]{:S(2)}) collective-permute-start(bf16[16,2176]{1,0:T(8,128)(2,1)S(1)} %get-tuple-element.40), channel_id=1, source_target_pairs={{0,8},{4,12},{8,0},{12,4},{1,9},{5,13},{9,1},{13,5},{2,10},{6,14},... | collective-permute-start | bytes 208904 | tf_op jit(solution)/shard_map/ppermute | solution.py:52
  23.0 5.6 %collective-permute-start.11 = (bf16[16,2048]{1,0:T(8,128)(2,1)S(1)}, bf16[16,2048]{1,0:T(8,128)(2,1)S(1)}, u32[]{:S(2)}, u32[]{:S(2)}) collective-permute-start(bf16[16,2048]{1,0:T(8,128)(2,1)S(1)} %get-tuple-element.44), channel_id=1, source_target_pairs={{0,4},{4,0},{8,12},{12,8},{1,5},{5,1},{9,13},{13,9},{2,6},{6,2},{1... | collective-permute-start | bytes 196616 | tf_op jit(solution)/shard_map/ppermute | solution.py:52
  24.8 7.9 %collective-permute-start.10 = (bf16[16,2176]{1,0:T(8,128)(2,1)S(1)}, bf16[16,2176]{1,0:T(8,128)(2,1)S(1)}, u32[]{:S(2)}, u32[]{:S(2)}) collective-permute-start(bf16[16,2176]{1,0:T(8,128)(2,1)S(1)} %get-tuple-element.43), channel_id=1, source_target_pairs={{0,4},{4,0},{8,12},{12,8},{1,5},{5,1},{9,13},{13,9},{2,6},{6,2},{1... | collective-permute-start | bytes 208904 | tf_op jit(solution)/shard_map/ppermute | solution.py:52
  25.0 7.6 %collective-permute-start.13 = (bf16[16,2176]{1,0:T(8,128)(2,1)S(1)}, bf16[16,2176]{1,0:T(8,128)(2,1)S(1)}, u32[]{:S(2)}, u32[]{:S(2)}) collective-permute-start(bf16[16,2176]{1,0:T(8,128)(2,1)S(1)} %get-tuple-element.47), channel_id=1, source_target_pairs={{0,12},{4,8},{8,4},{12,0},{1,13},{5,9},{9,5},{13,1},{2,14},{6,10},... | collective-permute-start | bytes 208904 | tf_op jit(solution)/shard_map/ppermute | solution.py:52
  28.6 7.0 %collective-permute-start.12 = (bf16[16,2048]{1,0:T(8,128)(2,1)S(1)}, bf16[16,2048]{1,0:T(8,128)(2,1)S(1)}, u32[]{:S(2)}, u32[]{:S(2)}) collective-permute-start(bf16[16,2048]{1,0:T(8,128)(2,1)S(1)} %relay.2), channel_id=1, source_target_pairs={{0,8},{4,12},{8,0},{12,4},{1,9},{5,13},{9,1},{13,5},{2,10},{6,14},... | collective-permute-start | bytes 196616 | tf_op jit(solution)/shard_map/ppermute | solution.py:52
  30.2 5.3 %collective-permute-start.9 = (bf16[16,2048]{1,0:T(8,128)(2,1)S(1)}, bf16[16,2048]{1,0:T(8,128)(2,1)S(1)}, u32[]{:S(2)}, u32[]{:S(2)}) collective-permute-start(bf16[16,2048]{1,0:T(8,128)(2,1)S(1)} %get-tuple-element.42), channel_id=1, source_target_pairs={{0,4},{4,0},{8,12},{12,8},{1,5},{5,1},{9,13},{13,9},{2,6},{6,2},{1... | collective-permute-start | bytes 196616 | tf_op jit(solution)/shard_map/ppermute | solution.py:52
  32.8 6.5 %collective-permute-start.15 = (bf16[4,8192]{1,0:T(4,128)(2,1)S(1)}, bf16[4,8192]{1,0:T(4,128)(2,1)S(1)}, u32[]{:S(2)}, u32[]{:S(2)}) collective-permute-start(bf16[4,8192]{1,0:T(4,128)(2,1)S(1)} %get-tuple-element.50), channel_id=1, source_target_pairs={{0,8},{4,12},{8,0},{12,4},{1,9},{5,13},{9,1},{13,5},{2,10},{6,14},... | collective-permute-start | bytes 196616 | tf_op jit(solution)/shard_map/ppermute | solution.py:52
  35.8 8.7 %collective-permute-start.14 = (bf16[4,16384]{1,0:T(4,128)(2,1)S(1)}, bf16[4,16384]{1,0:T(4,128)(2,1)S(1)}, u32[]{:S(2)}, u32[]{:S(2)}) collective-permute-start(bf16[4,16384]{1,0:T(4,128)(2,1)S(1)} %get-tuple-element.49.refs_0_.refs_3_), channel_id=1, source_target_pairs={{0,4},{4,0},{8,12},{12,8},{1,5},{5,1},{9,13},{13,9},{2,6},{6,2},{1... | collective-permute-start | bytes 393224 | tf_op jit(solution)/shard_map/ppermute | solution.py:52
  36.8 6.2 %collective-permute-start.18 = (bf16[4,8192]{1,0:T(4,128)(2,1)S(1)}, bf16[4,8192]{1,0:T(4,128)(2,1)S(1)}, u32[]{:S(2)}, u32[]{:S(2)}) collective-permute-start(bf16[4,8192]{1,0:T(4,128)(2,1)S(1)} %get-tuple-element.51), channel_id=1, source_target_pairs={{0,12},{4,8},{8,4},{12,0},{1,13},{5,9},{9,5},{13,1},{2,14},{6,10},... | collective-permute-start | bytes 196616 | tf_op jit(solution)/shard_map/ppermute | solution.py:52
  38.6 5.9 %collective-permute-start.16 = (bf16[4,8192]{1,0:T(4,128)(2,1)S(1)}, bf16[4,8192]{1,0:T(4,128)(2,1)S(1)}, u32[]{:S(2)}, u32[]{:S(2)}) collective-permute-start(bf16[4,8192]{1,0:T(4,128)(2,1)S(1)} %get-tuple-element.51), channel_id=1, source_target_pairs={{0,8},{4,12},{8,0},{12,4},{1,9},{5,13},{9,1},{13,5},{2,10},{6,14},... | collective-permute-start | bytes 196616 | tf_op jit(solution)/shard_map/ppermute | solution.py:52
  39.3 5.1 %collective-permute-start.17 = (bf16[4,8192]{1,0:T(4,128)(2,1)S(1)}, bf16[4,8192]{1,0:T(4,128)(2,1)S(1)}, u32[]{:S(2)}, u32[]{:S(2)}) collective-permute-start(bf16[4,8192]{1,0:T(4,128)(2,1)S(1)} %collective-permute-done.15.refs_2_), channel_id=1, source_target_pairs={{0,4},{4,0},{8,12},{12,8},{1,5},{5,1},{9,13},{13,9},{2,6},{6,2},{1... | collective-permute-start | bytes 196616 | tf_op jit(solution)/shard_map/ppermute | solution.py:52
  45.6 3.2 %collective-permute-start.21 = (f32[16,256]{1,0:T(8,128)S(1)}, f32[16,256]{1,0:T(8,128)S(1)}, u32[]{:S(2)}, u32[]{:S(2)}) collective-permute-start(f32[16,256]{1,0:T(8,128)S(1)} %score_parts.3.refs_0_), channel_id=1, source_target_pairs={{0,3},{1,2},{2,1},{3,0},{4,7},{5,6},{6,5},{7,4},{8,11},{9,10},{10,... | collective-permute-start | bytes 49160 | tf_op jit(solution)/shard_map/ppermute | solution.py:129
  45.6 3.8 %collective-permute-start.20 = (f32[16,256]{1,0:T(8,128)S(1)}, f32[16,256]{1,0:T(8,128)S(1)}, u32[]{:S(2)}, u32[]{:S(2)}) collective-permute-start(f32[16,256]{1,0:T(8,128)S(1)} %score_parts.3.refs_0_), channel_id=1, source_target_pairs={{0,2},{1,3},{2,0},{3,1},{4,6},{5,7},{6,4},{7,5},{8,10},{9,11},{10,... | collective-permute-start | bytes 49160 | tf_op jit(solution)/shard_map/ppermute | solution.py:129
  46.9 2.6 %collective-permute-start.19 = (f32[16,256]{1,0:T(8,128)S(1)}, f32[16,256]{1,0:T(8,128)S(1)}, u32[]{:S(2)}, u32[]{:S(2)}) collective-permute-start(f32[16,256]{1,0:T(8,128)S(1)} %score_parts.3.refs_0_), channel_id=1, source_target_pairs={{0,1},{1,0},{2,3},{3,2},{4,5},{5,4},{6,7},{7,6},{8,9},{9,8},{10,11... | collective-permute-start | bytes 49160 | tf_op jit(solution)/shard_map/ppermute | solution.py:129
  50.1 8.4 %collective-permute-start.25 = (bf16[16,2176]{1,0:T(8,128)(2,1)S(1)}, bf16[16,2176]{1,0:T(8,128)(2,1)S(1)}, u32[]{:S(2)}, u32[]{:S(2)}) collective-permute-start(bf16[16,2176]{1,0:T(8,128)(2,1)S(1)} %get-tuple-element.59), channel_id=1, source_target_pairs={{0,8},{4,12},{8,0},{12,4},{1,9},{5,13},{9,1},{13,5},{2,10},{6,14},... | collective-permute-start | bytes 208904 | tf_op jit(solution)/shard_map/ppermute | solution.py:52
  52.2 5.2 %collective-permute-start.23 = (bf16[16,2048]{1,0:T(8,128)(2,1)S(1)}, bf16[16,2048]{1,0:T(8,128)(2,1)S(1)}, u32[]{:S(2)}, u32[]{:S(2)}) collective-permute-start(bf16[16,2048]{1,0:T(8,128)(2,1)S(1)} %get-tuple-element.57), channel_id=1, source_target_pairs={{0,4},{4,0},{8,12},{12,8},{1,5},{5,1},{9,13},{13,9},{2,6},{6,2},{1... | collective-permute-start | bytes 196616 | tf_op jit(solution)/shard_map/ppermute | solution.py:52
  53.9 7.0 %collective-permute-start.26 = (bf16[16,2176]{1,0:T(8,128)(2,1)S(1)}, bf16[16,2176]{1,0:T(8,128)(2,1)S(1)}, u32[]{:S(2)}, u32[]{:S(2)}) collective-permute-start(bf16[16,2176]{1,0:T(8,128)(2,1)S(1)} %get-tuple-element.60), channel_id=1, source_target_pairs={{0,12},{4,8},{8,4},{12,0},{1,13},{5,9},{9,5},{13,1},{2,14},{6,10},... | collective-permute-start | bytes 208904 | tf_op jit(solution)/shard_map/ppermute | solution.py:52
  55.2 7.8 %collective-permute-start.22 = (bf16[16,4224]{1,0:T(8,128)(2,1)S(1)}, bf16[16,4224]{1,0:T(8,128)(2,1)S(1)}, u32[]{:S(2)}, u32[]{:S(2)}) collective-permute-start(bf16[16,4224]{1,0:T(8,128)(2,1)S(1)} %get-tuple-element.56), channel_id=1, source_target_pairs={{0,4},{4,0},{8,12},{12,8},{1,5},{5,1},{9,13},{13,9},{2,6},{6,2},{1... | collective-permute-start | bytes 405512 | tf_op jit(solution)/shard_map/ppermute | solution.py:52
  57.4 5.5 %collective-permute-start.24 = (bf16[16,2048]{1,0:T(8,128)(2,1)S(1)}, bf16[16,2048]{1,0:T(8,128)(2,1)S(1)}, u32[]{:S(2)}, u32[]{:S(2)}) collective-permute-start(bf16[16,2048]{1,0:T(8,128)(2,1)S(1)} %relay.3), channel_id=1, source_target_pairs={{0,8},{4,12},{8,0},{12,4},{1,9},{5,13},{9,1},{13,5},{2,10},{6,14},... | collective-permute-start | bytes 196616 | tf_op jit(solution)/shard_map/ppermute | solution.py:52

commit v8 on v7

--- a/solution.py
+++ b/solution.py
@@ -372,7 +372,7 @@
             (3, direct_3_ref, behind_half),
         ]
     )
-    scale = tail[:, :1] + tail[:, TAIL // 2 : TAIL // 2 + 1] + 1.0
+    scale = 1.0 / (tail[:, :1] + tail[:, TAIL // 2 : TAIL // 2 + 1] + 1.0)
     for part in parts:
         for piece in chunks(half, 512):
             whole = pl.ds(part * half + piece.start, piece.size)
@@ -381,7 +381,7 @@
             terms += [(2, direct_2_ref, piece), (3, direct_3_ref, piece)] if part else [(2, joined_ref, piece)]
             spots = [pl.ds(q * quarter + whole.start, whole.size) for q in range(4)]
             owned = jnp.concatenate([owned_ref[:, spot].astype(jnp.float32) for spot in spots], axis=0)
-            new = ((total(terms) + owned) / scale).astype(out_ref.dtype)
+            new = ((total(terms) + owned) * scale).astype(out_ref.dtype)
             for q, spot in enumerate(spots):
                 out_ref[:, spot] = new[4 * q : 4 * q + 4]
                 for half_ref in half_refs:

time: 64.1 us -> 64.1 us (level)
  no operation moved by 1% of the time
where the time goes in v8:
time: 64.1 us; the launch traced here: 64 us
  starting transfers between devices  35.6 us (56%)
  waiting for transfers between devices  18.7 us (29%)
  Pallas kernels  9.6 us (15%)
    ppermute x21, starting transfers between devices, swap(): return lax.ppermute(value, 'frame', [(i, i ^ distance) for i in range(4)])  31.8 us
    ppermute x21, waiting for transfers between devices, swap(): return lax.ppermute(value, 'frame', [(i, i ^ distance) for i in range(4)])  14.3 us
    ppermute x6, waiting for transfers between devices, exchange_all(): lax.ppermute(part, axes, [(i, i ^ k) for i in range(size)])  4.43 us
    ppermute x6, starting transfers between devices, exchange_all(): lax.ppermute(part, axes, [(i, i ^ k) for i in range(size)])  3.79 us
    pallas_call x3, Pallas kernels, totals_call(): pl.pallas_call(kernel, in_specs=[IN_VMEM] * len(operands), out_specs=[IN_...  2.51 us
    pallas_call x2, Pallas kernels, score_parts(): pl.pallas_call(functools.partial(score_kernel, pieces), in_specs=[IN_VMEM...  2.38 us
    pallas_call x1, Pallas kernels, load_frames(): pl.pallas_call(functools.partial(load_kernel, dense), in_specs=[IN_VMEM]...  2.28 us
  transfers between devices with their start and end apart: 27, of which 16 were waited for; matrix products, arithmetic and copies ran while one was open for 0% of the time, Pallas kernels for 5%

profile of v8, /device:TPU:0, one launch (start us, length us, event | category | flops | bytes accessed | tf_op | source)
XLA Modules:
  0.0 64.0 jit_solution(12050288153464838986)
XLA Ops:
  0.0 1.1 %round_slices.1 = (bf16[4,16384]{1,0:T(4,128)(2,1)S(1)}, bf16[4,8192]{1,0:T(4,128)(2,1)S(1)}, bf16[4,8192]{1,0:T(4,128)(2,1)S(1)}) custom-call(f32[4,16384]{1,0:T(4,128)} %slices_ref.1), custom_call_target="tpu_custom_call" | custom-call | flops 5000000000 | bytes 524288 | tf_op jit(solution)/shard_map/round_slices/pallas_call | solution.py:85
  1.1 4.1 %collective-permute-start.1 = (bf16[4,8192]{1,0:T(4,128)(2,1)S(1)}, bf16[4,8192]{1,0:T(4,128)(2,1)S(1)}, u32[]{:S(2)}, u32[]{:S(2)}) collective-permute-start(bf16[4,8192]{1,0:T(4,128)(2,1)S(1)} %get-tuple-element.34), channel_id=1, source_target_pairs={{0,8},{4,12},{8,0},{12,4},{1,9},{5,13},{9,1},{13,5},{2,10},{6,14},... | collective-permute-start | bytes 196616 | tf_op jit(solution)/shard_map/ppermute | solution.py:52
  5.2 1.6 %collective-permute-start = (bf16[4,16384]{1,0:T(4,128)(2,1)S(1)}, bf16[4,16384]{1,0:T(4,128)(2,1)S(1)}, u32[]{:S(2)}, u32[]{:S(2)}) collective-permute-start(bf16[4,16384]{1,0:T(4,128)(2,1)S(1)} %get-tuple-element.33.refs_0_.owned_ref), channel_id=1, source_target_pairs={{0,4},{4,0},{8,12},{12,8},{1,5},{5,1},{9,13},{13,9},{2,6},{6,2},{1... | collective-permute-start | bytes 393224 | tf_op jit(solution)/shard_map/ppermute | solution.py:52
  6.8 0.0 collective-permute-start.4
  6.8 1.9 %collective-permute-start.2 = (bf16[4,8192]{1,0:T(4,128)(2,1)S(1)}, bf16[4,8192]{1,0:T(4,128)(2,1)S(1)}, u32[]{:S(2)}, u32[]{:S(2)}) collective-permute-start(bf16[4,8192]{1,0:T(4,128)(2,1)S(1)} %get-tuple-element.35), channel_id=1, source_target_pairs={{0,8},{4,12},{8,0},{12,4},{1,9},{5,13},{9,1},{13,5},{2,10},{6,14},... | collective-permute-start | bytes 196616 | tf_op jit(solution)/shard_map/ppermute | solution.py:52
  8.7 0.0 collective-permute-done.1.refs_2_
  8.7 2.5 %collective-permute-start.3 = (bf16[4,8192]{1,0:T(4,128)(2,1)S(1)}, bf16[4,8192]{1,0:T(4,128)(2,1)S(1)}, u32[]{:S(2)}, u32[]{:S(2)}) collective-permute-start(bf16[4,8192]{1,0:T(4,128)(2,1)S(1)} %collective-permute-done.1.refs_2_), channel_id=1, source_target_pairs={{0,4},{4,0},{8,12},{12,8},{1,5},{5,1},{9,13},{13,9},{2,6},{6,2},{1... | collective-permute-start | bytes 196616 | tf_op jit(solution)/shard_map/ppermute | solution.py:52
  11.2 2.3 %load_frames.1 = (bf16[16384,256]{1,0:T(8,128)(2,1)S(1)}, f32[16,256]{1,0:T(8,128)S(1)}) custom-call(bf16[256,16384]{1,0:T(8,128)(2,1)S(1)} %copy-done, s32[16]{0:T(128)} %orient_in_ref.1, f32[4096]{0:T(1024)} %log_prior_in_ref.1), custom_call_target="tpu_custom_call" | custom-call | bytes 25165824 | tf_op jit(solution)/shard_map/load_frames/pallas_call | solution.py:153
  13.5 0.2 collective-permute-done.4.refs_5_
  13.7 0.5 collective-permute-done.2.refs_3_
  14.3 0.5 collective-permute-done.3.refs_4_
  14.8 0.0 collective-permute-done.refs_1_
  14.8 1.2 %score_parts.2.refs_0_ = f32[16,256]{1,0:T(8,128)S(1)} custom-call(bf16[4,16384]{1,0:T(4,128)(2,1)S(1)} %get-tuple-element.33.refs_0_.owned_ref, bf16[4,16384]{1,0:T(4,128)(2,1)S(1)} %collective-permute-done.refs_1_, bf16[4,8192]{1,0:T(4,128)(2,1)S(1)} %collective-permute-done.1.refs_2_, bf16[4,8192]{1,0:T(4,128)(2,1)S(1)} %collective-permute-done.2.refs_3_, ...), custom_call_target="tpu_custom_call" | custom-call | flops 134217728 | bytes 8388608 | tf_op jit(solution)/shard_map/score_parts/pallas_call | solution.py:188
  16.0 0.7 %collective-permute-start.7 = (f32[16,256]{1,0:T(8,128)S(1)}, f32[16,256]{1,0:T(8,128)S(1)}, u32[]{:S(2)}, u32[]{:S(2)}) collective-permute-start(f32[16,256]{1,0:T(8,128)S(1)} %score_parts.2.refs_0_), channel_id=1, source_target_pairs={{0,3},{1,2},{2,1},{3,0},{4,7},{5,6},{6,5},{7,4},{8,11},{9,10},{10,... | collective-permute-start | bytes 49160 | tf_op jit(solution)/shard_map/ppermute | solution.py:129
  16.7 1.2 %collective-permute-start.6 = (f32[16,256]{1,0:T(8,128)S(1)}, f32[16,256]{1,0:T(8,128)S(1)}, u32[]{:S(2)}, u32[]{:S(2)}) collective-permute-start(f32[16,256]{1,0:T(8,128)S(1)} %score_parts.2.refs_0_), channel_id=1, source_target_pairs={{0,2},{1,3},{2,0},{3,1},{4,6},{5,7},{6,4},{7,5},{8,10},{9,11},{10,... | collective-permute-start | bytes 49160 | tf_op jit(solution)/shard_map/ppermute | solution.py:129
  17.8 0.1 collective-permute-start.5
  17.9 1.3 %collective-permute-done.7.refs_3_ = f32[16,256]{1,0:T(8,128)S(1)} collective-permute-done((f32[16,256]{1,0:T(8,128)S(1)}, f32[16,256]{1,0:T(8,128)S(1)}, u32[]{:S(2)}, u32[]{:S(2)}) %collective-permute-start.7) | collective-permute-done | bytes 16416 | tf_op jit(solution)/shard_map/ppermute | solution.py:129
  19.2 1.2 %collective-permute-done.6.refs_2_ = f32[16,256]{1,0:T(8,128)S(1)} collective-permute-done((f32[16,256]{1,0:T(8,128)S(1)}, f32[16,256]{1,0:T(8,128)S(1)}, u32[]{:S(2)}, u32[]{:S(2)}) %collective-permute-start.6) | collective-permute-done | bytes 16416 | tf_op jit(solution)/shard_map/ppermute | solution.py:129
  20.4 0.0 collective-permute-done.5.refs_1_
  20.4 1.2 %block_totals.3 = (bf16[16,4224]{1,0:T(8,128)(2,1)S(1)}, bf16[16,2048]{1,0:T(8,128)(2,1)S(1)}, bf16[16,2176]{1,0:T(8,128)(2,1)S(1)}, bf16[16,2048]{1,0:T(8,128)(...) custom-call(f32[16,256]{1,0:T(8,128)S(1)} %score_parts.2.refs_0_, ...), custom_call_target="tpu_custom_call" | custom-call | flops 67108864 | bytes 4194304 | tf_op jit(solution)/shard_map/block_totals/pallas_call | solution.py:295
  21.6 1.4 %collective-permute-start.8 = (bf16[16,2176]{1,0:T(8,128)(2,1)S(1)}, bf16[16,2176]{1,0:T(8,128)(2,1)S(1)}, u32[]{:S(2)}, u32[]{:S(2)}) collective-permute-start(bf16[16,2176]{1,0:T(8,128)(2,1)S(1)} %get-tuple-element.40), channel_id=1, source_target_pairs={{0,8},{4,12},{8,0},{12,4},{1,9},{5,13},{9,1},{13,5},{2,10},{6,14},... | collective-permute-start | bytes 208904 | tf_op jit(solution)/shard_map/ppermute | solution.py:52
  23.0 1.8 %collective-permute-start.11 = (bf16[16,2048]{1,0:T(8,128)(2,1)S(1)}, bf16[16,2048]{1,0:T(8,128)(2,1)S(1)}, u32[]{:S(2)}, u32[]{:S(2)}) collective-permute-start(bf16[16,2048]{1,0:T(8,128)(2,1)S(1)} %get-tuple-element.44), channel_id=1, source_target_pairs={{0,4},{4,0},{8,12},{12,8},{1,5},{5,1},{9,13},{13,9},{2,6},{6,2},{1... | collective-permute-start | bytes 196616 | tf_op jit(solution)/shard_map/ppermute | solution.py:52
  24.8 0.3 collective-permute-start.10
  25.0 2.2 %collective-permute-start.13 = (bf16[16,2176]{1,0:T(8,128)(2,1)S(1)}, bf16[16,2176]{1,0:T(8,128)(2,1)S(1)}, u32[]{:S(2)}, u32[]{:S(2)}) collective-permute-start(bf16[16,2176]{1,0:T(8,128)(2,1)S(1)} %get-tuple-element.47), channel_id=1, source_target_pairs={{0,12},{4,8},{8,4},{12,0},{1,13},{5,9},{9,5},{13,1},{2,14},{6,10},... | collective-permute-start | bytes 208904 | tf_op jit(solution)/shard_map/ppermute | solution.py:52
  27.2 1.4 %collective-permute-done.11.came_ref = bf16[16,2048]{1,0:T(8,128)(2,1)S(1)} collective-permute-done((bf16[16,2048]{1,0:T(8,128)(2,1)S(1)}, bf16[16,2048]{1,0:T(8,128)(2,1)S(1)}, u32[]{:S(2)}, u32[]{:S(2)}) %collective-permute-start.11) | collective-permute-done | bytes 65568 | tf_op jit(solution)/shard_map/ppermute | solution.py:52
  28.6 1.6 %collective-permute-start.12 = (bf16[16,2048]{1,0:T(8,128)(2,1)S(1)}, bf16[16,2048]{1,0:T(8,128)(2,1)S(1)}, u32[]{:S(2)}, u32[]{:S(2)}) collective-permute-start(bf16[16,2048]{1,0:T(8,128)(2,1)S(1)} %relay.2), channel_id=1, source_target_pairs={{0,8},{4,12},{8,0},{12,4},{1,9},{5,13},{9,1},{13,5},{2,10},{6,14},... | collective-permute-start | bytes 196616 | tf_op jit(solution)/shard_map/ppermute | solution.py:52
  30.2 0.0 collective-permute-done.8.in_ref
  30.2 2.1 %collective-permute-start.9 = (bf16[16,2048]{1,0:T(8,128)(2,1)S(1)}, bf16[16,2048]{1,0:T(8,128)(2,1)S(1)}, u32[]{:S(2)}, u32[]{:S(2)}) collective-permute-start(bf16[16,2048]{1,0:T(8,128)(2,1)S(1)} %get-tuple-element.42), channel_id=1, source_target_pairs={{0,4},{4,0},{8,12},{12,8},{1,5},{5,1},{9,13},{13,9},{2,6},{6,2},{1... | collective-permute-start | bytes 196616 | tf_op jit(solution)/shard_map/ppermute | solution.py:52
  32.3 0.4 collective-permute-done.13.in_ref
  32.7 0.0 collective-permute-done.10.near_1_ref
  32.7 0.2 update.3
  32.8 1.3 %collective-permute-start.15 = (bf16[4,8192]{1,0:T(4,128)(2,1)S(1)}, bf16[4,8192]{1,0:T(4,128)(2,1)S(1)}, u32[]{:S(2)}, u32[]{:S(2)}) collective-permute-start(bf16[4,8192]{1,0:T(4,128)(2,1)S(1)} %get-tuple-element.50), channel_id=1, source_target_pairs={{0,8},{4,12},{8,0},{12,4},{1,9},{5,13},{9,1},{13,5},{2,10},{6,14},... | collective-permute-start | bytes 196616 | tf_op jit(solution)/shard_map/ppermute | solution.py:52
  34.2 1.4 %collective-permute-done.12.joined_ref = bf16[16,2048]{1,0:T(8,128)(2,1)S(1)} collective-permute-done((bf16[16,2048]{1,0:T(8,128)(2,1)S(1)}, bf16[16,2048]{1,0:T(8,128)(2,1)S(1)}, u32[]{:S(2)}, u32[]{:S(2)}) %collective-permute-start.12) | collective-permute-done | bytes 65568 | tf_op jit(solution)/shard_map/ppermute | solution.py:52
  35.6 0.0 collective-permute-done.9.near_0_ref
  35.6 0.2 update.4
  35.7 1.1 %collective-permute-start.14 = (bf16[4,16384]{1,0:T(4,128)(2,1)S(1)}, bf16[4,16384]{1,0:T(4,128)(2,1)S(1)}, u32[]{:S(2)}, u32[]{:S(2)}) collective-permute-start(bf16[4,16384]{1,0:T(4,128)(2,1)S(1)} %get-tuple-element.49.refs_0_.refs_3_), channel_id=1, source_target_pairs={{0,4},{4,0},{8,12},{12,8},{1,5},{5,1},{9,13},{13,9},{2,6},{6,2},{1... | collective-permute-start | bytes 393224 | tf_op jit(solution)/shard_map/ppermute | solution.py:52
  36.8 1.7 %collective-permute-start.18 = (bf16[4,8192]{1,0:T(4,128)(2,1)S(1)}, bf16[4,8192]{1,0:T(4,128)(2,1)S(1)}, u32[]{:S(2)}, u32[]{:S(2)}) collective-permute-start(bf16[4,8192]{1,0:T(4,128)(2,1)S(1)} %get-tuple-element.51), channel_id=1, source_target_pairs={{0,12},{4,8},{8,4},{12,0},{1,13},{5,9},{9,5},{13,1},{2,14},{6,10},... | collective-permute-start | bytes 196616 | tf_op jit(solution)/shard_map/ppermute | solution.py:52
  38.6 0.7 %collective-permute-start.16 = (bf16[4,8192]{1,0:T(4,128)(2,1)S(1)}, bf16[4,8192]{1,0:T(4,128)(2,1)S(1)}, u32[]{:S(2)}, u32[]{:S(2)}) collective-permute-start(bf16[4,8192]{1,0:T(4,128)(2,1)S(1)} %get-tuple-element.51), channel_id=1, source_target_pairs={{0,8},{4,12},{8,0},{12,4},{1,9},{5,13},{9,1},{13,5},{2,10},{6,14},... | collective-permute-start | bytes 196616 | tf_op jit(solution)/shard_map/ppermute | solution.py:52
  39.3 0.0 collective-permute-done.15.refs_2_
  39.3 1.9 %collective-permute-start.17 = (bf16[4,8192]{1,0:T(4,128)(2,1)S(1)}, bf16[4,8192]{1,0:T(4,128)(2,1)S(1)}, u32[]{:S(2)}, u32[]{:S(2)}) collective-permute-start(bf16[4,8192]{1,0:T(4,128)(2,1)S(1)} %collective-permute-done.15.refs_2_), channel_id=1, source_target_pairs={{0,4},{4,0},{8,12},{12,8},{1,5},{5,1},{9,13},{13,9},{2,6},{6,2},{1... | collective-permute-start | bytes 196616 | tf_op jit(solution)/shard_map/ppermute | solution.py:52
  41.2 1.8 %collective-permute-done.18.refs_5_ = bf16[4,8192]{1,0:T(4,128)(2,1)S(1)} collective-permute-done((bf16[4,8192]{1,0:T(4,128)(2,1)S(1)}, bf16[4,8192]{1,0:T(4,128)(2,1)S(1)}, u32[]{:S(2)}, u32[]{:S(2)}) %collective-permute-start.18) | collective-permute-done | bytes 65568 | tf_op jit(solution)/shard_map/ppermute | solution.py:52
  43.0 1.4 %collective-permute-done.16.refs_3_ = bf16[4,8192]{1,0:T(4,128)(2,1)S(1)} collective-permute-done((bf16[4,8192]{1,0:T(4,128)(2,1)S(1)}, bf16[4,8192]{1,0:T(4,128)(2,1)S(1)}, u32[]{:S(2)}, u32[]{:S(2)}) %collective-permute-start.16) | collective-permute-done | bytes 65568 | tf_op jit(solution)/shard_map/ppermute | solution.py:52
  44.4 0.0 collective-permute-done.17.refs_4_
  44.4 0.0 collective-permute-done.14.refs_1_
  44.4 1.2 %score_parts.3.refs_0_ = f32[16,256]{1,0:T(8,128)S(1)} custom-call(bf16[4,16384]{1,0:T(4,128)(2,1)S(1)} %get-tuple-element.49.refs_0_.refs_3_, bf16[4,16384]{1,0:T(4,128)(2,1)S(1)} %collective-permute-done.14.refs_1_, bf16[4,8192]{1,0:T(4,128)(2,1)S(1)} %collective-permute-done.15.refs_2_, bf16[4,8192]{1,0:T(4,128)(2,1)S(1)} %collective-permute-done.16.refs_3_, ...), custom_call_target="tpu_custom_call" | custom-call | flops 134217728 | bytes 8388608 | tf_op jit(solution)/shard_map/score_parts/pallas_call | solution.py:188
  45.6 0.0 collective-permute-start.21
  45.6 1.3 %collective-permute-start.20 = (f32[16,256]{1,0:T(8,128)S(1)}, f32[16,256]{1,0:T(8,128)S(1)}, u32[]{:S(2)}, u32[]{:S(2)}) collective-permute-start(f32[16,256]{1,0:T(8,128)S(1)} %score_parts.3.refs_0_), channel_id=1, source_target_pairs={{0,2},{1,3},{2,0},{3,1},{4,6},{5,7},{6,4},{7,5},{8,10},{9,11},{10,... | collective-permute-start | bytes 49160 | tf_op jit(solution)/shard_map/ppermute | solution.py:129
  46.9 0.6 collective-permute-start.19
  47.5 1.3 %collective-permute-done.21.refs_3_ = f32[16,256]{1,0:T(8,128)S(1)} collective-permute-done((f32[16,256]{1,0:T(8,128)S(1)}, f32[16,256]{1,0:T(8,128)S(1)}, u32[]{:S(2)}, u32[]{:S(2)}) %collective-permute-start.21) | collective-permute-done | bytes 16416 | tf_op jit(solution)/shard_map/ppermute | solution.py:129
  48.8 0.6 collective-permute-done.20.refs_2_
  49.4 0.0 collective-permute-done.19.refs_1_
  49.4 0.7 %block_totals.4 = (bf16[16,4224]{1,0:T(8,128)(2,1)S(1)}, bf16[16,4224]{1,0:T(8,128)(2,1)S(1)}, bf16[16,2176]{1,0:T(8,128)(2,1)S(1)}, bf16[16,2176]{1,0:T(8,128)(2,1)S(1)}, f32[16,256]{1,0:T(8,128)S(1)}) custom-call(f32[16,256]{1,0:T(8,128)S(1)} %score_parts.3.refs_0_, f32[16,256]{1,0:T(8,128)S(1)} %collective-permute-done.19.refs_1_, ...), custom_call_target="tpu_custom_call" | custom-call | flops 67108864 | bytes 4194304 | tf_op jit(solution)/shard_map/block_totals/pallas_call | solution.py:295
  50.1 1.4 %collective-permute-start.25 = (bf16[16,2176]{1,0:T(8,128)(2,1)S(1)}, bf16[16,2176]{1,0:T(8,128)(2,1)S(1)}, u32[]{:S(2)}, u32[]{:S(2)}) collective-permute-start(bf16[16,2176]{1,0:T(8,128)(2,1)S(1)} %get-tuple-element.59), channel_id=1, source_target_pairs={{0,8},{4,12},{8,0},{12,4},{1,9},{5,13},{9,1},{13,5},{2,10},{6,14},... | collective-permute-start | bytes 208904 | tf_op jit(solution)/shard_map/ppermute | solution.py:52
  51.5 0.6 %block_totals.5 = (bf16[16,4224]{1,0:T(8,128)(2,1)S(1)}, bf16[16,4224]{1,0:T(8,128)(2,1)S(1)}, bf16[16,2048]{1,0:T(8,128)(2,1)S(1)}, bf16[16,2048]{1,0:T(8,128)(2,1)S(1)}) custom-call(f32[16,256]{1,0:T(8,128)S(1)} %get-tuple-element.52.weights_ref, bf16[256,16384]{1,0:T(8,128)(2,1)S(1)} %copy-done, ...), custom_call_target="tpu_custom_call", output_to_operand_aliasing={{0}: (2, {}), {1}: (3, {})} | custom-call | flops 67108864 | bytes 4194304 | tf_op jit(solution)/shard_map/block_totals/pallas_call | solution.py:295
  52.1 1.7 %collective-permute-start.23 = (bf16[16,2048]{1,0:T(8,128)(2,1)S(1)}, bf16[16,2048]{1,0:T(8,128)(2,1)S(1)}, u32[]{:S(2)}, u32[]{:S(2)}) collective-permute-start(bf16[16,2048]{1,0:T(8,128)(2,1)S(1)} %get-tuple-element.57), channel_id=1, source_target_pairs={{0,4},{4,0},{8,12},{12,8},{1,5},{5,1},{9,13},{13,9},{2,6},{6,2},{1... | collective-permute-start | bytes 196616 | tf_op jit(solution)/shard_map/ppermute | solution.py:52
  53.9 1.4 %collective-permute-start.26 = (bf16[16,2176]{1,0:T(8,128)(2,1)S(1)}, bf16[16,2176]{1,0:T(8,128)(2,1)S(1)}, u32[]{:S(2)}, u32[]{:S(2)}) collective-permute-start(bf16[16,2176]{1,0:T(8,128)(2,1)S(1)} %get-tuple-element.60), channel_id=1, source_target_pairs={{0,12},{4,8},{8,4},{12,0},{1,13},{5,9},{9,5},{13,1},{2,14},{6,10},... | collective-permute-start | bytes 208904 | tf_op jit(solution)/shard_map/ppermute | solution.py:52
  55.2 0.1 collective-permute-start.22
  55.4 2.0 %collective-permute-done.23.came_ref = bf16[16,2048]{1,0:T(8,128)(2,1)S(1)} collective-permute-done((bf16[16,2048]{1,0:T(8,128)(2,1)S(1)}, bf16[16,2048]{1,0:T(8,128)(2,1)S(1)}, u32[]{:S(2)}, u32[]{:S(2)}) %collective-permute-start.23) | collective-permute-done | bytes 65568 | tf_op jit(solution)/shard_map/ppermute | solution.py:52
  57.4 1.0 %collective-permute-start.24 = (bf16[16,2048]{1,0:T(8,128)(2,1)S(1)}, bf16[16,2048]{1,0:T(8,128)(2,1)S(1)}, u32[]{:S(2)}, u32[]{:S(2)}) collective-permute-start(bf16[16,2048]{1,0:T(8,128)(2,1)S(1)} %relay.3), channel_id=1, source_target_pairs={{0,8},{4,12},{8,0},{12,4},{1,9},{5,13},{9,1},{13,5},{2,10},{6,14},... | collective-permute-start | bytes 196616 | tf_op jit(solution)/shard_map/ppermute | solution.py:52
  58.5 0.0 collective-permute-done.25.in_ref
  58.5 2.4 %collective-permute-done.26.in_ref = bf16[16,2176]{1,0:T(8,128)(2,1)S(1)} collective-permute-done((bf16[16,2176]{1,0:T(8,128)(2,1)S(1)}, bf16[16,2176]{1,0:T(8,128)(2,1)S(1)}, u32[]{:S(2)}, u32[]{:S(2)}) %collective-permute-start.26) | collective-permute-done | bytes 69664 | tf_op jit(solution)/shard_map/ppermute | solution.py:52
  60.9 2.0 %collective-permute-done.24.refs_0_ = bf16[16,2048]{1,0:T(8,128)(2,1)S(1)} collective-permute-done((bf16[16,2048]{1,0:T(8,128)(2,1)S(1)}, bf16[16,2048]{1,0:T(8,128)(2,1)S(1)}, u32[]{:S(2)}, u32[]{:S(2)}) %collective-permute-start.24) | collective-permute-done | bytes 65568 | tf_op jit(solution)/shard_map/ppermute | solution.py:52
  62.9 0.1 collective-permute-done.22.near_ref
  63.1 0.9 %update.5 = f32[4,16384]{1,0:T(4,128)} custom-call(bf16[16,4224]{1,0:T(8,128)(2,1)S(1)} %get-tuple-element.55.own_ref, bf16[16,4224]{1,0:T(8,128)(2,1)S(1)} %collective-permute-done.22.near_ref, bf16[16,2048]{1,0:T(8,128)(2,1)S(1)} %collective-permute-done.24.refs_0_, bf16[16,2176]{1,0:T(8,128)(2,1)S(1)} %early.6.refs_1_, ...), custom_call_target="tpu_custom_call" | custom-call | flops 540672 | bytes 811008 | tf_op jit(solution)/shard_map/update/pallas_call | solution.py:397
  (8 shorter events, 0.1 us)
Async XLA Ops:
  0.0 11.2 %copy-start = (bf16[256,16384]{1,0:T(8,128)(2,1)S(1)}, bf16[256,16384]{1,0:T(8,128)(2,1)}, u32[]{:S(2)}) copy-start(bf16[256,16384]{1,0:T(8,128)(2,1)} %frames_ref) | copy-start | bytes 25165828
  1.1 7.6 %collective-permute-start.1 = (bf16[4,8192]{1,0:T(4,128)(2,1)S(1)}, bf16[4,8192]{1,0:T(4,128)(2,1)S(1)}, u32[]{:S(2)}, u32[]{:S(2)}) collective-permute-start(bf16[4,8192]{1,0:T(4,128)(2,1)S(1)} %get-tuple-element.34), channel_id=1, source_target_pairs={{0,8},{4,12},{8,0},{12,4},{1,9},{5,13},{9,1},{13,5},{2,10},{6,14},... | collective-permute-start | bytes 196616 | tf_op jit(solution)/shard_map/ppermute | solution.py:52
  5.2 9.6 %collective-permute-start = (bf16[4,16384]{1,0:T(4,128)(2,1)S(1)}, bf16[4,16384]{1,0:T(4,128)(2,1)S(1)}, u32[]{:S(2)}, u32[]{:S(2)}) collective-permute-start(bf16[4,16384]{1,0:T(4,128)(2,1)S(1)} %get-tuple-element.33.refs_0_.owned_ref), channel_id=1, source_target_pairs={{0,4},{4,0},{8,12},{12,8},{1,5},{5,1},{9,13},{13,9},{2,6},{6,2},{1... | collective-permute-start | bytes 393224 | tf_op jit(solution)/shard_map/ppermute | solution.py:52
  6.8 6.9 %collective-permute-start.4 = (bf16[4,8192]{1,0:T(4,128)(2,1)S(1)}, bf16[4,8192]{1,0:T(4,128)(2,1)S(1)}, u32[]{:S(2)}, u32[]{:S(2)}) collective-permute-start(bf16[4,8192]{1,0:T(4,128)(2,1)S(1)} %get-tuple-element.35), channel_id=1, source_target_pairs={{0,12},{4,8},{8,4},{12,0},{1,13},{5,9},{9,5},{13,1},{2,14},{6,10},... | collective-permute-start | bytes 196616 | tf_op jit(solution)/shard_map/ppermute | solution.py:52
  6.8 7.4 %collective-permute-start.2 = (bf16[4,8192]{1,0:T(4,128)(2,1)S(1)}, bf16[4,8192]{1,0:T(4,128)(2,1)S(1)}, u32[]{:S(2)}, u32[]{:S(2)}) collective-permute-start(bf16[4,8192]{1,0:T(4,128)(2,1)S(1)} %get-tuple-element.35), channel_id=1, source_target_pairs={{0,8},{4,12},{8,0},{12,4},{1,9},{5,13},{9,1},{13,5},{2,10},{6,14},... | collective-permute-start | bytes 196616 | tf_op jit(solution)/shard_map/ppermute | solution.py:52
  8.7 6.1 %collective-permute-start.3 = (bf16[4,8192]{1,0:T(4,128)(2,1)S(1)}, bf16[4,8192]{1,0:T(4,128)(2,1)S(1)}, u32[]{:S(2)}, u32[]{:S(2)}) collective-permute-start(bf16[4,8192]{1,0:T(4,128)(2,1)S(1)} %collective-permute-done.1.refs_2_), channel_id=1, source_target_pairs={{0,4},{4,0},{8,12},{12,8},{1,5},{5,1},{9,13},{13,9},{2,6},{6,2},{1... | collective-permute-start | bytes 196616 | tf_op jit(solution)/shard_map/ppermute | solution.py:52
  16.0 3.2 %collective-permute-start.7 = (f32[16,256]{1,0:T(8,128)S(1)}, f32[16,256]{1,0:T(8,128)S(1)}, u32[]{:S(2)}, u32[]{:S(2)}) collective-permute-start(f32[16,256]{1,0:T(8,128)S(1)} %score_parts.2.refs_0_), channel_id=1, source_target_pairs={{0,3},{1,2},{2,1},{3,0},{4,7},{5,6},{6,5},{7,4},{8,11},{9,10},{10,... | collective-permute-start | bytes 49160 | tf_op jit(solution)/shard_map/ppermute | solution.py:129
  16.7 3.7 %collective-permute-start.6 = (f32[16,256]{1,0:T(8,128)S(1)}, f32[16,256]{1,0:T(8,128)S(1)}, u32[]{:S(2)}, u32[]{:S(2)}) collective-permute-start(f32[16,256]{1,0:T(8,128)S(1)} %score_parts.2.refs_0_), channel_id=1, source_target_pairs={{0,2},{1,3},{2,0},{3,1},{4,6},{5,7},{6,4},{7,5},{8,10},{9,11},{10,... | collective-permute-start | bytes 49160 | tf_op jit(solution)/shard_map/ppermute | solution.py:129
  17.8 2.6 %collective-permute-start.5 = (f32[16,256]{1,0:T(8,128)S(1)}, f32[16,256]{1,0:T(8,128)S(1)}, u32[]{:S(2)}, u32[]{:S(2)}) collective-permute-start(f32[16,256]{1,0:T(8,128)S(1)} %score_parts.2.refs_0_), channel_id=1, source_target_pairs={{0,1},{1,0},{2,3},{3,2},{4,5},{5,4},{6,7},{7,6},{8,9},{9,8},{10,11... | collective-permute-start | bytes 49160 | tf_op jit(solution)/shard_map/ppermute | solution.py:129
  21.6 8.6 %collective-permute-start.8 = (bf16[16,2176]{1,0:T(8,128)(2,1)S(1)}, bf16[16,2176]{1,0:T(8,128)(2,1)S(1)}, u32[]{:S(2)}, u32[]{:S(2)}) collective-permute-start(bf16[16,2176]{1,0:T(8,128)(2,1)S(1)} %get-tuple-element.40), channel_id=1, source_target_pairs={{0,8},{4,12},{8,0},{12,4},{1,9},{5,13},{9,1},{13,5},{2,10},{6,14},... | collective-permute-start | bytes 208904 | tf_op jit(solution)/shard_map/ppermute | solution.py:52
  23.0 5.6 %collective-permute-start.11 = (bf16[16,2048]{1,0:T(8,128)(2,1)S(1)}, bf16[16,2048]{1,0:T(8,128)(2,1)S(1)}, u32[]{:S(2)}, u32[]{:S(2)}) collective-permute-start(bf16[16,2048]{1,0:T(8,128)(2,1)S(1)} %get-tuple-element.44), channel_id=1, source_target_pairs={{0,4},{4,0},{8,12},{12,8},{1,5},{5,1},{9,13},{13,9},{2,6},{6,2},{1... | collective-permute-start | bytes 196616 | tf_op jit(solution)/shard_map/ppermute | solution.py:52
  24.8 7.9 %collective-permute-start.10 = (bf16[16,2176]{1,0:T(8,128)(2,1)S(1)}, bf16[16,2176]{1,0:T(8,128)(2,1)S(1)}, u32[]{:S(2)}, u32[]{:S(2)}) collective-permute-start(bf16[16,2176]{1,0:T(8,128)(2,1)S(1)} %get-tuple-element.43), channel_id=1, source_target_pairs={{0,4},{4,0},{8,12},{12,8},{1,5},{5,1},{9,13},{13,9},{2,6},{6,2},{1... | collective-permute-start | bytes 208904 | tf_op jit(solution)/shard_map/ppermute | solution.py:52
  25.0 7.6 %collective-permute-start.13 = (bf16[16,2176]{1,0:T(8,128)(2,1)S(1)}, bf16[16,2176]{1,0:T(8,128)(2,1)S(1)}, u32[]{:S(2)}, u32[]{:S(2)}) collective-permute-start(bf16[16,2176]{1,0:T(8,128)(2,1)S(1)} %get-tuple-element.47), channel_id=1, source_target_pairs={{0,12},{4,8},{8,4},{12,0},{1,13},{5,9},{9,5},{13,1},{2,14},{6,10},... | collective-permute-start | bytes 208904 | tf_op jit(solution)/shard_map/ppermute | solution.py:52
  28.6 7.0 %collective-permute-start.12 = (bf16[16,2048]{1,0:T(8,128)(2,1)S(1)}, bf16[16,2048]{1,0:T(8,128)(2,1)S(1)}, u32[]{:S(2)}, u32[]{:S(2)}) collective-permute-start(bf16[16,2048]{1,0:T(8,128)(2,1)S(1)} %relay.2), channel_id=1, source_target_pairs={{0,8},{4,12},{8,0},{12,4},{1,9},{5,13},{9,1},{13,5},{2,10},{6,14},... | collective-permute-start | bytes 196616 | tf_op jit(solution)/shard_map/ppermute | solution.py:52
  30.2 5.3 %collective-permute-start.9 = (bf16[16,2048]{1,0:T(8,128)(2,1)S(1)}, bf16[16,2048]{1,0:T(8,128)(2,1)S(1)}, u32[]{:S(2)}, u32[]{:S(2)}) collective-permute-start(bf16[16,2048]{1,0:T(8,128)(2,1)S(1)} %get-tuple-element.42), channel_id=1, source_target_pairs={{0,4},{4,0},{8,12},{12,8},{1,5},{5,1},{9,13},{13,9},{2,6},{6,2},{1... | collective-permute-start | bytes 196616 | tf_op jit(solution)/shard_map/ppermute | solution.py:52
  32.8 6.5 %collective-permute-start.15 = (bf16[4,8192]{1,0:T(4,128)(2,1)S(1)}, bf16[4,8192]{1,0:T(4,128)(2,1)S(1)}, u32[]{:S(2)}, u32[]{:S(2)}) collective-permute-start(bf16[4,8192]{1,0:T(4,128)(2,1)S(1)} %get-tuple-element.50), channel_id=1, source_target_pairs={{0,8},{4,12},{8,0},{12,4},{1,9},{5,13},{9,1},{13,5},{2,10},{6,14},... | collective-permute-start | bytes 196616 | tf_op jit(solution)/shard_map/ppermute | solution.py:52
  35.7 8.7 %collective-permute-start.14 = (bf16[4,16384]{1,0:T(4,128)(2,1)S(1)}, bf16[4,16384]{1,0:T(4,128)(2,1)S(1)}, u32[]{:S(2)}, u32[]{:S(2)}) collective-permute-start(bf16[4,16384]{1,0:T(4,128)(2,1)S(1)} %get-tuple-element.49.refs_0_.refs_3_), channel_id=1, source_target_pairs={{0,4},{4,0},{8,12},{12,8},{1,5},{5,1},{9,13},{13,9},{2,6},{6,2},{1... | collective-permute-start | bytes 393224 | tf_op jit(solution)/shard_map/ppermute | solution.py:52
  36.8 6.2 %collective-permute-start.18 = (bf16[4,8192]{1,0:T(4,128)(2,1)S(1)}, bf16[4,8192]{1,0:T(4,128)(2,1)S(1)}, u32[]{:S(2)}, u32[]{:S(2)}) collective-permute-start(bf16[4,8192]{1,0:T(4,128)(2,1)S(1)} %get-tuple-element.51), channel_id=1, source_target_pairs={{0,12},{4,8},{8,4},{12,0},{1,13},{5,9},{9,5},{13,1},{2,14},{6,10},... | collective-permute-start | bytes 196616 | tf_op jit(solution)/shard_map/ppermute | solution.py:52
  38.6 5.9 %collective-permute-start.16 = (bf16[4,8192]{1,0:T(4,128)(2,1)S(1)}, bf16[4,8192]{1,0:T(4,128)(2,1)S(1)}, u32[]{:S(2)}, u32[]{:S(2)}) collective-permute-start(bf16[4,8192]{1,0:T(4,128)(2,1)S(1)} %get-tuple-element.51), channel_id=1, source_target_pairs={{0,8},{4,12},{8,0},{12,4},{1,9},{5,13},{9,1},{13,5},{2,10},{6,14},... | collective-permute-start | bytes 196616 | tf_op jit(solution)/shard_map/ppermute | solution.py:52
  39.3 5.1 %collective-permute-start.17 = (bf16[4,8192]{1,0:T(4,128)(2,1)S(1)}, bf16[4,8192]{1,0:T(4,128)(2,1)S(1)}, u32[]{:S(2)}, u32[]{:S(2)}) collective-permute-start(bf16[4,8192]{1,0:T(4,128)(2,1)S(1)} %collective-permute-done.15.refs_2_), channel_id=1, source_target_pairs={{0,4},{4,0},{8,12},{12,8},{1,5},{5,1},{9,13},{13,9},{2,6},{6,2},{1... | collective-permute-start | bytes 196616 | tf_op jit(solution)/shard_map/ppermute | solution.py:52
  45.6 3.2 %collective-permute-start.21 = (f32[16,256]{1,0:T(8,128)S(1)}, f32[16,256]{1,0:T(8,128)S(1)}, u32[]{:S(2)}, u32[]{:S(2)}) collective-permute-start(f32[16,256]{1,0:T(8,128)S(1)} %score_parts.3.refs_0_), channel_id=1, source_target_pairs={{0,3},{1,2},{2,1},{3,0},{4,7},{5,6},{6,5},{7,4},{8,11},{9,10},{10,... | collective-permute-start | bytes 49160 | tf_op jit(solution)/shard_map/ppermute | solution.py:129
  45.6 3.8 %collective-permute-start.20 = (f32[16,256]{1,0:T(8,128)S(1)}, f32[16,256]{1,0:T(8,128)S(1)}, u32[]{:S(2)}, u32[]{:S(2)}) collective-permute-start(f32[16,256]{1,0:T(8,128)S(1)} %score_parts.3.refs_0_), channel_id=1, source_target_pairs={{0,2},{1,3},{2,0},{3,1},{4,6},{5,7},{6,4},{7,5},{8,10},{9,11},{10,... | collective-permute-start | bytes 49160 | tf_op jit(solution)/shard_map/ppermute | solution.py:129
  46.9 2.5 %collective-permute-start.19 = (f32[16,256]{1,0:T(8,128)S(1)}, f32[16,256]{1,0:T(8,128)S(1)}, u32[]{:S(2)}, u32[]{:S(2)}) collective-permute-start(f32[16,256]{1,0:T(8,128)S(1)} %score_parts.3.refs_0_), channel_id=1, source_target_pairs={{0,1},{1,0},{2,3},{3,2},{4,5},{5,4},{6,7},{7,6},{8,9},{9,8},{10,11... | collective-permute-start | bytes 49160 | tf_op jit(solution)/shard_map/ppermute | solution.py:129
  50.1 8.4 %collective-permute-start.25 = (bf16[16,2176]{1,0:T(8,128)(2,1)S(1)}, bf16[16,2176]{1,0:T(8,128)(2,1)S(1)}, u32[]{:S(2)}, u32[]{:S(2)}) collective-permute-start(bf16[16,2176]{1,0:T(8,128)(2,1)S(1)} %get-tuple-element.59), channel_id=1, source_target_pairs={{0,8},{4,12},{8,0},{12,4},{1,9},{5,13},{9,1},{13,5},{2,10},{6,14},... | collective-permute-start | bytes 208904 | tf_op jit(solution)/shard_map/ppermute | solution.py:52
  52.1 5.3 %collective-permute-start.23 = (bf16[16,2048]{1,0:T(8,128)(2,1)S(1)}, bf16[16,2048]{1,0:T(8,128)(2,1)S(1)}, u32[]{:S(2)}, u32[]{:S(2)}) collective-permute-start(bf16[16,2048]{1,0:T(8,128)(2,1)S(1)} %get-tuple-element.57), channel_id=1, source_target_pairs={{0,4},{4,0},{8,12},{12,8},{1,5},{5,1},{9,13},{13,9},{2,6},{6,2},{1... | collective-permute-start | bytes 196616 | tf_op jit(solution)/shard_map/ppermute | solution.py:52
  53.9 7.0 %collective-permute-start.26 = (bf16[16,2176]{1,0:T(8,128)(2,1)S(1)}, bf16[16,2176]{1,0:T(8,128)(2,1)S(1)}, u32[]{:S(2)}, u32[]{:S(2)}) collective-permute-start(bf16[16,2176]{1,0:T(8,128)(2,1)S(1)} %get-tuple-element.60), channel_id=1, source_target_pairs={{0,12},{4,8},{8,4},{12,0},{1,13},{5,9},{9,5},{13,1},{2,14},{6,10},... | collective-permute-start | bytes 208904 | tf_op jit(solution)/shard_map/ppermute | solution.py:52
  55.2 7.8 %collective-permute-start.22 = (bf16[16,4224]{1,0:T(8,128)(2,1)S(1)}, bf16[16,4224]{1,0:T(8,128)(2,1)S(1)}, u32[]{:S(2)}, u32[]{:S(2)}) collective-permute-start(bf16[16,4224]{1,0:T(8,128)(2,1)S(1)} %get-tuple-element.56), channel_id=1, source_target_pairs={{0,4},{4,0},{8,12},{12,8},{1,5},{5,1},{9,13},{13,9},{2,6},{6,2},{1... | collective-permute-start | bytes 405512 | tf_op jit(solution)/shard_map/ppermute | solution.py:52
  57.4 5.5 %collective-permute-start.24 = (bf16[16,2048]{1,0:T(8,128)(2,1)S(1)}, bf16[16,2048]{1,0:T(8,128)(2,1)S(1)}, u32[]{:S(2)}, u32[]{:S(2)}) collective-permute-start(bf16[16,2048]{1,0:T(8,128)(2,1)S(1)} %relay.3), channel_id=1, source_target_pairs={{0,8},{4,12},{8,0},{12,4},{1,9},{5,13},{9,1},{13,5},{2,10},{6,14},... | collective-permute-start | bytes 196616 | tf_op jit(solution)/shard_map/ppermute | solution.py:52
